TPU v7x, 512 devices: a whole 4x4x16 slice. The times are simulated.
512 devices in a mesh: dp: 32 (over z_lo, x), mp: 16 (over y, z_hi, core).
Axes of the slice: x: 4, y: 4, z: 16 (z_hi: 2, z_lo: 8; z = z_hi * 8 + z_lo), core: 2. Of those that a mesh axis runs over, the one named last changes fastest.
Arguments:
- queries: bfloat16 [32, 512, 2048], P('dp', 'mp'), may hold values from -6 to 6
- keys: bfloat16 [32, 512, 1024], P('dp'), may hold values from -6 to 6
- values: bfloat16 [32, 512, 1024], P('dp'), may hold values from -6 to 6
- stream: bfloat16 [32, 512, 3584], P('dp', None, 'mp'), may hold values from -6 to 6
- out_proj: bfloat16 [2048, 3584], P(None, 'mp'), may hold values from -0.125 to 0.125
- norm_gain: float32 [3584], P('mp'), may hold values from 0.1 to 1.9
- tag_proj: bfloat16 [3584, 128], P('mp'), may hold values from -0.03125 to 0.03125
- direction: float32 [2048, 3584], P('dp', 'mp'), may hold values from -120 to 120
- starts: int32 [32, 4], P('dp'), may hold values from 0 to 511, as said below
- tags: int32 [32, 512], P('dp'), may hold values from 0 to 127
Outputs:
- iterate: float32 [2048, 3584], P('dp', 'mp')
Inputs may be any that keep to these rules, and one draw needn't show every extreme that they name: `starts`: each sequence's first entry is 0 and the entries rise strictly, so every file holds one token or more.
All inputs are finite; a program needn't handle non-finite values.
Results may differ from a plain program's by a relative error of at most 0.0032.
Values may be sent and summed in bfloat16 or wider, within the bound.
No kernel may reach another device: no remote copies, remote signals or barrier semaphores. Data moves between devices by JAX's collectives and lax.ppermute only.
A program may use at most 64 MiB of HBM per device.

v0:
```python
import jax
import jax.numpy as jnp
from jax import lax
from jax.sharding import PartitionSpec as P

D = 3584
HD = 256
HQ = 8
HK = 4
TAGS = 128
WINDOW = 256
ITERS = 2


DAMP = 0.01
NORM_EPS = 1e-06
MEAN_EPS = 1e-06


def attend(query, key, value, start, offset):
    num_q = query.shape[0]
    num_k = key.shape[0]
    group = HQ // HK
    q_heads = query.reshape(num_q, HK, group, HD)
    k_heads = key.reshape(num_k, HK, HD)
    v_heads = value.reshape(num_k, HK, HD)
    scores = jnp.einsum(
        "qgrd,kgd->grqk", q_heads, k_heads, preferred_element_type=jnp.float32
    ) / jnp.sqrt(jnp.float32(HD))
    scores = 50.0 * jnp.tanh(scores / 50.0)
    q_pos = offset + jnp.arange(num_q, dtype=jnp.int32)
    k_pos = jnp.arange(num_k, dtype=jnp.int32)
    q_file = jnp.sum((start[None, :] <= q_pos[:, None]).astype(jnp.int32), 1) - 1
    k_file = jnp.sum((start[None, :] <= k_pos[:, None]).astype(jnp.int32), 1) - 1
    allowed = (
        (q_file[:, None] == k_file[None, :])
        & (k_pos[None, :] <= q_pos[:, None])
        & (q_pos[:, None] - k_pos[None, :] < WINDOW)
    )
    expo = jnp.where(allowed[None, None], jnp.exp(scores), 0.0)
    weights = (expo / jnp.sum(expo, -1, keepdims=True)).astype(jnp.bfloat16)
    out = jnp.einsum("grqk,kgd->qgrd", weights, v_heads, preferred_element_type=jnp.float32)
    return out.reshape(num_q, HQ * HD).astype(jnp.bfloat16)


def local(queries, keys, values, stream, out_proj, norm_gain, tag_proj, direction, starts, tags):
    q_rows = queries.shape[1]
    offset = lax.axis_index("mp") * q_rows
    local_out = attend(queries[0], keys[0], values[0], starts[0], offset)
    attn = lax.all_gather(local_out[None], "mp", axis=1, tiled=True)[0]
    count = HQ * HD * D
    early_norm = lax.psum(jnp.sum(direction * direction), ("dp", "mp"))
    h_loc = stream[0].astype(jnp.float32) + jnp.dot(
        attn, out_proj, preferred_element_type=jnp.float32
    )
    wide = tag_proj.astype(jnp.float32)
    sumsq, zval = lax.psum(
        (
            jnp.sum(h_loc * h_loc, -1),
            jnp.dot(h_loc * norm_gain, wide, precision=lax.Precision.HIGHEST),
        ),
        "mp",
    )
    rscale = (sumsq / D + NORM_EPS) ** (-0.5)
    tanh_val = jnp.tanh(rscale[:, None] * zval / 30.0)
    slope = 1.0 - tanh_val * tanh_val
    expo = jnp.exp(30.0 * tanh_val)
    probs = expo / jnp.sum(expo, -1, keepdims=True)
    onehot = (tags[0][:, None] == jnp.arange(TAGS, dtype=jnp.int32)[None, :]).astype(jnp.float32)
    dlogit = probs - onehot
    wgrad = dlogit * slope
    rho = jnp.sum(wgrad * zval, -1)
    cube = rscale**3 / D
    sigma = jnp.float32(1.0)
    current = direction
    for step in range(ITERS):
        hdot = jnp.dot(
            attn,
            lax.all_gather(current.astype(jnp.bfloat16), "dp", axis=0, tiled=True),
            preferred_element_type=jnp.float32,
        )
        along, zdot = lax.psum(
            (
                jnp.sum(h_loc * hdot, -1),
                jnp.dot(hdot * norm_gain, wide, precision=lax.Precision.HIGHEST),
            ),
            "mp",
        )
        rdot = -cube * along
        mdot = rdot[:, None] * zval + rscale[:, None] * zdot
        ldot = slope * mdot
        pdot = probs * (ldot - jnp.sum(probs * ldot, -1, keepdims=True))
        wdot = pdot * slope - dlogit * 2.0 * tanh_val * slope * mdot / 30.0
        rhodot = jnp.sum(wdot * zval + wgrad * zdot, -1)
        mixed = rdot[:, None] * wgrad + rscale[:, None] * wdot
        back = jnp.dot(mixed, wide.T, precision=lax.Precision.HIGHEST) * norm_gain
        coeff = rhodot * cube + 3.0 * rho * rscale * rscale * rdot / D
        curvature_gdot = back - coeff[:, None] * h_loc - (rho * cube)[:, None] * hdot
        gdot = curvature_gdot.astype(jnp.bfloat16)
        hvp_rows = lax.psum_scatter(
            lax.dot_general(
                attn, gdot, (((0,), (0,)), ((), ())), preferred_element_type=jnp.float32
            ),
            "dp",
            scatter_dimension=0,
            tiled=True,
        )
        if step == 0:
            product_sq = lax.psum(jnp.sum(hvp_rows * hvp_rows), ("dp", "mp"))
            sigma = 2.0 * jnp.sqrt(
                (product_sq / count + MEAN_EPS) / (early_norm / count + MEAN_EPS)
            )
        current = direction + (1.0 - DAMP) * current - hvp_rows / sigma
    return current


def solution(mesh):
    return jax.shard_map(
        local,
        mesh=mesh,
        in_specs=(
            P("dp", "mp", None),
            P("dp", None, None),
            P("dp", None, None),
            P("dp", None, "mp"),
            P(None, "mp"),
            P("mp"),
            P("mp", None),
            P("dp", "mp"),
            P("dp", None),
            P("dp", None),
        ),
        out_specs=P("dp", "mp"),
        check_vma=False,
    )
```

profile of v0, /device:TPU:16, one launch (start us, length us, event | category | flops | bytes accessed | tf_op | source)
XLA Modules:
  0.0 1408.4 jit_solution(14377447355392589989)
XLA Ops:
  6.5 0.0 copy-start
  6.5 0.0 all-gather.2.cloned.1.call-start
  6.5 0.9 convert_reduce_fusion
  7.4 0.7 convert_reduce_fusion.1
  8.2 1.0 reshape_squeeze.10
  9.2 2.7 reshape_squeeze.9
  11.8 0.0 copy-done.6
  11.8 0.8 reshape_squeeze.11
  12.6 0.1 fusion.56
  12.7 1.7 fusion.14
  14.4 0.0 copy-start.7
  14.4 0.4 fusion.24
  14.8 0.1 copy.21
  14.9 0.7 convert_element_type.52
  15.7 0.0 all-gather.2.cloned.1.call-update
  15.7 0.0 all-reduce.8.cloned.1.call-start
  15.7 0.0 copy-done.7
  15.7 0.6 multiply_reduce_fusion.6
  16.4 145.8 %all_gather.10 = bf16[2048,224]{1,0:T(8,128)(2,1)} all-gather(bf16[64,224]{1,0:T(8,128)(2,1)S(1)} %get-tuple-element.16), channel_id=1, replica_groups=mesh['dp'=32,'mp'=16] {'dp'}, dimensions={0}, use_global_device_ids=true | all-gather | bytes 946176 | tf_op jit(solution)/shard_map/all_gather | solution.py:79
  162.2 2.8 fusion.6
  165.0 0.0 copy-done.9
  165.0 0.0 copy-done.14
  165.1 1.4 fusion.29
  166.4 0.0 copy-done
  166.4 0.0 copy-done.20
  166.5 1.4 multiply_reduce_fusion.1
  167.9 1.4 fusion.31
  169.3 0.0 all-reduce.8.cloned.1.call-update
  169.3 0.0 reduce-scatter.3.cloned.1.call-start
  169.3 57.4 %all-reduce.1 = (f32[512]{0:T(512)S(1)}, f32[512]{0:T(512)S(1)}) all-reduce(f32[512]{0:T(512)} %get-tuple-element.6, f32[512]{0:T(512)S(1)} %get-tuple-element.5), channel_id=1, replica_groups=mesh['dp'=32,'mp'=16] {'mp'}, use_global_device_ids=true, to_apply=%region_4.5 | all-reduce | flops 1024 | bytes 8192 | tf_op jit(solution)/shard_map/psum | solution.py:57
  226.7 183.7 %all-reduce.8.cloned.1.call-done = (f32[512,128]{1,0:T(8,128)}, f32[512,128]{1,0:T(8,128)}) async-done(((f32[512,128]{1,0:T(8,128)}, f32[512,128]{1,0:T(8,128)}), (f32[512,128]{1,0:T(8,128)}, f32[512,128]{1,0:T(8,128)})) %all-reduce.8.cloned.1.call-update) | async-done | bytes 524304 | tf_op jit(solution)/shard_map/psum | solution.py:82
  410.5 0.0 copy-done.17
  410.5 1.2 fusion.45
  411.7 1.4 multiply_reduce_fusion.5
  413.1 1.6 add_reduce_fusion.1
  414.7 0.7 multiply_add_fusion.4
  415.4 0.6 copy-done.18
  416.0 2.0 fusion.23
  418.0 2.1 fusion.4
  420.1 0.0 reduce-scatter.3.cloned.1.call-update
  420.1 0.0 all-reduce.6.cloned.1.call-start
  420.2 252.8 %reduce-scatter.3.cloned.1.call-done = f32[64,224]{1,0:T(8,128)} async-done(((f32[2048,224]{1,0:T(8,128)}), f32[64,224]{1,0:T(8,128)}) %reduce-scatter.3.cloned.1.call-update) | async-done | bytes 57360 | tf_op jit(solution)/shard_map/reduce_scatter | solution.py:100
  672.9 1.5 multiply_reduce_fusion.7
  674.4 98.3 %all-reduce = (f32[]{:T(128)}, f32[]{:T(128)}) all-reduce(f32[]{:T(128)} %multiply_reduce_fusion.7, f32[]{:T(128)} %get-tuple-element.15), channel_id=1, replica_groups=mesh['dp'=32,'mp'=16] {'dp','mp'}, use_global_device_ids=true, to_apply=%region_15.16 | all-reduce | flops 2 | bytes 16 | tf_op jit(solution)/shard_map/psum | solution.py:109
  774.0 0.9 fusion.57
  774.9 119.3 %all_gather.11 = bf16[2048,224]{1,0:T(8,128)(2,1)S(1)} all-gather(bf16[64,224]{1,0:T(8,128)(2,1)S(1)} %fusion.57), channel_id=1, replica_groups=mesh['dp'=32,'mp'=16] {'dp'}, dimensions={0}, use_global_device_ids=true | all-gather | bytes 946176 | tf_op jit(solution)/shard_map/all_gather | solution.py:79
  894.2 0.0 copy-start.19
  894.2 1.9 multiply_reduce_fusion
  896.1 0.0 copy-start.4
  896.1 0.8 copy-done.4
  896.9 0.0 copy-done.15
  896.9 1.4 fusion.27
  898.2 0.0 all-reduce.6.cloned.1.call-update
  898.3 0.0 reduce-scatter.5.cloned.1.call-start
  898.3 57.4 %psum.62 = f32[512]{0:T(512)S(1)} all-reduce(f32[512]{0:T(512)S(1)} %get-tuple-element.22), channel_id=1, replica_groups=mesh['dp'=32,'mp'=16] {'mp'}, use_global_device_ids=true, to_apply=%region_19.20 | all-reduce | flops 512 | bytes 4096 | tf_op jit(solution)/shard_map/psum | solution.py:82
  955.7 184.4 %all-reduce.6.cloned.1.call-done = f32[512,128]{1,0:T(8,128)} async-done(((f32[512,128]{1,0:T(8,128)}), f32[512,128]{1,0:T(8,128)}) %all-reduce.6.cloned.1.call-update) | async-done | bytes 262160 | tf_op jit(solution)/shard_map/psum | solution.py:82
  1140.1 1.3 multiply_reduce_fusion.3
  1141.4 1.5 add_reduce_fusion
  1142.9 0.0 copy-done.19
  1142.9 2.0 fusion.22
  1144.9 2.1 fusion
  1147.0 0.0 reduce-scatter.5.cloned.1.call-update
  1147.1 253.4 %reduce-scatter.5.cloned.1.call-done = f32[64,224]{1,0:T(8,128)} async-done(((f32[2048,224]{1,0:T(8,128)}), f32[64,224]{1,0:T(8,128)}) %reduce-scatter.5.cloned.1.call-update) | async-done | bytes 57360 | tf_op jit(solution)/shard_map/reduce_scatter | solution.py:100
  1400.4 1.5 divide_subtract_fusion
  (34 shorter events, 0.1 us)
Async XLA Ops:
  6.5 159.9 %copy-start = (bf16[2048,224]{0,1:T(8,128)(2,1)S(1)}, bf16[2048,224]{0,1:T(8,128)(2,1)}, u32[]{:S(2)}) copy-start(bf16[2048,224]{0,1:T(8,128)(2,1)} %param.14) | copy-start | bytes 2752516
  6.5 5.3 copy-start.6
  6.5 155.7 %all-gather.2.cloned.1.call-start = ((), (), s32[]{:S(2)}) async-start(), calls=%async_computation.2 | async-start | bytes 2228224 | tf_op jit(solution)/shard_map/all_gather | solution.py:50
  14.4 1.3 copy-start.7
  15.7 394.8 %all-reduce.8.cloned.1.call-start = ((), (), s32[]{:S(2)}) async-start(), calls=%async_computation.6 | async-start | bytes 1048576 | tf_op jit(solution)/shard_map/psum | solution.py:82
  16.3 148.7 %copy-start.9 = (bf16[224,128]{1,0:T(8,128)(2,1)S(1)}, bf16[224,128]{1,0:T(8,128)(2,1)}, u32[]{:S(2)}) copy-start(bf16[224,128]{1,0:T(8,128)(2,1)} %param.16) | copy-start | bytes 172036
  16.4 148.7 %copy-start.14 = (f32[224]{0:T(256)S(1)}, f32[224]{0:T(256)}, u32[]{:S(2)}) copy-start(f32[224]{0:T(256)} %param.15) | copy-start | bytes 2692
  162.2 4.3 copy-start.1
  162.2 4.3 copy-start.20
  165.1 2.8 copy-start.5
  166.4 1.4 copy-start.10
  167.9 250.1 %copy-start.3 = (f32[512,224]{0,1:T(8,128)}, f32[512,224]{0,1:T(8,128)S(1)}, u32[]{:S(2)}) copy-start(f32[512,224]{0,1:T(8,128)S(1)} %get-tuple-element.21) | copy-start | bytes 1376260
  169.3 503.6 %reduce-scatter.3.cloned.1.call-start = ((), (), s32[]{:S(2)}) async-start(), calls=%async_computation.3 | async-start | bytes 2162688 | tf_op jit(solution)/shard_map/reduce_scatter | solution.py:100
  226.7 183.7 %copy-start.17 = (f32[512]{0:T(512)}, f32[512]{0:T(512)S(1)}, u32[]{:S(2)}) copy-start(f32[512]{0:T(512)S(1)} %get-tuple-element.12) | copy-start | bytes 6148
  414.7 0.7 copy-start.12
  415.4 0.6 copy-start.18
  420.1 720.0 %all-reduce.6.cloned.1.call-start = ((), (), s32[]{:S(2)}) async-start(), calls=%async_computation.4 | async-start | bytes 524288 | tf_op jit(solution)/shard_map/psum | solution.py:82
  894.2 2.7 copy-start.11
  894.2 2.7 copy-start.15
  894.2 245.9 %copy-start.2 = (f32[512,128]{1,0:T(8,128)S(1)}, f32[512,128]{1,0:T(8,128)}, u32[]{:S(2)}) copy-start(f32[512,128]{1,0:T(8,128)} %get-tuple-element.14) | copy-start | bytes 786436
  894.2 247.2 %copy-start.16 = (s32[1,512]{1,0:T(1,128)S(1)}, s32[1,512]{1,0:T(1,128)}, u32[]{:S(2)}) copy-start(s32[1,512]{1,0:T(1,128)} %param.19) | copy-start | bytes 6148
  894.2 248.7 %copy-start.13 = (f32[512]{0:T(512)S(1)}, f32[512]{0:T(512)}, u32[]{:S(2)}) copy-start(f32[512]{0:T(512)} %copy-done.12) | copy-start | bytes 6148
  894.2 248.7 %copy-start.19 = (f32[512]{0:T(512)S(1)}, f32[512]{0:T(512)}, u32[]{:S(2)}) copy-start(f32[512]{0:T(512)} %copy-done.18) | copy-start | bytes 6148
  896.1 0.8 copy-start.4
  898.3 502.2 %reduce-scatter.5.cloned.1.call-start = ((), (), s32[]{:S(2)}) async-start(), calls=%async_computation.5 | async-start | bytes 2162688 | tf_op jit(solution)/shard_map/reduce_scatter | solution.py:100
  1147.0 253.4 %copy-start.8 = (f32[64,224]{1,0:T(8,128)S(1)}, f32[64,224]{1,0:T(8,128)}, u32[]{:S(2)}) copy-start(f32[64,224]{1,0:T(8,128)} %reduce-scatter.3.cloned.1.call-done) | copy-start | bytes 172036
Sparse Core Ops, SparseCore 0:
  15.8 95.8 all-gather.1
  169.4 241.0 all-reduce.7
  420.2 252.6 reduce-scatter.2
  898.4 241.6 all-reduce.5
  1147.2 253.1 reduce-scatter.4
where the time goes:
time: 1410 us
  waiting for transfers between devices  874 us (62%)
  blocking collectives  478 us (34%)
  matrix products  20.5 us (1%)
  between operations  14.7 us (1%)
    reduce_scatter x2, waiting for transfers between devices, local(): lax.psum_scatter(lax.dot_general(attn, gdot, (((0,), (0,)), ((), ())), pr...  506 us
    psum x2, waiting for transfers between devices, local(): lax.psum((jnp.sum(h_loc * hdot, -1), jnp.dot(hdot * norm_gain, wide, prec...  368 us
    all_gather x2, blocking collectives, local(): lax.all_gather(current.astype(jnp.bfloat16), 'dp', axis=0, tiled=True)  265 us
    psum x1, blocking collectives, local(): product_sq = lax.psum(jnp.sum(hvp_rows * hvp_rows), ('dp', 'mp'))  98.3 us
    psum x1, blocking collectives, local(): lax.psum((jnp.sum(h_loc * h_loc, -1), jnp.dot(h_loc * norm_gain, wide, pr...  57.4 us
    psum x1, blocking collectives, local(): lax.psum((jnp.sum(h_loc * hdot, -1), jnp.dot(hdot * norm_gain, wide, prec...  57.4 us
  transfers between devices with their start and end apart: 5, of which 4 were waited for; matrix products, arithmetic and copies ran while one was open for 0% of the time, Pallas kernels for 0%

commit v1 on v0

v1 whole, which is shorter than its diff:
```python
import jax
import jax.numpy as jnp
from jax import lax
from jax.sharding import Mesh, PartitionSpec as P

D = 3584
HD = 256
HQ = 8
HK = 4
TAGS = 128
WINDOW = 256
DAMP = 0.01
NORM_EPS = 1e-06
MEAN_EPS = 1e-06
ZL, X, Y, ZH, C = 8, 4, 4, 2, 2
BF = jnp.bfloat16
F32 = jnp.float32


def attend(query, key, value, start, offset):
    num_q = query.shape[0]
    num_k = key.shape[0]
    group = HQ // HK
    q_heads = query.reshape(num_q, HK, group, HD)
    k_heads = key.reshape(num_k, HK, HD)
    v_heads = value.reshape(num_k, HK, HD)
    scores = jnp.einsum(
        "qgrd,kgd->grqk", q_heads, k_heads, preferred_element_type=F32
    ) / jnp.sqrt(F32(HD))
    scores = 50.0 * jnp.tanh(scores / 50.0)
    q_pos = offset + jnp.arange(num_q, dtype=jnp.int32)
    k_pos = jnp.arange(num_k, dtype=jnp.int32)
    q_file = jnp.sum((start[None, :] <= q_pos[:, None]).astype(jnp.int32), 1) - 1
    k_file = jnp.sum((start[None, :] <= k_pos[:, None]).astype(jnp.int32), 1) - 1
    allowed = (
        (q_file[:, None] == k_file[None, :])
        & (k_pos[None, :] <= q_pos[:, None])
        & (q_pos[:, None] - k_pos[None, :] < WINDOW)
    )
    expo = jnp.where(allowed[None, None], jnp.exp(scores), 0.0)
    weights = (expo / jnp.sum(expo, -1, keepdims=True)).astype(BF)
    out = jnp.einsum("grqk,kgd->qgrd", weights, v_heads, preferred_element_type=F32)
    return out.reshape(num_q, HQ * HD).astype(BF)


def swap(x, axis):
    return lax.ppermute(x, axis, [(0, 1), (1, 0)])


def spread(x, axis, n):
    return lax.all_to_all(jnp.broadcast_to(x[None], (n,) + x.shape), axis, 0, 0, tiled=True)


def deal(x, axis):
    return lax.all_to_all(x, axis, 0, 0, tiled=True)


def paired(mine, theirs, axis):
    first = lax.axis_index(axis) == 0
    return jnp.stack([jnp.where(first, mine, theirs), jnp.where(first, theirs, mine)])


def dot(a, b):
    return jnp.dot(a, b, preferred_element_type=F32)


def split2(x):
    hi = x.astype(BF)
    return hi, (x - hi.astype(F32)).astype(BF)


def gather_rows(block, total):
    hi, lo = split2(total)
    mid, low = hi, lo
    row = jnp.concatenate([jnp.full((1, 112), mid, BF), jnp.full((1, 112), low, BF)], 1)
    load = jnp.concatenate([block.astype(BF), jnp.broadcast_to(row, (16, 224))], 0)
    by_zl = spread(load, "zl", ZL)
    by_all = spread(by_zl, "x", X)
    rows = by_all[:, :, :64].transpose(1, 0, 2, 3).reshape(2048, 224)
    sums = by_all[:, :, 64].astype(F32)
    return rows, jnp.sum(sums[..., 0] + sums[..., 112])


def scatter_rows(product):
    by_x = product.astype(BF).reshape(ZL, X, 64, 224).transpose(1, 0, 2, 3)
    part = jnp.sum(deal(by_x, "x").astype(F32), 0)
    return jnp.sum(deal(part.astype(BF), "zl").astype(F32), 0)


def tokens_sum(load):
    part = jnp.sum(deal(load, ("c", "y")), 0)
    return part + swap(part, "zh")


def local(queries, keys, values, stream, out_proj, norm_gain, tag_proj, direction, starts, tags):
    core = lax.axis_index("c")
    ypos = lax.axis_index("y")
    mp_index = (ypos * ZH + lax.axis_index("zh")) * C + core
    count = HQ * HD * D
    u0, early_norm = gather_rows(direction, jnp.sum(direction * direction))

    mine = attend(queries[0], keys[0], values[0], starts[0], mp_index * 32)
    pair = paired(mine, swap(mine, "zh"), "zh").reshape(64, 2048)
    half = spread(pair, "y", Y).reshape(256, 2048)
    attn = paired(half, swap(half, "c"), "c").reshape(512, 2048)
    toks = stream[0].reshape(Y, ZH, C, 32, 224).transpose(2, 0, 1, 3, 4).reshape(512, 224)
    tag_own = tags[0].reshape(Y, ZH, C, 32).transpose(2, 0, 1, 3).reshape(C * Y, 64)[core * Y + ypos]

    wide = tag_proj.astype(F32)
    gained = norm_gain[:, None] * wide

    def sums(h, hd):
        return jnp.sum(h * hd, -1).reshape(8, 1, 64)

    def tag_scores(hd):
        return jnp.dot(hd, gained, precision=lax.Precision.HIGHEST).reshape(8, 64, TAGS)

    h_loc = toks.astype(F32) + dot(attn, out_proj)
    hdot0 = dot(attn, u0)
    load = jnp.concatenate(
        [
            tag_scores(h_loc),
            tag_scores(hdot0),
            jnp.pad(jnp.concatenate([sums(h_loc, h_loc), sums(h_loc, hdot0)], 2), ((0, 0), (0, 7), (0, 0))),
        ],
        1,
    )
    total = tokens_sum(load)
    zval, zdot0 = total[:64], total[64:128]
    sumsq, along0 = total[128, :64], total[128, 64:]

    rscale = (sumsq / D + NORM_EPS) ** (-0.5)
    tanh_val = jnp.tanh(rscale[:, None] * zval / 30.0)
    slope = 1.0 - tanh_val * tanh_val
    expo = jnp.exp(30.0 * tanh_val)
    probs = expo / jnp.sum(expo, -1, keepdims=True)
    onehot = (tag_own[:, None] == jnp.arange(TAGS, dtype=jnp.int32)[None, :]).astype(F32)
    dlogit = probs - onehot
    wgrad = dlogit * slope
    rho = jnp.sum(wgrad * zval, -1)
    cube = rscale**3 / D

    def backward(along, zdot, hdot):
        rdot = -cube * along
        mdot = rdot[:, None] * zval + rscale[:, None] * zdot
        ldot = slope * mdot
        pdot = probs * (ldot - jnp.sum(probs * ldot, -1, keepdims=True))
        wdot = pdot * slope - dlogit * 2.0 * tanh_val * slope * mdot / 30.0
        rhodot = jnp.sum(wdot * zval + wgrad * zdot, -1)
        mixed = rdot[:, None] * wgrad + rscale[:, None] * wdot
        coeff = rhodot * cube + 3.0 * rho * rscale * rscale * rdot / D
        row = jnp.concatenate([coeff, rho * cube])[None]
        out = spread(jnp.concatenate([mixed, jnp.pad(row, ((0, 7), (0, 0)))], 0), ("c", "y"), 8)
        mixed_all = out[:, :64].reshape(512, TAGS)
        coeff_all = out[:, 64, :64].reshape(512, 1)
        rc_all = out[:, 64, 64:].reshape(512, 1)
        back = jnp.dot(mixed_all, gained.T, precision=lax.Precision.HIGHEST)
        gdot = (back - coeff_all * h_loc - rc_all * hdot).astype(BF)
        return scatter_rows(
            lax.dot_general(attn, gdot, (((0,), (0,)), ((), ())), preferred_element_type=F32)
        )

    rows0 = backward(along0, zdot0, hdot0)
    full0, row_sq = gather_rows(rows0, jnp.sum(rows0 * rows0))
    moved = dot(attn, full0)
    lane = jnp.arange(64)[None, None, :]
    scalars = jnp.where(lane == 0, row_sq, jnp.where(lane == 1, early_norm, 0.0))
    load = jnp.concatenate(
        [
            tag_scores(moved),
            jnp.pad(
                jnp.concatenate([sums(h_loc, moved), jnp.broadcast_to(scalars, (8, 1, 64))], 2),
                ((0, 0), (0, 7), (0, 0)),
            ),
        ],
        1,
    )
    total = tokens_sum(load)
    product_sq, norm_sq = total[64, 64], total[64, 65]
    sigma = 2.0 * jnp.sqrt((product_sq / count + MEAN_EPS) / (norm_sq / count + MEAN_EPS))
    inv = 1.0 / sigma
    keep = 2.0 - DAMP
    rows1 = backward(
        keep * along0 - total[64, :64] * inv,
        keep * zdot0 - total[:64] * inv,
        keep * hdot0 - moved * inv,
    )
    damp = 1.0 - DAMP
    return (1.0 + damp * keep) * direction - (damp * rows0 + rows1) * inv


def solution(mesh):
    fine = Mesh(mesh.devices.reshape(ZL, X, Y, ZH, C), ("zl", "x", "y", "zh", "c"))
    dp, mp = ("zl", "x"), ("y", "zh", "c")
    return jax.shard_map(
        local,
        mesh=fine,
        in_specs=(
            P(dp, mp, None),
            P(dp, None, None),
            P(dp, None, None),
            P(dp, None, mp),
            P(None, mp),
            P(mp),
            P(mp, None),
            P(dp, mp),
            P(dp, None),
            P(dp, None),
        ),
        out_specs=P(dp, mp),
        check_vma=False,
    )
```

time: 1410 us -> 371 us (0.26)
  the two profiles are of different devices: /device:TPU:16 before, /device:TPU:32 now
where the time goes in v1:
time: 371 us; the launch traced here: 369 us
  blocking collectives  165 us (44%)
  waiting for transfers between devices  74.5 us (20%)
  starting transfers between devices  50 us (13%)
  local copies, waits for them, and re-layouts  32.8 us (9%)
  other arithmetic  24.9 us (7%)
  matrix products  17.7 us (5%)
  between operations  4.68 us (1%)
    all_to_all x5, blocking collectives, deal(): return lax.all_to_all(x, axis, 0, 0, tiled=True)  94.5 us
    all_to_all x4, blocking collectives, spread(): lax.all_to_all(jnp.broadcast_to(x[None], (n,) + x.shape), axis, 0, 0, til...  70.1 us
    all_to_all x3, waiting for transfers between devices, spread(): lax.all_to_all(jnp.broadcast_to(x[None], (n,) + x.shape), axis, 0, 0, til...  36.4 us
    ppermute x4, starting transfers between devices, swap(): return lax.ppermute(x, axis, [(0, 1), (1, 0)])  32.6 us
    ppermute x4, waiting for transfers between devices, swap(): return lax.ppermute(x, axis, [(0, 1), (1, 0)])  29.4 us
    all_to_all x3, starting transfers between devices, spread(): lax.all_to_all(jnp.broadcast_to(x[None], (n,) + x.shape), axis, 0, 0, til...  13.2 us
    all_to_all x1, waiting for transfers between devices, deal(): return lax.all_to_all(x, axis, 0, 0, tiled=True)  8.72 us
  transfers between devices with their start and end apart: 8, of which 7 were waited for; matrix products, arithmetic and copies ran while one was open for 3% of the time, Pallas kernels for 0%

profile of v1, /device:TPU:32, one launch (start us, length us, event | category | flops | bytes accessed | tf_op | source)
XLA Modules:
  0.0 369.3 jit_solution(14554037160968362282)
XLA Ops:
  0.0 0.9 convert_reduce_fusion.2
  1.6 1.0 reshape_squeeze.18
  2.6 2.7 reshape_squeeze.8
  6.2 1.7 fusion.4
  8.5 14.8 %collective-permute-start = (bf16[32,2048]{1,0:T(8,128)(2,1)S(1)}, bf16[32,2048]{1,0:T(8,128)(2,1)S(1)}, u32[]{:S(2)}, u32[]{:S(2)}) collective-permute-start(bf16[32,2048]{1,0:T(8,128)(2,1)S(1)} %convert_element_type.105), channel_id=1, source_target_pairs={{0,2},{2,0},{1,3},{3,1},{4,6},{6,4},{5,7},{7,5},{8,10},{10,8},{9,1... | collective-permute-start | bytes 393224 | tf_op jit(solution)/shard_map/ppermute | solution.py:47
  23.3 12.0 %collective-permute-done = bf16[32,2048]{1,0:T(8,128)(2,1)S(1)} collective-permute-done((bf16[32,2048]{1,0:T(8,128)(2,1)S(1)}, bf16[32,2048]{1,0:T(8,128)(2,1)S(1)}, u32[]{:S(2)}, u32[]{:S(2)}) %collective-permute-start) | collective-permute-done | bytes 131104 | tf_op jit(solution)/shard_map/ppermute | solution.py:47
  35.4 1.1 broadcast_in_dim.54
  36.5 4.5 %all-to-all-start = ((bf16[4,64,2048]{2,1,0:T(8,128)(2,1)}), bf16[4,64,2048]{2,1,0:T(8,128)(2,1)S(1)}, u32[]{:S(2)}, u32[]{:S(2)}) async-start(bf16[4,64,2048]{2,1,0:T(8,128)(2,1)} %broadcast_in_dim.54), calls=%async_computation | async-start | bytes 2097152 | tf_op jit(solution)/shard_map/all_to_all | solution.py:51
  43.0 12.4 %all-to-all-done = bf16[4,64,2048]{2,1,0:T(8,128)(2,1)S(1)} async-done(((bf16[4,64,2048]{2,1,0:T(8,128)(2,1)}), bf16[4,64,2048]{2,1,0:T(8,128)(2,1)S(1)}, u32[]{:S(2)}, u32[]{:S(2)}) %all-to-all-start) | async-done | bytes 1048608 | tf_op jit(solution)/shard_map/all_to_all | solution.py:51
  55.4 26.1 %all_to_all.65 = bf16[8,80,224]{2,1,0:T(8,128)(2,1)S(1)} all-to-all(bf16[8,80,224]{2,1,0:T(8,128)(2,1)S(1)} %broadcast_in_dim.57), channel_id=1, replica_groups=mesh['zl'=8,'x'=4,'y'=4,'zh'=2,'c'=2] {'zl'}, dimensions={0} | all-to-all | bytes 573440 | tf_op jit(solution)/shard_map/all_to_all | solution.py:51
  81.6 1.2 broadcast_in_dim.58
  82.7 4.3 %all-to-all-start.2 = ((bf16[4,8,80,224]{3,2,1,0:T(8,128)(2,1)}), bf16[4,8,80,224]{3,2,1,0:T(8,128)(2,1)S(1)}, u32[]{:S(2)}, u32[]{:S(2)}) async-start(bf16[4,8,80,224]{3,2,1,0:T(8,128)(2,1)} %broadcast_in_dim.58), calls=%async_computation.2 | async-start | bytes 2621440 | tf_op jit(solution)/shard_map/all_to_all | solution.py:51
  87.0 1.9 collective-permute-start.1
  88.9 1.8 copy.44
  90.7 1.0 convert_bitcast_fusion
  92.5 2.0 copy.46
  94.6 8.9 %all-to-all-done.2 = bf16[4,8,80,224]{3,2,1,0:T(8,128)(2,1)S(1)} async-done(((bf16[4,8,80,224]{3,2,1,0:T(8,128)(2,1)}), bf16[4,8,80,224]{3,2,1,0:T(8,128)(2,1)S(1)}, u32[]{:S(2)}, u32[]{:S(2)}) %all-to-all-start.2) | async-done | bytes 1146912 | tf_op jit(solution)/shard_map/all_to_all | solution.py:51
  103.7 0.8 copy-done.2
  104.5 1.4 select_bitcast_fusion.1
  107.1 0.9 multiply_reduce_fusion.2
  108.2 2.1 fusion.16
  110.3 1.1 fusion.17
  111.4 0.9 pad_maximum_fusion.1
  112.3 4.2 %all-to-all-start.3 = ((f32[8,136,128]{2,1,0:T(8,128)}), f32[8,136,128]{2,1,0:T(8,128)}, u32[]{:S(2)}, u32[]{:S(2)}) async-start(f32[8,136,128]{2,1,0:T(8,128)} %pad_maximum_fusion.1), calls=%async_computation.3 | async-start | bytes 1114112 | tf_op jit(solution)/shard_map/all_to_all | solution.py:55
  117.9 8.7 %all-to-all-done.3 = f32[8,136,128]{2,1,0:T(8,128)} async-done(((f32[8,136,128]{2,1,0:T(8,128)}), f32[8,136,128]{2,1,0:T(8,128)}, u32[]{:S(2)}, u32[]{:S(2)}) %all-to-all-start.3) | async-done | bytes 557088 | tf_op jit(solution)/shard_map/all_to_all | solution.py:55
  126.6 1.1 reduce_sum.210
  127.7 8.0 %collective-permute-start.2 = (f32[136,128]{1,0:T(8,128)S(1)}, f32[136,128]{1,0:T(8,128)S(1)}, u32[]{:S(2)}, u32[]{:S(2)}) collective-permute-start(f32[136,128]{1,0:T(8,128)S(1)} %reduce_sum.210), channel_id=1, source_target_pairs={{0,2},{2,0},{1,3},{3,1},{4,6},{6,4},{5,7},{7,5},{8,10},{10,8},{9,1... | collective-permute-start | bytes 208904 | tf_op jit(solution)/shard_map/ppermute | solution.py:47
  135.7 10.1 %collective-permute-done.2 = f32[136,128]{1,0:T(8,128)S(1)} collective-permute-done((f32[136,128]{1,0:T(8,128)S(1)}, f32[136,128]{1,0:T(8,128)S(1)}, u32[]{:S(2)}, u32[]{:S(2)}) %collective-permute-start.2) | collective-permute-done | bytes 69664 | tf_op jit(solution)/shard_map/ppermute | solution.py:47
  145.8 0.9 add.118
  148.2 10.1 %all_to_all.66 = f32[8,72,128]{2,1,0:T(8,128)S(1)} all-to-all(f32[8,72,128]{2,1,0:T(8,128)S(1)} %broadcast_in_dim.60), channel_id=1, replica_groups=mesh['zl'=8,'x'=4,'y'=4,'zh'=2,'c'=2] {'c','y'}, dimensions={0} | all-to-all | bytes 589824 | tf_op jit(solution)/shard_map/all_to_all | solution.py:51
  159.7 1.3 mul.355
  161.0 1.3 mul.358
  162.4 1.0 slice.93
  163.3 1.6 fusion.8
  164.9 1.6 convolution_convert_fusion.1
  166.5 2.3 copy.49
  168.8 1.3 copy.50
  170.1 18.8 %all_to_all.67 = bf16[4,8,64,224]{3,2,1,0:T(8,128)(2,1)} all-to-all(bf16[4,8,64,224]{3,2,1,0:T(8,128)(2,1)S(1)} %copy.50), channel_id=1, replica_groups=mesh['zl'=8,'x'=4,'y'=4,'zh'=2,'c'=2] {'x'}, dimensions={0} | all-to-all | bytes 1835008 | tf_op jit(solution)/shard_map/all_to_all | solution.py:55
  188.9 2.2 reduce_sum.215
  191.1 23.8 %all_to_all.68 = bf16[8,64,224]{2,1,0:T(8,128)(2,1)S(1)} all-to-all(bf16[8,64,224]{2,1,0:T(8,128)(2,1)} %reduce_sum.215), channel_id=1, replica_groups=mesh['zl'=8,'x'=4,'y'=4,'zh'=2,'c'=2] {'zl'}, dimensions={0} | all-to-all | bytes 458752 | tf_op jit(solution)/shard_map/all_to_all | solution.py:55
  215.6 1.3 fusion.44
  219.0 23.8 %all_to_all.69 = bf16[8,80,224]{2,1,0:T(8,128)(2,1)S(1)} all-to-all(bf16[8,80,224]{2,1,0:T(8,128)(2,1)S(1)} %broadcast_in_dim.63), channel_id=1, replica_groups=mesh['zl'=8,'x'=4,'y'=4,'zh'=2,'c'=2] {'zl'}, dimensions={0} | all-to-all | bytes 573440 | tf_op jit(solution)/shard_map/all_to_all | solution.py:51
  242.8 1.2 broadcast_in_dim.66
  243.9 4.5 %all-to-all-start.8 = ((bf16[4,8,80,224]{3,2,1,0:T(8,128)(2,1)}), bf16[4,8,80,224]{3,2,1,0:T(8,128)(2,1)}, u32[]{:S(2)}, u32[]{:S(2)}) async-start(bf16[4,8,80,224]{3,2,1,0:T(8,128)(2,1)} %broadcast_in_dim.66), calls=%async_computation.8 | async-start | bytes 2621440 | tf_op jit(solution)/shard_map/all_to_all | solution.py:51
  248.5 0.9 slice_convert_fusion
  250.0 15.1 %all-to-all-done.8 = bf16[4,8,80,224]{3,2,1,0:T(8,128)(2,1)} async-done(((bf16[4,8,80,224]{3,2,1,0:T(8,128)(2,1)}), bf16[4,8,80,224]{3,2,1,0:T(8,128)(2,1)}, u32[]{:S(2)}, u32[]{:S(2)}) %all-to-all-start.8) | async-done | bytes 1146912 | tf_op jit(solution)/shard_map/all_to_all | solution.py:51
  265.1 1.3 slice_bitcast_fusion
  266.5 2.2 multiply_reduce_fusion
  268.6 0.9 slice_convert_fusion.1
  270.2 1.3 reshape.232
  271.5 2.1 fusion.15
  273.6 1.6 fusion.31
  275.1 1.2 compare_select_fusion.1
  277.1 10.8 %all_to_all.70 = f32[8,72,128]{2,1,0:T(8,128)} all-to-all(f32[8,72,128]{2,1,0:T(8,128)S(1)} %select_maximum_fusion), channel_id=1, replica_groups=mesh['zl'=8,'x'=4,'y'=4,'zh'=2,'c'=2] {'c','y'}, dimensions={0} | all-to-all | bytes 589824 | tf_op jit(solution)/shard_map/all_to_all | solution.py:55
  288.0 1.6 reduce_sum.221
  289.6 7.9 %collective-permute-start.3 = (f32[72,128]{1,0:T(8,128)}, f32[72,128]{1,0:T(8,128)S(1)}, u32[]{:S(2)}, u32[]{:S(2)}) collective-permute-start(f32[72,128]{1,0:T(8,128)} %reduce_sum.221), channel_id=1, source_target_pairs={{0,2},{2,0},{1,3},{3,1},{4,6},{6,4},{5,7},{7,5},{8,10},{10,8},{9,1... | collective-permute-start | bytes 110600 | tf_op jit(solution)/shard_map/ppermute | solution.py:47
  297.5 7.2 %collective-permute-done.3 = f32[72,128]{1,0:T(8,128)S(1)} collective-permute-done((f32[72,128]{1,0:T(8,128)}, f32[72,128]{1,0:T(8,128)S(1)}, u32[]{:S(2)}, u32[]{:S(2)}) %collective-permute-start.3) | collective-permute-done | bytes 36896 | tf_op jit(solution)/shard_map/ppermute | solution.py:47
  310.2 10.1 %all_to_all.71 = f32[8,72,128]{2,1,0:T(8,128)S(1)} all-to-all(f32[8,72,128]{2,1,0:T(8,128)S(1)} %broadcast_in_dim.73), channel_id=1, replica_groups=mesh['zl'=8,'x'=4,'y'=4,'zh'=2,'c'=2] {'c','y'}, dimensions={0} | all-to-all | bytes 589824 | tf_op jit(solution)/shard_map/all_to_all | solution.py:51
  321.3 1.0 slice.107
  322.3 1.8 fusion.7
  324.1 1.6 convolution_convert_fusion
  325.7 1.5 copy.52
  327.3 18.2 %all_to_all.72 = bf16[4,8,64,224]{3,2,1,0:T(8,128)(2,1)S(1)} all-to-all(bf16[4,8,64,224]{3,2,1,0:T(8,128)(2,1)S(1)} %copy.53), channel_id=1, replica_groups=mesh['zl'=8,'x'=4,'y'=4,'zh'=2,'c'=2] {'x'}, dimensions={0} | all-to-all | bytes 1835008 | tf_op jit(solution)/shard_map/all_to_all | solution.py:55
  345.7 22.9 %all_to_all.73 = bf16[8,64,224]{2,1,0:T(8,128)(2,1)S(1)} all-to-all(bf16[8,64,224]{2,1,0:T(8,128)(2,1)S(1)} %reduce_sum.224), channel_id=1, replica_groups=mesh['zl'=8,'x'=4,'y'=4,'zh'=2,'c'=2] {'zl'}, dimensions={0} | all-to-all | bytes 458752 | tf_op jit(solution)/shard_map/all_to_all | solution.py:55
  (105 shorter events, 19.2 us)
Async XLA Ops:
  0.0 106.9 %copy-start = (bf16[2048,224]{0,1:T(8,128)(2,1)S(1)}, bf16[2048,224]{0,1:T(8,128)(2,1)}, u32[]{:S(2)}) copy-start(bf16[2048,224]{0,1:T(8,128)(2,1)} %param.14) | copy-start | bytes 2752516
  0.0 5.3 %copy-start.7 = (bf16[1,512,1024]{2,1,0:T(8,128)(2,1)S(1)}, bf16[1,512,1024]{2,1,0:T(8,128)(2,1)}, u32[]{:S(2)}) copy-start(bf16[1,512,1024]{2,1,0:T(8,128)(2,1)} %param.12) | copy-start | bytes 3145732
  8.5 26.9 %collective-permute-start = (bf16[32,2048]{1,0:T(8,128)(2,1)S(1)}, bf16[32,2048]{1,0:T(8,128)(2,1)S(1)}, u32[]{:S(2)}, u32[]{:S(2)}) collective-permute-start(bf16[32,2048]{1,0:T(8,128)(2,1)S(1)} %convert_element_type.105), channel_id=1, source_target_pairs={{0,2},{2,0},{1,3},{3,1},{4,6},{6,4},{5,7},{7,5},{8,10},{10,8},{9,1... | collective-permute-start | bytes 393224 | tf_op jit(solution)/shard_map/ppermute | solution.py:47
  35.4 5.6 %copy-start.11 = (f32[64,224]{1,0:T(8,128)S(1)}, f32[64,224]{1,0:T(8,128)}, u32[]{:S(2)}) copy-start(f32[64,224]{1,0:T(8,128)} %param.17) | copy-start | bytes 172036
  36.5 18.9 %all-to-all-start = ((bf16[4,64,2048]{2,1,0:T(8,128)(2,1)}), bf16[4,64,2048]{2,1,0:T(8,128)(2,1)S(1)}, u32[]{:S(2)}, u32[]{:S(2)}) async-start(bf16[4,64,2048]{2,1,0:T(8,128)(2,1)} %broadcast_in_dim.54), calls=%async_computation | async-start | bytes 2097152 | tf_op jit(solution)/shard_map/all_to_all | solution.py:51
  82.7 20.8 %all-to-all-start.2 = ((bf16[4,8,80,224]{3,2,1,0:T(8,128)(2,1)}), bf16[4,8,80,224]{3,2,1,0:T(8,128)(2,1)S(1)}, u32[]{:S(2)}, u32[]{:S(2)}) async-start(bf16[4,8,80,224]{3,2,1,0:T(8,128)(2,1)} %broadcast_in_dim.58), calls=%async_computation.2 | async-start | bytes 2621440 | tf_op jit(solution)/shard_map/all_to_all | solution.py:51
  87.0 17.5 %collective-permute-start.1 = (bf16[256,2048]{1,0:T(8,128)(2,1)S(1)}, bf16[256,2048]{1,0:T(8,128)(2,1)}, u32[]{:S(2)}, u32[]{:S(2)}) collective-permute-start(bf16[256,2048]{1,0:T(8,128)(2,1)S(1)} %bitcast.96), channel_id=1, source_target_pairs={{0,1},{1,0},{2,3},{3,2},{4,5},{5,4},{6,7},{7,6},{8,9},{9,8},{10,11... | collective-permute-start | bytes 3145736 | tf_op jit(solution)/shard_map/ppermute | solution.py:47
  103.5 1.1 copy-start.2
  106.1 1.0 copy-start.3
  107.1 0.9 copy-start.1
  107.1 1.0 copy-start.4
  107.1 1.0 copy-start.13
  108.0 9.0 %copy-start.16 = (s32[1,512]{1,0:T(1,128)S(1)}, s32[1,512]{1,0:T(1,128)}, u32[]{:S(2)}) copy-start(s32[1,512]{1,0:T(1,128)} %param.19) | copy-start | bytes 6148
  112.3 14.3 %all-to-all-start.3 = ((f32[8,136,128]{2,1,0:T(8,128)}), f32[8,136,128]{2,1,0:T(8,128)}, u32[]{:S(2)}, u32[]{:S(2)}) async-start(f32[8,136,128]{2,1,0:T(8,128)} %pad_maximum_fusion.1), calls=%async_computation.3 | async-start | bytes 1114112 | tf_op jit(solution)/shard_map/all_to_all | solution.py:55
  127.7 8.0 %copy-start.10 = (f32[136,128]{1,0:T(8,128)}, f32[136,128]{1,0:T(8,128)S(1)}, u32[]{:S(2)}) copy-start(f32[136,128]{1,0:T(8,128)S(1)} %reduce_sum.210) | copy-start | bytes 208900
  127.7 18.1 %collective-permute-start.2 = (f32[136,128]{1,0:T(8,128)S(1)}, f32[136,128]{1,0:T(8,128)S(1)}, u32[]{:S(2)}, u32[]{:S(2)}) collective-permute-start(f32[136,128]{1,0:T(8,128)S(1)} %reduce_sum.210), channel_id=1, source_target_pairs={{0,2},{2,0},{1,3},{3,1},{4,6},{6,4},{5,7},{7,5},{8,10},{10,8},{9,1... | collective-permute-start | bytes 208904 | tf_op jit(solution)/shard_map/ppermute | solution.py:47
  135.7 12.0 %copy-start.14 = (s32[64]{0:T(128)}, s32[64]{0:T(128)S(1)}, u32[]{:S(2)}) copy-start(s32[64]{0:T(128)S(1)} %dynamic-slice_bitcast_fusion) | copy-start | bytes 772
  147.5 0.6 copy-start.15
  147.6 0.6 copy-start.17
  158.3 0.7 copy-start.5
  214.9 0.6 copy-start.8
  243.9 21.1 %all-to-all-start.8 = ((bf16[4,8,80,224]{3,2,1,0:T(8,128)(2,1)}), bf16[4,8,80,224]{3,2,1,0:T(8,128)(2,1)}, u32[]{:S(2)}, u32[]{:S(2)}) async-start(bf16[4,8,80,224]{3,2,1,0:T(8,128)(2,1)} %broadcast_in_dim.66), calls=%async_computation.8 | async-start | bytes 2621440 | tf_op jit(solution)/shard_map/all_to_all | solution.py:51
  289.6 15.2 %collective-permute-start.3 = (f32[72,128]{1,0:T(8,128)}, f32[72,128]{1,0:T(8,128)S(1)}, u32[]{:S(2)}, u32[]{:S(2)}) collective-permute-start(f32[72,128]{1,0:T(8,128)} %reduce_sum.221), channel_id=1, source_target_pairs={{0,2},{2,0},{1,3},{3,1},{4,6},{6,4},{5,7},{7,5},{8,10},{10,8},{9,1... | collective-permute-start | bytes 110600 | tf_op jit(solution)/shard_map/ppermute | solution.py:47
  320.4 0.7 copy-start.6
  327.3 41.4 %copy-start.9 = (f32[64,224]{1,0:T(8,128)S(1)}, f32[64,224]{1,0:T(8,128)}, u32[]{:S(2)}) copy-start(f32[64,224]{1,0:T(8,128)} %copy-done.8) | copy-start | bytes 172036
  327.3 41.4 %copy-start.12 = (f32[64,224]{1,0:T(8,128)S(1)}, f32[64,224]{1,0:T(8,128)}, u32[]{:S(2)}) copy-start(f32[64,224]{1,0:T(8,128)} %param.17) | copy-start | bytes 172036

commit v2 on v1

--- a/solution.py
+++ b/solution.py
@@ -69,16 +69,14 @@
     return hi, (x - hi.astype(F32)).astype(BF)
 
 
-def gather_rows(block, total):
-    hi, lo = split2(total)
-    mid, low = hi, lo
-    row = jnp.concatenate([jnp.full((1, 112), mid, BF), jnp.full((1, 112), low, BF)], 1)
-    load = jnp.concatenate([block.astype(BF), jnp.broadcast_to(row, (16, 224))], 0)
-    by_zl = spread(load, "zl", ZL)
-    by_all = spread(by_zl, "x", X)
-    rows = by_all[:, :, :64].transpose(1, 0, 2, 3).reshape(2048, 224)
-    sums = by_all[:, :, 64].astype(F32)
-    return rows, jnp.sum(sums[..., 0] + sums[..., 112])
+def row_load(block):
+    hi, lo = split2(jnp.sum(block * block, -1, keepdims=True))
+    return jnp.concatenate([block.astype(BF), hi, lo, jnp.zeros((64, 30), BF)], 1)
+
+
+def whole_rows(by_all):
+    rows = by_all[..., :224].transpose(1, 0, 2, 3).reshape(2048, 224)
+    return rows, jnp.sum(by_all[..., 224:226].astype(F32))
 
 
 def scatter_rows(product):
@@ -97,10 +95,12 @@
     ypos = lax.axis_index("y")
     mp_index = (ypos * ZH + lax.axis_index("zh")) * C + core
     count = HQ * HD * D
-    u0, early_norm = gather_rows(direction, jnp.sum(direction * direction))
-
+    by_zl = spread(row_load(direction), "zl", ZL)
     mine = attend(queries[0], keys[0], values[0], starts[0], mp_index * 32)
-    pair = paired(mine, swap(mine, "zh"), "zh").reshape(64, 2048)
+    mine, by_zl = lax.optimization_barrier((mine, by_zl))
+    theirs, by_all = lax.optimization_barrier((swap(mine, "zh"), spread(by_zl, "x", X)))
+    u0, early_norm = whole_rows(by_all)
+    pair = paired(mine, theirs, "zh").reshape(64, 2048)
     half = spread(pair, "y", Y).reshape(256, 2048)
     attn = paired(half, swap(half, "c"), "c").reshape(512, 2048)
     toks = stream[0].reshape(Y, ZH, C, 32, 224).transpose(2, 0, 1, 3, 4).reshape(512, 224)
@@ -161,7 +161,7 @@
         )
 
     rows0 = backward(along0, zdot0, hdot0)
-    full0, row_sq = gather_rows(rows0, jnp.sum(rows0 * rows0))
+    full0, row_sq = whole_rows(spread(spread(row_load(rows0), "zl", ZL), "x", X))
     moved = dot(attn, full0)
     lane = jnp.arange(64)[None, None, :]
     scalars = jnp.where(lane == 0, row_sq, jnp.where(lane == 1, early_norm, 0.0))

time: 371 us -> 341 us (0.919)
  waiting for transfers between devices: 74.5 us -> 51.1 us
  blocking collectives: 165 us -> 158 us
    all_to_all x3, waiting for transfers between devices: 36.4 us -> 16.7 us  [spread(): lax.all_to_all(jnp.broadcast_to(x[None], (n,) + x.shape), axis, 0, 0, til...]
    all_to_all x4, blocking collectives: 70.1 us -> 57.2 us  [spread(): lax.all_to_all(jnp.broadcast_to(x[None], (n,) + x.shape), axis, 0, 0, til...]
    all_to_all x3, starting transfers between devices: 13.2 us -> 21.4 us  [spread(): lax.all_to_all(jnp.broadcast_to(x[None], (n,) + x.shape), axis, 0, 0, til...]
    ppermute x4, starting transfers between devices: 32.6 us -> 26.5 us  [swap(): return lax.ppermute(x, axis, [(0, 1), (1, 0)])]
    all_to_all x5, blocking collectives: 94.5 us -> 100 us  [deal(): return lax.all_to_all(x, axis, 0, 0, tiled=True)]
  transfers between devices with their start and end apart: 8 -> 8, of which waited for: 7 -> 6; matrix products, arithmetic and copies ran while one was open for 3% -> 5% of each run, Pallas kernels for 0% -> 0%
where the time goes in v2:
time: 341 us; the launch traced here: 339 us
  blocking collectives  158 us (46%)
  starting transfers between devices  52.1 us (15%)
  waiting for transfers between devices  51.1 us (15%)
  local copies, waits for them, and re-layouts  32.6 us (10%)
  other arithmetic  26 us (8%)
  matrix products  17.7 us (5%)
    all_to_all x5, blocking collectives, deal(): return lax.all_to_all(x, axis, 0, 0, tiled=True)  100 us
    all_to_all x4, blocking collectives, spread(): lax.all_to_all(jnp.broadcast_to(x[None], (n,) + x.shape), axis, 0, 0, til...  57.2 us
    ppermute x4, starting transfers between devices, swap(): return lax.ppermute(x, axis, [(0, 1), (1, 0)])  26.5 us
    ppermute x4, waiting for transfers between devices, swap(): return lax.ppermute(x, axis, [(0, 1), (1, 0)])  25.8 us
    all_to_all x3, starting transfers between devices, spread(): lax.all_to_all(jnp.broadcast_to(x[None], (n,) + x.shape), axis, 0, 0, til...  21.4 us
    all_to_all x3, waiting for transfers between devices, spread(): lax.all_to_all(jnp.broadcast_to(x[None], (n,) + x.shape), axis, 0, 0, til...  16.7 us
    all_to_all x1, waiting for transfers between devices, deal(): return lax.all_to_all(x, axis, 0, 0, tiled=True)  8.72 us
  transfers between devices with their start and end apart: 8, of which 6 were waited for; matrix products, arithmetic and copies ran while one was open for 5% of the time, Pallas kernels for 0%

profile of v2, /device:TPU:32, one launch (start us, length us, event | category | flops | bytes accessed | tf_op | source)
XLA Modules:
  0.0 339.1 jit_solution(872164370400228459)
XLA Ops:
  0.0 1.1 fusion.45
  2.3 12.6 %all-to-all-start = ((bf16[8,64,256]{2,1,0:T(8,128)(2,1)}), bf16[8,64,256]{2,1,0:T(8,128)(2,1)S(1)}, u32[]{:S(2)}, u32[]{:S(2)}) async-start(bf16[8,64,256]{2,1,0:T(8,128)(2,1)} %broadcast_in_dim.45), calls=%async_computation | async-start | bytes 524288 | tf_op jit(solution)/shard_map/all_to_all | solution.py:51
  16.4 1.0 reshape_squeeze.18
  17.4 2.7 reshape_squeeze.8
  21.0 1.7 fusion.4
  23.2 8.0 %all-to-all-done = bf16[8,64,256]{2,1,0:T(8,128)(2,1)S(1)} async-done(((bf16[8,64,256]{2,1,0:T(8,128)(2,1)}), bf16[8,64,256]{2,1,0:T(8,128)(2,1)S(1)}, u32[]{:S(2)}, u32[]{:S(2)}) %all-to-all-start) | async-done | bytes 262176 | tf_op jit(solution)/shard_map/all_to_all | solution.py:51
  31.2 1.1 broadcast_in_dim.46
  32.3 4.3 %all-to-all-start.1 = ((bf16[4,8,64,256]{3,2,1,0:T(8,128)(2,1)}), bf16[4,8,64,256]{3,2,1,0:T(8,128)(2,1)S(1)}, u32[]{:S(2)}, u32[]{:S(2)}) async-start(bf16[4,8,64,256]{3,2,1,0:T(8,128)(2,1)} %broadcast_in_dim.46), calls=%async_computation.1 | async-start | bytes 2097152 | tf_op jit(solution)/shard_map/all_to_all | solution.py:51
  36.6 8.2 %collective-permute-start = (bf16[32,2048]{1,0:T(8,128)(2,1)S(1)}, bf16[32,2048]{1,0:T(8,128)(2,1)S(1)}, u32[]{:S(2)}, u32[]{:S(2)}) collective-permute-start(bf16[32,2048]{1,0:T(8,128)(2,1)S(1)} %convert_element_type.155), channel_id=1, source_target_pairs={{0,2},{2,0},{1,3},{3,1},{4,6},{6,4},{5,7},{7,5},{8,10},{10,8},{9,1... | collective-permute-start | bytes 393224 | tf_op jit(solution)/shard_map/ppermute | solution.py:47
  44.8 11.5 %collective-permute-done = bf16[32,2048]{1,0:T(8,128)(2,1)S(1)} collective-permute-done((bf16[32,2048]{1,0:T(8,128)(2,1)S(1)}, bf16[32,2048]{1,0:T(8,128)(2,1)S(1)}, u32[]{:S(2)}, u32[]{:S(2)}) %collective-permute-start) | collective-permute-done | bytes 131104 | tf_op jit(solution)/shard_map/ppermute | solution.py:47
  56.5 15.2 %all_to_all.65 = bf16[4,64,2048]{2,1,0:T(8,128)(2,1)S(1)} all-to-all(bf16[4,64,2048]{2,1,0:T(8,128)(2,1)S(1)} %broadcast_in_dim.48), channel_id=1, replica_groups=mesh['zl'=8,'x'=4,'y'=4,'zh'=2,'c'=2] {'y'}, dimensions={0} | all-to-all | bytes 2097152 | tf_op jit(solution)/shard_map/all_to_all | solution.py:51
  71.7 1.9 collective-permute-start.1
  73.6 1.1 copy.76
  74.7 0.8 copy.77
  75.5 2.0 copy.78
  77.7 1.4 select_bitcast_fusion.1
  79.3 0.8 fusion.47
  80.3 0.9 multiply_reduce_fusion.2
  81.4 2.1 fusion.16
  83.5 1.1 fusion.17
  84.6 0.8 pad_maximum_fusion.1
  85.5 4.2 %all-to-all-start.3 = ((f32[8,136,128]{2,1,0:T(8,128)}), f32[8,136,128]{2,1,0:T(8,128)}, u32[]{:S(2)}, u32[]{:S(2)}) async-start(f32[8,136,128]{2,1,0:T(8,128)} %pad_maximum_fusion.1), calls=%async_computation.3 | async-start | bytes 1114112 | tf_op jit(solution)/shard_map/all_to_all | solution.py:55
  91.0 8.7 %all-to-all-done.3 = f32[8,136,128]{2,1,0:T(8,128)} async-done(((f32[8,136,128]{2,1,0:T(8,128)}), f32[8,136,128]{2,1,0:T(8,128)}, u32[]{:S(2)}, u32[]{:S(2)}) %all-to-all-start.3) | async-done | bytes 557088 | tf_op jit(solution)/shard_map/all_to_all | solution.py:55
  99.7 1.1 reduce_sum.215
  100.8 8.1 %collective-permute-start.2 = (f32[136,128]{1,0:T(8,128)S(1)}, f32[136,128]{1,0:T(8,128)S(1)}, u32[]{:S(2)}, u32[]{:S(2)}) collective-permute-start(f32[136,128]{1,0:T(8,128)S(1)} %reduce_sum.215), channel_id=1, source_target_pairs={{0,2},{2,0},{1,3},{3,1},{4,6},{6,4},{5,7},{7,5},{8,10},{10,8},{9,1... | collective-permute-start | bytes 208904 | tf_op jit(solution)/shard_map/ppermute | solution.py:47
  109.0 7.8 %collective-permute-done.2 = f32[136,128]{1,0:T(8,128)S(1)} collective-permute-done((f32[136,128]{1,0:T(8,128)S(1)}, f32[136,128]{1,0:T(8,128)S(1)}, u32[]{:S(2)}, u32[]{:S(2)}) %collective-permute-start.2) | collective-permute-done | bytes 69664 | tf_op jit(solution)/shard_map/ppermute | solution.py:47
  116.8 0.9 add.106
  119.1 10.5 %all_to_all.66 = f32[8,72,128]{2,1,0:T(8,128)S(1)} all-to-all(f32[8,72,128]{2,1,0:T(8,128)S(1)} %broadcast_in_dim.50), channel_id=1, replica_groups=mesh['zl'=8,'x'=4,'y'=4,'zh'=2,'c'=2] {'c','y'}, dimensions={0} | all-to-all | bytes 589824 | tf_op jit(solution)/shard_map/all_to_all | solution.py:51
  131.1 1.4 mul.355
  132.4 1.3 mul.358
  133.7 1.0 slice.76
  134.7 1.6 fusion.8
  136.3 1.6 convolution_convert_fusion.1
  137.9 2.3 copy.81
  140.2 1.3 copy.82
  141.5 21.1 %all_to_all.67 = bf16[4,8,64,224]{3,2,1,0:T(8,128)(2,1)} all-to-all(bf16[4,8,64,224]{3,2,1,0:T(8,128)(2,1)S(1)} %copy.82), channel_id=1, replica_groups=mesh['zl'=8,'x'=4,'y'=4,'zh'=2,'c'=2] {'x'}, dimensions={0} | all-to-all | bytes 1835008 | tf_op jit(solution)/shard_map/all_to_all | solution.py:55
  162.6 2.2 reduce_sum.220
  164.8 24.4 %all_to_all.68 = bf16[8,64,224]{2,1,0:T(8,128)(2,1)S(1)} all-to-all(bf16[8,64,224]{2,1,0:T(8,128)(2,1)} %reduce_sum.220), channel_id=1, replica_groups=mesh['zl'=8,'x'=4,'y'=4,'zh'=2,'c'=2] {'zl'}, dimensions={0} | all-to-all | bytes 458752 | tf_op jit(solution)/shard_map/all_to_all | solution.py:55
  191.8 1.4 copy.83
  193.2 1.4 copy.84
  194.5 0.9 maximum_maximum_fusion.1
  195.4 21.1 %all_to_all.69 = bf16[8,64,256]{2,1,0:T(8,128)(2,1)S(1)} all-to-all(bf16[8,64,256]{2,1,0:T(8,128)(2,1)S(1)} %broadcast_in_dim.51), channel_id=1, replica_groups=mesh['zl'=8,'x'=4,'y'=4,'zh'=2,'c'=2] {'zl'}, dimensions={0} | all-to-all | bytes 524288 | tf_op jit(solution)/shard_map/all_to_all | solution.py:51
  216.5 1.1 broadcast_in_dim.52
  217.6 4.4 %all-to-all-start.8 = ((bf16[4,8,64,256]{3,2,1,0:T(8,128)(2,1)}), bf16[4,8,64,256]{3,2,1,0:T(8,128)(2,1)}, u32[]{:S(2)}, u32[]{:S(2)}) async-start(bf16[4,8,64,256]{3,2,1,0:T(8,128)(2,1)} %broadcast_in_dim.52), calls=%async_computation.8 | async-start | bytes 2097152 | tf_op jit(solution)/shard_map/all_to_all | solution.py:51
  222.1 2.1 convert_reduce_fusion
  224.1 8.7 %all-to-all-done.8 = bf16[4,8,64,256]{3,2,1,0:T(8,128)(2,1)} async-done(((bf16[4,8,64,256]{3,2,1,0:T(8,128)(2,1)}), bf16[4,8,64,256]{3,2,1,0:T(8,128)(2,1)}, u32[]{:S(2)}, u32[]{:S(2)}) %all-to-all-start.8) | async-done | bytes 1048608 | tf_op jit(solution)/shard_map/all_to_all | solution.py:51
  232.8 1.3 slice_bitcast_fusion
  234.2 2.2 multiply_reduce_fusion
  236.4 1.3 reshape.274
  237.7 2.1 fusion.15
  239.8 2.1 convert_reduce_fusion.1
  241.9 1.4 compare_select_fusion.1
  244.0 10.8 %all_to_all.70 = f32[8,72,128]{2,1,0:T(8,128)} all-to-all(f32[8,72,128]{2,1,0:T(8,128)S(1)} %select_maximum_fusion), channel_id=1, replica_groups=mesh['zl'=8,'x'=4,'y'=4,'zh'=2,'c'=2] {'c','y'}, dimensions={0} | all-to-all | bytes 589824 | tf_op jit(solution)/shard_map/all_to_all | solution.py:55
  254.9 1.6 reduce_sum.227
  256.5 8.3 %collective-permute-start.3 = (f32[72,128]{1,0:T(8,128)}, f32[72,128]{1,0:T(8,128)S(1)}, u32[]{:S(2)}, u32[]{:S(2)}) collective-permute-start(f32[72,128]{1,0:T(8,128)} %reduce_sum.227), channel_id=1, source_target_pairs={{0,2},{2,0},{1,3},{3,1},{4,6},{6,4},{5,7},{7,5},{8,10},{10,8},{9,1... | collective-permute-start | bytes 110600 | tf_op jit(solution)/shard_map/ppermute | solution.py:47
  264.8 6.5 %collective-permute-done.3 = f32[72,128]{1,0:T(8,128)S(1)} collective-permute-done((f32[72,128]{1,0:T(8,128)}, f32[72,128]{1,0:T(8,128)S(1)}, u32[]{:S(2)}, u32[]{:S(2)}) %collective-permute-start.3) | collective-permute-done | bytes 36896 | tf_op jit(solution)/shard_map/ppermute | solution.py:47
  274.4 0.8 multiply_add_fusion
  276.7 10.5 %all_to_all.71 = f32[8,72,128]{2,1,0:T(8,128)S(1)} all-to-all(f32[8,72,128]{2,1,0:T(8,128)S(1)} %broadcast_in_dim.61), channel_id=1, replica_groups=mesh['zl'=8,'x'=4,'y'=4,'zh'=2,'c'=2] {'c','y'}, dimensions={0} | all-to-all | bytes 589824 | tf_op jit(solution)/shard_map/all_to_all | solution.py:51
  288.1 1.0 slice.85
  289.1 1.8 fusion.7
  290.9 1.6 convolution_convert_fusion
  292.5 1.5 copy.86
  294.1 18.2 %all_to_all.72 = bf16[4,8,64,224]{3,2,1,0:T(8,128)(2,1)S(1)} all-to-all(bf16[4,8,64,224]{3,2,1,0:T(8,128)(2,1)S(1)} %copy.87), channel_id=1, replica_groups=mesh['zl'=8,'x'=4,'y'=4,'zh'=2,'c'=2] {'x'}, dimensions={0} | all-to-all | bytes 1835008 | tf_op jit(solution)/shard_map/all_to_all | solution.py:55
  312.5 25.8 %all_to_all.73 = bf16[8,64,224]{2,1,0:T(8,128)(2,1)S(1)} all-to-all(bf16[8,64,224]{2,1,0:T(8,128)(2,1)S(1)} %reduce_sum.230), channel_id=1, replica_groups=mesh['zl'=8,'x'=4,'y'=4,'zh'=2,'c'=2] {'zl'}, dimensions={0} | all-to-all | bytes 458752 | tf_op jit(solution)/shard_map/all_to_all | solution.py:55
  (106 shorter events, 17.7 us)
Async XLA Ops:
  0.0 80.1 %copy-start = (bf16[2048,224]{0,1:T(8,128)(2,1)S(1)}, bf16[2048,224]{0,1:T(8,128)(2,1)}, u32[]{:S(2)}) copy-start(bf16[2048,224]{0,1:T(8,128)(2,1)} %param.14) | copy-start | bytes 2752516
  0.0 20.1 %copy-start.7 = (bf16[1,512,1024]{2,1,0:T(8,128)(2,1)S(1)}, bf16[1,512,1024]{2,1,0:T(8,128)(2,1)}, u32[]{:S(2)}) copy-start(bf16[1,512,1024]{2,1,0:T(8,128)(2,1)} %param.12) | copy-start | bytes 3145732
  1.5 0.8 copy-start.15
  2.3 28.9 %all-to-all-start = ((bf16[8,64,256]{2,1,0:T(8,128)(2,1)}), bf16[8,64,256]{2,1,0:T(8,128)(2,1)S(1)}, u32[]{:S(2)}, u32[]{:S(2)}) async-start(bf16[8,64,256]{2,1,0:T(8,128)(2,1)} %broadcast_in_dim.45), calls=%async_computation | async-start | bytes 524288 | tf_op jit(solution)/shard_map/all_to_all | solution.py:51
  32.3 24.0 %all-to-all-start.1 = ((bf16[4,8,64,256]{3,2,1,0:T(8,128)(2,1)}), bf16[4,8,64,256]{3,2,1,0:T(8,128)(2,1)S(1)}, u32[]{:S(2)}, u32[]{:S(2)}) async-start(bf16[4,8,64,256]{3,2,1,0:T(8,128)(2,1)} %broadcast_in_dim.46), calls=%async_computation.1 | async-start | bytes 2097152 | tf_op jit(solution)/shard_map/all_to_all | solution.py:51
  36.6 19.7 %collective-permute-start = (bf16[32,2048]{1,0:T(8,128)(2,1)S(1)}, bf16[32,2048]{1,0:T(8,128)(2,1)S(1)}, u32[]{:S(2)}, u32[]{:S(2)}) collective-permute-start(bf16[32,2048]{1,0:T(8,128)(2,1)S(1)} %convert_element_type.155), channel_id=1, source_target_pairs={{0,2},{2,0},{1,3},{3,1},{4,6},{6,4},{5,7},{7,5},{8,10},{10,8},{9,1... | collective-permute-start | bytes 393224 | tf_op jit(solution)/shard_map/ppermute | solution.py:47
  56.3 21.2 %copy-start.2 = (bf16[4,8,64,256]{3,2,1,0:T(8,128)(2,1)}, bf16[4,8,64,256]{3,2,1,0:T(8,128)(2,1)S(1)}, u32[]{:S(2)}) copy-start(bf16[4,8,64,256]{3,2,1,0:T(8,128)(2,1)S(1)} %all-to-all-done.1) | copy-start | bytes 3145732
  71.7 6.1 %collective-permute-start.1 = (bf16[256,2048]{1,0:T(8,128)(2,1)S(1)}, bf16[256,2048]{1,0:T(8,128)(2,1)}, u32[]{:S(2)}, u32[]{:S(2)}) collective-permute-start(bf16[256,2048]{1,0:T(8,128)(2,1)S(1)} %bitcast.104), channel_id=1, source_target_pairs={{0,1},{1,0},{2,3},{3,2},{4,5},{5,4},{6,7},{7,6},{8,9},{9,8},{10,11... | collective-permute-start | bytes 3145736 | tf_op jit(solution)/shard_map/ppermute | solution.py:47
  79.3 1.0 copy-start.3
  80.3 0.9 copy-start.1
  80.3 1.0 copy-start.4
  80.3 1.0 copy-start.12
  81.2 9.0 %copy-start.16 = (s32[1,512]{1,0:T(1,128)S(1)}, s32[1,512]{1,0:T(1,128)}, u32[]{:S(2)}) copy-start(s32[1,512]{1,0:T(1,128)} %param.19) | copy-start | bytes 6148
  85.5 14.3 %all-to-all-start.3 = ((f32[8,136,128]{2,1,0:T(8,128)}), f32[8,136,128]{2,1,0:T(8,128)}, u32[]{:S(2)}, u32[]{:S(2)}) async-start(f32[8,136,128]{2,1,0:T(8,128)} %pad_maximum_fusion.1), calls=%async_computation.3 | async-start | bytes 1114112 | tf_op jit(solution)/shard_map/all_to_all | solution.py:55
  100.8 8.2 %copy-start.10 = (f32[136,128]{1,0:T(8,128)}, f32[136,128]{1,0:T(8,128)S(1)}, u32[]{:S(2)}) copy-start(f32[136,128]{1,0:T(8,128)S(1)} %reduce_sum.215) | copy-start | bytes 208900
  100.8 16.0 %collective-permute-start.2 = (f32[136,128]{1,0:T(8,128)S(1)}, f32[136,128]{1,0:T(8,128)S(1)}, u32[]{:S(2)}, u32[]{:S(2)}) collective-permute-start(f32[136,128]{1,0:T(8,128)S(1)} %reduce_sum.215), channel_id=1, source_target_pairs={{0,2},{2,0},{1,3},{3,1},{4,6},{6,4},{5,7},{7,5},{8,10},{10,8},{9,1... | collective-permute-start | bytes 208904 | tf_op jit(solution)/shard_map/ppermute | solution.py:47
  109.0 9.7 %copy-start.13 = (s32[64]{0:T(128)}, s32[64]{0:T(128)S(1)}, u32[]{:S(2)}) copy-start(s32[64]{0:T(128)S(1)} %dynamic-slice_bitcast_fusion) | copy-start | bytes 772
  118.5 0.6 copy-start.14
  118.6 0.5 copy-start.17
  129.6 0.7 copy-start.5
  189.3 0.6 copy-start.8
  217.6 15.2 %all-to-all-start.8 = ((bf16[4,8,64,256]{3,2,1,0:T(8,128)(2,1)}), bf16[4,8,64,256]{3,2,1,0:T(8,128)(2,1)}, u32[]{:S(2)}, u32[]{:S(2)}) async-start(bf16[4,8,64,256]{3,2,1,0:T(8,128)(2,1)} %broadcast_in_dim.52), calls=%async_computation.8 | async-start | bytes 2097152 | tf_op jit(solution)/shard_map/all_to_all | solution.py:51
  256.5 14.8 %collective-permute-start.3 = (f32[72,128]{1,0:T(8,128)}, f32[72,128]{1,0:T(8,128)S(1)}, u32[]{:S(2)}, u32[]{:S(2)}) collective-permute-start(f32[72,128]{1,0:T(8,128)} %reduce_sum.227), channel_id=1, source_target_pairs={{0,2},{2,0},{1,3},{3,1},{4,6},{6,4},{5,7},{7,5},{8,10},{10,8},{9,1... | collective-permute-start | bytes 110600 | tf_op jit(solution)/shard_map/ppermute | solution.py:47
  287.2 0.7 copy-start.6
  294.1 44.3 %copy-start.9 = (f32[64,224]{1,0:T(8,128)S(1)}, f32[64,224]{1,0:T(8,128)}, u32[]{:S(2)}) copy-start(f32[64,224]{1,0:T(8,128)} %copy-done.8) | copy-start | bytes 172036
  294.1 44.3 %copy-start.11 = (f32[64,224]{1,0:T(8,128)S(1)}, f32[64,224]{1,0:T(8,128)}, u32[]{:S(2)}) copy-start(f32[64,224]{1,0:T(8,128)} %param.17) | copy-start | bytes 172036

commit v3 on v2

v3 whole, which is shorter than its diff:
```python
import functools

import jax
import jax.numpy as jnp
from jax import lax
from jax.experimental import pallas as pl
from jax.experimental.pallas import tpu as pltpu
from jax.sharding import Mesh, PartitionSpec as P

D = 3584
HD = 256
HQ = 8
HK = 4
TAGS = 128
WINDOW = 256
DAMP = 0.01
KEEP = 2.0 - DAMP
NORM_EPS = 1e-06
MEAN_EPS = 1e-06
ZL, X, Y, ZH, C = 8, 4, 4, 2, 2
ROWS = HQ * HD
COLS = 224
WIDE = 256
COUNT = HQ * HD * D
SPAN = 288
BF = jnp.bfloat16
F32 = jnp.float32
CONTRACT0 = (((0,), (0,)), ((), ()))
CONTRACT1 = (((1,), (1,)), ((), ()))


def call(kernel, out_shape, *args, smem=0):
    specs = [pl.BlockSpec(memory_space=pltpu.SMEM)] * smem
    specs += [pl.BlockSpec(memory_space=pltpu.VMEM)] * (len(args) - smem)
    scratch = kernel.keywords.pop("scratch", ()) if isinstance(kernel, functools.partial) else ()
    many = isinstance(out_shape, (tuple, list))
    vmem = pl.BlockSpec(memory_space=pltpu.VMEM)
    return pl.pallas_call(
        kernel,
        out_shape=out_shape,
        in_specs=specs,
        out_specs=[vmem] * len(out_shape) if many else vmem,
        scratch_shapes=scratch,
        compiler_params=pltpu.CompilerParams(vmem_limit_bytes=40 * 2**20),
    )(*args)


def shape(*dims, dtype=F32):
    return jax.ShapeDtypeStruct(dims, dtype)


def dot(a, b):
    return jnp.dot(a, b, preferred_element_type=F32)


def three(x):
    a = x.astype(BF)
    rest = x - a.astype(F32)
    b = rest.astype(BF)
    return a, b, (rest - b.astype(F32)).astype(BF)


def attend_kernel(place, starts, q_ref, k_ref, v_ref, o_ref):
    offset = place[1]
    first = pl.multiple_of(jnp.maximum(offset - WINDOW, 0), 32)
    q_row = lax.broadcasted_iota(jnp.int32, (64, 1), 0)
    q_pos = offset + jnp.where(q_row < 32, q_row, q_row - 32)
    k_pos = first + lax.broadcasted_iota(jnp.int32, (1, SPAN), 1)
    q_file = jnp.zeros((64, 1), jnp.int32)
    k_file = jnp.zeros((1, SPAN), jnp.int32)
    for f in range(4):
        q_file += jnp.where(starts[0, f] <= q_pos, 1, 0)
        k_file += jnp.where(starts[0, f] <= k_pos, 1, 0)
    allowed = (q_file == k_file) & (k_pos <= q_pos) & (q_pos - k_pos < WINDOW)
    for g in range(HK):
        q = jnp.concatenate(
            [q_ref[:, (2 * g + r) * HD : (2 * g + r + 1) * HD] for r in range(2)], 0
        )
        cols = slice(g * HD, (g + 1) * HD)
        scores = lax.dot_general(
            q, k_ref[pl.ds(first, SPAN), cols], CONTRACT1, preferred_element_type=F32
        )
        scores = 50.0 * jnp.tanh(scores * (1.0 / 16.0) / 50.0)
        expo = jnp.where(allowed, jnp.exp(scores), 0.0)
        weights = (expo / jnp.sum(expo, -1, keepdims=True)).astype(BF)
        out = dot(weights, v_ref[pl.ds(first, SPAN), cols]).astype(BF)
        for r in range(2):
            o_ref[:, (2 * g + r) * HD : (2 * g + r + 1) * HD] = out[r * 32 : r * 32 + 32]


def row_block(block):
    total = jnp.sum(block * block, -1, keepdims=True)
    hi = total.astype(BF)
    lo = (total - hi.astype(F32)).astype(BF)
    lane = lax.broadcasted_iota(jnp.int32, (64, WIDE - COLS), 1)
    tail = jnp.where(lane == 0, hi.astype(F32), jnp.where(lane == 1, lo.astype(F32), 0.0))
    return jnp.concatenate([block, tail], 1).astype(BF)


def direction_kernel(d_ref, o_ref):
    load = row_block(d_ref[...])
    for i in range(ZL):
        o_ref[i] = load


def sum_x_kernel(i_ref, o_ref):
    total = i_ref[0].astype(F32)
    for i in range(1, X):
        total += i_ref[i].astype(F32)
    o_ref[...] = total.astype(BF)


def sum_zl(i_ref):
    total = i_ref[0].astype(F32)
    for i in range(1, ZL):
        total += i_ref[i].astype(F32)
    return total


def sum_rows_kernel(i_ref, rows_ref, o_ref):
    total = sum_zl(i_ref)
    rows_ref[...] = total
    load = row_block(total)
    for i in range(ZL):
        o_ref[i] = load


def last_kernel(i_ref, rows_ref, d_ref, inv_ref, o_ref):
    damp = 1.0 - DAMP
    inv = inv_ref[0:1, 0:1]
    o_ref[...] = (1.0 + damp * KEEP) * d_ref[...] - (
        damp * rows_ref[...] + sum_zl(i_ref)
    ) * inv


def natural_rows(u_ref, rows_ref):
    for zl in range(ZL):
        for x in range(X):
            at = (zl * X + x) * 64
            rows_ref[at : at + 64, :] = u_ref[x, zl]
    return jnp.sum(rows_ref[:, COLS : COLS + 2].astype(F32))


def scores_of(x, gain, tag_ref):
    return sum(dot(part, tag_ref[...]) for part in three(x * gain))


def put_sums(load_ref, block, row, sums, scalar):
    lane = lax.broadcasted_iota(jnp.int32, (256, 128), 1)
    table = jnp.full((256, 128), scalar, F32)
    for i, s in enumerate(sums):
        table = jnp.where(lane == i, s, table)
    table = table.T
    for i in range(Y):
        load_ref[block + i, row : row + 8, 0:64] = table[0:8, i * 64 : (i + 1) * 64]
        load_ref[block + i, row : row + 8, 64:128] = table[0:8, 0:64]


def first_kernel(
    place, own_ref, oth_ref, u_ref, proj_ref, s_ref, gain_ref, tag_ref, h_ref, hd_ref, load_ref, rows_ref
):
    norm = natural_rows(u_ref, rows_ref)
    gain = gain_ref[...]
    for half, a_ref in enumerate((own_ref, oth_ref)):
        c = place[0] if half == 0 else 1 - place[0]
        at = pl.multiple_of(c * 256, 256)
        a = a_ref[...].reshape(256, ROWS)
        s = jnp.concatenate(
            [s_ref[y, zh, pl.ds(c, 1)][0] for y in range(Y) for zh in range(ZH)], 0
        )
        h = s.astype(F32) + dot(a, proj_ref[...])
        hd = dot(a, rows_ref[...])[:, :COLS]
        h_ref[pl.ds(at, 256), :] = h
        hd_ref[pl.ds(at, 256), :] = hd
        z = scores_of(h, gain, tag_ref)
        zd = scores_of(hd, gain, tag_ref)
        for i in range(Y):
            load_ref[c * Y + i, 0:64, :] = z[i * 64 : i * 64 + 64]
            load_ref[c * Y + i, 64:128, :] = zd[i * 64 : i * 64 + 64]
        sums = (jnp.sum(h * h, -1, keepdims=True), jnp.sum(h * hd, -1, keepdims=True))
        put_sums(load_ref, c * Y, 128, sums, norm)


def moved_kernel(place, own_ref, oth_ref, u_ref, h_ref, gain_ref, tag_ref, mv_ref, load_ref, rows_ref):
    norm = natural_rows(u_ref, rows_ref)
    gain = gain_ref[...]
    for half, a_ref in enumerate((own_ref, oth_ref)):
        c = place[0] if half == 0 else 1 - place[0]
        at = pl.multiple_of(c * 256, 256)
        moved = dot(a_ref[...].reshape(256, ROWS), rows_ref[...])[:, :COLS]
        mv_ref[pl.ds(at, 256), :] = moved
        z = scores_of(moved, gain, tag_ref)
        for i in range(Y):
            load_ref[c * Y + i, 0:64, :] = z[i * 64 : i * 64 + 64]
        sums = (jnp.sum(h_ref[pl.ds(at, 256), :] * moved, -1, keepdims=True),)
        put_sums(load_ref, c * Y, 64, sums, norm)


def sum_parts_kernel(i_ref, o_ref):
    total = i_ref[0]
    for i in range(1, 8):
        total += i_ref[i]
    o_ref[...] = total


def columns_of(rows):
    return jnp.concatenate([rows, jnp.zeros((120, 128), F32)], 0).T[:64]


def backward(zval, sumsq, tags, along, zdot, o_ref):
    rscale = lax.rsqrt(sumsq / D + NORM_EPS)
    tanh_val = jnp.tanh(rscale * zval / 30.0)
    slope = 1.0 - tanh_val * tanh_val
    expo = jnp.exp(30.0 * tanh_val)
    probs = expo / jnp.sum(expo, -1, keepdims=True)
    onehot = (tags == lax.broadcasted_iota(jnp.int32, (64, TAGS), 1)).astype(F32)
    dlogit = probs - onehot
    wgrad = dlogit * slope
    rho = jnp.sum(wgrad * zval, -1, keepdims=True)
    cube = rscale * rscale * rscale / D
    rdot = -cube * along
    mdot = rdot * zval + rscale * zdot
    ldot = slope * mdot
    pdot = probs * (ldot - jnp.sum(probs * ldot, -1, keepdims=True))
    wdot = pdot * slope - dlogit * 2.0 * tanh_val * slope * mdot / 30.0
    rhodot = jnp.sum(wdot * zval + wgrad * zdot, -1, keepdims=True)
    mixed = rdot * wgrad + rscale * wdot
    coeff = rhodot * cube + 3.0 * rho * rscale * rscale * rdot / D
    lane = lax.broadcasted_iota(jnp.int32, (64, 128), 1)
    table = jnp.where(lane == 0, coeff, jnp.where(lane == 1, rho * cube, 0.0))
    tail = jnp.concatenate([table, jnp.zeros((64, 128), F32)], 0).T[0:8]
    for i in range(8):
        o_ref[i, 0:64, :] = mixed
        o_ref[i, 64:72, :] = tail


def tokens0_kernel(mine_ref, their_ref, tag_ref, total_ref, o_ref):
    total_ref[...] = mine_ref[...] + their_ref[...]
    columns = columns_of(total_ref[128:136, :])
    backward(
        total_ref[0:64, :], columns[:, 0:1], tag_ref[...], columns[:, 1:2], total_ref[64:128, :], o_ref
    )


def tokens1_kernel(mine_ref, their_ref, total_ref, tag_ref, o_ref, inv_ref):
    moved = mine_ref[...] + their_ref[...]
    product_sq = moved[65:66, 0:1]
    norm_sq = total_ref[130:131, 0:1]
    sigma = 2.0 * jnp.sqrt((product_sq / COUNT + MEAN_EPS) / (norm_sq / COUNT + MEAN_EPS))
    inv = 1.0 / sigma
    inv_ref[...] = jnp.broadcast_to(inv, (8, 128))
    columns0 = columns_of(total_ref[128:136, :])
    columns1 = columns_of(moved[64:72])
    along = KEEP * columns0[:, 1:2] - columns1[:, 0:1] * inv
    zdot = KEEP * total_ref[64:128, :] - moved[0:64] * inv
    backward(total_ref[0:64, :], columns0[:, 0:1], tag_ref[...], along, zdot, o_ref)


def product_kernel(second, place, m_ref, h_ref, hd_ref, *rest):
    if second:
        mv_ref, inv_ref, *rest = rest
    own_ref, oth_ref, gain_ref, tag_ref, o_ref, g_ref = rest
    gain = gain_ref[...]
    for c in range(C):
        span = slice(c * 256, c * 256 + 256)
        mixed = jnp.concatenate([m_ref[c * Y + i, 0:64, :] for i in range(Y)], 0)
        back = sum(
            lax.dot_general(part, tag_ref[...], CONTRACT1, preferred_element_type=F32)
            for part in three(mixed)
        )
        columns = jnp.concatenate([columns_of(m_ref[c * Y + i, 64:72, :]) for i in range(Y)], 0)
        hd = hd_ref[span, :]
        if second:
            hd = KEEP * hd - mv_ref[span, :] * inv_ref[0:1, 0:1]
        g = back * gain - columns[:, 0:1] * h_ref[span, :] - columns[:, 1:2] * hd
        g_ref[span, :] = g.astype(BF)
    own_at = pl.multiple_of(place[0] * 256, 256)
    oth_at = pl.multiple_of((1 - place[0]) * 256, 256)
    g_own = g_ref[pl.ds(own_at, 256), :]
    g_oth = g_ref[pl.ds(oth_at, 256), :]
    for zl in range(ZL):
        cols = slice(zl * 256, zl * 256 + 256)
        part = lax.dot_general(
            own_ref[:, :, cols].reshape(256, 256), g_own, CONTRACT0, preferred_element_type=F32
        ) + lax.dot_general(
            oth_ref[:, :, cols].reshape(256, 256), g_oth, CONTRACT0, preferred_element_type=F32
        )
        for x in range(X):
            o_ref[x, zl] = part[x * 64 : x * 64 + 64].astype(BF)


def swap(x, axis):
    return lax.ppermute(x, axis, [(0, 1), (1, 0)])


def deal(x, axis):
    return lax.all_to_all(x, axis, 0, 0, tiled=True)


def spread(x, axis, n):
    return deal(jnp.broadcast_to(x[None], (n,) + x.shape), axis)


def local(queries, keys, values, stream, out_proj, norm_gain, tag_proj, direction, starts, tags):
    core = lax.axis_index("c")
    ypos = lax.axis_index("y")
    zhpos = lax.axis_index("zh")
    place = jnp.stack([core, ((ypos * ZH + zhpos) * C + core) * 32]).astype(jnp.int32)
    own_tags = tags[0].reshape(Y, ZH, C, 32).transpose(2, 0, 1, 3).reshape(C * Y, 64)[core * Y + ypos]
    own_tags = own_tags[:, None]
    toks = stream[0].reshape(Y, ZH, C, 32, COLS)
    gain = norm_gain[None]

    by_zl = deal(call(direction_kernel, shape(ZL, 64, WIDE, dtype=BF), direction), "zl")
    mine = call(
        attend_kernel, shape(32, ROWS, dtype=BF), place, starts, queries[0], keys[0], values[0], smem=2
    )
    mine, by_zl = lax.optimization_barrier((mine, by_zl))
    theirs, u0 = lax.optimization_barrier(
        (swap(mine, "zh"), spread(by_zl.reshape(ZL * 64, WIDE), "x", X).reshape(X, ZL, 64, WIDE))
    )
    low = zhpos == 0
    pair = jnp.stack([jnp.where(low, mine, theirs), jnp.where(low, theirs, mine)])
    own = spread(pair.reshape(64, ROWS), "y", Y)
    other = swap(own, "c")

    def product(second, *args):
        sent = call(
            functools.partial(product_kernel, second, scratch=[pltpu.VMEM((512, COLS), BF)]),
            shape(X, ZL, 64, COLS, dtype=BF),
            place,
            *args,
            own,
            other,
            gain,
            tag_proj,
            smem=1,
        )
        part = call(sum_x_kernel, shape(ZL, 64, COLS, dtype=BF), deal(sent, "x"))
        return deal(part, "zl")

    def token_sum(load, kernel, outs, *args):
        part = call(sum_parts_kernel, shape(load.shape[1], 128), deal(load, ("c", "y")))
        return call(kernel, outs, part, swap(part, "zh"), *args, own_tags)

    rows_scratch = [pltpu.VMEM((ROWS, WIDE), BF)]
    h_loc, hdot0, load = call(
        functools.partial(first_kernel, scratch=rows_scratch),
        (shape(512, COLS), shape(512, COLS), shape(8, 136, 128)),
        place,
        own,
        other,
        u0,
        out_proj,
        toks,
        gain,
        tag_proj,
        smem=1,
    )
    total, mixed = token_sum(load, tokens0_kernel, (shape(136, 128), shape(8, 72, 128)))
    rows0, sent = call(
        sum_rows_kernel,
        (shape(64, COLS), shape(ZL, 64, WIDE, dtype=BF)),
        product(False, deal(mixed, ("c", "y")), h_loc, hdot0),
    )
    full0 = spread(deal(sent, "zl").reshape(ZL * 64, WIDE), "x", X).reshape(X, ZL, 64, WIDE)
    moved, load = call(
        functools.partial(moved_kernel, scratch=rows_scratch),
        (shape(512, COLS), shape(8, 72, 128)),
        place,
        own,
        other,
        full0,
        h_loc,
        gain,
        tag_proj,
        smem=1,
    )
    mixed, inv = token_sum(load, tokens1_kernel, (shape(8, 72, 128), shape(8, 128)), total)
    arrived = product(True, deal(mixed, ("c", "y")), h_loc, hdot0, moved, inv)
    return call(last_kernel, shape(64, COLS), arrived, rows0, direction, inv)


def solution(mesh):
    fine = Mesh(mesh.devices.reshape(ZL, X, Y, ZH, C), ("zl", "x", "y", "zh", "c"))
    dp, mp = ("zl", "x"), ("y", "zh", "c")
    return jax.shard_map(
        local,
        mesh=fine,
        in_specs=(
            P(dp, mp, None),
            P(dp, None, None),
            P(dp, None, None),
            P(dp, None, mp),
            P(None, mp),
            P(mp),
            P(mp, None),
            P(dp, mp),
            P(dp, None),
            P(dp, None),
        ),
        out_specs=P(dp, mp),
        check_vma=False,
    )
```

time: 341 us -> 293 us (0.86)
  other arithmetic: 26 us -> 0.79 us
  local copies, waits for them, and re-layouts: 32.6 us -> 13.3 us
  matrix products: 17.7 us -> 0 us
  Pallas kernels: 0 us -> 13.3 us
  blocking collectives: 158 us -> 170 us
  starting transfers between devices: 52.1 us -> 47.4 us
  waiting for transfers between devices: 51.1 us -> 46.4 us
    all_to_all x5 -> x10, blocking collectives: 100 us -> 170 us  [deal(): return lax.all_to_all(x, axis, 0, 0, tiled=True)]
    all_to_all x4 -> x0, blocking collectives: 57.2 us -> none  [spread(): lax.all_to_all(jnp.broadcast_to(x[None], (n,) + x.shape), axis, 0, 0, til...]
    all_to_all x3 -> x0, starting transfers between devices: 21.4 us -> none  [spread(): lax.all_to_all(jnp.broadcast_to(x[None], (n,) + x.shape), axis, 0, 0, til...]
    dot_general x12 -> x0, matrix products: 17.7 us -> none  [the longest x3 5.24 us: tag_scores(): jnp.dot(hd, gained, precision=lax.Precision.HIGHEST).reshape(8, 64, TAGS)]
    all_to_all x3 -> x0, waiting for transfers between devices: 16.7 us -> none  [spread(): lax.all_to_all(jnp.broadcast_to(x[None], (n,) + x.shape), axis, 0, 0, til...]
    all_to_all x1 -> x3, starting transfers between devices: 4.19 us -> 20.6 us  [deal(): return lax.all_to_all(x, axis, 0, 0, tiled=True)]
    pallas_call x0 -> x14, Pallas kernels: none -> 13.3 us  [call(): pl.pallas_call(kernel, out_shape=out_shape, in_specs=specs, out_specs=[vm...]
    reduce_sum x14 -> x0, other arithmetic: 11.6 us -> none  [the longest x2 4.13 us: whole_rows(): return (rows, jnp.sum(by_all[..., 224:226].astype(F32)))]
  transfers between devices with their start and end apart: 8 -> 7, of which waited for: 6 -> 6; matrix products, arithmetic and copies ran while one was open for 5% -> 1% of each run, Pallas kernels for 0% -> 1%
where the time goes in v3:
time: 293 us; the launch traced here: 291 us
  blocking collectives  170 us (58%)
  starting transfers between devices  47.4 us (16%)
  waiting for transfers between devices  46.4 us (16%)
  local copies, waits for them, and re-layouts  13.3 us (5%)
  Pallas kernels  13.3 us (5%)
    all_to_all x10, blocking collectives, deal(): return lax.all_to_all(x, axis, 0, 0, tiled=True)  170 us
    ppermute x4, starting transfers between devices, swap(): return lax.ppermute(x, axis, [(0, 1), (1, 0)])  26.8 us
    ppermute x4, waiting for transfers between devices, swap(): return lax.ppermute(x, axis, [(0, 1), (1, 0)])  26.6 us
    all_to_all x3, starting transfers between devices, deal(): return lax.all_to_all(x, axis, 0, 0, tiled=True)  20.6 us
    all_to_all x3, waiting for transfers between devices, deal(): return lax.all_to_all(x, axis, 0, 0, tiled=True)  19.8 us
    pallas_call x14, Pallas kernels, call(): pl.pallas_call(kernel, out_shape=out_shape, in_specs=specs, out_specs=[vm...  13.3 us
    unnamed x37, local copies, waits for them, and re-layouts  11.8 us
  transfers between devices with their start and end apart: 7, of which 6 were waited for; matrix products, arithmetic and copies ran while one was open for 1% of the time, Pallas kernels for 1%

profile of v3, /device:TPU:32, one launch (start us, length us, event | category | flops | bytes accessed | tf_op | source)
XLA Modules:
  0.0 291.5 jit_solution(9369152412312940021)
XLA Ops:
  0.0 0.8 copy-done.9
  0.8 0.9 shard_map.101
  1.7 12.8 %all-to-all-start = ((bf16[8,64,256]{2,1,0:T(8,128)(2,1)}), bf16[8,64,256]{2,1,0:T(8,128)(2,1)S(1)}, u32[]{:S(2)}, u32[]{:S(2)}) async-start(bf16[8,64,256]{2,1,0:T(8,128)(2,1)} %shard_map.101), calls=%async_computation | async-start | bytes 524288 | tf_op jit(solution)/shard_map/all_to_all | solution.py:297
  14.5 0.1 pad_add_fusion.place
  14.6 0.0 copy-done.11
  14.6 0.7 copy-done.13
  15.2 1.2 copy-done.5
  16.4 1.2 copy-done.6
  17.7 1.8 shard_map.100
  19.5 11.3 %all-to-all-done = bf16[8,64,256]{2,1,0:T(8,128)(2,1)S(1)} async-done(((bf16[8,64,256]{2,1,0:T(8,128)(2,1)}), bf16[8,64,256]{2,1,0:T(8,128)(2,1)S(1)}, u32[]{:S(2)}, u32[]{:S(2)}) %all-to-all-start) | async-done | bytes 262176 | tf_op jit(solution)/shard_map/all_to_all | solution.py:297
  30.8 1.1 broadcast_in_dim.25
  31.8 4.3 %all-to-all-start.1 = ((bf16[4,512,256]{2,1,0:T(8,128)(2,1)}), bf16[4,512,256]{2,1,0:T(8,128)(2,1)S(1)}, u32[]{:S(2)}, u32[]{:S(2)}) async-start(bf16[4,512,256]{2,1,0:T(8,128)(2,1)} %broadcast_in_dim.25), calls=%async_computation.1 | async-start | bytes 2097152 | tf_op jit(solution)/shard_map/all_to_all | solution.py:297
  36.1 8.2 %collective-permute-start = (bf16[32,2048]{1,0:T(8,128)(2,1)S(1)}, bf16[32,2048]{1,0:T(8,128)(2,1)S(1)}, u32[]{:S(2)}, u32[]{:S(2)}) collective-permute-start(bf16[32,2048]{1,0:T(8,128)(2,1)S(1)} %shard_map.100), channel_id=1, source_target_pairs={{0,2},{2,0},{1,3},{3,1},{4,6},{6,4},{5,7},{7,5},{8,10},{10,8},{9,1... | collective-permute-start | bytes 393224 | tf_op jit(solution)/shard_map/ppermute | solution.py:293
  44.3 11.5 %collective-permute-done = bf16[32,2048]{1,0:T(8,128)(2,1)S(1)} collective-permute-done((bf16[32,2048]{1,0:T(8,128)(2,1)S(1)}, bf16[32,2048]{1,0:T(8,128)(2,1)S(1)}, u32[]{:S(2)}, u32[]{:S(2)}) %collective-permute-start) | collective-permute-done | bytes 131104 | tf_op jit(solution)/shard_map/ppermute | solution.py:293
  55.8 0.0 all-to-all-done.1
  55.9 0.9 copy-done
  56.8 0.1 broadcast_in_dim.27
  56.9 0.0 copy-start.14
  56.9 15.3 %all_to_all.65.own_ref.rest_0_.rest_2_ = bf16[4,64,2048]{2,1,0:T(8,128)(2,1)S(1)} all-to-all(bf16[4,64,2048]{2,1,0:T(8,128)(2,1)S(1)} %broadcast_in_dim.27), channel_id=1, replica_groups=mesh['zl'=8,'x'=4,'y'=4,'zh'=2,'c'=2] {'y'}, dimensions={0} | all-to-all | bytes 2097152 | tf_op jit(solution)/shard_map/all_to_all | solution.py:297
  72.2 2.0 collective-permute-start.1
  74.3 0.0 copy-done.14
  74.3 1.3 copy.12.proj_ref
  75.6 0.0 copy-done.15
  75.6 0.1 copy.11
  75.7 1.2 collective-permute-done.1.oth_ref.rest_1_.rest_3_
  76.9 0.7 copy-done.12
  77.6 1.2 copy-done.1
  78.8 1.2 copy-done.2
  80.0 2.4 shard_map.102
  82.5 0.8 copy-done.3
  83.3 0.8 copy-done.8
  84.1 3.5 %all-to-all-start.3 = ((f32[8,136,128]{2,1,0:T(8,128)}), f32[8,136,128]{2,1,0:T(8,128)S(1)}, u32[]{:S(2)}, u32[]{:S(2)}) async-start(f32[8,136,128]{2,1,0:T(8,128)} %copy-done.8), calls=%async_computation.3 | async-start | bytes 1114112 | tf_op jit(solution)/shard_map/all_to_all | solution.py:297
  87.7 0.0 copy-start.16
  87.7 0.5 broadcast.3
  88.2 0.2 copy-done.16
  88.4 0.7 reduce.3
  89.0 0.1 reshape_squeeze.7
  89.1 0.1 reshape.13
  89.2 8.5 %all-to-all-done.3.i_ref = f32[8,136,128]{2,1,0:T(8,128)S(1)} async-done(((f32[8,136,128]{2,1,0:T(8,128)}), f32[8,136,128]{2,1,0:T(8,128)S(1)}, u32[]{:S(2)}, u32[]{:S(2)}) %all-to-all-start.3) | async-done | bytes 557088 | tf_op jit(solution)/shard_map/all_to_all | solution.py:297
  97.7 8.3 %collective-permute-start.2 = (f32[136,128]{1,0:T(8,128)S(1)}, f32[136,128]{1,0:T(8,128)S(1)}, u32[]{:S(2)}, u32[]{:S(2)}) collective-permute-start(f32[136,128]{1,0:T(8,128)S(1)} %shard_map.103.mine_ref), channel_id=1, source_target_pairs={{0,2},{2,0},{1,3},{3,1},{4,6},{6,4},{5,7},{7,5},{8,10},{10,8},{9,1... | collective-permute-start | bytes 208904 | tf_op jit(solution)/shard_map/ppermute | solution.py:293
  106.0 0.1 copy.14.tag_ref
  106.1 7.7 %collective-permute-done.2.their_ref = f32[136,128]{1,0:T(8,128)S(1)} collective-permute-done((f32[136,128]{1,0:T(8,128)S(1)}, f32[136,128]{1,0:T(8,128)S(1)}, u32[]{:S(2)}, u32[]{:S(2)}) %collective-permute-start.2) | collective-permute-done | bytes 69664 | tf_op jit(solution)/shard_map/ppermute | solution.py:293
  113.8 0.6 shard_map.104
  114.4 10.5 %all_to_all.66.m_ref = f32[8,72,128]{2,1,0:T(8,128)S(1)} all-to-all(f32[8,72,128]{2,1,0:T(8,128)S(1)} %get-tuple-element.25), channel_id=1, replica_groups=mesh['zl'=8,'x'=4,'y'=4,'zh'=2,'c'=2] {'c','y'}, dimensions={0} | all-to-all | bytes 589824 | tf_op jit(solution)/shard_map/all_to_all | solution.py:297
  124.9 1.8 shard_map.105
  126.6 21.0 %all_to_all.67.i_ref = bf16[4,8,64,224]{3,2,1,0:T(8,128)(2,1)S(1)} all-to-all(bf16[4,8,64,224]{3,2,1,0:T(8,128)(2,1)S(1)} %shard_map.105), channel_id=1, replica_groups=mesh['zl'=8,'x'=4,'y'=4,'zh'=2,'c'=2] {'x'}, dimensions={0} | all-to-all | bytes 1835008 | tf_op jit(solution)/shard_map/all_to_all | solution.py:297
  147.7 0.1 shard_map.106
  147.8 24.2 %all_to_all.68.i_ref = bf16[8,64,224]{2,1,0:T(8,128)(2,1)S(1)} all-to-all(bf16[8,64,224]{2,1,0:T(8,128)(2,1)S(1)} %shard_map.106), channel_id=1, replica_groups=mesh['zl'=8,'x'=4,'y'=4,'zh'=2,'c'=2] {'zl'}, dimensions={0} | all-to-all | bytes 458752 | tf_op jit(solution)/shard_map/all_to_all | solution.py:297
  172.0 0.2 shard_map.107
  172.2 21.1 %all_to_all.69 = bf16[8,64,256]{2,1,0:T(8,128)(2,1)S(1)} all-to-all(bf16[8,64,256]{2,1,0:T(8,128)(2,1)S(1)} %get-tuple-element.28), channel_id=1, replica_groups=mesh['zl'=8,'x'=4,'y'=4,'zh'=2,'c'=2] {'zl'}, dimensions={0} | all-to-all | bytes 524288 | tf_op jit(solution)/shard_map/all_to_all | solution.py:297
  193.3 0.1 broadcast_in_dim.30
  193.3 13.3 %all_to_all.70 = bf16[4,512,256]{2,1,0:T(8,128)(2,1)S(1)} all-to-all(bf16[4,512,256]{2,1,0:T(8,128)(2,1)S(1)} %broadcast_in_dim.30), channel_id=1, replica_groups=mesh['zl'=8,'x'=4,'y'=4,'zh'=2,'c'=2] {'x'}, dimensions={0} | all-to-all | bytes 2097152 | tf_op jit(solution)/shard_map/all_to_all | solution.py:297
  206.6 2.3 shard_map.108
  208.9 10.1 %all_to_all.71.i_ref = f32[8,72,128]{2,1,0:T(8,128)S(1)} all-to-all(f32[8,72,128]{2,1,0:T(8,128)S(1)} %get-tuple-element.29), channel_id=1, replica_groups=mesh['zl'=8,'x'=4,'y'=4,'zh'=2,'c'=2] {'c','y'}, dimensions={0} | all-to-all | bytes 589824 | tf_op jit(solution)/shard_map/all_to_all | solution.py:297
  219.1 8.3 %collective-permute-start.3 = (f32[72,128]{1,0:T(8,128)S(1)}, f32[72,128]{1,0:T(8,128)S(1)}, u32[]{:S(2)}, u32[]{:S(2)}) collective-permute-start(f32[72,128]{1,0:T(8,128)S(1)} %shard_map.109.mine_ref), channel_id=1, source_target_pairs={{0,2},{2,0},{1,3},{3,1},{4,6},{6,4},{5,7},{7,5},{8,10},{10,8},{9,1... | collective-permute-start | bytes 110600 | tf_op jit(solution)/shard_map/ppermute | solution.py:293
  227.4 6.2 %collective-permute-done.3.their_ref = f32[72,128]{1,0:T(8,128)S(1)} collective-permute-done((f32[72,128]{1,0:T(8,128)S(1)}, f32[72,128]{1,0:T(8,128)S(1)}, u32[]{:S(2)}, u32[]{:S(2)}) %collective-permute-start.3) | collective-permute-done | bytes 36896 | tf_op jit(solution)/shard_map/ppermute | solution.py:293
  233.7 0.6 shard_map.110
  234.3 10.5 %all_to_all.72.m_ref = f32[8,72,128]{2,1,0:T(8,128)S(1)} all-to-all(f32[8,72,128]{2,1,0:T(8,128)S(1)} %get-tuple-element.31), channel_id=1, replica_groups=mesh['zl'=8,'x'=4,'y'=4,'zh'=2,'c'=2] {'c','y'}, dimensions={0} | all-to-all | bytes 589824 | tf_op jit(solution)/shard_map/all_to_all | solution.py:297
  244.8 1.8 shard_map.111
  246.6 18.1 %all_to_all.73.i_ref = bf16[4,8,64,224]{3,2,1,0:T(8,128)(2,1)S(1)} all-to-all(bf16[4,8,64,224]{3,2,1,0:T(8,128)(2,1)S(1)} %shard_map.111), channel_id=1, replica_groups=mesh['zl'=8,'x'=4,'y'=4,'zh'=2,'c'=2] {'x'}, dimensions={0} | all-to-all | bytes 1835008 | tf_op jit(solution)/shard_map/all_to_all | solution.py:297
  264.7 0.1 shard_map.112
  264.8 0.0 copy-start.10
  264.8 26.0 %all_to_all.74.i_ref = bf16[8,64,224]{2,1,0:T(8,128)(2,1)S(1)} all-to-all(bf16[8,64,224]{2,1,0:T(8,128)(2,1)S(1)} %shard_map.112), channel_id=1, replica_groups=mesh['zl'=8,'x'=4,'y'=4,'zh'=2,'c'=2] {'zl'}, dimensions={0} | all-to-all | bytes 458752 | tf_op jit(solution)/shard_map/all_to_all | solution.py:297
  290.8 0.7 shard_map.113
  (23 shorter events, 0.1 us)
Async XLA Ops:
  0.0 0.8 copy-start.9
  1.7 12.8 %copy-start.11 = (bf16[1,32,2048]{2,1,0:T(8,128)(2,1)S(1)}, bf16[1,32,2048]{2,1,0:T(8,128)(2,1)}, u32[]{:S(2)}) copy-start(bf16[1,32,2048]{2,1,0:T(8,128)(2,1)} %param.10) | copy-start | bytes 393220
  1.7 29.0 %all-to-all-start = ((bf16[8,64,256]{2,1,0:T(8,128)(2,1)}), bf16[8,64,256]{2,1,0:T(8,128)(2,1)S(1)}, u32[]{:S(2)}, u32[]{:S(2)}) async-start(bf16[8,64,256]{2,1,0:T(8,128)(2,1)} %shard_map.101), calls=%async_computation | async-start | bytes 524288 | tf_op jit(solution)/shard_map/all_to_all | solution.py:297
  14.6 0.7 copy-start.13
  15.2 1.2 copy-start.5
  16.4 1.2 copy-start.6
  31.8 24.0 %all-to-all-start.1 = ((bf16[4,512,256]{2,1,0:T(8,128)(2,1)}), bf16[4,512,256]{2,1,0:T(8,128)(2,1)S(1)}, u32[]{:S(2)}, u32[]{:S(2)}) async-start(bf16[4,512,256]{2,1,0:T(8,128)(2,1)} %broadcast_in_dim.25), calls=%async_computation.1 | async-start | bytes 2097152 | tf_op jit(solution)/shard_map/all_to_all | solution.py:297
  36.1 19.7 %collective-permute-start = (bf16[32,2048]{1,0:T(8,128)(2,1)S(1)}, bf16[32,2048]{1,0:T(8,128)(2,1)S(1)}, u32[]{:S(2)}, u32[]{:S(2)}) collective-permute-start(bf16[32,2048]{1,0:T(8,128)(2,1)S(1)} %shard_map.100), channel_id=1, source_target_pairs={{0,2},{2,0},{1,3},{3,1},{4,6},{6,4},{5,7},{7,5},{8,10},{10,8},{9,1... | collective-permute-start | bytes 393224 | tf_op jit(solution)/shard_map/ppermute | solution.py:293
  55.8 1.0 copy-start
  56.9 17.4 %copy-start.14 = (bf16[2048,224]{0,1:T(8,128)(2,1)S(1)}, bf16[2048,224]{0,1:T(8,128)(2,1)}, u32[]{:S(2)}) copy-start(bf16[2048,224]{0,1:T(8,128)(2,1)} %param.14) | copy-start | bytes 2752516
  72.2 3.4 %copy-start.15 = (bf16[1,512,224]{1,2,0:T(8,128)(2,1)S(1)}, bf16[1,512,224]{1,2,0:T(8,128)(2,1)}, u32[]{:S(2)}) copy-start(bf16[1,512,224]{1,2,0:T(8,128)(2,1)} %param.13) | copy-start | bytes 688132
  72.2 4.7 %collective-permute-start.1 = (bf16[4,64,2048]{2,1,0:T(8,128)(2,1)S(1)}, bf16[4,64,2048]{2,1,0:T(8,128)(2,1)S(1)}, u32[]{:S(2)}, u32[]{:S(2)}) collective-permute-start(bf16[4,64,2048]{2,1,0:T(8,128)(2,1)S(1)} %all_to_all.65.own_ref.rest_0_.rest_2_), channel_id=1, source_target_pairs={{0,1},{1,0},{2,3},{3,2},{4,5},{5,4},{6,7},{7,6},{8,9},{9,8},{10,11... | collective-permute-start | bytes 3145736 | tf_op jit(solution)/shard_map/ppermute | solution.py:293
  75.6 1.3 copy-start.7
  76.9 0.7 copy-start.12
  77.6 1.2 copy-start.1
  78.8 1.2 copy-start.2
  82.5 0.8 copy-start.3
  83.3 0.8 copy-start.8
  84.1 13.5 %all-to-all-start.3 = ((f32[8,136,128]{2,1,0:T(8,128)}), f32[8,136,128]{2,1,0:T(8,128)S(1)}, u32[]{:S(2)}, u32[]{:S(2)}) async-start(f32[8,136,128]{2,1,0:T(8,128)} %copy-done.8), calls=%async_computation.3 | async-start | bytes 1114112 | tf_op jit(solution)/shard_map/all_to_all | solution.py:297
  87.7 0.7 copy-start.16
  97.7 27.2 %copy-start.4 = (f32[512,224]{1,0:T(8,128)S(1)}, f32[512,224]{1,0:T(8,128)}, u32[]{:S(2)}) copy-start(f32[512,224]{1,0:T(8,128)} %copy-done.3) | copy-start | bytes 1376260
  97.7 16.1 %collective-permute-start.2 = (f32[136,128]{1,0:T(8,128)S(1)}, f32[136,128]{1,0:T(8,128)S(1)}, u32[]{:S(2)}, u32[]{:S(2)}) collective-permute-start(f32[136,128]{1,0:T(8,128)S(1)} %shard_map.103.mine_ref), channel_id=1, source_target_pairs={{0,2},{2,0},{1,3},{3,1},{4,6},{6,4},{5,7},{7,5},{8,10},{10,8},{9,1... | collective-permute-start | bytes 208904 | tf_op jit(solution)/shard_map/ppermute | solution.py:293
  219.1 14.6 %collective-permute-start.3 = (f32[72,128]{1,0:T(8,128)S(1)}, f32[72,128]{1,0:T(8,128)S(1)}, u32[]{:S(2)}, u32[]{:S(2)}) collective-permute-start(f32[72,128]{1,0:T(8,128)S(1)} %shard_map.109.mine_ref), channel_id=1, source_target_pairs={{0,2},{2,0},{1,3},{3,1},{4,6},{6,4},{5,7},{7,5},{8,10},{10,8},{9,1... | collective-permute-start | bytes 110600 | tf_op jit(solution)/shard_map/ppermute | solution.py:293
  264.8 26.0 %copy-start.10 = (f32[64,224]{1,0:T(8,128)S(1)}, f32[64,224]{1,0:T(8,128)}, u32[]{:S(2)}) copy-start(f32[64,224]{1,0:T(8,128)} %d_ref.3) | copy-start | bytes 172036

commit v4 on v3

--- a/solution.py
+++ b/solution.py
@@ -29,9 +29,10 @@
 CONTRACT1 = (((1,), (1,)), ((), ()))
 
 
-def call(kernel, out_shape, *args, smem=0):
+def call(kernel, out_shape, *args, smem=0, far=0):
     specs = [pl.BlockSpec(memory_space=pltpu.SMEM)] * smem
-    specs += [pl.BlockSpec(memory_space=pltpu.VMEM)] * (len(args) - smem)
+    specs += [pl.BlockSpec(memory_space=pl.ANY)] * far
+    specs += [pl.BlockSpec(memory_space=pltpu.VMEM)] * (len(args) - smem - far)
     scratch = kernel.keywords.pop("scratch", ()) if isinstance(kernel, functools.partial) else ()
     many = isinstance(out_shape, (tuple, list))
     vmem = pl.BlockSpec(memory_space=pltpu.VMEM)
@@ -133,12 +134,22 @@
     ) * inv
 
 
-def natural_rows(u_ref, rows_ref):
-    for zl in range(ZL):
-        for x in range(X):
-            at = (zl * X + x) * 64
-            rows_ref[at : at + 64, :] = u_ref[x, zl]
-    return jnp.sum(rows_ref[:, COLS : COLS + 2].astype(F32))
+def start_rows(u_refs, xs, rows_ref, sems):
+    copies = [
+        pltpu.make_async_copy(u, rows_ref.at[:, x], sems.at[i]) for i, (u, x) in enumerate(zip(u_refs, xs))
+    ]
+    for copy in copies:
+        copy.start()
+    return copies
+
+
+def await_rows(copies, rows_ref):
+    for copy in copies:
+        copy.wait()
+    return (
+        rows_ref[...].reshape(ROWS, WIDE),
+        jnp.sum(rows_ref[:, :, :, COLS : COLS + 2].astype(F32)),
+    )
 
 
 def scores_of(x, gain, tag_ref):
@@ -157,10 +168,13 @@
 
 
 def first_kernel(
-    place, own_ref, oth_ref, u_ref, proj_ref, s_ref, gain_ref, tag_ref, h_ref, hd_ref, load_ref, rows_ref
+    place, u0, u1, u2, u3, own_ref, oth_ref, proj_ref, s_ref, gain_ref, tag_ref, h_ref, hd_ref, load_ref,
+    rows_ref, sems,
 ):
-    norm = natural_rows(u_ref, rows_ref)
+    xs = [lax.rem(place[2] + X - r, X) for r in range(X)]
+    copies = start_rows((u0, u1, u2, u3), xs, rows_ref, sems)
     gain = gain_ref[...]
+    halves = []
     for half, a_ref in enumerate((own_ref, oth_ref)):
         c = place[0] if half == 0 else 1 - place[0]
         at = pl.multiple_of(c * 256, 256)
@@ -168,26 +182,34 @@
         s = jnp.concatenate(
             [s_ref[y, zh, pl.ds(c, 1)][0] for y in range(Y) for zh in range(ZH)], 0
         )
-        h = s.astype(F32) + dot(a, proj_ref[...])
-        hd = dot(a, rows_ref[...])[:, :COLS]
+        h = s.astype(F32) + lax.dot_general(a, proj_ref[...], CONTRACT1, preferred_element_type=F32)
         h_ref[pl.ds(at, 256), :] = h
+        z = scores_of(h, gain, tag_ref)
+        for i in range(Y):
+            load_ref[c * Y + i, 0:64, :] = z[i * 64 : i * 64 + 64]
+        halves.append((c, at, a_ref))
+    rows, norm = await_rows(copies, rows_ref)
+    for c, at, a_ref in halves:
+        h = h_ref[pl.ds(at, 256), :]
+        hd = dot(a_ref[...].reshape(256, ROWS), rows)[:, :COLS]
         hd_ref[pl.ds(at, 256), :] = hd
-        z = scores_of(h, gain, tag_ref)
         zd = scores_of(hd, gain, tag_ref)
         for i in range(Y):
-            load_ref[c * Y + i, 0:64, :] = z[i * 64 : i * 64 + 64]
             load_ref[c * Y + i, 64:128, :] = zd[i * 64 : i * 64 + 64]
         sums = (jnp.sum(h * h, -1, keepdims=True), jnp.sum(h * hd, -1, keepdims=True))
         put_sums(load_ref, c * Y, 128, sums, norm)
 
 
-def moved_kernel(place, own_ref, oth_ref, u_ref, h_ref, gain_ref, tag_ref, mv_ref, load_ref, rows_ref):
-    norm = natural_rows(u_ref, rows_ref)
+def moved_kernel(
+    place, u_ref, own_ref, oth_ref, h_ref, gain_ref, tag_ref, mv_ref, load_ref, rows_ref, sems
+):
+    copies = start_rows([u_ref.at[x] for x in range(X)], range(X), rows_ref, sems)
+    rows, norm = await_rows(copies, rows_ref)
     gain = gain_ref[...]
     for half, a_ref in enumerate((own_ref, oth_ref)):
         c = place[0] if half == 0 else 1 - place[0]
         at = pl.multiple_of(c * 256, 256)
-        moved = dot(a_ref[...].reshape(256, ROWS), rows_ref[...])[:, :COLS]
+        moved = dot(a_ref[...].reshape(256, ROWS), rows)[:, :COLS]
         mv_ref[pl.ds(at, 256), :] = moved
         z = scores_of(moved, gain, tag_ref)
         for i in range(Y):
@@ -305,7 +327,8 @@
     core = lax.axis_index("c")
     ypos = lax.axis_index("y")
     zhpos = lax.axis_index("zh")
-    place = jnp.stack([core, ((ypos * ZH + zhpos) * C + core) * 32]).astype(jnp.int32)
+    offset = ((ypos * ZH + zhpos) * C + core) * 32
+    place = jnp.stack([core, offset, lax.axis_index("x")]).astype(jnp.int32)
     own_tags = tags[0].reshape(Y, ZH, C, 32).transpose(2, 0, 1, 3).reshape(C * Y, 64)[core * Y + ypos]
     own_tags = own_tags[:, None]
     toks = stream[0].reshape(Y, ZH, C, 32, COLS)
@@ -315,13 +338,13 @@
     mine = call(
         attend_kernel, shape(32, ROWS, dtype=BF), place, starts, queries[0], keys[0], values[0], smem=2
     )
-    mine, by_zl = lax.optimization_barrier((mine, by_zl))
-    theirs, u0 = lax.optimization_barrier(
-        (swap(mine, "zh"), spread(by_zl.reshape(ZL * 64, WIDE), "x", X).reshape(X, ZL, 64, WIDE))
-    )
+    theirs, by_zl = lax.optimization_barrier((swap(mine, "zh"), by_zl))
+    u0 = [by_zl] + [
+        lax.ppermute(by_zl, "x", [(i, (i + r) % X) for i in range(X)]) for r in range(1, X)
+    ]
     low = zhpos == 0
     pair = jnp.stack([jnp.where(low, mine, theirs), jnp.where(low, theirs, mine)])
-    own = spread(pair.reshape(64, ROWS), "y", Y)
+    own, *u0 = lax.optimization_barrier((spread(pair.reshape(64, ROWS), "y", Y), *u0))
     other = swap(own, "c")
 
     def product(second, *args):
@@ -343,19 +366,20 @@
         part = call(sum_parts_kernel, shape(load.shape[1], 128), deal(load, ("c", "y")))
         return call(kernel, outs, part, swap(part, "zh"), *args, own_tags)
 
-    rows_scratch = [pltpu.VMEM((ROWS, WIDE), BF)]
+    rows_scratch = [pltpu.VMEM((ZL, X, 64, WIDE), BF), pltpu.SemaphoreType.DMA((X,))]
     h_loc, hdot0, load = call(
         functools.partial(first_kernel, scratch=rows_scratch),
         (shape(512, COLS), shape(512, COLS), shape(8, 136, 128)),
         place,
+        *u0,
         own,
         other,
-        u0,
-        out_proj,
+        out_proj.T,
         toks,
         gain,
         tag_proj,
         smem=1,
+        far=X,
     )
     total, mixed = token_sum(load, tokens0_kernel, (shape(136, 128), shape(8, 72, 128)))
     rows0, sent = call(
@@ -368,13 +392,14 @@
         functools.partial(moved_kernel, scratch=rows_scratch),
         (shape(512, COLS), shape(8, 72, 128)),
         place,
+        full0,
         own,
         other,
-        full0,
         h_loc,
         gain,
         tag_proj,
         smem=1,
+        far=1,
     )
     mixed, inv = token_sum(load, tokens1_kernel, (shape(8, 72, 128), shape(8, 128)), total)
     arrived = product(True, deal(mixed, ("c", "y")), h_loc, hdot0, moved, inv)

time: 293 us -> 292 us (level)
  blocking collectives: 170 us -> 160 us
  starting transfers between devices: 47.4 us -> 56.8 us
    all_to_all x3, waiting for transfers between devices: 19.8 us -> 8.56 us  [deal(): return lax.all_to_all(x, axis, 0, 0, tiled=True)]
    ppermute x0 -> x3, starting transfers between devices: none -> 10.3 us  [local(): lax.ppermute(by_zl, 'x', [(i, (i + r) % X) for i in range(X)])]
    all_to_all x10 -> x9, blocking collectives: 170 us -> 160 us  [deal(): return lax.all_to_all(x, axis, 0, 0, tiled=True)]
    ppermute x0 -> x3, waiting for transfers between devices: none -> 8.55 us  [local(): lax.ppermute(by_zl, 'x', [(i, (i + r) % X) for i in range(X)])]
    unnamed x37 -> x36, local copies, waits for them, and re-layouts: 11.8 us -> 11.8 us
  transfers between devices with their start and end apart: 7 -> 10, of which waited for: 6 -> 8; matrix products, arithmetic and copies ran while one was open for 1% -> 1% of each run, Pallas kernels for 1% -> 1%
where the time goes in v4:
time: 292 us; the launch traced here: 291 us
  blocking collectives  160 us (55%)
  starting transfers between devices  56.8 us (19%)
  waiting for transfers between devices  44.5 us (15%)
  Pallas kernels  15.3 us (5%)
  local copies, waits for them, and re-layouts  13.2 us (5%)
    all_to_all x9, blocking collectives, deal(): return lax.all_to_all(x, axis, 0, 0, tiled=True)  160 us
    ppermute x4, waiting for transfers between devices, swap(): return lax.ppermute(x, axis, [(0, 1), (1, 0)])  27.4 us
    ppermute x4, starting transfers between devices, swap(): return lax.ppermute(x, axis, [(0, 1), (1, 0)])  24.7 us
    all_to_all x3, starting transfers between devices, deal(): return lax.all_to_all(x, axis, 0, 0, tiled=True)  21.7 us
    pallas_call x14, Pallas kernels, call(): pl.pallas_call(kernel, out_shape=out_shape, in_specs=specs, out_specs=[vm...  15.3 us
    unnamed x36, local copies, waits for them, and re-layouts  11.8 us
    ppermute x3, starting transfers between devices, local(): lax.ppermute(by_zl, 'x', [(i, (i + r) % X) for i in range(X)])  10.3 us
    all_to_all x3, waiting for transfers between devices, deal(): return lax.all_to_all(x, axis, 0, 0, tiled=True)  8.56 us
  transfers between devices with their start and end apart: 10, of which 8 were waited for; matrix products, arithmetic and copies ran while one was open for 1% of the time, Pallas kernels for 1%

profile of v4, /device:TPU:32, one launch (start us, length us, event | category | flops | bytes accessed | tf_op | source)
XLA Modules:
  0.0 290.6 jit_solution(4740848618196943684)
XLA Ops:
  0.0 0.8 copy-done.11
  0.8 0.9 shard_map.101
  1.7 12.8 %all-to-all-start = ((bf16[8,64,256]{2,1,0:T(8,128)(2,1)}), bf16[8,64,256]{2,1,0:T(8,128)(2,1)S(1)}, u32[]{:S(2)}, u32[]{:S(2)}) async-start(bf16[8,64,256]{2,1,0:T(8,128)(2,1)} %shard_map.101), calls=%async_computation | async-start | bytes 524288 | tf_op jit(solution)/shard_map/all_to_all | solution.py:319
  14.5 0.1 pad_add_fusion.place
  14.5 0.0 copy-done.13
  14.5 0.7 copy-done.15
  15.2 1.2 copy-done.2
  16.4 1.2 copy-done.3
  17.7 1.8 shard_map.100
  19.4 8.2 %collective-permute-start = (bf16[32,2048]{1,0:T(8,128)(2,1)S(1)}, bf16[32,2048]{1,0:T(8,128)(2,1)S(1)}, u32[]{:S(2)}, u32[]{:S(2)}) collective-permute-start(bf16[32,2048]{1,0:T(8,128)(2,1)S(1)} %shard_map.100), channel_id=1, source_target_pairs={{0,2},{2,0},{1,3},{3,1},{4,6},{6,4},{5,7},{7,5},{8,10},{10,8},{9,1... | collective-permute-start | bytes 393224 | tf_op jit(solution)/shard_map/ppermute | solution.py:315
  27.7 10.9 %collective-permute-done = bf16[32,2048]{1,0:T(8,128)(2,1)S(1)} collective-permute-done((bf16[32,2048]{1,0:T(8,128)(2,1)S(1)}, bf16[32,2048]{1,0:T(8,128)(2,1)S(1)}, u32[]{:S(2)}, u32[]{:S(2)}) %collective-permute-start) | collective-permute-done | bytes 131104 | tf_op jit(solution)/shard_map/ppermute | solution.py:315
  38.6 0.0 all-to-all-done.u0
  38.7 1.1 broadcast_in_dim.18
  39.8 4.5 %all-to-all-start.1 = ((bf16[4,64,2048]{2,1,0:T(8,128)(2,1)}), bf16[4,64,2048]{2,1,0:T(8,128)(2,1)S(1)}, u32[]{:S(2)}, u32[]{:S(2)}) async-start(bf16[4,64,2048]{2,1,0:T(8,128)(2,1)} %broadcast_in_dim.18), calls=%async_computation.1 | async-start | bytes 2097152 | tf_op jit(solution)/shard_map/all_to_all | solution.py:319
  44.2 4.8 %collective-permute-start.3 = (bf16[8,64,256]{2,1,0:T(8,128)(2,1)S(1)}, bf16[8,64,256]{2,1,0:T(8,128)(2,1)S(1)}, u32[]{:S(2)}, u32[]{:S(2)}) collective-permute-start(bf16[8,64,256]{2,1,0:T(8,128)(2,1)S(1)} %all-to-all-done.u0), channel_id=1, source_target_pairs={{0,48},{16,0},{32,16},{48,32},{1,49},{17,1},{33,17},{49,33},{2,50}... | collective-permute-start | bytes 786440 | tf_op jit(solution)/shard_map/ppermute | solution.py:343
  49.0 2.7 collective-permute-start.2
  51.7 2.8 collective-permute-start.1
  54.5 3.5 %collective-permute-done.3.u3 = bf16[8,64,256]{2,1,0:T(8,128)(2,1)S(1)} collective-permute-done((bf16[8,64,256]{2,1,0:T(8,128)(2,1)S(1)}, bf16[8,64,256]{2,1,0:T(8,128)(2,1)S(1)}, u32[]{:S(2)}, u32[]{:S(2)}) %collective-permute-start.3) | collective-permute-done | bytes 262176 | tf_op jit(solution)/shard_map/ppermute | solution.py:343
  58.0 2.4 collective-permute-done.2.u2
  60.4 2.7 collective-permute-done.1.u1
  63.1 0.7 copy-done.9
  63.8 0.0 all-to-all-done.1.own_ref.rest_0_.rest_2_
  63.8 1.9 collective-permute-start.4
  65.7 1.1 copy.11
  66.8 1.5 collective-permute-done.4.oth_ref.rest_1_.rest_3_
  68.3 0.7 copy-done.14
  69.0 1.2 copy-done.5
  70.2 0.9 copy-done.8
  71.2 0.9 copy-done.10
  72.1 4.2 %shard_map.102 = (f32[512,224]{1,0:T(8,128)S(1)}, f32[512,224]{1,0:T(8,128)S(1)}, f32[8,136,128]{2,1,0:T(8,128)S(1)}) custom-call(s32[3]{0:T(128)S(1)} %pad_add_fusion.place, bf16[8,64,256]{2,1,0:T(8,128)(2,1)S(1)} %all-to-all-done.u0, bf16[8,64,256]{2,1,0:T(8,128)(2,1)S(1)} %copy-done.10, bf16[8,64,256]{2,1,0:T(8,128)(2,1)S(1)} %copy-done.8, ...), custom_call_target="tpu_custom_call" | custom-call | tf_op jit(solution)/shard_map/pallas_call | solution.py:39
  76.3 0.8 copy-done
  77.1 0.8 copy-done.6
  77.9 4.5 %all-to-all-start.2 = ((f32[8,136,128]{2,1,0:T(8,128)}), f32[8,136,128]{2,1,0:T(8,128)S(1)}, u32[]{:S(2)}, u32[]{:S(2)}) async-start(f32[8,136,128]{2,1,0:T(8,128)} %copy-done.6), calls=%async_computation.2 | async-start | bytes 1114112 | tf_op jit(solution)/shard_map/all_to_all | solution.py:319
  82.5 0.5 broadcast.3
  83.0 0.2 copy-done.16
  83.2 0.7 reduce.3
  83.8 0.1 reshape_squeeze.7
  83.9 0.1 reshape.8
  84.0 8.6 %all-to-all-done.2.i_ref = f32[8,136,128]{2,1,0:T(8,128)S(1)} async-done(((f32[8,136,128]{2,1,0:T(8,128)}), f32[8,136,128]{2,1,0:T(8,128)S(1)}, u32[]{:S(2)}, u32[]{:S(2)}) %all-to-all-start.2) | async-done | bytes 557088 | tf_op jit(solution)/shard_map/all_to_all | solution.py:319
  92.6 6.7 %collective-permute-start.5 = (f32[136,128]{1,0:T(8,128)S(1)}, f32[136,128]{1,0:T(8,128)S(1)}, u32[]{:S(2)}, u32[]{:S(2)}) collective-permute-start(f32[136,128]{1,0:T(8,128)S(1)} %shard_map.103.mine_ref), channel_id=1, source_target_pairs={{0,2},{2,0},{1,3},{3,1},{4,6},{6,4},{5,7},{7,5},{8,10},{10,8},{9,1... | collective-permute-start | bytes 208904 | tf_op jit(solution)/shard_map/ppermute | solution.py:315
  99.3 0.1 copy.13.tag_ref
  99.4 8.2 %collective-permute-done.5.their_ref = f32[136,128]{1,0:T(8,128)S(1)} collective-permute-done((f32[136,128]{1,0:T(8,128)S(1)}, f32[136,128]{1,0:T(8,128)S(1)}, u32[]{:S(2)}, u32[]{:S(2)}) %collective-permute-start.5) | collective-permute-done | bytes 69664 | tf_op jit(solution)/shard_map/ppermute | solution.py:315
  107.6 0.6 shard_map.104
  108.2 10.6 %all_to_all.60.m_ref = f32[8,72,128]{2,1,0:T(8,128)S(1)} all-to-all(f32[8,72,128]{2,1,0:T(8,128)S(1)} %get-tuple-element.31), channel_id=1, replica_groups=mesh['zl'=8,'x'=4,'y'=4,'zh'=2,'c'=2] {'c','y'}, dimensions={0} | all-to-all | bytes 589824 | tf_op jit(solution)/shard_map/all_to_all | solution.py:319
  118.8 1.8 shard_map.105
  120.6 18.1 %all_to_all.61.i_ref = bf16[4,8,64,224]{3,2,1,0:T(8,128)(2,1)S(1)} all-to-all(bf16[4,8,64,224]{3,2,1,0:T(8,128)(2,1)S(1)} %shard_map.105), channel_id=1, replica_groups=mesh['zl'=8,'x'=4,'y'=4,'zh'=2,'c'=2] {'x'}, dimensions={0} | all-to-all | bytes 1835008 | tf_op jit(solution)/shard_map/all_to_all | solution.py:319
  138.7 0.1 shard_map.106
  138.8 31.8 %all_to_all.62.i_ref = bf16[8,64,224]{2,1,0:T(8,128)(2,1)S(1)} all-to-all(bf16[8,64,224]{2,1,0:T(8,128)(2,1)S(1)} %shard_map.106), channel_id=1, replica_groups=mesh['zl'=8,'x'=4,'y'=4,'zh'=2,'c'=2] {'zl'}, dimensions={0} | all-to-all | bytes 458752 | tf_op jit(solution)/shard_map/all_to_all | solution.py:319
  170.6 0.2 shard_map.107
  170.8 21.1 %all_to_all.63 = bf16[8,64,256]{2,1,0:T(8,128)(2,1)S(1)} all-to-all(bf16[8,64,256]{2,1,0:T(8,128)(2,1)S(1)} %get-tuple-element.34), channel_id=1, replica_groups=mesh['zl'=8,'x'=4,'y'=4,'zh'=2,'c'=2] {'zl'}, dimensions={0} | all-to-all | bytes 524288 | tf_op jit(solution)/shard_map/all_to_all | solution.py:319
  191.9 0.1 broadcast_in_dim.21
  192.0 13.3 %all_to_all.64 = bf16[4,512,256]{2,1,0:T(8,128)(2,1)S(1)} all-to-all(bf16[4,512,256]{2,1,0:T(8,128)(2,1)S(1)} %broadcast_in_dim.21), channel_id=1, replica_groups=mesh['zl'=8,'x'=4,'y'=4,'zh'=2,'c'=2] {'x'}, dimensions={0} | all-to-all | bytes 2097152 | tf_op jit(solution)/shard_map/all_to_all | solution.py:319
  205.3 2.4 shard_map.108
  207.8 10.1 %all_to_all.65.i_ref = f32[8,72,128]{2,1,0:T(8,128)S(1)} all-to-all(f32[8,72,128]{2,1,0:T(8,128)S(1)} %get-tuple-element.35), channel_id=1, replica_groups=mesh['zl'=8,'x'=4,'y'=4,'zh'=2,'c'=2] {'c','y'}, dimensions={0} | all-to-all | bytes 589824 | tf_op jit(solution)/shard_map/all_to_all | solution.py:319
  217.9 7.9 %collective-permute-start.6 = (f32[72,128]{1,0:T(8,128)S(1)}, f32[72,128]{1,0:T(8,128)S(1)}, u32[]{:S(2)}, u32[]{:S(2)}) collective-permute-start(f32[72,128]{1,0:T(8,128)S(1)} %shard_map.109.mine_ref), channel_id=1, source_target_pairs={{0,2},{2,0},{1,3},{3,1},{4,6},{6,4},{5,7},{7,5},{8,10},{10,8},{9,1... | collective-permute-start | bytes 110600 | tf_op jit(solution)/shard_map/ppermute | solution.py:315
  225.8 6.7 %collective-permute-done.6.their_ref = f32[72,128]{1,0:T(8,128)S(1)} collective-permute-done((f32[72,128]{1,0:T(8,128)S(1)}, f32[72,128]{1,0:T(8,128)S(1)}, u32[]{:S(2)}, u32[]{:S(2)}) %collective-permute-start.6) | collective-permute-done | bytes 36896 | tf_op jit(solution)/shard_map/ppermute | solution.py:315
  232.5 0.6 shard_map.110
  233.1 10.5 %all_to_all.66.m_ref = f32[8,72,128]{2,1,0:T(8,128)S(1)} all-to-all(f32[8,72,128]{2,1,0:T(8,128)S(1)} %get-tuple-element.37), channel_id=1, replica_groups=mesh['zl'=8,'x'=4,'y'=4,'zh'=2,'c'=2] {'c','y'}, dimensions={0} | all-to-all | bytes 589824 | tf_op jit(solution)/shard_map/all_to_all | solution.py:319
  243.6 1.8 shard_map.111
  245.4 18.1 %all_to_all.67.i_ref = bf16[4,8,64,224]{3,2,1,0:T(8,128)(2,1)S(1)} all-to-all(bf16[4,8,64,224]{3,2,1,0:T(8,128)(2,1)S(1)} %shard_map.111), channel_id=1, replica_groups=mesh['zl'=8,'x'=4,'y'=4,'zh'=2,'c'=2] {'x'}, dimensions={0} | all-to-all | bytes 1835008 | tf_op jit(solution)/shard_map/all_to_all | solution.py:319
  263.5 0.1 shard_map.112
  263.6 0.0 copy-start.12
  263.7 26.3 %all_to_all.68.i_ref = bf16[8,64,224]{2,1,0:T(8,128)(2,1)S(1)} all-to-all(bf16[8,64,224]{2,1,0:T(8,128)(2,1)S(1)} %shard_map.112), channel_id=1, replica_groups=mesh['zl'=8,'x'=4,'y'=4,'zh'=2,'c'=2] {'zl'}, dimensions={0} | all-to-all | bytes 458752 | tf_op jit(solution)/shard_map/all_to_all | solution.py:319
  289.9 0.7 shard_map.113
  (26 shorter events, 0.2 us)
Async XLA Ops:
  0.0 0.8 copy-start.11
  1.7 12.8 %copy-start.13 = (bf16[1,32,2048]{2,1,0:T(8,128)(2,1)S(1)}, bf16[1,32,2048]{2,1,0:T(8,128)(2,1)}, u32[]{:S(2)}) copy-start(bf16[1,32,2048]{2,1,0:T(8,128)(2,1)} %param.10) | copy-start | bytes 393220
  1.7 36.9 %all-to-all-start = ((bf16[8,64,256]{2,1,0:T(8,128)(2,1)}), bf16[8,64,256]{2,1,0:T(8,128)(2,1)S(1)}, u32[]{:S(2)}, u32[]{:S(2)}) async-start(bf16[8,64,256]{2,1,0:T(8,128)(2,1)} %shard_map.101), calls=%async_computation | async-start | bytes 524288 | tf_op jit(solution)/shard_map/all_to_all | solution.py:319
  14.5 0.7 copy-start.15
  15.2 1.2 copy-start.2
  16.4 1.2 copy-start.3
  19.4 19.2 %collective-permute-start = (bf16[32,2048]{1,0:T(8,128)(2,1)S(1)}, bf16[32,2048]{1,0:T(8,128)(2,1)S(1)}, u32[]{:S(2)}, u32[]{:S(2)}) collective-permute-start(bf16[32,2048]{1,0:T(8,128)(2,1)S(1)} %shard_map.100), channel_id=1, source_target_pairs={{0,2},{2,0},{1,3},{3,1},{4,6},{6,4},{5,7},{7,5},{8,10},{10,8},{9,1... | collective-permute-start | bytes 393224 | tf_op jit(solution)/shard_map/ppermute | solution.py:315
  39.8 24.0 %all-to-all-start.1 = ((bf16[4,64,2048]{2,1,0:T(8,128)(2,1)}), bf16[4,64,2048]{2,1,0:T(8,128)(2,1)S(1)}, u32[]{:S(2)}, u32[]{:S(2)}) async-start(bf16[4,64,2048]{2,1,0:T(8,128)(2,1)} %broadcast_in_dim.18), calls=%async_computation.1 | async-start | bytes 2097152 | tf_op jit(solution)/shard_map/all_to_all | solution.py:319
  44.2 24.1 %copy-start.4 = (bf16[224,128]{1,0:T(8,128)(2,1)S(1)}, bf16[224,128]{1,0:T(8,128)(2,1)}, u32[]{:S(2)}) copy-start(bf16[224,128]{1,0:T(8,128)(2,1)} %rest_5_.1) | copy-start | bytes 172036
  44.2 13.8 %collective-permute-start.3 = (bf16[8,64,256]{2,1,0:T(8,128)(2,1)S(1)}, bf16[8,64,256]{2,1,0:T(8,128)(2,1)S(1)}, u32[]{:S(2)}, u32[]{:S(2)}) collective-permute-start(bf16[8,64,256]{2,1,0:T(8,128)(2,1)S(1)} %all-to-all-done.u0), channel_id=1, source_target_pairs={{0,48},{16,0},{32,16},{48,32},{1,49},{17,1},{33,17},{49,33},{2,50}... | collective-permute-start | bytes 786440 | tf_op jit(solution)/shard_map/ppermute | solution.py:343
  49.0 11.4 %collective-permute-start.2 = (bf16[8,64,256]{2,1,0:T(8,128)(2,1)S(1)}, bf16[8,64,256]{2,1,0:T(8,128)(2,1)S(1)}, u32[]{:S(2)}, u32[]{:S(2)}) collective-permute-start(bf16[8,64,256]{2,1,0:T(8,128)(2,1)S(1)} %all-to-all-done.u0), channel_id=1, source_target_pairs={{0,32},{16,48},{32,0},{48,16},{1,33},{17,49},{33,1},{49,17},{2,34}... | collective-permute-start | bytes 786440 | tf_op jit(solution)/shard_map/ppermute | solution.py:343
  51.7 11.4 %collective-permute-start.1 = (bf16[8,64,256]{2,1,0:T(8,128)(2,1)S(1)}, bf16[8,64,256]{2,1,0:T(8,128)(2,1)S(1)}, u32[]{:S(2)}, u32[]{:S(2)}) collective-permute-start(bf16[8,64,256]{2,1,0:T(8,128)(2,1)S(1)} %all-to-all-done.u0), channel_id=1, source_target_pairs={{0,16},{16,32},{32,48},{48,0},{1,17},{17,33},{33,49},{49,1},{2,18}... | collective-permute-start | bytes 786440 | tf_op jit(solution)/shard_map/ppermute | solution.py:343
  60.4 8.0 %copy-start.7 = (bf16[8,64,256]{2,1,0:T(8,128)(2,1)}, bf16[8,64,256]{2,1,0:T(8,128)(2,1)S(1)}, u32[]{:S(2)}) copy-start(bf16[8,64,256]{2,1,0:T(8,128)(2,1)S(1)} %collective-permute-done.2.u2) | copy-start | bytes 786436
  63.1 0.7 copy-start.9
  63.8 4.5 %collective-permute-start.4 = (bf16[4,64,2048]{2,1,0:T(8,128)(2,1)S(1)}, bf16[4,64,2048]{2,1,0:T(8,128)(2,1)S(1)}, u32[]{:S(2)}, u32[]{:S(2)}) collective-permute-start(bf16[4,64,2048]{2,1,0:T(8,128)(2,1)S(1)} %all-to-all-done.1.own_ref.rest_0_.rest_2_), channel_id=1, source_target_pairs={{0,1},{1,0},{2,3},{3,2},{4,5},{5,4},{6,7},{7,6},{8,9},{9,8},{10,11... | collective-permute-start | bytes 3145736 | tf_op jit(solution)/shard_map/ppermute | solution.py:315
  68.3 0.7 copy-start.14
  69.0 1.2 copy-start.5
  70.2 0.9 copy-start.8
  71.2 0.9 copy-start.10
  76.3 0.8 copy-start
  77.1 0.8 copy-start.6
  77.9 14.6 %all-to-all-start.2 = ((f32[8,136,128]{2,1,0:T(8,128)}), f32[8,136,128]{2,1,0:T(8,128)S(1)}, u32[]{:S(2)}, u32[]{:S(2)}) async-start(f32[8,136,128]{2,1,0:T(8,128)} %copy-done.6), calls=%async_computation.2 | async-start | bytes 1114112 | tf_op jit(solution)/shard_map/all_to_all | solution.py:319
  82.5 0.7 copy-start.16
  92.6 26.3 %copy-start.1 = (f32[512,224]{1,0:T(8,128)S(1)}, f32[512,224]{1,0:T(8,128)}, u32[]{:S(2)}) copy-start(f32[512,224]{1,0:T(8,128)} %copy-done) | copy-start | bytes 1376260
  92.6 15.0 %collective-permute-start.5 = (f32[136,128]{1,0:T(8,128)S(1)}, f32[136,128]{1,0:T(8,128)S(1)}, u32[]{:S(2)}, u32[]{:S(2)}) collective-permute-start(f32[136,128]{1,0:T(8,128)S(1)} %shard_map.103.mine_ref), channel_id=1, source_target_pairs={{0,2},{2,0},{1,3},{3,1},{4,6},{6,4},{5,7},{7,5},{8,10},{10,8},{9,1... | collective-permute-start | bytes 208904 | tf_op jit(solution)/shard_map/ppermute | solution.py:315
  217.9 14.6 %collective-permute-start.6 = (f32[72,128]{1,0:T(8,128)S(1)}, f32[72,128]{1,0:T(8,128)S(1)}, u32[]{:S(2)}, u32[]{:S(2)}) collective-permute-start(f32[72,128]{1,0:T(8,128)S(1)} %shard_map.109.mine_ref), channel_id=1, source_target_pairs={{0,2},{2,0},{1,3},{3,1},{4,6},{6,4},{5,7},{7,5},{8,10},{10,8},{9,1... | collective-permute-start | bytes 110600 | tf_op jit(solution)/shard_map/ppermute | solution.py:315
  263.6 26.3 %copy-start.12 = (f32[64,224]{1,0:T(8,128)S(1)}, f32[64,224]{1,0:T(8,128)}, u32[]{:S(2)}) copy-start(f32[64,224]{1,0:T(8,128)} %d_ref.3) | copy-start | bytes 172036

commit v5 on v4

--- a/solution.py
+++ b/solution.py
@@ -23,6 +23,7 @@
 WIDE = 256
 COUNT = HQ * HD * D
 SPAN = 288
+PACK = 112
 BF = jnp.bfloat16
 F32 = jnp.float32
 CONTRACT0 = (((0,), (0,)), ((), ()))
@@ -32,6 +33,10 @@
 def call(kernel, out_shape, *args, smem=0, far=0):
     specs = [pl.BlockSpec(memory_space=pltpu.SMEM)] * smem
     specs += [pl.BlockSpec(memory_space=pl.ANY)] * far
+    args = [
+        pltpu.with_memory_space_constraint(a, pltpu.HBM) if smem <= i < smem + far else a
+        for i, a in enumerate(args)
+    ]
     specs += [pl.BlockSpec(memory_space=pltpu.VMEM)] * (len(args) - smem - far)
     scratch = kernel.keywords.pop("scratch", ()) if isinstance(kernel, functools.partial) else ()
     many = isinstance(out_shape, (tuple, list))
@@ -61,9 +66,13 @@
     return a, b, (rest - b.astype(F32)).astype(BF)
 
 
-def attend_kernel(place, starts, q_ref, k_ref, v_ref, o_ref):
+def attend_kernel(place, starts, k_far, v_far, q_ref, o_ref, k_ref, v_ref, sems):
     offset = place[1]
     first = pl.multiple_of(jnp.maximum(offset - WINDOW, 0), 32)
+    k_copy = pltpu.make_async_copy(k_far.at[pl.ds(first, SPAN)], k_ref, sems.at[0])
+    v_copy = pltpu.make_async_copy(v_far.at[pl.ds(first, SPAN)], v_ref, sems.at[1])
+    k_copy.start()
+    v_copy.start()
     q_row = lax.broadcasted_iota(jnp.int32, (64, 1), 0)
     q_pos = offset + jnp.where(q_row < 32, q_row, q_row - 32)
     k_pos = first + lax.broadcasted_iota(jnp.int32, (1, SPAN), 1)
@@ -73,18 +82,20 @@
         q_file += jnp.where(starts[0, f] <= q_pos, 1, 0)
         k_file += jnp.where(starts[0, f] <= k_pos, 1, 0)
     allowed = (q_file == k_file) & (k_pos <= q_pos) & (q_pos - k_pos < WINDOW)
+    k_copy.wait()
+    v_copy.wait()
     for g in range(HK):
         q = jnp.concatenate(
             [q_ref[:, (2 * g + r) * HD : (2 * g + r + 1) * HD] for r in range(2)], 0
         )
         cols = slice(g * HD, (g + 1) * HD)
         scores = lax.dot_general(
-            q, k_ref[pl.ds(first, SPAN), cols], CONTRACT1, preferred_element_type=F32
+            q, k_ref[:, cols], CONTRACT1, preferred_element_type=F32
         )
         scores = 50.0 * jnp.tanh(scores * (1.0 / 16.0) / 50.0)
         expo = jnp.where(allowed, jnp.exp(scores), 0.0)
         weights = (expo / jnp.sum(expo, -1, keepdims=True)).astype(BF)
-        out = dot(weights, v_ref[pl.ds(first, SPAN), cols]).astype(BF)
+        out = dot(weights, v_ref[:, cols]).astype(BF)
         for r in range(2):
             o_ref[:, (2 * g + r) * HD : (2 * g + r + 1) * HD] = out[r * 32 : r * 32 + 32]
 
@@ -98,6 +109,18 @@
     return jnp.concatenate([block, tail], 1).astype(BF)
 
 
+def packed(block):
+    last = jnp.concatenate([block[48:64, at : at + 32] for at in (128, 160, 192)], 0)
+    tail = jnp.concatenate([block[0:48, 128:COLS], last], 1)
+    return jnp.concatenate([block[:, 0:128], tail], 0)
+
+
+def unpacked(block):
+    last = jnp.concatenate([block[at : at + 16, 96:128] for at in (64, 80, 96)], 1)
+    tail = jnp.concatenate([block[64:112, 0:96], last], 0)
+    return jnp.concatenate([block[0:64], tail], 1)
+
+
 def direction_kernel(d_ref, o_ref):
     load = row_block(d_ref[...])
     for i in range(ZL):
@@ -115,7 +138,7 @@
     total = i_ref[0].astype(F32)
     for i in range(1, ZL):
         total += i_ref[i].astype(F32)
-    return total
+    return unpacked(total)
 
 
 def sum_rows_kernel(i_ref, rows_ref, o_ref):
@@ -168,13 +191,16 @@
 
 
 def first_kernel(
-    place, u0, u1, u2, u3, own_ref, oth_ref, proj_ref, s_ref, gain_ref, tag_ref, h_ref, hd_ref, load_ref,
-    rows_ref, sems,
+    place, proj_far, u0, u1, u2, u3, own_ref, oth_ref, s_ref, gain_ref, tag_ref, h_ref, hd_ref, load_ref,
+    proj_ref, rows_ref, sems,
 ):
+    proj_copy = pltpu.make_async_copy(proj_far, proj_ref, sems.at[X])
+    proj_copy.start()
     xs = [lax.rem(place[2] + X - r, X) for r in range(X)]
     copies = start_rows((u0, u1, u2, u3), xs, rows_ref, sems)
     gain = gain_ref[...]
     halves = []
+    proj_copy.wait()
     for half, a_ref in enumerate((own_ref, oth_ref)):
         c = place[0] if half == 0 else 1 - place[0]
         at = pl.multiple_of(c * 256, 256)
@@ -182,7 +208,7 @@
         s = jnp.concatenate(
             [s_ref[y, zh, pl.ds(c, 1)][0] for y in range(Y) for zh in range(ZH)], 0
         )
-        h = s.astype(F32) + lax.dot_general(a, proj_ref[...], CONTRACT1, preferred_element_type=F32)
+        h = s.astype(F32) + dot(a, proj_ref[...])
         h_ref[pl.ds(at, 256), :] = h
         z = scores_of(h, gain, tag_ref)
         for i in range(Y):
@@ -308,7 +334,7 @@
             oth_ref[:, :, cols].reshape(256, 256), g_oth, CONTRACT0, preferred_element_type=F32
         )
         for x in range(X):
-            o_ref[x, zl] = part[x * 64 : x * 64 + 64].astype(BF)
+            o_ref[x, zl] = packed(part[x * 64 : x * 64 + 64]).astype(BF)
 
 
 def swap(x, axis):
@@ -336,21 +362,36 @@
 
     by_zl = deal(call(direction_kernel, shape(ZL, 64, WIDE, dtype=BF), direction), "zl")
     mine = call(
-        attend_kernel, shape(32, ROWS, dtype=BF), place, starts, queries[0], keys[0], values[0], smem=2
-    )
-    theirs, by_zl = lax.optimization_barrier((swap(mine, "zh"), by_zl))
+        functools.partial(
+            attend_kernel,
+            scratch=[pltpu.VMEM((SPAN, HK * HD), BF)] * 2 + [pltpu.SemaphoreType.DMA((2,))],
+        ),
+        shape(32, ROWS, dtype=BF),
+        place,
+        starts,
+        keys[0],
+        values[0],
+        queries[0],
+        smem=2,
+        far=2,
+    )
+    mine, by_zl = lax.optimization_barrier((mine, by_zl))
+    theirs = swap(mine, "zh")
     u0 = [by_zl] + [
         lax.ppermute(by_zl, "x", [(i, (i + r) % X) for i in range(X)]) for r in range(1, X)
     ]
+    theirs, *u0 = lax.optimization_barrier((theirs, *u0))
     low = zhpos == 0
     pair = jnp.stack([jnp.where(low, mine, theirs), jnp.where(low, theirs, mine)])
-    own, *u0 = lax.optimization_barrier((spread(pair.reshape(64, ROWS), "y", Y), *u0))
+    own, toks, own_tags, proj = lax.optimization_barrier(
+        (spread(pair.reshape(64, ROWS), "y", Y), toks, own_tags, out_proj)
+    )
     other = swap(own, "c")
 
     def product(second, *args):
         sent = call(
             functools.partial(product_kernel, second, scratch=[pltpu.VMEM((512, COLS), BF)]),
-            shape(X, ZL, 64, COLS, dtype=BF),
+            shape(X, ZL, PACK, 128, dtype=BF),
             place,
             *args,
             own,
@@ -359,27 +400,27 @@
             tag_proj,
             smem=1,
         )
-        part = call(sum_x_kernel, shape(ZL, 64, COLS, dtype=BF), deal(sent, "x"))
+        part = call(sum_x_kernel, shape(ZL, PACK, 128, dtype=BF), deal(sent, "x"))
         return deal(part, "zl")
 
     def token_sum(load, kernel, outs, *args):
         part = call(sum_parts_kernel, shape(load.shape[1], 128), deal(load, ("c", "y")))
         return call(kernel, outs, part, swap(part, "zh"), *args, own_tags)
 
-    rows_scratch = [pltpu.VMEM((ZL, X, 64, WIDE), BF), pltpu.SemaphoreType.DMA((X,))]
+    rows_scratch = [pltpu.VMEM((ZL, X, 64, WIDE), BF), pltpu.SemaphoreType.DMA((X + 1,))]
     h_loc, hdot0, load = call(
-        functools.partial(first_kernel, scratch=rows_scratch),
+        functools.partial(first_kernel, scratch=[pltpu.VMEM((ROWS, COLS), BF)] + rows_scratch),
         (shape(512, COLS), shape(512, COLS), shape(8, 136, 128)),
         place,
+        proj,
         *u0,
         own,
         other,
-        out_proj.T,
         toks,
         gain,
         tag_proj,
         smem=1,
-        far=X,
+        far=X + 1,
     )
     total, mixed = token_sum(load, tokens0_kernel, (shape(136, 128), shape(8, 72, 128)))
     rows0, sent = call(

time: 292 us -> 296 us (1.014)
  local copies, waits for them, and re-layouts: 13.2 us -> 6.5 us
  Pallas kernels: 15.3 us -> 21.6 us
  waiting for transfers between devices: 44.5 us -> 50 us
    all_to_all x3 -> x2, waiting for transfers between devices: 8.56 us -> 21.7 us  [deal(): return lax.all_to_all(x, axis, 0, 0, tiled=True)]
    ppermute x3, waiting for transfers between devices: 8.55 us -> 0.01 us  [local(): lax.ppermute(by_zl, 'x', [(i, (i + r) % X) for i in range(X)])]
    unnamed x36 -> x28, local copies, waits for them, and re-layouts: 11.8 us -> 3.7 us
    pallas_call x14, Pallas kernels: 15.3 us -> 21.6 us  [call(): pl.pallas_call(kernel, out_shape=out_shape, in_specs=specs, out_specs=[vm...]
    all_to_all x3 -> x2, starting transfers between devices: 21.7 us -> 17.4 us  [deal(): return lax.all_to_all(x, axis, 0, 0, tiled=True)]
    all_to_all x9 -> x10, blocking collectives: 160 us -> 161 us  [deal(): return lax.all_to_all(x, axis, 0, 0, tiled=True)]
  transfers between devices with their start and end apart: 10 -> 9, of which waited for: 8 -> 6; matrix products, arithmetic and copies ran while one was open for 1% -> 1% of each run, Pallas kernels for 1% -> 1%
where the time goes in v5:
time: 296 us; the launch traced here: 295 us
  blocking collectives  161 us (54%)
  starting transfers between devices  54.9 us (19%)
  waiting for transfers between devices  50 us (17%)
  Pallas kernels  21.6 us (7%)
  local copies, waits for them, and re-layouts  6.5 us (2%)
    all_to_all x10, blocking collectives, deal(): return lax.all_to_all(x, axis, 0, 0, tiled=True)  161 us
    ppermute x4, waiting for transfers between devices, swap(): return lax.ppermute(x, axis, [(0, 1), (1, 0)])  28.3 us
    ppermute x4, starting transfers between devices, swap(): return lax.ppermute(x, axis, [(0, 1), (1, 0)])  26.2 us
    all_to_all x2, waiting for transfers between devices, deal(): return lax.all_to_all(x, axis, 0, 0, tiled=True)  21.7 us
    pallas_call x14, Pallas kernels, call(): pl.pallas_call(kernel, out_shape=out_shape, in_specs=specs, out_specs=[vm...  21.6 us
    all_to_all x2, starting transfers between devices, deal(): return lax.all_to_all(x, axis, 0, 0, tiled=True)  17.4 us
    ppermute x3, starting transfers between devices, local(): lax.ppermute(by_zl, 'x', [(i, (i + r) % X) for i in range(X)])  11.4 us
  transfers between devices with their start and end apart: 9, of which 6 were waited for; matrix products, arithmetic and copies ran while one was open for 1% of the time, Pallas kernels for 1%

profile of v5, /device:TPU:32, one launch (start us, length us, event | category | flops | bytes accessed | tf_op | source)
XLA Modules:
  0.0 294.7 jit_solution(8789181860940454437)
XLA Ops:
  0.0 0.8 copy-done.1
  0.8 0.9 shard_map.101
  1.7 12.8 %all-to-all-start = ((bf16[8,64,256]{2,1,0:T(8,128)(2,1)}), bf16[8,64,256]{2,1,0:T(8,128)(2,1)S(1)}, u32[]{:S(2)}, u32[]{:S(2)}) async-start(bf16[8,64,256]{2,1,0:T(8,128)(2,1)} %shard_map.101), calls=%async_computation | async-start | bytes 524288 | tf_op jit(solution)/shard_map/all_to_all | solution.py:345
  14.5 0.1 pad_add_fusion.place
  14.6 0.0 copy-done.3
  14.6 0.7 copy-done.5
  15.2 3.1 %shard_map.100 = bf16[32,2048]{1,0:T(8,128)(2,1)S(1)} custom-call(s32[3]{0:T(128)S(1)} %pad_add_fusion.place, s32[1,4]{1,0:T(1,128)S(1)} %copy-done.5, bf16[512,1024]{1,0:T(8,128)(2,1)} %bitcast.27, bf16[512,1024]{1,0:T(8,128)(2,1)} %bitcast.28, bf16[32,2048]{1,0:T(8,128)(2,1)S(1)} %bitcast.19), custom_call_target="tpu_custom_call" | custom-call | tf_op jit(solution)/shard_map/pallas_call | solution.py:44
  18.3 12.5 %all-to-all-done.u0 = bf16[8,64,256]{2,1,0:T(8,128)(2,1)S(1)} async-done(((bf16[8,64,256]{2,1,0:T(8,128)(2,1)}), bf16[8,64,256]{2,1,0:T(8,128)(2,1)S(1)}, u32[]{:S(2)}, u32[]{:S(2)}) %all-to-all-start) | async-done | bytes 262176 | tf_op jit(solution)/shard_map/all_to_all | solution.py:345
  30.8 3.4 %collective-permute-start.1 = (bf16[8,64,256]{2,1,0:T(8,128)(2,1)S(1)}, bf16[8,64,256]{2,1,0:T(8,128)(2,1)S(1)}, u32[]{:S(2)}, u32[]{:S(2)}) collective-permute-start(bf16[8,64,256]{2,1,0:T(8,128)(2,1)S(1)} %all-to-all-done.u0), channel_id=1, source_target_pairs={{0,16},{16,32},{32,48},{48,0},{1,17},{17,33},{33,49},{49,1},{2,18}... | collective-permute-start | bytes 786440 | tf_op jit(solution)/shard_map/ppermute | solution.py:381
  34.2 4.6 %collective-permute-start.2 = (bf16[8,64,256]{2,1,0:T(8,128)(2,1)S(1)}, bf16[8,64,256]{2,1,0:T(8,128)(2,1)S(1)}, u32[]{:S(2)}, u32[]{:S(2)}) collective-permute-start(bf16[8,64,256]{2,1,0:T(8,128)(2,1)S(1)} %all-to-all-done.u0), channel_id=1, source_target_pairs={{0,32},{16,48},{32,0},{48,16},{1,33},{17,49},{33,1},{49,17},{2,34}... | collective-permute-start | bytes 786440 | tf_op jit(solution)/shard_map/ppermute | solution.py:381
  38.8 3.3 %collective-permute-start.3 = (bf16[8,64,256]{2,1,0:T(8,128)(2,1)S(1)}, bf16[8,64,256]{2,1,0:T(8,128)(2,1)S(1)}, u32[]{:S(2)}, u32[]{:S(2)}) collective-permute-start(bf16[8,64,256]{2,1,0:T(8,128)(2,1)S(1)} %all-to-all-done.u0), channel_id=1, source_target_pairs={{0,48},{16,0},{32,16},{48,32},{1,49},{17,1},{33,17},{49,33},{2,50}... | collective-permute-start | bytes 786440 | tf_op jit(solution)/shard_map/ppermute | solution.py:381
  42.1 8.2 %collective-permute-start = (bf16[32,2048]{1,0:T(8,128)(2,1)S(1)}, bf16[32,2048]{1,0:T(8,128)(2,1)S(1)}, u32[]{:S(2)}, u32[]{:S(2)}) collective-permute-start(bf16[32,2048]{1,0:T(8,128)(2,1)S(1)} %shard_map.100), channel_id=1, source_target_pairs={{0,2},{2,0},{1,3},{3,1},{4,6},{6,4},{5,7},{7,5},{8,10},{10,8},{9,1... | collective-permute-start | bytes 393224 | tf_op jit(solution)/shard_map/ppermute | solution.py:341
  50.4 12.1 %collective-permute-done = bf16[32,2048]{1,0:T(8,128)(2,1)S(1)} collective-permute-done((bf16[32,2048]{1,0:T(8,128)(2,1)S(1)}, bf16[32,2048]{1,0:T(8,128)(2,1)S(1)}, u32[]{:S(2)}, u32[]{:S(2)}) %collective-permute-start) | collective-permute-done | bytes 131104 | tf_op jit(solution)/shard_map/ppermute | solution.py:341
  62.4 0.0 collective-permute-done.1.u1
  62.4 0.0 collective-permute-done.2.u2
  62.4 0.7 copy-done.8
  63.1 0.0 collective-permute-done.3.u3
  63.2 0.0 copy-done.6
  63.2 0.7 copy-done.9
  63.9 1.1 broadcast_in_dim.18
  65.0 0.0 copy-done.10
  65.0 4.6 %all-to-all-start.1 = ((bf16[4,64,2048]{2,1,0:T(8,128)(2,1)}), bf16[4,64,2048]{2,1,0:T(8,128)(2,1)S(1)}, u32[]{:S(2)}, u32[]{:S(2)}) async-start(bf16[4,64,2048]{2,1,0:T(8,128)(2,1)} %broadcast_in_dim.18), calls=%async_computation.1 | async-start | bytes 2097152 | tf_op jit(solution)/shard_map/all_to_all | solution.py:345
  69.6 0.5 broadcast.3
  70.1 0.2 copy-done.12
  70.3 0.7 reduce.3
  71.0 0.1 reshape_squeeze.7
  71.1 0.1 reshape.8
  71.1 0.0 copy-done.11
  71.2 0.1 copy.11
  71.3 9.2 %all-to-all-done.1.own_ref.rest_0_.rest_2_ = bf16[4,64,2048]{2,1,0:T(8,128)(2,1)S(1)} async-done(((bf16[4,64,2048]{2,1,0:T(8,128)(2,1)}), bf16[4,64,2048]{2,1,0:T(8,128)(2,1)S(1)}, u32[]{:S(2)}, u32[]{:S(2)}) %all-to-all-start.1) | async-done | bytes 1048608 | tf_op jit(solution)/shard_map/all_to_all | solution.py:345
  80.5 2.0 collective-permute-start.4
  82.6 0.0 copy-done.7
  82.6 1.3 copy.13.proj_far
  83.9 1.3 collective-permute-done.4.oth_ref.rest_1_.rest_3_
  85.2 0.0 copy-done
  85.2 0.0 copy-done.4
  85.2 5.3 %shard_map.102 = (f32[512,224]{1,0:T(8,128)S(1)}, f32[512,224]{1,0:T(8,128)S(1)}, f32[8,136,128]{2,1,0:T(8,128)S(1)}) custom-call(s32[3]{0:T(128)S(1)} %pad_add_fusion.place, bf16[2048,224]{1,0:T(8,128)(2,1)} %copy.13.proj_far, bf16[8,64,256]{2,1,0:T(8,128)(2,1)} %copy-done.6, bf16[8,64,256]{2,1,0:T(8,128)(2,1)} %copy-done.8, bf16[8,64,256]{2,1,0:T(8,128)(2,1)} %copy-done.9, ...), custom_call_target="tpu_custom_call" | custom-call | tf_op jit(solution)/shard_map/pallas_call | solution.py:44
  90.5 12.9 %all_to_all.60.i_ref = f32[8,136,128]{2,1,0:T(8,128)S(1)} all-to-all(f32[8,136,128]{2,1,0:T(8,128)S(1)} %get-tuple-element.37), channel_id=1, replica_groups=mesh['zl'=8,'x'=4,'y'=4,'zh'=2,'c'=2] {'c','y'}, dimensions={0} | all-to-all | bytes 1114112 | tf_op jit(solution)/shard_map/all_to_all | solution.py:345
  103.5 8.2 %collective-permute-start.5 = (f32[136,128]{1,0:T(8,128)S(1)}, f32[136,128]{1,0:T(8,128)S(1)}, u32[]{:S(2)}, u32[]{:S(2)}) collective-permute-start(f32[136,128]{1,0:T(8,128)S(1)} %shard_map.103.mine_ref), channel_id=1, source_target_pairs={{0,2},{2,0},{1,3},{3,1},{4,6},{6,4},{5,7},{7,5},{8,10},{10,8},{9,1... | collective-permute-start | bytes 208904 | tf_op jit(solution)/shard_map/ppermute | solution.py:341
  111.7 0.1 copy.14.tag_ref
  111.8 8.1 %collective-permute-done.5.their_ref = f32[136,128]{1,0:T(8,128)S(1)} collective-permute-done((f32[136,128]{1,0:T(8,128)S(1)}, f32[136,128]{1,0:T(8,128)S(1)}, u32[]{:S(2)}, u32[]{:S(2)}) %collective-permute-start.5) | collective-permute-done | bytes 69664 | tf_op jit(solution)/shard_map/ppermute | solution.py:341
  119.9 0.6 shard_map.104
  120.5 10.1 %all_to_all.61.m_ref = f32[8,72,128]{2,1,0:T(8,128)S(1)} all-to-all(f32[8,72,128]{2,1,0:T(8,128)S(1)} %get-tuple-element.39), channel_id=1, replica_groups=mesh['zl'=8,'x'=4,'y'=4,'zh'=2,'c'=2] {'c','y'}, dimensions={0} | all-to-all | bytes 589824 | tf_op jit(solution)/shard_map/all_to_all | solution.py:345
  130.6 3.2 %shard_map.105 = bf16[4,8,112,128]{3,2,1,0:T(8,128)(2,1)S(1)} custom-call(s32[3]{0:T(128)S(1)} %pad_add_fusion.place, f32[8,72,128]{2,1,0:T(8,128)S(1)} %all_to_all.61.m_ref, f32[512,224]{1,0:T(8,128)S(1)} %get-tuple-element.40.h_ref, f32[512,224]{1,0:T(8,128)S(1)} %get-tuple-element.41.hd_ref, ...), custom_call_target="tpu_custom_call" | custom-call | tf_op jit(solution)/shard_map/pallas_call | solution.py:44
  133.8 16.7 %all_to_all.62.i_ref = bf16[4,8,112,128]{3,2,1,0:T(8,128)(2,1)S(1)} all-to-all(bf16[4,8,112,128]{3,2,1,0:T(8,128)(2,1)S(1)} %shard_map.105), channel_id=1, replica_groups=mesh['zl'=8,'x'=4,'y'=4,'zh'=2,'c'=2] {'x'}, dimensions={0} | all-to-all | bytes 1835008 | tf_op jit(solution)/shard_map/all_to_all | solution.py:345
  150.5 0.1 shard_map.106
  150.6 23.7 %all_to_all.63.i_ref = bf16[8,112,128]{2,1,0:T(8,128)(2,1)S(1)} all-to-all(bf16[8,112,128]{2,1,0:T(8,128)(2,1)S(1)} %shard_map.106), channel_id=1, replica_groups=mesh['zl'=8,'x'=4,'y'=4,'zh'=2,'c'=2] {'zl'}, dimensions={0} | all-to-all | bytes 458752 | tf_op jit(solution)/shard_map/all_to_all | solution.py:345
  174.3 0.2 shard_map.107
  174.5 21.2 %all_to_all.64 = bf16[8,64,256]{2,1,0:T(8,128)(2,1)S(1)} all-to-all(bf16[8,64,256]{2,1,0:T(8,128)(2,1)S(1)} %get-tuple-element.42), channel_id=1, replica_groups=mesh['zl'=8,'x'=4,'y'=4,'zh'=2,'c'=2] {'zl'}, dimensions={0} | all-to-all | bytes 524288 | tf_op jit(solution)/shard_map/all_to_all | solution.py:345
  195.7 0.1 broadcast_in_dim.21
  195.8 14.0 %all_to_all.65 = bf16[4,512,256]{2,1,0:T(8,128)(2,1)} all-to-all(bf16[4,512,256]{2,1,0:T(8,128)(2,1)S(1)} %broadcast_in_dim.21), channel_id=1, replica_groups=mesh['zl'=8,'x'=4,'y'=4,'zh'=2,'c'=2] {'x'}, dimensions={0} | all-to-all | bytes 2097152 | tf_op jit(solution)/shard_map/all_to_all | solution.py:345
  209.8 3.5 %shard_map.108 = (f32[512,224]{1,0:T(8,128)S(1)}, f32[8,72,128]{2,1,0:T(8,128)S(1)}) custom-call(s32[3]{0:T(128)S(1)} %pad_add_fusion.place, bf16[4,8,64,256]{3,2,1,0:T(8,128)(2,1)} %bitcast.24, bf16[4,64,2048]{2,1,0:T(8,128)(2,1)S(1)} %all-to-all-done.1.own_ref.rest_0_.rest_2_, bf16[4,64,2048]{2,1,0:T(8,128)(2,1)S(1)} %collective-permute-done.4.oth_ref.rest_1_.rest_3_, ...), custom_call_target="tpu_custom_call" | custom-call | tf_op jit(solution)/shard_map/pallas_call | solution.py:44
  213.3 10.1 %all_to_all.66.i_ref = f32[8,72,128]{2,1,0:T(8,128)S(1)} all-to-all(f32[8,72,128]{2,1,0:T(8,128)S(1)} %get-tuple-element.43), channel_id=1, replica_groups=mesh['zl'=8,'x'=4,'y'=4,'zh'=2,'c'=2] {'c','y'}, dimensions={0} | all-to-all | bytes 589824 | tf_op jit(solution)/shard_map/all_to_all | solution.py:345
  223.5 7.7 %collective-permute-start.6 = (f32[72,128]{1,0:T(8,128)S(1)}, f32[72,128]{1,0:T(8,128)S(1)}, u32[]{:S(2)}, u32[]{:S(2)}) collective-permute-start(f32[72,128]{1,0:T(8,128)S(1)} %shard_map.109.mine_ref), channel_id=1, source_target_pairs={{0,2},{2,0},{1,3},{3,1},{4,6},{6,4},{5,7},{7,5},{8,10},{10,8},{9,1... | collective-permute-start | bytes 110600 | tf_op jit(solution)/shard_map/ppermute | solution.py:341
  231.2 6.8 %collective-permute-done.6.their_ref = f32[72,128]{1,0:T(8,128)S(1)} collective-permute-done((f32[72,128]{1,0:T(8,128)S(1)}, f32[72,128]{1,0:T(8,128)S(1)}, u32[]{:S(2)}, u32[]{:S(2)}) %collective-permute-start.6) | collective-permute-done | bytes 36896 | tf_op jit(solution)/shard_map/ppermute | solution.py:341
  238.0 0.6 shard_map.110
  238.6 10.5 %all_to_all.67.m_ref = f32[8,72,128]{2,1,0:T(8,128)S(1)} all-to-all(f32[8,72,128]{2,1,0:T(8,128)S(1)} %get-tuple-element.45), channel_id=1, replica_groups=mesh['zl'=8,'x'=4,'y'=4,'zh'=2,'c'=2] {'c','y'}, dimensions={0} | all-to-all | bytes 589824 | tf_op jit(solution)/shard_map/all_to_all | solution.py:345
  249.1 3.2 %shard_map.111 = bf16[4,8,112,128]{3,2,1,0:T(8,128)(2,1)S(1)} custom-call(s32[3]{0:T(128)S(1)} %pad_add_fusion.place, f32[8,72,128]{2,1,0:T(8,128)S(1)} %all_to_all.67.m_ref, f32[512,224]{1,0:T(8,128)S(1)} %get-tuple-element.40.h_ref, f32[512,224]{1,0:T(8,128)S(1)} %get-tuple-element.41.hd_ref, f32[512,224]{1,0:T(8,128)S(1)} %get-tuple-element.46.rest_0_, ...), custom_call_target="tpu_custom_call" | custom-call | tf_op jit(solution)/shard_map/pallas_call | solution.py:44
  252.4 16.7 %all_to_all.68.i_ref = bf16[4,8,112,128]{3,2,1,0:T(8,128)(2,1)S(1)} all-to-all(bf16[4,8,112,128]{3,2,1,0:T(8,128)(2,1)S(1)} %shard_map.111), channel_id=1, replica_groups=mesh['zl'=8,'x'=4,'y'=4,'zh'=2,'c'=2] {'x'}, dimensions={0} | all-to-all | bytes 1835008 | tf_op jit(solution)/shard_map/all_to_all | solution.py:345
  269.0 0.1 shard_map.112
  269.2 0.0 copy-start.2
  269.2 24.8 %all_to_all.69.i_ref = bf16[8,112,128]{2,1,0:T(8,128)(2,1)S(1)} all-to-all(bf16[8,112,128]{2,1,0:T(8,128)(2,1)S(1)} %shard_map.112), channel_id=1, replica_groups=mesh['zl'=8,'x'=4,'y'=4,'zh'=2,'c'=2] {'zl'}, dimensions={0} | all-to-all | bytes 458752 | tf_op jit(solution)/shard_map/all_to_all | solution.py:345
  294.0 0.0 copy-done.2
  294.0 0.7 shard_map.113
  (18 shorter events, 0.1 us)
Async XLA Ops:
  0.0 0.8 copy-start.1
  1.7 12.8 %copy-start.3 = (bf16[1,32,2048]{2,1,0:T(8,128)(2,1)S(1)}, bf16[1,32,2048]{2,1,0:T(8,128)(2,1)}, u32[]{:S(2)}) copy-start(bf16[1,32,2048]{2,1,0:T(8,128)(2,1)} %param.10) | copy-start | bytes 393220
  1.7 29.0 %all-to-all-start = ((bf16[8,64,256]{2,1,0:T(8,128)(2,1)}), bf16[8,64,256]{2,1,0:T(8,128)(2,1)S(1)}, u32[]{:S(2)}, u32[]{:S(2)}) async-start(bf16[8,64,256]{2,1,0:T(8,128)(2,1)} %shard_map.101), calls=%async_computation | async-start | bytes 524288 | tf_op jit(solution)/shard_map/all_to_all | solution.py:345
  14.6 0.7 copy-start.5
  30.8 32.4 %copy-start.6 = (bf16[8,64,256]{2,1,0:T(8,128)(2,1)}, bf16[8,64,256]{2,1,0:T(8,128)(2,1)S(1)}, u32[]{:S(2)}) copy-start(bf16[8,64,256]{2,1,0:T(8,128)(2,1)S(1)} %all-to-all-done.u0) | copy-start | bytes 786436
  30.8 31.7 %collective-permute-start.1 = (bf16[8,64,256]{2,1,0:T(8,128)(2,1)S(1)}, bf16[8,64,256]{2,1,0:T(8,128)(2,1)S(1)}, u32[]{:S(2)}, u32[]{:S(2)}) collective-permute-start(bf16[8,64,256]{2,1,0:T(8,128)(2,1)S(1)} %all-to-all-done.u0), channel_id=1, source_target_pairs={{0,16},{16,32},{32,48},{48,0},{1,17},{17,33},{33,49},{49,1},{2,18}... | collective-permute-start | bytes 786440 | tf_op jit(solution)/shard_map/ppermute | solution.py:381
  34.2 28.3 %collective-permute-start.2 = (bf16[8,64,256]{2,1,0:T(8,128)(2,1)S(1)}, bf16[8,64,256]{2,1,0:T(8,128)(2,1)S(1)}, u32[]{:S(2)}, u32[]{:S(2)}) collective-permute-start(bf16[8,64,256]{2,1,0:T(8,128)(2,1)S(1)} %all-to-all-done.u0), channel_id=1, source_target_pairs={{0,32},{16,48},{32,0},{48,16},{1,33},{17,49},{33,1},{49,17},{2,34}... | collective-permute-start | bytes 786440 | tf_op jit(solution)/shard_map/ppermute | solution.py:381
  38.8 24.3 %collective-permute-start.3 = (bf16[8,64,256]{2,1,0:T(8,128)(2,1)S(1)}, bf16[8,64,256]{2,1,0:T(8,128)(2,1)S(1)}, u32[]{:S(2)}, u32[]{:S(2)}) collective-permute-start(bf16[8,64,256]{2,1,0:T(8,128)(2,1)S(1)} %all-to-all-done.u0), channel_id=1, source_target_pairs={{0,48},{16,0},{32,16},{48,32},{1,49},{17,1},{33,17},{49,33},{2,50}... | collective-permute-start | bytes 786440 | tf_op jit(solution)/shard_map/ppermute | solution.py:381
  42.1 20.3 %collective-permute-start = (bf16[32,2048]{1,0:T(8,128)(2,1)S(1)}, bf16[32,2048]{1,0:T(8,128)(2,1)S(1)}, u32[]{:S(2)}, u32[]{:S(2)}) collective-permute-start(bf16[32,2048]{1,0:T(8,128)(2,1)S(1)} %shard_map.100), channel_id=1, source_target_pairs={{0,2},{2,0},{1,3},{3,1},{4,6},{6,4},{5,7},{7,5},{8,10},{10,8},{9,1... | collective-permute-start | bytes 393224 | tf_op jit(solution)/shard_map/ppermute | solution.py:341
  62.4 0.7 copy-start.8
  63.1 0.7 copy-start.9
  63.1 1.9 copy-start.10
  65.0 6.1 %copy-start.11 = (bf16[1,512,224]{1,2,0:T(8,128)(2,1)S(1)}, bf16[1,512,224]{1,2,0:T(8,128)(2,1)}, u32[]{:S(2)}) copy-start(bf16[1,512,224]{1,2,0:T(8,128)(2,1)} %param.13) | copy-start | bytes 688132
  65.0 17.5 %copy-start.7 = (bf16[2048,224]{0,1:T(8,128)(2,1)S(1)}, bf16[2048,224]{0,1:T(8,128)(2,1)}, u32[]{:S(2)}) copy-start(bf16[2048,224]{0,1:T(8,128)(2,1)} %param.14) | copy-start | bytes 2752516
  65.0 15.5 %all-to-all-start.1 = ((bf16[4,64,2048]{2,1,0:T(8,128)(2,1)}), bf16[4,64,2048]{2,1,0:T(8,128)(2,1)S(1)}, u32[]{:S(2)}, u32[]{:S(2)}) async-start(bf16[4,64,2048]{2,1,0:T(8,128)(2,1)} %broadcast_in_dim.18), calls=%async_computation.1 | async-start | bytes 2097152 | tf_op jit(solution)/shard_map/all_to_all | solution.py:345
  69.6 0.7 copy-start.12
  80.5 4.7 %copy-start = (bf16[224,128]{1,0:T(8,128)(2,1)S(1)}, bf16[224,128]{1,0:T(8,128)(2,1)}, u32[]{:S(2)}) copy-start(bf16[224,128]{1,0:T(8,128)(2,1)} %rest_5_.1) | copy-start | bytes 172036
  80.5 4.7 %collective-permute-start.4 = (bf16[4,64,2048]{2,1,0:T(8,128)(2,1)S(1)}, bf16[4,64,2048]{2,1,0:T(8,128)(2,1)S(1)}, u32[]{:S(2)}, u32[]{:S(2)}) collective-permute-start(bf16[4,64,2048]{2,1,0:T(8,128)(2,1)S(1)} %all-to-all-done.1.own_ref.rest_0_.rest_2_), channel_id=1, source_target_pairs={{0,1},{1,0},{2,3},{3,2},{4,5},{5,4},{6,7},{7,6},{8,9},{9,8},{10,11... | collective-permute-start | bytes 3145736 | tf_op jit(solution)/shard_map/ppermute | solution.py:341
  83.9 1.3 copy-start.4
  103.5 16.4 %collective-permute-start.5 = (f32[136,128]{1,0:T(8,128)S(1)}, f32[136,128]{1,0:T(8,128)S(1)}, u32[]{:S(2)}, u32[]{:S(2)}) collective-permute-start(f32[136,128]{1,0:T(8,128)S(1)} %shard_map.103.mine_ref), channel_id=1, source_target_pairs={{0,2},{2,0},{1,3},{3,1},{4,6},{6,4},{5,7},{7,5},{8,10},{10,8},{9,1... | collective-permute-start | bytes 208904 | tf_op jit(solution)/shard_map/ppermute | solution.py:341
  223.5 14.6 %collective-permute-start.6 = (f32[72,128]{1,0:T(8,128)S(1)}, f32[72,128]{1,0:T(8,128)S(1)}, u32[]{:S(2)}, u32[]{:S(2)}) collective-permute-start(f32[72,128]{1,0:T(8,128)S(1)} %shard_map.109.mine_ref), channel_id=1, source_target_pairs={{0,2},{2,0},{1,3},{3,1},{4,6},{6,4},{5,7},{7,5},{8,10},{10,8},{9,1... | collective-permute-start | bytes 110600 | tf_op jit(solution)/shard_map/ppermute | solution.py:341
  269.2 24.8 %copy-start.2 = (f32[64,224]{1,0:T(8,128)S(1)}, f32[64,224]{1,0:T(8,128)}, u32[]{:S(2)}) copy-start(f32[64,224]{1,0:T(8,128)} %d_ref.3) | copy-start | bytes 172036

commit v6 on v5

--- a/solution.py
+++ b/solution.py
@@ -22,7 +22,7 @@
 COLS = 224
 WIDE = 256
 COUNT = HQ * HD * D
-SPAN = 288
+SPAN = 352
 PACK = 112
 BF = jnp.bfloat16
 F32 = jnp.float32
@@ -66,17 +66,18 @@
     return a, b, (rest - b.astype(F32)).astype(BF)
 
 
-def attend_kernel(place, starts, k_far, v_far, q_ref, o_ref, k_ref, v_ref, sems):
-    offset = place[1]
-    first = pl.multiple_of(jnp.maximum(offset - WINDOW, 0), 32)
+def attend_kernel(place, starts, k_far, v_far, own_ref, oth_ref, o_ref, k_ref, v_ref, sems):
+    own_at, oth_at, zh = place[1], place[2], place[3]
+    first = pl.multiple_of(jnp.maximum(jnp.minimum(own_at, oth_at) - WINDOW, 0), 32)
     k_copy = pltpu.make_async_copy(k_far.at[pl.ds(first, SPAN)], k_ref, sems.at[0])
     v_copy = pltpu.make_async_copy(v_far.at[pl.ds(first, SPAN)], v_ref, sems.at[1])
     k_copy.start()
     v_copy.start()
-    q_row = lax.broadcasted_iota(jnp.int32, (64, 1), 0)
-    q_pos = offset + jnp.where(q_row < 32, q_row, q_row - 32)
+    row = lax.broadcasted_iota(jnp.int32, (128, 1), 0)
+    within = jnp.where(row < 64, row, row - 64)
+    q_pos = jnp.where(within < 32, within + own_at, within - 32 + oth_at)
     k_pos = first + lax.broadcasted_iota(jnp.int32, (1, SPAN), 1)
-    q_file = jnp.zeros((64, 1), jnp.int32)
+    q_file = jnp.zeros((128, 1), jnp.int32)
     k_file = jnp.zeros((1, SPAN), jnp.int32)
     for f in range(4):
         q_file += jnp.where(starts[0, f] <= q_pos, 1, 0)
@@ -85,19 +86,18 @@
     k_copy.wait()
     v_copy.wait()
     for g in range(HK):
-        q = jnp.concatenate(
-            [q_ref[:, (2 * g + r) * HD : (2 * g + r + 1) * HD] for r in range(2)], 0
-        )
+        heads = [slice((2 * g + r) * HD, (2 * g + r + 1) * HD) for r in range(2)]
+        q = jnp.concatenate([ref[:, head] for head in heads for ref in (own_ref, oth_ref)], 0)
         cols = slice(g * HD, (g + 1) * HD)
-        scores = lax.dot_general(
-            q, k_ref[:, cols], CONTRACT1, preferred_element_type=F32
-        )
+        scores = lax.dot_general(q, k_ref[:, cols], CONTRACT1, preferred_element_type=F32)
         scores = 50.0 * jnp.tanh(scores * (1.0 / 16.0) / 50.0)
         expo = jnp.where(allowed, jnp.exp(scores), 0.0)
         weights = (expo / jnp.sum(expo, -1, keepdims=True)).astype(BF)
         out = dot(weights, v_ref[:, cols]).astype(BF)
-        for r in range(2):
-            o_ref[:, (2 * g + r) * HD : (2 * g + r + 1) * HD] = out[r * 32 : r * 32 + 32]
+        for r, head in enumerate(heads):
+            for y in range(Y):
+                o_ref[y, zh, :, head] = out[r * 64 : r * 64 + 32]
+                o_ref[y, 1 - zh, :, head] = out[r * 64 + 32 : r * 64 + 64]
 
 
 def row_block(block):
@@ -196,7 +196,7 @@
 ):
     proj_copy = pltpu.make_async_copy(proj_far, proj_ref, sems.at[X])
     proj_copy.start()
-    xs = [lax.rem(place[2] + X - r, X) for r in range(X)]
+    xs = [lax.rem(place[4] + X - r, X) for r in range(X)]
     copies = start_rows((u0, u1, u2, u3), xs, rows_ref, sems)
     gain = gain_ref[...]
     halves = []
@@ -227,10 +227,11 @@
 
 
 def moved_kernel(
-    place, u_ref, own_ref, oth_ref, h_ref, gain_ref, tag_ref, mv_ref, load_ref, rows_ref, sems
+    place, u_ref, own_ref, oth_ref, h_ref, gain_ref, tag_ref, mv_ref, load_ref, rows_ref
 ):
-    copies = start_rows([u_ref.at[x] for x in range(X)], range(X), rows_ref, sems)
-    rows, norm = await_rows(copies, rows_ref)
+    for x in range(X):
+        rows_ref[:, x] = u_ref[x]
+    rows, norm = await_rows((), rows_ref)
     gain = gain_ref[...]
     for half, a_ref in enumerate((own_ref, oth_ref)):
         c = place[0] if half == 0 else 1 - place[0]
@@ -353,38 +354,35 @@
     core = lax.axis_index("c")
     ypos = lax.axis_index("y")
     zhpos = lax.axis_index("zh")
-    offset = ((ypos * ZH + zhpos) * C + core) * 32
-    place = jnp.stack([core, offset, lax.axis_index("x")]).astype(jnp.int32)
+    own_at = ((ypos * ZH + zhpos) * C + core) * 32
+    oth_at = ((ypos * ZH + 1 - zhpos) * C + core) * 32
+    place = jnp.stack([core, own_at, oth_at, zhpos, lax.axis_index("x")]).astype(jnp.int32)
     own_tags = tags[0].reshape(Y, ZH, C, 32).transpose(2, 0, 1, 3).reshape(C * Y, 64)[core * Y + ypos]
     own_tags = own_tags[:, None]
     toks = stream[0].reshape(Y, ZH, C, 32, COLS)
     gain = norm_gain[None]
 
     by_zl = deal(call(direction_kernel, shape(ZL, 64, WIDE, dtype=BF), direction), "zl")
-    mine = call(
+    pair = call(
         functools.partial(
             attend_kernel,
             scratch=[pltpu.VMEM((SPAN, HK * HD), BF)] * 2 + [pltpu.SemaphoreType.DMA((2,))],
         ),
-        shape(32, ROWS, dtype=BF),
+        shape(Y, ZH, 32, ROWS, dtype=BF),
         place,
         starts,
         keys[0],
         values[0],
         queries[0],
+        swap(queries[0], "zh"),
         smem=2,
         far=2,
     )
-    mine, by_zl = lax.optimization_barrier((mine, by_zl))
-    theirs = swap(mine, "zh")
     u0 = [by_zl] + [
         lax.ppermute(by_zl, "x", [(i, (i + r) % X) for i in range(X)]) for r in range(1, X)
     ]
-    theirs, *u0 = lax.optimization_barrier((theirs, *u0))
-    low = zhpos == 0
-    pair = jnp.stack([jnp.where(low, mine, theirs), jnp.where(low, theirs, mine)])
-    own, toks, own_tags, proj = lax.optimization_barrier(
-        (spread(pair.reshape(64, ROWS), "y", Y), toks, own_tags, out_proj)
+    own, toks, own_tags, proj, *u0 = lax.optimization_barrier(
+        (deal(pair.reshape(Y, 64, ROWS), "y"), toks, own_tags, out_proj, *u0)
     )
     other = swap(own, "c")
 
@@ -430,7 +428,7 @@
     )
     full0 = spread(deal(sent, "zl").reshape(ZL * 64, WIDE), "x", X).reshape(X, ZL, 64, WIDE)
     moved, load = call(
-        functools.partial(moved_kernel, scratch=rows_scratch),
+        functools.partial(moved_kernel, scratch=rows_scratch[:1]),
         (shape(512, COLS), shape(8, 72, 128)),
         place,
         full0,
@@ -440,7 +438,6 @@
         gain,
         tag_proj,
         smem=1,
-        far=1,
     )
     mixed, inv = token_sum(load, tokens1_kernel, (shape(8, 72, 128), shape(8, 128)), total)
     arrived = product(True, deal(mixed, ("c", "y")), h_loc, hdot0, moved, inv)

time: 296 us -> 284 us (0.959)
  waiting for transfers between devices: 50 us -> 28.4 us
  blocking collectives: 161 us -> 170 us
    all_to_all x2, waiting for transfers between devices: 21.7 us -> 4.08 us  [deal(): return lax.all_to_all(x, axis, 0, 0, tiled=True)]
    all_to_all x10, blocking collectives: 161 us -> 170 us  [deal(): return lax.all_to_all(x, axis, 0, 0, tiled=True)]
    ppermute x4, waiting for transfers between devices: 28.3 us -> 22.1 us  [swap(): return lax.ppermute(x, axis, [(0, 1), (1, 0)])]
  transfers between devices with their start and end apart: 9 -> 9, of which waited for: 6 -> 6; matrix products, arithmetic and copies ran while one was open for 1% -> 1% of each run, Pallas kernels for 1% -> 2%
where the time goes in v6:
time: 284 us; the launch traced here: 283 us
  blocking collectives  170 us (60%)
  starting transfers between devices  55.5 us (20%)
  waiting for transfers between devices  28.4 us (10%)
  Pallas kernels  21.7 us (8%)
  local copies, waits for them, and re-layouts  5.72 us (2%)
    all_to_all x10, blocking collectives, deal(): return lax.all_to_all(x, axis, 0, 0, tiled=True)  170 us
    ppermute x4, starting transfers between devices, swap(): return lax.ppermute(x, axis, [(0, 1), (1, 0)])  26.8 us
    ppermute x4, waiting for transfers between devices, swap(): return lax.ppermute(x, axis, [(0, 1), (1, 0)])  22.1 us
    pallas_call x14, Pallas kernels, call(): pl.pallas_call(kernel, out_shape=out_shape, in_specs=specs, out_specs=[vm...  21.7 us
    all_to_all x2, starting transfers between devices, deal(): return lax.all_to_all(x, axis, 0, 0, tiled=True)  17.4 us
    ppermute x3, starting transfers between devices, local(): lax.ppermute(by_zl, 'x', [(i, (i + r) % X) for i in range(X)])  11.4 us
  transfers between devices with their start and end apart: 9, of which 6 were waited for; matrix products, arithmetic and copies ran while one was open for 1% of the time, Pallas kernels for 2%

profile of v6, /device:TPU:32, one launch (start us, length us, event | category | flops | bytes accessed | tf_op | source)
XLA Modules:
  0.0 282.6 jit_solution(5615254294481756408)
XLA Ops:
  0.0 0.8 copy-done.1
  0.8 0.9 shard_map.101
  1.7 12.8 %all-to-all-start.1 = ((bf16[8,64,256]{2,1,0:T(8,128)(2,1)}), bf16[8,64,256]{2,1,0:T(8,128)(2,1)S(1)}, u32[]{:S(2)}, u32[]{:S(2)}) async-start(bf16[8,64,256]{2,1,0:T(8,128)(2,1)} %shard_map.101), calls=%async_computation.1 | async-start | bytes 524288 | tf_op jit(solution)/shard_map/all_to_all | solution.py:346
  14.5 0.0 copy-done.3
  14.5 8.2 %collective-permute-start = (bf16[32,2048]{1,0:T(8,128)(2,1)S(1)}, bf16[32,2048]{1,0:T(8,128)(2,1)S(1)}, u32[]{:S(2)}, u32[]{:S(2)}) collective-permute-start(bf16[32,2048]{1,0:T(8,128)(2,1)S(1)} %bitcast.18), channel_id=1, source_target_pairs={{0,2},{2,0},{1,3},{3,1},{4,6},{6,4},{5,7},{7,5},{8,10},{10,8},{9,1... | collective-permute-start | bytes 393224 | tf_op jit(solution)/shard_map/ppermute | solution.py:342
  22.7 0.1 stack.23.place
  22.8 7.9 %collective-permute-done.oth_ref = bf16[32,2048]{1,0:T(8,128)(2,1)S(1)} collective-permute-done((bf16[32,2048]{1,0:T(8,128)(2,1)S(1)}, bf16[32,2048]{1,0:T(8,128)(2,1)S(1)}, u32[]{:S(2)}, u32[]{:S(2)}) %collective-permute-start) | collective-permute-done | bytes 131104 | tf_op jit(solution)/shard_map/ppermute | solution.py:342
  30.6 0.7 copy-done.5
  31.3 4.3 %shard_map.100 = bf16[4,2,32,2048]{3,2,1,0:T(8,128)(2,1)} custom-call(s32[5]{0:T(128)S(1)} %stack.23.place, s32[1,4]{1,0:T(1,128)S(1)} %copy-done.5, bf16[512,1024]{1,0:T(8,128)(2,1)} %bitcast.25, bf16[512,1024]{1,0:T(8,128)(2,1)} %bitcast.26, bf16[32,2048]{1,0:T(8,128)(2,1)S(1)} %bitcast.19, bf16[32,2048]{1,0:T(8,128)(2,1)S(1)} %collective-permute-done.oth_ref), custom_call_target="tpu_custom_call" | custom-call | tf_op jit(solution)/shard_map/pallas_call | solution.py:44
  35.6 4.1 %all-to-all-done.1.u0 = bf16[8,64,256]{2,1,0:T(8,128)(2,1)S(1)} async-done(((bf16[8,64,256]{2,1,0:T(8,128)(2,1)}), bf16[8,64,256]{2,1,0:T(8,128)(2,1)S(1)}, u32[]{:S(2)}, u32[]{:S(2)}) %all-to-all-start.1) | async-done | bytes 262176 | tf_op jit(solution)/shard_map/all_to_all | solution.py:346
  39.7 4.6 %all-to-all-start = ((bf16[4,64,2048]{2,1,0:T(8,128)(2,1)}), bf16[4,64,2048]{2,1,0:T(8,128)(2,1)S(1)}, u32[]{:S(2)}, u32[]{:S(2)}) async-start(bf16[4,64,2048]{2,1,0:T(8,128)(2,1)} %bitcast.8), calls=%async_computation | async-start | bytes 2097152 | tf_op jit(solution)/shard_map/all_to_all | solution.py:346
  44.3 3.4 %collective-permute-start.1 = (bf16[8,64,256]{2,1,0:T(8,128)(2,1)S(1)}, bf16[8,64,256]{2,1,0:T(8,128)(2,1)S(1)}, u32[]{:S(2)}, u32[]{:S(2)}) collective-permute-start(bf16[8,64,256]{2,1,0:T(8,128)(2,1)S(1)} %all-to-all-done.1.u0), channel_id=1, source_target_pairs={{0,16},{16,32},{32,48},{48,0},{1,17},{17,33},{33,49},{49,1},{2,18}... | collective-permute-start | bytes 786440 | tf_op jit(solution)/shard_map/ppermute | solution.py:382
  47.7 4.6 %collective-permute-start.2 = (bf16[8,64,256]{2,1,0:T(8,128)(2,1)S(1)}, bf16[8,64,256]{2,1,0:T(8,128)(2,1)S(1)}, u32[]{:S(2)}, u32[]{:S(2)}) collective-permute-start(bf16[8,64,256]{2,1,0:T(8,128)(2,1)S(1)} %all-to-all-done.1.u0), channel_id=1, source_target_pairs={{0,32},{16,48},{32,0},{48,16},{1,33},{17,49},{33,1},{49,17},{2,34}... | collective-permute-start | bytes 786440 | tf_op jit(solution)/shard_map/ppermute | solution.py:382
  52.3 0.0 copy-done.6
  52.3 3.3 %collective-permute-start.3 = (bf16[8,64,256]{2,1,0:T(8,128)(2,1)S(1)}, bf16[8,64,256]{2,1,0:T(8,128)(2,1)S(1)}, u32[]{:S(2)}, u32[]{:S(2)}) collective-permute-start(bf16[8,64,256]{2,1,0:T(8,128)(2,1)S(1)} %all-to-all-done.1.u0), channel_id=1, source_target_pairs={{0,48},{16,0},{32,16},{48,32},{1,49},{17,1},{33,17},{49,33},{2,50}... | collective-permute-start | bytes 786440 | tf_op jit(solution)/shard_map/ppermute | solution.py:382
  55.7 0.0 copy-start.11
  55.7 0.5 broadcast.3
  56.2 0.2 copy-done.11
  56.4 0.7 reduce.3
  57.0 0.1 reshape_squeeze.7
  57.1 0.1 reshape.11
  57.2 1.1 copy.11
  58.3 0.0 all-to-all-done.own_ref.rest_0_.rest_2_
  58.3 0.0 collective-permute-done.1.u1
  58.3 0.0 copy-start.8
  58.3 0.0 collective-permute-done.2.u2
  58.4 0.0 copy-start.9
  58.4 2.2 collective-permute-done.3.u3
  60.6 0.0 copy-done.8
  60.6 0.0 copy-done.9
  60.6 0.7 copy-done.10
  61.3 2.0 collective-permute-start.4
  63.4 0.0 copy-done.7
  63.4 1.3 copy.13.proj_far
  64.7 1.3 collective-permute-done.4.oth_ref.rest_1_.rest_3_
  66.0 0.0 copy-done
  66.0 0.0 copy-done.4
  66.0 5.3 %shard_map.102 = (f32[512,224]{1,0:T(8,128)S(1)}, f32[512,224]{1,0:T(8,128)S(1)}, f32[8,136,128]{2,1,0:T(8,128)S(1)}) custom-call(s32[5]{0:T(128)S(1)} %stack.23.place, bf16[2048,224]{1,0:T(8,128)(2,1)} %copy.13.proj_far, bf16[8,64,256]{2,1,0:T(8,128)(2,1)} %copy-done.6, bf16[8,64,256]{2,1,0:T(8,128)(2,1)} %copy-done.8, bf16[8,64,256]{2,1,0:T(8,128)(2,1)} %copy-done.9, ...), custom_call_target="tpu_custom_call" | custom-call | tf_op jit(solution)/shard_map/pallas_call | solution.py:44
  71.3 15.2 %all_to_all.60.i_ref = f32[8,136,128]{2,1,0:T(8,128)S(1)} all-to-all(f32[8,136,128]{2,1,0:T(8,128)S(1)} %get-tuple-element.31), channel_id=1, replica_groups=mesh['zl'=8,'x'=4,'y'=4,'zh'=2,'c'=2] {'c','y'}, dimensions={0} | all-to-all | bytes 1114112 | tf_op jit(solution)/shard_map/all_to_all | solution.py:346
  86.6 9.0 %collective-permute-start.5 = (f32[136,128]{1,0:T(8,128)S(1)}, f32[136,128]{1,0:T(8,128)S(1)}, u32[]{:S(2)}, u32[]{:S(2)}) collective-permute-start(f32[136,128]{1,0:T(8,128)S(1)} %shard_map.103.mine_ref), channel_id=1, source_target_pairs={{0,2},{2,0},{1,3},{3,1},{4,6},{6,4},{5,7},{7,5},{8,10},{10,8},{9,1... | collective-permute-start | bytes 208904 | tf_op jit(solution)/shard_map/ppermute | solution.py:342
  95.6 0.1 copy.14.tag_ref
  95.7 5.9 %collective-permute-done.5.their_ref = f32[136,128]{1,0:T(8,128)S(1)} collective-permute-done((f32[136,128]{1,0:T(8,128)S(1)}, f32[136,128]{1,0:T(8,128)S(1)}, u32[]{:S(2)}, u32[]{:S(2)}) %collective-permute-start.5) | collective-permute-done | bytes 69664 | tf_op jit(solution)/shard_map/ppermute | solution.py:342
  101.5 0.6 shard_map.104
  102.1 10.2 %all_to_all.61.m_ref = f32[8,72,128]{2,1,0:T(8,128)S(1)} all-to-all(f32[8,72,128]{2,1,0:T(8,128)S(1)} %get-tuple-element.33), channel_id=1, replica_groups=mesh['zl'=8,'x'=4,'y'=4,'zh'=2,'c'=2] {'c','y'}, dimensions={0} | all-to-all | bytes 589824 | tf_op jit(solution)/shard_map/all_to_all | solution.py:346
  112.3 3.2 %shard_map.105 = bf16[4,8,112,128]{3,2,1,0:T(8,128)(2,1)S(1)} custom-call(s32[5]{0:T(128)S(1)} %stack.23.place, f32[8,72,128]{2,1,0:T(8,128)S(1)} %all_to_all.61.m_ref, f32[512,224]{1,0:T(8,128)S(1)} %get-tuple-element.34.h_ref, f32[512,224]{1,0:T(8,128)S(1)} %get-tuple-element.35.hd_ref, bf16[4,64,2048]{2,1,0:T(8,128)(2,1)S(1)} %all-to-all-done.own_ref.rest_0_.rest_2_, ...), custom_call_target="tpu_custom_call" | custom-call | tf_op jit(solution)/shard_map/pallas_call | solution.py:44
  115.5 17.7 %all_to_all.62.i_ref = bf16[4,8,112,128]{3,2,1,0:T(8,128)(2,1)S(1)} all-to-all(bf16[4,8,112,128]{3,2,1,0:T(8,128)(2,1)S(1)} %shard_map.105), channel_id=1, replica_groups=mesh['zl'=8,'x'=4,'y'=4,'zh'=2,'c'=2] {'x'}, dimensions={0} | all-to-all | bytes 1835008 | tf_op jit(solution)/shard_map/all_to_all | solution.py:346
  133.2 0.1 shard_map.106
  133.3 31.6 %all_to_all.63.i_ref = bf16[8,112,128]{2,1,0:T(8,128)(2,1)S(1)} all-to-all(bf16[8,112,128]{2,1,0:T(8,128)(2,1)S(1)} %shard_map.106), channel_id=1, replica_groups=mesh['zl'=8,'x'=4,'y'=4,'zh'=2,'c'=2] {'zl'}, dimensions={0} | all-to-all | bytes 458752 | tf_op jit(solution)/shard_map/all_to_all | solution.py:346
  164.9 0.2 shard_map.107
  165.1 20.5 %all_to_all.64 = bf16[8,64,256]{2,1,0:T(8,128)(2,1)S(1)} all-to-all(bf16[8,64,256]{2,1,0:T(8,128)(2,1)S(1)} %get-tuple-element.36), channel_id=1, replica_groups=mesh['zl'=8,'x'=4,'y'=4,'zh'=2,'c'=2] {'zl'}, dimensions={0} | all-to-all | bytes 524288 | tf_op jit(solution)/shard_map/all_to_all | solution.py:346
  185.7 0.1 broadcast_in_dim.12
  185.7 13.3 %all_to_all.65 = bf16[4,512,256]{2,1,0:T(8,128)(2,1)S(1)} all-to-all(bf16[4,512,256]{2,1,0:T(8,128)(2,1)S(1)} %broadcast_in_dim.12), channel_id=1, replica_groups=mesh['zl'=8,'x'=4,'y'=4,'zh'=2,'c'=2] {'x'}, dimensions={0} | all-to-all | bytes 2097152 | tf_op jit(solution)/shard_map/all_to_all | solution.py:346
  199.0 2.3 shard_map.108
  201.4 10.1 %all_to_all.66.i_ref = f32[8,72,128]{2,1,0:T(8,128)S(1)} all-to-all(f32[8,72,128]{2,1,0:T(8,128)S(1)} %get-tuple-element.37), channel_id=1, replica_groups=mesh['zl'=8,'x'=4,'y'=4,'zh'=2,'c'=2] {'c','y'}, dimensions={0} | all-to-all | bytes 589824 | tf_op jit(solution)/shard_map/all_to_all | solution.py:346
  211.5 7.5 %collective-permute-start.6 = (f32[72,128]{1,0:T(8,128)S(1)}, f32[72,128]{1,0:T(8,128)S(1)}, u32[]{:S(2)}, u32[]{:S(2)}) collective-permute-start(f32[72,128]{1,0:T(8,128)S(1)} %shard_map.109.mine_ref), channel_id=1, source_target_pairs={{0,2},{2,0},{1,3},{3,1},{4,6},{6,4},{5,7},{7,5},{8,10},{10,8},{9,1... | collective-permute-start | bytes 110600 | tf_op jit(solution)/shard_map/ppermute | solution.py:342
  219.0 7.1 %collective-permute-done.6.their_ref = f32[72,128]{1,0:T(8,128)S(1)} collective-permute-done((f32[72,128]{1,0:T(8,128)S(1)}, f32[72,128]{1,0:T(8,128)S(1)}, u32[]{:S(2)}, u32[]{:S(2)}) %collective-permute-start.6) | collective-permute-done | bytes 36896 | tf_op jit(solution)/shard_map/ppermute | solution.py:342
  226.1 0.6 shard_map.110
  226.7 11.0 %all_to_all.67.m_ref = f32[8,72,128]{2,1,0:T(8,128)S(1)} all-to-all(f32[8,72,128]{2,1,0:T(8,128)S(1)} %get-tuple-element.39), channel_id=1, replica_groups=mesh['zl'=8,'x'=4,'y'=4,'zh'=2,'c'=2] {'c','y'}, dimensions={0} | all-to-all | bytes 589824 | tf_op jit(solution)/shard_map/all_to_all | solution.py:346
  237.6 3.3 %shard_map.111 = bf16[4,8,112,128]{3,2,1,0:T(8,128)(2,1)S(1)} custom-call(s32[5]{0:T(128)S(1)} %stack.23.place, f32[8,72,128]{2,1,0:T(8,128)S(1)} %all_to_all.67.m_ref, f32[512,224]{1,0:T(8,128)S(1)} %get-tuple-element.34.h_ref, f32[512,224]{1,0:T(8,128)S(1)} %get-tuple-element.35.hd_ref, f32[512,224]{1,0:T(8,128)S(1)} %get-tuple-element.40.rest_0_, ...), custom_call_target="tpu_custom_call" | custom-call | tf_op jit(solution)/shard_map/pallas_call | solution.py:44
  240.9 16.7 %all_to_all.68.i_ref = bf16[4,8,112,128]{3,2,1,0:T(8,128)(2,1)S(1)} all-to-all(bf16[4,8,112,128]{3,2,1,0:T(8,128)(2,1)S(1)} %shard_map.111), channel_id=1, replica_groups=mesh['zl'=8,'x'=4,'y'=4,'zh'=2,'c'=2] {'x'}, dimensions={0} | all-to-all | bytes 1835008 | tf_op jit(solution)/shard_map/all_to_all | solution.py:346
  257.6 0.1 shard_map.112
  257.7 0.0 copy-start.2
  257.7 24.1 %all_to_all.69.i_ref = bf16[8,112,128]{2,1,0:T(8,128)(2,1)S(1)} all-to-all(bf16[8,112,128]{2,1,0:T(8,128)(2,1)S(1)} %shard_map.112), channel_id=1, replica_groups=mesh['zl'=8,'x'=4,'y'=4,'zh'=2,'c'=2] {'zl'}, dimensions={0} | all-to-all | bytes 458752 | tf_op jit(solution)/shard_map/all_to_all | solution.py:346
  281.8 0.7 shard_map.113
  (13 shorter events, 0.1 us)
Async XLA Ops:
  0.0 0.8 copy-start.1
  1.7 12.8 %copy-start.3 = (bf16[1,32,2048]{2,1,0:T(8,128)(2,1)S(1)}, bf16[1,32,2048]{2,1,0:T(8,128)(2,1)}, u32[]{:S(2)}) copy-start(bf16[1,32,2048]{2,1,0:T(8,128)(2,1)} %param.10) | copy-start | bytes 393220
  1.7 38.0 %all-to-all-start.1 = ((bf16[8,64,256]{2,1,0:T(8,128)(2,1)}), bf16[8,64,256]{2,1,0:T(8,128)(2,1)S(1)}, u32[]{:S(2)}, u32[]{:S(2)}) async-start(bf16[8,64,256]{2,1,0:T(8,128)(2,1)} %shard_map.101), calls=%async_computation.1 | async-start | bytes 524288 | tf_op jit(solution)/shard_map/all_to_all | solution.py:346
  14.5 16.2 %collective-permute-start = (bf16[32,2048]{1,0:T(8,128)(2,1)S(1)}, bf16[32,2048]{1,0:T(8,128)(2,1)S(1)}, u32[]{:S(2)}, u32[]{:S(2)}) collective-permute-start(bf16[32,2048]{1,0:T(8,128)(2,1)S(1)} %bitcast.18), channel_id=1, source_target_pairs={{0,2},{2,0},{1,3},{3,1},{4,6},{6,4},{5,7},{7,5},{8,10},{10,8},{9,1... | collective-permute-start | bytes 393224 | tf_op jit(solution)/shard_map/ppermute | solution.py:342
  30.6 0.7 copy-start.5
  39.7 12.6 %copy-start.6 = (bf16[8,64,256]{2,1,0:T(8,128)(2,1)}, bf16[8,64,256]{2,1,0:T(8,128)(2,1)S(1)}, u32[]{:S(2)}) copy-start(bf16[8,64,256]{2,1,0:T(8,128)(2,1)S(1)} %all-to-all-done.1.u0) | copy-start | bytes 786436
  39.7 23.7 %copy-start.7 = (bf16[2048,224]{0,1:T(8,128)(2,1)S(1)}, bf16[2048,224]{0,1:T(8,128)(2,1)}, u32[]{:S(2)}) copy-start(bf16[2048,224]{0,1:T(8,128)(2,1)} %param.14) | copy-start | bytes 2752516
  39.7 18.6 %all-to-all-start = ((bf16[4,64,2048]{2,1,0:T(8,128)(2,1)}), bf16[4,64,2048]{2,1,0:T(8,128)(2,1)S(1)}, u32[]{:S(2)}, u32[]{:S(2)}) async-start(bf16[4,64,2048]{2,1,0:T(8,128)(2,1)} %bitcast.8), calls=%async_computation | async-start | bytes 2097152 | tf_op jit(solution)/shard_map/all_to_all | solution.py:346
  44.3 14.0 %collective-permute-start.1 = (bf16[8,64,256]{2,1,0:T(8,128)(2,1)S(1)}, bf16[8,64,256]{2,1,0:T(8,128)(2,1)S(1)}, u32[]{:S(2)}, u32[]{:S(2)}) collective-permute-start(bf16[8,64,256]{2,1,0:T(8,128)(2,1)S(1)} %all-to-all-done.1.u0), channel_id=1, source_target_pairs={{0,16},{16,32},{32,48},{48,0},{1,17},{17,33},{33,49},{49,1},{2,18}... | collective-permute-start | bytes 786440 | tf_op jit(solution)/shard_map/ppermute | solution.py:382
  47.7 10.7 %collective-permute-start.2 = (bf16[8,64,256]{2,1,0:T(8,128)(2,1)S(1)}, bf16[8,64,256]{2,1,0:T(8,128)(2,1)S(1)}, u32[]{:S(2)}, u32[]{:S(2)}) collective-permute-start(bf16[8,64,256]{2,1,0:T(8,128)(2,1)S(1)} %all-to-all-done.1.u0), channel_id=1, source_target_pairs={{0,32},{16,48},{32,0},{48,16},{1,33},{17,49},{33,1},{49,17},{2,34}... | collective-permute-start | bytes 786440 | tf_op jit(solution)/shard_map/ppermute | solution.py:382
  52.3 8.3 %collective-permute-start.3 = (bf16[8,64,256]{2,1,0:T(8,128)(2,1)S(1)}, bf16[8,64,256]{2,1,0:T(8,128)(2,1)S(1)}, u32[]{:S(2)}, u32[]{:S(2)}) collective-permute-start(bf16[8,64,256]{2,1,0:T(8,128)(2,1)S(1)} %all-to-all-done.1.u0), channel_id=1, source_target_pairs={{0,48},{16,0},{32,16},{48,32},{1,49},{17,1},{33,17},{49,33},{2,50}... | collective-permute-start | bytes 786440 | tf_op jit(solution)/shard_map/ppermute | solution.py:382
  55.7 0.7 copy-start.11
  58.3 2.3 copy-start.8
  58.4 2.3 copy-start.9
  60.6 0.7 copy-start.10
  61.3 4.7 %copy-start = (bf16[224,128]{1,0:T(8,128)(2,1)S(1)}, bf16[224,128]{1,0:T(8,128)(2,1)}, u32[]{:S(2)}) copy-start(bf16[224,128]{1,0:T(8,128)(2,1)} %rest_5_.1) | copy-start | bytes 172036
  61.3 4.7 %collective-permute-start.4 = (bf16[4,64,2048]{2,1,0:T(8,128)(2,1)S(1)}, bf16[4,64,2048]{2,1,0:T(8,128)(2,1)S(1)}, u32[]{:S(2)}, u32[]{:S(2)}) collective-permute-start(bf16[4,64,2048]{2,1,0:T(8,128)(2,1)S(1)} %all-to-all-done.own_ref.rest_0_.rest_2_), channel_id=1, source_target_pairs={{0,1},{1,0},{2,3},{3,2},{4,5},{5,4},{6,7},{7,6},{8,9},{9,8},{10,11... | collective-permute-start | bytes 3145736 | tf_op jit(solution)/shard_map/ppermute | solution.py:342
  64.7 1.3 copy-start.4
  86.6 15.0 %collective-permute-start.5 = (f32[136,128]{1,0:T(8,128)S(1)}, f32[136,128]{1,0:T(8,128)S(1)}, u32[]{:S(2)}, u32[]{:S(2)}) collective-permute-start(f32[136,128]{1,0:T(8,128)S(1)} %shard_map.103.mine_ref), channel_id=1, source_target_pairs={{0,2},{2,0},{1,3},{3,1},{4,6},{6,4},{5,7},{7,5},{8,10},{10,8},{9,1... | collective-permute-start | bytes 208904 | tf_op jit(solution)/shard_map/ppermute | solution.py:342
  211.5 14.6 %collective-permute-start.6 = (f32[72,128]{1,0:T(8,128)S(1)}, f32[72,128]{1,0:T(8,128)S(1)}, u32[]{:S(2)}, u32[]{:S(2)}) collective-permute-start(f32[72,128]{1,0:T(8,128)S(1)} %shard_map.109.mine_ref), channel_id=1, source_target_pairs={{0,2},{2,0},{1,3},{3,1},{4,6},{6,4},{5,7},{7,5},{8,10},{10,8},{9,1... | collective-permute-start | bytes 110600 | tf_op jit(solution)/shard_map/ppermute | solution.py:342
  257.7 24.1 %copy-start.2 = (f32[64,224]{1,0:T(8,128)S(1)}, f32[64,224]{1,0:T(8,128)}, u32[]{:S(2)}) copy-start(f32[64,224]{1,0:T(8,128)} %d_ref.3) | copy-start | bytes 172036

commit v7 on v6

--- a/solution.py
+++ b/solution.py
@@ -110,9 +110,13 @@
 
 
 def packed(block):
-    last = jnp.concatenate([block[48:64, at : at + 32] for at in (128, 160, 192)], 0)
-    tail = jnp.concatenate([block[0:48, 128:COLS], last], 1)
-    return jnp.concatenate([block[:, 0:128], tail], 0)
+    tail = block[:, 128:256]
+    lane = lax.broadcasted_iota(jnp.int32, (16, 128), 1)
+    parts = [
+        jnp.where(lane < 96, tail[16 * i : 16 * i + 16], pltpu.roll(tail[48:64], 96 - 32 * i, 1))
+        for i in range(3)
+    ]
+    return jnp.concatenate([block[:, 0:128], *parts], 0)
 
 
 def unpacked(block):
@@ -155,6 +159,17 @@
     o_ref[...] = (1.0 + damp * KEEP) * d_ref[...] - (
         damp * rows_ref[...] + sum_zl(i_ref)
     ) * inv
+
+
+def turn_kernel(proj_ref, s_ref, oproj_ref, os_ref):
+    for i in range(4):
+        span = slice(i * 512, i * 512 + 512)
+        oproj_ref[span, :] = proj_ref[:, span].astype(F32).T.astype(BF)
+    s = s_ref[...].astype(F32).T.astype(BF)
+    for i in range(Y * ZH):
+        for c in range(C):
+            at = (i * C + c) * 32
+            os_ref[c, i * 32 : i * 32 + 32, :] = s[at : at + 32]
 
 
 def start_rows(u_refs, xs, rows_ref, sems):
@@ -191,24 +206,18 @@
 
 
 def first_kernel(
-    place, proj_far, u0, u1, u2, u3, own_ref, oth_ref, s_ref, gain_ref, tag_ref, h_ref, hd_ref, load_ref,
-    proj_ref, rows_ref, sems,
+    place, u0, u1, u2, u3, own_ref, oth_ref, proj_ref, s_ref, gain_ref, tag_ref, h_ref, hd_ref, load_ref,
+    rows_ref, sems,
 ):
-    proj_copy = pltpu.make_async_copy(proj_far, proj_ref, sems.at[X])
-    proj_copy.start()
     xs = [lax.rem(place[4] + X - r, X) for r in range(X)]
     copies = start_rows((u0, u1, u2, u3), xs, rows_ref, sems)
     gain = gain_ref[...]
     halves = []
-    proj_copy.wait()
     for half, a_ref in enumerate((own_ref, oth_ref)):
         c = place[0] if half == 0 else 1 - place[0]
         at = pl.multiple_of(c * 256, 256)
         a = a_ref[...].reshape(256, ROWS)
-        s = jnp.concatenate(
-            [s_ref[y, zh, pl.ds(c, 1)][0] for y in range(Y) for zh in range(ZH)], 0
-        )
-        h = s.astype(F32) + dot(a, proj_ref[...])
+        h = s_ref[c].astype(F32) + dot(a, proj_ref[...])
         h_ref[pl.ds(at, 256), :] = h
         z = scores_of(h, gain, tag_ref)
         for i in range(Y):
@@ -322,7 +331,8 @@
         if second:
             hd = KEEP * hd - mv_ref[span, :] * inv_ref[0:1, 0:1]
         g = back * gain - columns[:, 0:1] * h_ref[span, :] - columns[:, 1:2] * hd
-        g_ref[span, :] = g.astype(BF)
+        g_ref[span, 0:COLS] = g.astype(BF)
+        g_ref[span, COLS:WIDE] = jnp.zeros((256, WIDE - COLS), BF)
     own_at = pl.multiple_of(place[0] * 256, 256)
     oth_at = pl.multiple_of((1 - place[0]) * 256, 256)
     g_own = g_ref[pl.ds(own_at, 256), :]
@@ -359,10 +369,18 @@
     place = jnp.stack([core, own_at, oth_at, zhpos, lax.axis_index("x")]).astype(jnp.int32)
     own_tags = tags[0].reshape(Y, ZH, C, 32).transpose(2, 0, 1, 3).reshape(C * Y, 64)[core * Y + ypos]
     own_tags = own_tags[:, None]
-    toks = stream[0].reshape(Y, ZH, C, 32, COLS)
     gain = norm_gain[None]
 
     by_zl = deal(call(direction_kernel, shape(ZL, 64, WIDE, dtype=BF), direction), "zl")
+    proj, toks = call(
+        turn_kernel,
+        (shape(ROWS, COLS, dtype=BF), shape(C, 256, COLS, dtype=BF)),
+        out_proj.T,
+        stream[0].T,
+    )
+    theirs, proj, toks, own_tags = lax.optimization_barrier(
+        (swap(queries[0], "zh"), proj, toks, own_tags)
+    )
     pair = call(
         functools.partial(
             attend_kernel,
@@ -374,21 +392,19 @@
         keys[0],
         values[0],
         queries[0],
-        swap(queries[0], "zh"),
+        theirs,
         smem=2,
         far=2,
     )
     u0 = [by_zl] + [
         lax.ppermute(by_zl, "x", [(i, (i + r) % X) for i in range(X)]) for r in range(1, X)
     ]
-    own, toks, own_tags, proj, *u0 = lax.optimization_barrier(
-        (deal(pair.reshape(Y, 64, ROWS), "y"), toks, own_tags, out_proj, *u0)
-    )
+    own, *u0 = lax.optimization_barrier((deal(pair.reshape(Y, 64, ROWS), "y"), *u0))
     other = swap(own, "c")
 
     def product(second, *args):
         sent = call(
-            functools.partial(product_kernel, second, scratch=[pltpu.VMEM((512, COLS), BF)]),
+            functools.partial(product_kernel, second, scratch=[pltpu.VMEM((512, WIDE), BF)]),
             shape(X, ZL, PACK, 128, dtype=BF),
             place,
             *args,
@@ -405,20 +421,20 @@
         part = call(sum_parts_kernel, shape(load.shape[1], 128), deal(load, ("c", "y")))
         return call(kernel, outs, part, swap(part, "zh"), *args, own_tags)
 
-    rows_scratch = [pltpu.VMEM((ZL, X, 64, WIDE), BF), pltpu.SemaphoreType.DMA((X + 1,))]
+    rows_scratch = [pltpu.VMEM((ZL, X, 64, WIDE), BF), pltpu.SemaphoreType.DMA((X,))]
     h_loc, hdot0, load = call(
-        functools.partial(first_kernel, scratch=[pltpu.VMEM((ROWS, COLS), BF)] + rows_scratch),
+        functools.partial(first_kernel, scratch=rows_scratch),
         (shape(512, COLS), shape(512, COLS), shape(8, 136, 128)),
         place,
-        proj,
         *u0,
         own,
         other,
+        proj,
         toks,
         gain,
         tag_proj,
         smem=1,
-        far=X + 1,
+        far=X,
     )
     total, mixed = token_sum(load, tokens0_kernel, (shape(136, 128), shape(8, 72, 128)))
     rows0, sent = call(

time: 284 us -> 281 us (0.989)
    pallas_call x14 -> x15, Pallas kernels: 21.7 us -> 18.9 us  [call(): pl.pallas_call(kernel, out_shape=out_shape, in_specs=specs, out_specs=[vm...]
    unnamed x26 -> x27, local copies, waits for them, and re-layouts: 3.97 us -> 6.01 us
  transfers between devices with their start and end apart: 9 -> 9, of which waited for: 6 -> 7; matrix products, arithmetic and copies ran while one was open for 1% -> 1% of each run, Pallas kernels for 2% -> 2%
where the time goes in v7:
time: 281 us; the launch traced here: 280 us
  blocking collectives  171 us (61%)
  starting transfers between devices  55.3 us (20%)
  waiting for transfers between devices  27.2 us (10%)
  Pallas kernels  18.9 us (7%)
  local copies, waits for them, and re-layouts  6.44 us (2%)
    all_to_all x10, blocking collectives, deal(): return lax.all_to_all(x, axis, 0, 0, tiled=True)  171 us
    ppermute x4, starting transfers between devices, swap(): return lax.ppermute(x, axis, [(0, 1), (1, 0)])  26.6 us
    ppermute x4, waiting for transfers between devices, swap(): return lax.ppermute(x, axis, [(0, 1), (1, 0)])  19.3 us
    pallas_call x15, Pallas kernels, call(): pl.pallas_call(kernel, out_shape=out_shape, in_specs=specs, out_specs=[vm...  18.9 us
    all_to_all x2, starting transfers between devices, deal(): return lax.all_to_all(x, axis, 0, 0, tiled=True)  17.2 us
    ppermute x3, starting transfers between devices, local(): lax.ppermute(by_zl, 'x', [(i, (i + r) % X) for i in range(X)])  11.5 us
    unnamed x27, local copies, waits for them, and re-layouts  6.01 us
  transfers between devices with their start and end apart: 9, of which 7 were waited for; matrix products, arithmetic and copies ran while one was open for 1% of the time, Pallas kernels for 2%

profile of v7, /device:TPU:32, one launch (start us, length us, event | category | flops | bytes accessed | tf_op | source)
XLA Modules:
  0.0 280.0 jit_solution(16351169509725710051)
XLA Ops:
  0.0 0.9 copy-done.4
  0.9 0.9 shard_map.102
  1.8 12.6 %all-to-all-start.1 = ((bf16[8,64,256]{2,1,0:T(8,128)(2,1)}), bf16[8,64,256]{2,1,0:T(8,128)(2,1)S(1)}, u32[]{:S(2)}, u32[]{:S(2)}) async-start(bf16[8,64,256]{2,1,0:T(8,128)(2,1)} %shard_map.102), calls=%async_computation.1 | async-start | bytes 524288 | tf_op jit(solution)/shard_map/all_to_all | solution.py:356
  14.4 8.2 %collective-permute-start = (bf16[32,2048]{1,0:T(8,128)(2,1)}, bf16[32,2048]{1,0:T(8,128)(2,1)S(1)}, u32[]{:S(2)}, u32[]{:S(2)}) collective-permute-start(bf16[32,2048]{1,0:T(8,128)(2,1)} %bitcast.22), channel_id=1, source_target_pairs={{0,2},{2,0},{1,3},{3,1},{4,6},{6,4},{5,7},{7,5},{8,10},{10,8},{9,1... | collective-permute-start | bytes 393224 | tf_op jit(solution)/shard_map/ppermute | solution.py:352
  22.7 0.5 broadcast.3
  23.2 1.3 reduce.3
  24.5 0.1 reshape_squeeze.3
  24.6 0.1 reshape.10
  24.7 0.0 copy-done.3
  24.7 0.9 copy-done.6
  25.6 0.4 shard_map.100
  26.0 0.0 copy-start
  26.0 1.0 copy-done
  27.1 0.1 stack.23.place
  27.1 3.7 %collective-permute-done.oth_ref = bf16[32,2048]{1,0:T(8,128)(2,1)S(1)} collective-permute-done((bf16[32,2048]{1,0:T(8,128)(2,1)}, bf16[32,2048]{1,0:T(8,128)(2,1)S(1)}, u32[]{:S(2)}, u32[]{:S(2)}) %collective-permute-start) | collective-permute-done | bytes 131104 | tf_op jit(solution)/shard_map/ppermute | solution.py:352
  30.9 0.0 copy-done.7
  30.9 0.7 copy-done.9
  31.5 4.2 %shard_map.101 = bf16[4,2,32,2048]{3,2,1,0:T(8,128)(2,1)} custom-call(s32[5]{0:T(128)S(1)} %stack.23.place, s32[1,4]{1,0:T(1,128)S(1)} %copy-done.9, bf16[512,1024]{1,0:T(8,128)(2,1)} %bitcast.29, bf16[512,1024]{1,0:T(8,128)(2,1)} %bitcast.30, bf16[32,2048]{1,0:T(8,128)(2,1)S(1)} %bitcast.23, bf16[32,2048]{1,0:T(8,128)(2,1)S(1)} %collective-permute-done.oth_ref), custom_call_target="tpu_custom_call" | custom-call | tf_op jit(solution)/shard_map/pallas_call | solution.py:44
  35.8 3.6 %all-to-all-done.1.u0 = bf16[8,64,256]{2,1,0:T(8,128)(2,1)S(1)} async-done(((bf16[8,64,256]{2,1,0:T(8,128)(2,1)}), bf16[8,64,256]{2,1,0:T(8,128)(2,1)S(1)}, u32[]{:S(2)}, u32[]{:S(2)}) %all-to-all-start.1) | async-done | bytes 262176 | tf_op jit(solution)/shard_map/all_to_all | solution.py:356
  39.4 4.6 %all-to-all-start = ((bf16[4,64,2048]{2,1,0:T(8,128)(2,1)}), bf16[4,64,2048]{2,1,0:T(8,128)(2,1)S(1)}, u32[]{:S(2)}, u32[]{:S(2)}) async-start(bf16[4,64,2048]{2,1,0:T(8,128)(2,1)} %bitcast.13), calls=%async_computation | async-start | bytes 2097152 | tf_op jit(solution)/shard_map/all_to_all | solution.py:356
  44.0 3.5 %collective-permute-start.1 = (bf16[8,64,256]{2,1,0:T(8,128)(2,1)S(1)}, bf16[8,64,256]{2,1,0:T(8,128)(2,1)S(1)}, u32[]{:S(2)}, u32[]{:S(2)}) collective-permute-start(bf16[8,64,256]{2,1,0:T(8,128)(2,1)S(1)} %all-to-all-done.1.u0), channel_id=1, source_target_pairs={{0,16},{16,32},{32,48},{48,0},{1,17},{17,33},{33,49},{49,1},{2,18}... | collective-permute-start | bytes 786440 | tf_op jit(solution)/shard_map/ppermute | solution.py:400
  47.5 4.6 %collective-permute-start.2 = (bf16[8,64,256]{2,1,0:T(8,128)(2,1)S(1)}, bf16[8,64,256]{2,1,0:T(8,128)(2,1)S(1)}, u32[]{:S(2)}, u32[]{:S(2)}) collective-permute-start(bf16[8,64,256]{2,1,0:T(8,128)(2,1)S(1)} %all-to-all-done.1.u0), channel_id=1, source_target_pairs={{0,32},{16,48},{32,0},{48,16},{1,33},{17,49},{33,1},{49,17},{2,34}... | collective-permute-start | bytes 786440 | tf_op jit(solution)/shard_map/ppermute | solution.py:400
  52.1 0.0 copy-done.10
  52.2 3.3 %collective-permute-start.3 = (bf16[8,64,256]{2,1,0:T(8,128)(2,1)S(1)}, bf16[8,64,256]{2,1,0:T(8,128)(2,1)}, u32[]{:S(2)}, u32[]{:S(2)}) collective-permute-start(bf16[8,64,256]{2,1,0:T(8,128)(2,1)S(1)} %all-to-all-done.1.u0), channel_id=1, source_target_pairs={{0,48},{16,0},{32,16},{48,32},{1,49},{17,1},{33,17},{49,33},{2,50}... | collective-permute-start | bytes 786440 | tf_op jit(solution)/shard_map/ppermute | solution.py:400
  55.5 0.0 all-to-all-done.own_ref.rest_0_.rest_2_
  55.5 0.0 collective-permute-done.1.u1
  55.5 0.0 copy-start.11
  55.5 1.8 collective-permute-done.2.u2
  57.4 0.0 copy-done.11
  57.4 0.7 copy-done.12
  58.1 2.5 collective-permute-done.3.u3
  60.5 1.9 collective-permute-start.4
  62.4 2.6 collective-permute-done.4.oth_ref.rest_1_.rest_3_
  65.1 0.0 copy-done.2
  65.1 0.0 copy-done.8
  65.1 1.2 copy-done.1
  66.3 5.0 %shard_map.103 = (f32[512,224]{1,0:T(8,128)S(1)}, f32[512,224]{1,0:T(8,128)S(1)}, f32[8,136,128]{2,1,0:T(8,128)S(1)}) custom-call(s32[5]{0:T(128)S(1)} %stack.23.place, bf16[8,64,256]{2,1,0:T(8,128)(2,1)} %copy-done.10, bf16[8,64,256]{2,1,0:T(8,128)(2,1)} %copy-done.11, bf16[8,64,256]{2,1,0:T(8,128)(2,1)} %copy-done.12, ...), custom_call_target="tpu_custom_call" | custom-call | tf_op jit(solution)/shard_map/pallas_call | solution.py:44
  71.3 15.2 %all_to_all.60.i_ref = f32[8,136,128]{2,1,0:T(8,128)S(1)} all-to-all(f32[8,136,128]{2,1,0:T(8,128)S(1)} %get-tuple-element.37), channel_id=1, replica_groups=mesh['zl'=8,'x'=4,'y'=4,'zh'=2,'c'=2] {'c','y'}, dimensions={0} | all-to-all | bytes 1114112 | tf_op jit(solution)/shard_map/all_to_all | solution.py:356
  86.5 9.3 %collective-permute-start.5 = (f32[136,128]{1,0:T(8,128)S(1)}, f32[136,128]{1,0:T(8,128)S(1)}, u32[]{:S(2)}, u32[]{:S(2)}) collective-permute-start(f32[136,128]{1,0:T(8,128)S(1)} %shard_map.104.mine_ref), channel_id=1, source_target_pairs={{0,2},{2,0},{1,3},{3,1},{4,6},{6,4},{5,7},{7,5},{8,10},{10,8},{9,1... | collective-permute-start | bytes 208904 | tf_op jit(solution)/shard_map/ppermute | solution.py:352
  95.8 0.1 copy.12.tag_ref
  95.9 5.5 %collective-permute-done.5.their_ref = f32[136,128]{1,0:T(8,128)S(1)} collective-permute-done((f32[136,128]{1,0:T(8,128)S(1)}, f32[136,128]{1,0:T(8,128)S(1)}, u32[]{:S(2)}, u32[]{:S(2)}) %collective-permute-start.5) | collective-permute-done | bytes 69664 | tf_op jit(solution)/shard_map/ppermute | solution.py:352
  101.5 0.6 shard_map.105
  102.0 10.1 %all_to_all.61.m_ref = f32[8,72,128]{2,1,0:T(8,128)S(1)} all-to-all(f32[8,72,128]{2,1,0:T(8,128)S(1)} %get-tuple-element.39), channel_id=1, replica_groups=mesh['zl'=8,'x'=4,'y'=4,'zh'=2,'c'=2] {'c','y'}, dimensions={0} | all-to-all | bytes 589824 | tf_op jit(solution)/shard_map/all_to_all | solution.py:356
  112.2 1.8 shard_map.106
  114.0 17.7 %all_to_all.62.i_ref = bf16[4,8,112,128]{3,2,1,0:T(8,128)(2,1)S(1)} all-to-all(bf16[4,8,112,128]{3,2,1,0:T(8,128)(2,1)S(1)} %shard_map.106), channel_id=1, replica_groups=mesh['zl'=8,'x'=4,'y'=4,'zh'=2,'c'=2] {'x'}, dimensions={0} | all-to-all | bytes 1835008 | tf_op jit(solution)/shard_map/all_to_all | solution.py:356
  131.7 0.1 shard_map.107
  131.8 32.3 %all_to_all.63.i_ref = bf16[8,112,128]{2,1,0:T(8,128)(2,1)S(1)} all-to-all(bf16[8,112,128]{2,1,0:T(8,128)(2,1)S(1)} %shard_map.107), channel_id=1, replica_groups=mesh['zl'=8,'x'=4,'y'=4,'zh'=2,'c'=2] {'zl'}, dimensions={0} | all-to-all | bytes 458752 | tf_op jit(solution)/shard_map/all_to_all | solution.py:356
  164.1 0.2 shard_map.108
  164.3 20.5 %all_to_all.64 = bf16[8,64,256]{2,1,0:T(8,128)(2,1)S(1)} all-to-all(bf16[8,64,256]{2,1,0:T(8,128)(2,1)S(1)} %get-tuple-element.42), channel_id=1, replica_groups=mesh['zl'=8,'x'=4,'y'=4,'zh'=2,'c'=2] {'zl'}, dimensions={0} | all-to-all | bytes 524288 | tf_op jit(solution)/shard_map/all_to_all | solution.py:356
  184.9 0.1 broadcast_in_dim.12
  184.9 13.3 %all_to_all.65 = bf16[4,512,256]{2,1,0:T(8,128)(2,1)S(1)} all-to-all(bf16[4,512,256]{2,1,0:T(8,128)(2,1)S(1)} %broadcast_in_dim.12), channel_id=1, replica_groups=mesh['zl'=8,'x'=4,'y'=4,'zh'=2,'c'=2] {'x'}, dimensions={0} | all-to-all | bytes 2097152 | tf_op jit(solution)/shard_map/all_to_all | solution.py:356
  198.2 2.3 shard_map.109
  200.5 10.1 %all_to_all.66.i_ref = f32[8,72,128]{2,1,0:T(8,128)S(1)} all-to-all(f32[8,72,128]{2,1,0:T(8,128)S(1)} %get-tuple-element.43), channel_id=1, replica_groups=mesh['zl'=8,'x'=4,'y'=4,'zh'=2,'c'=2] {'c','y'}, dimensions={0} | all-to-all | bytes 589824 | tf_op jit(solution)/shard_map/all_to_all | solution.py:356
  210.7 7.2 %collective-permute-start.6 = (f32[72,128]{1,0:T(8,128)S(1)}, f32[72,128]{1,0:T(8,128)S(1)}, u32[]{:S(2)}, u32[]{:S(2)}) collective-permute-start(f32[72,128]{1,0:T(8,128)S(1)} %shard_map.110.mine_ref), channel_id=1, source_target_pairs={{0,2},{2,0},{1,3},{3,1},{4,6},{6,4},{5,7},{7,5},{8,10},{10,8},{9,1... | collective-permute-start | bytes 110600 | tf_op jit(solution)/shard_map/ppermute | solution.py:352
  217.8 7.4 %collective-permute-done.6.their_ref = f32[72,128]{1,0:T(8,128)S(1)} collective-permute-done((f32[72,128]{1,0:T(8,128)S(1)}, f32[72,128]{1,0:T(8,128)S(1)}, u32[]{:S(2)}, u32[]{:S(2)}) %collective-permute-start.6) | collective-permute-done | bytes 36896 | tf_op jit(solution)/shard_map/ppermute | solution.py:352
  225.3 0.6 shard_map.111
  225.8 11.0 %all_to_all.67.m_ref = f32[8,72,128]{2,1,0:T(8,128)S(1)} all-to-all(f32[8,72,128]{2,1,0:T(8,128)S(1)} %get-tuple-element.45), channel_id=1, replica_groups=mesh['zl'=8,'x'=4,'y'=4,'zh'=2,'c'=2] {'c','y'}, dimensions={0} | all-to-all | bytes 589824 | tf_op jit(solution)/shard_map/all_to_all | solution.py:356
  236.9 1.8 shard_map.112
  238.7 16.7 %all_to_all.68.i_ref = bf16[4,8,112,128]{3,2,1,0:T(8,128)(2,1)S(1)} all-to-all(bf16[4,8,112,128]{3,2,1,0:T(8,128)(2,1)S(1)} %shard_map.112), channel_id=1, replica_groups=mesh['zl'=8,'x'=4,'y'=4,'zh'=2,'c'=2] {'x'}, dimensions={0} | all-to-all | bytes 1835008 | tf_op jit(solution)/shard_map/all_to_all | solution.py:356
  255.4 0.1 shard_map.113
  255.5 0.0 copy-start.5
  255.5 23.8 %all_to_all.69.i_ref = bf16[8,112,128]{2,1,0:T(8,128)(2,1)S(1)} all-to-all(bf16[8,112,128]{2,1,0:T(8,128)(2,1)S(1)} %shard_map.113), channel_id=1, replica_groups=mesh['zl'=8,'x'=4,'y'=4,'zh'=2,'c'=2] {'zl'}, dimensions={0} | all-to-all | bytes 458752 | tf_op jit(solution)/shard_map/all_to_all | solution.py:356
  279.3 0.0 copy-done.5
  279.3 0.7 shard_map.114
  (14 shorter events, 0.1 us)
Async XLA Ops:
  0.0 24.7 %copy-start.3 = (bf16[2048,224]{0,1:T(8,128)(2,1)S(1)}, bf16[2048,224]{0,1:T(8,128)(2,1)}, u32[]{:S(2)}) copy-start(bf16[2048,224]{0,1:T(8,128)(2,1)} %param.14) | copy-start | bytes 2752516
  0.0 0.9 copy-start.4
  1.8 37.6 %all-to-all-start.1 = ((bf16[8,64,256]{2,1,0:T(8,128)(2,1)}), bf16[8,64,256]{2,1,0:T(8,128)(2,1)S(1)}, u32[]{:S(2)}, u32[]{:S(2)}) async-start(bf16[8,64,256]{2,1,0:T(8,128)(2,1)} %shard_map.102), calls=%async_computation.1 | async-start | bytes 524288 | tf_op jit(solution)/shard_map/all_to_all | solution.py:356
  14.4 16.5 %collective-permute-start = (bf16[32,2048]{1,0:T(8,128)(2,1)}, bf16[32,2048]{1,0:T(8,128)(2,1)S(1)}, u32[]{:S(2)}, u32[]{:S(2)}) collective-permute-start(bf16[32,2048]{1,0:T(8,128)(2,1)} %bitcast.22), channel_id=1, source_target_pairs={{0,2},{2,0},{1,3},{3,1},{4,6},{6,4},{5,7},{7,5},{8,10},{10,8},{9,1... | collective-permute-start | bytes 393224 | tf_op jit(solution)/shard_map/ppermute | solution.py:352
  24.7 0.9 copy-start.6
  25.6 5.3 %copy-start.7 = (bf16[1,32,2048]{2,1,0:T(8,128)(2,1)S(1)}, bf16[1,32,2048]{2,1,0:T(8,128)(2,1)}, u32[]{:S(2)}) copy-start(bf16[1,32,2048]{2,1,0:T(8,128)(2,1)} %param.10) | copy-start | bytes 393220
  26.0 1.0 copy-start
  30.9 0.7 copy-start.9
  39.4 12.8 %copy-start.10 = (bf16[8,64,256]{2,1,0:T(8,128)(2,1)}, bf16[8,64,256]{2,1,0:T(8,128)(2,1)S(1)}, u32[]{:S(2)}) copy-start(bf16[8,64,256]{2,1,0:T(8,128)(2,1)S(1)} %all-to-all-done.1.u0) | copy-start | bytes 786436
  39.4 25.7 %copy-start.2 = (bf16[224,128]{1,0:T(8,128)(2,1)S(1)}, bf16[224,128]{1,0:T(8,128)(2,1)}, u32[]{:S(2)}) copy-start(bf16[224,128]{1,0:T(8,128)(2,1)} %rest_5_.1) | copy-start | bytes 172036
  39.4 16.1 %all-to-all-start = ((bf16[4,64,2048]{2,1,0:T(8,128)(2,1)}), bf16[4,64,2048]{2,1,0:T(8,128)(2,1)S(1)}, u32[]{:S(2)}, u32[]{:S(2)}) async-start(bf16[4,64,2048]{2,1,0:T(8,128)(2,1)} %bitcast.13), calls=%async_computation | async-start | bytes 2097152 | tf_op jit(solution)/shard_map/all_to_all | solution.py:356
  44.0 21.1 %copy-start.8 = (f32[224]{0:T(256)S(1)}, f32[224]{0:T(256)}, u32[]{:S(2)}) copy-start(f32[224]{0:T(256)} %param.15) | copy-start | bytes 2692
  44.0 11.5 %collective-permute-start.1 = (bf16[8,64,256]{2,1,0:T(8,128)(2,1)S(1)}, bf16[8,64,256]{2,1,0:T(8,128)(2,1)S(1)}, u32[]{:S(2)}, u32[]{:S(2)}) collective-permute-start(bf16[8,64,256]{2,1,0:T(8,128)(2,1)S(1)} %all-to-all-done.1.u0), channel_id=1, source_target_pairs={{0,16},{16,32},{32,48},{48,0},{1,17},{17,33},{33,49},{49,1},{2,18}... | collective-permute-start | bytes 786440 | tf_op jit(solution)/shard_map/ppermute | solution.py:400
  47.5 9.9 %collective-permute-start.2 = (bf16[8,64,256]{2,1,0:T(8,128)(2,1)S(1)}, bf16[8,64,256]{2,1,0:T(8,128)(2,1)S(1)}, u32[]{:S(2)}, u32[]{:S(2)}) collective-permute-start(bf16[8,64,256]{2,1,0:T(8,128)(2,1)S(1)} %all-to-all-done.1.u0), channel_id=1, source_target_pairs={{0,32},{16,48},{32,0},{48,16},{1,33},{17,49},{33,1},{49,17},{2,34}... | collective-permute-start | bytes 786440 | tf_op jit(solution)/shard_map/ppermute | solution.py:400
  52.2 8.4 %collective-permute-start.3 = (bf16[8,64,256]{2,1,0:T(8,128)(2,1)S(1)}, bf16[8,64,256]{2,1,0:T(8,128)(2,1)}, u32[]{:S(2)}, u32[]{:S(2)}) collective-permute-start(bf16[8,64,256]{2,1,0:T(8,128)(2,1)S(1)} %all-to-all-done.1.u0), channel_id=1, source_target_pairs={{0,48},{16,0},{32,16},{48,32},{1,49},{17,1},{33,17},{49,33},{2,50}... | collective-permute-start | bytes 786440 | tf_op jit(solution)/shard_map/ppermute | solution.py:400
  55.5 1.8 copy-start.11
  57.4 0.7 copy-start.12
  60.5 4.5 %collective-permute-start.4 = (bf16[4,64,2048]{2,1,0:T(8,128)(2,1)S(1)}, bf16[4,64,2048]{2,1,0:T(8,128)(2,1)S(1)}, u32[]{:S(2)}, u32[]{:S(2)}) collective-permute-start(bf16[4,64,2048]{2,1,0:T(8,128)(2,1)S(1)} %all-to-all-done.own_ref.rest_0_.rest_2_), channel_id=1, source_target_pairs={{0,1},{1,0},{2,3},{3,2},{4,5},{5,4},{6,7},{7,6},{8,9},{9,8},{10,11... | collective-permute-start | bytes 3145736 | tf_op jit(solution)/shard_map/ppermute | solution.py:352
  65.1 1.2 copy-start.1
  86.5 14.9 %collective-permute-start.5 = (f32[136,128]{1,0:T(8,128)S(1)}, f32[136,128]{1,0:T(8,128)S(1)}, u32[]{:S(2)}, u32[]{:S(2)}) collective-permute-start(f32[136,128]{1,0:T(8,128)S(1)} %shard_map.104.mine_ref), channel_id=1, source_target_pairs={{0,2},{2,0},{1,3},{3,1},{4,6},{6,4},{5,7},{7,5},{8,10},{10,8},{9,1... | collective-permute-start | bytes 208904 | tf_op jit(solution)/shard_map/ppermute | solution.py:352
  210.7 14.6 %collective-permute-start.6 = (f32[72,128]{1,0:T(8,128)S(1)}, f32[72,128]{1,0:T(8,128)S(1)}, u32[]{:S(2)}, u32[]{:S(2)}) collective-permute-start(f32[72,128]{1,0:T(8,128)S(1)} %shard_map.110.mine_ref), channel_id=1, source_target_pairs={{0,2},{2,0},{1,3},{3,1},{4,6},{6,4},{5,7},{7,5},{8,10},{10,8},{9,1... | collective-permute-start | bytes 110600 | tf_op jit(solution)/shard_map/ppermute | solution.py:352
  255.5 23.8 %copy-start.5 = (f32[64,224]{1,0:T(8,128)S(1)}, f32[64,224]{1,0:T(8,128)}, u32[]{:S(2)}) copy-start(f32[64,224]{1,0:T(8,128)} %d_ref.3) | copy-start | bytes 172036

commit v8 on v7

--- a/solution.py
+++ b/solution.py
@@ -93,11 +93,14 @@
         scores = 50.0 * jnp.tanh(scores * (1.0 / 16.0) / 50.0)
         expo = jnp.where(allowed, jnp.exp(scores), 0.0)
         weights = (expo / jnp.sum(expo, -1, keepdims=True)).astype(BF)
-        out = dot(weights, v_ref[:, cols]).astype(BF)
-        for r, head in enumerate(heads):
+        out = dot(weights, v_ref[:, cols])
+        for x in range(X):
+            span = slice(x * 64, x * 64 + 64)
+            both = jnp.concatenate([out[0:64, span], out[64:128, span]], 1).astype(BF)
+            at = x * 512 + g * 128
             for y in range(Y):
-                o_ref[y, zh, :, head] = out[r * 64 : r * 64 + 32]
-                o_ref[y, 1 - zh, :, head] = out[r * 64 + 32 : r * 64 + 64]
+                o_ref[y, zh, :, at : at + 128] = both[0:32]
+                o_ref[y, 1 - zh, :, at : at + 128] = both[32:64]
 
 
 def row_block(block):
@@ -164,7 +167,10 @@
 def turn_kernel(proj_ref, s_ref, oproj_ref, os_ref):
     for i in range(4):
         span = slice(i * 512, i * 512 + 512)
-        oproj_ref[span, :] = proj_ref[:, span].astype(F32).T.astype(BF)
+        rows = proj_ref[:, span].astype(F32).T.astype(BF)
+        for j in range(8):
+            at = (j % X) * 512 + (2 * i + j // X) * 64
+            oproj_ref[at : at + 64, :] = rows[j * 64 : j * 64 + 64]
     s = s_ref[...].astype(F32).T.astype(BF)
     for i in range(Y * ZH):
         for c in range(C):
@@ -172,93 +178,111 @@
             os_ref[c, i * 32 : i * 32 + 32, :] = s[at : at + 32]
 
 
-def start_rows(u_refs, xs, rows_ref, sems):
-    copies = [
-        pltpu.make_async_copy(u, rows_ref.at[:, x], sems.at[i]) for i, (u, x) in enumerate(zip(u_refs, xs))
-    ]
+def square_of(rows):
+    return jnp.sum(rows[:, COLS : COLS + 2].astype(F32))
+
+
+def scores_of(x, gain, tag_ref):
+    return sum(dot(part, tag_ref[...]) for part in three(x * gain))
+
+
+def two(x):
+    hi = x.astype(BF).astype(F32)
+    return hi, (x - hi).astype(BF).astype(F32)
+
+
+def rows_of(columns, count):
+    lane = lax.broadcasted_iota(jnp.int32, (count, 128), 1)
+    table = jnp.zeros((count, 128), F32)
+    for i, column in enumerate(columns):
+        hi, lo = two(column)
+        table = jnp.where(lane == 2 * i, hi, jnp.where(lane == 2 * i + 1, lo, table))
+    if count < 128:
+        table = jnp.concatenate([table, jnp.zeros((128 - count, 128), F32)], 0)
+    return table.T[0:16]
+
+
+def put_scores(load_ref, block, row, z):
+    for i in range(Y):
+        load_ref[block + i, row : row + 64, :] = z[i * 64 : i * 64 + 64].astype(BF)
+
+
+def put_sums(load_ref, block, row, sums, scalar):
+    rows = rows_of((*sums, jnp.full((256, 1), scalar, F32)), 256)
+    for i in range(Y):
+        own = rows[:, i * 64 : i * 64 + 64]
+        load_ref[block + i, row : row + 16, :] = jnp.concatenate([own, own], 1).astype(BF)
+
+
+def first_kernel(
+    place, proj_far, u0, u1, u2, u3, own_ref, oth_ref, s_ref, gain_ref, tag_ref, h_ref, hd_ref, load_ref,
+    proj_ref, rows_ref, sems,
+):
+    copies = []
+    for r in range(X):
+        span = pl.ds(r * 512, 512)
+        copies.append(pltpu.make_async_copy(proj_far.at[span], proj_ref.at[span], sems.at[r]))
+    for r, u in enumerate((u0, u1, u2, u3)):
+        copies.append(pltpu.make_async_copy(u, rows_ref.at[r], sems.at[X + r]))
     for copy in copies:
         copy.start()
-    return copies
-
-
-def await_rows(copies, rows_ref):
-    for copy in copies:
-        copy.wait()
-    return (
-        rows_ref[...].reshape(ROWS, WIDE),
-        jnp.sum(rows_ref[:, :, :, COLS : COLS + 2].astype(F32)),
-    )
-
-
-def scores_of(x, gain, tag_ref):
-    return sum(dot(part, tag_ref[...]) for part in three(x * gain))
-
-
-def put_sums(load_ref, block, row, sums, scalar):
-    lane = lax.broadcasted_iota(jnp.int32, (256, 128), 1)
-    table = jnp.full((256, 128), scalar, F32)
-    for i, s in enumerate(sums):
-        table = jnp.where(lane == i, s, table)
-    table = table.T
-    for i in range(Y):
-        load_ref[block + i, row : row + 8, 0:64] = table[0:8, i * 64 : (i + 1) * 64]
-        load_ref[block + i, row : row + 8, 64:128] = table[0:8, 0:64]
-
-
-def first_kernel(
-    place, u0, u1, u2, u3, own_ref, oth_ref, proj_ref, s_ref, gain_ref, tag_ref, h_ref, hd_ref, load_ref,
-    rows_ref, sems,
-):
-    xs = [lax.rem(place[4] + X - r, X) for r in range(X)]
-    copies = start_rows((u0, u1, u2, u3), xs, rows_ref, sems)
     gain = gain_ref[...]
     halves = []
     for half, a_ref in enumerate((own_ref, oth_ref)):
         c = place[0] if half == 0 else 1 - place[0]
-        at = pl.multiple_of(c * 256, 256)
-        a = a_ref[...].reshape(256, ROWS)
-        h = s_ref[c].astype(F32) + dot(a, proj_ref[...])
+        halves.append((c, pl.multiple_of(c * 256, 256), a_ref))
+    hs = [s_ref[c].astype(F32) for c, _, _ in halves]
+    for r in range(X):
+        copies[r].wait()
+        span = slice(r * 512, r * 512 + 512)
+        for i, (_, _, a_ref) in enumerate(halves):
+            hs[i] += dot(a_ref[:, :, span].reshape(256, 512), proj_ref[span, :])
+    for h, (c, at, _) in zip(hs, halves):
         h_ref[pl.ds(at, 256), :] = h
         z = scores_of(h, gain, tag_ref)
-        for i in range(Y):
-            load_ref[c * Y + i, 0:64, :] = z[i * 64 : i * 64 + 64]
-        halves.append((c, at, a_ref))
-    rows, norm = await_rows(copies, rows_ref)
-    for c, at, a_ref in halves:
-        h = h_ref[pl.ds(at, 256), :]
-        hd = dot(a_ref[...].reshape(256, ROWS), rows)[:, :COLS]
+        z_hi = z.astype(BF).astype(F32)
+        put_scores(load_ref, c * Y, 0, z_hi)
+        put_scores(load_ref, c * Y, 64, z - z_hi)
+    hds = [jnp.zeros((256, WIDE), F32)] * 2
+    norm = 0.0
+    for r in range(X):
+        copies[X + r].wait()
+        x = lax.rem(place[4] + X - r, X)
+        span = pl.ds(pl.multiple_of(x * 512, 512), 512)
+        norm += square_of(rows_ref[r])
+        for i, (_, _, a_ref) in enumerate(halves):
+            hds[i] += dot(a_ref[:, :, span].reshape(256, 512), rows_ref[r])
+    for h, hd, (c, at, _) in zip(hs, hds, halves):
+        hd = hd[:, :COLS]
         hd_ref[pl.ds(at, 256), :] = hd
-        zd = scores_of(hd, gain, tag_ref)
-        for i in range(Y):
-            load_ref[c * Y + i, 64:128, :] = zd[i * 64 : i * 64 + 64]
+        put_scores(load_ref, c * Y, 128, scores_of(hd, gain, tag_ref))
         sums = (jnp.sum(h * h, -1, keepdims=True), jnp.sum(h * hd, -1, keepdims=True))
-        put_sums(load_ref, c * Y, 128, sums, norm)
-
-
-def moved_kernel(
-    place, u_ref, own_ref, oth_ref, h_ref, gain_ref, tag_ref, mv_ref, load_ref, rows_ref
-):
-    for x in range(X):
-        rows_ref[:, x] = u_ref[x]
-    rows, norm = await_rows((), rows_ref)
+        put_sums(load_ref, c * Y, 192, sums, norm)
+
+
+def moved_kernel(place, u_ref, own_ref, oth_ref, h_ref, gain_ref, tag_ref, mv_ref, load_ref):
+    norm = square_of(u_ref[...])
     gain = gain_ref[...]
     for half, a_ref in enumerate((own_ref, oth_ref)):
         c = place[0] if half == 0 else 1 - place[0]
         at = pl.multiple_of(c * 256, 256)
-        moved = dot(a_ref[...].reshape(256, ROWS), rows)[:, :COLS]
+        moved = dot(a_ref[...].reshape(256, ROWS), u_ref[...])[:, :COLS]
         mv_ref[pl.ds(at, 256), :] = moved
-        z = scores_of(moved, gain, tag_ref)
-        for i in range(Y):
-            load_ref[c * Y + i, 0:64, :] = z[i * 64 : i * 64 + 64]
+        put_scores(load_ref, c * Y, 0, scores_of(moved, gain, tag_ref))
         sums = (jnp.sum(h_ref[pl.ds(at, 256), :] * moved, -1, keepdims=True),)
         put_sums(load_ref, c * Y, 64, sums, norm)
 
 
 def sum_parts_kernel(i_ref, o_ref):
-    total = i_ref[0]
+    total = i_ref[0].astype(F32)
     for i in range(1, 8):
-        total += i_ref[i]
-    o_ref[...] = total
+        total += i_ref[i].astype(F32)
+    scores = total[: total.shape[0] - 16]
+    if scores.shape[0] == 192:
+        scores = jnp.concatenate([scores[0:64] + scores[64:128], scores[128:192]], 0)
+    sums = total[total.shape[0] - 16 :]
+    joined = [sums[2 * i : 2 * i + 1] + sums[2 * i + 1 : 2 * i + 2] for i in range(8)]
+    o_ref[...] = jnp.concatenate([scores, *joined], 0)
 
 
 def columns_of(rows):
@@ -284,12 +308,11 @@
     rhodot = jnp.sum(wdot * zval + wgrad * zdot, -1, keepdims=True)
     mixed = rdot * wgrad + rscale * wdot
     coeff = rhodot * cube + 3.0 * rho * rscale * rscale * rdot / D
-    lane = lax.broadcasted_iota(jnp.int32, (64, 128), 1)
-    table = jnp.where(lane == 0, coeff, jnp.where(lane == 1, rho * cube, 0.0))
-    tail = jnp.concatenate([table, jnp.zeros((64, 128), F32)], 0).T[0:8]
+    mixed = mixed.astype(BF)
+    tail = rows_of((coeff, rho * cube), 64).astype(BF)
     for i in range(8):
         o_ref[i, 0:64, :] = mixed
-        o_ref[i, 64:72, :] = tail
+        o_ref[i, 64:80, :] = tail
 
 
 def tokens0_kernel(mine_ref, their_ref, tag_ref, total_ref, o_ref):
@@ -322,30 +345,30 @@
     for c in range(C):
         span = slice(c * 256, c * 256 + 256)
         mixed = jnp.concatenate([m_ref[c * Y + i, 0:64, :] for i in range(Y)], 0)
-        back = sum(
-            lax.dot_general(part, tag_ref[...], CONTRACT1, preferred_element_type=F32)
-            for part in three(mixed)
+        back = lax.dot_general(mixed, tag_ref[...], CONTRACT1, preferred_element_type=F32)
+        columns = jnp.concatenate(
+            [columns_of(m_ref[c * Y + i, 64:80, :].astype(F32)[0:8]) for i in range(Y)], 0
         )
-        columns = jnp.concatenate([columns_of(m_ref[c * Y + i, 64:72, :]) for i in range(Y)], 0)
+        coeff, cubed = columns[:, 0:1] + columns[:, 1:2], columns[:, 2:3] + columns[:, 3:4]
         hd = hd_ref[span, :]
         if second:
             hd = KEEP * hd - mv_ref[span, :] * inv_ref[0:1, 0:1]
-        g = back * gain - columns[:, 0:1] * h_ref[span, :] - columns[:, 1:2] * hd
+        g = back * gain - coeff * h_ref[span, :] - cubed * hd
         g_ref[span, 0:COLS] = g.astype(BF)
         g_ref[span, COLS:WIDE] = jnp.zeros((256, WIDE - COLS), BF)
     own_at = pl.multiple_of(place[0] * 256, 256)
     oth_at = pl.multiple_of((1 - place[0]) * 256, 256)
     g_own = g_ref[pl.ds(own_at, 256), :]
     g_oth = g_ref[pl.ds(oth_at, 256), :]
-    for zl in range(ZL):
-        cols = slice(zl * 256, zl * 256 + 256)
+    for j in range(8):
+        cols = slice(j * 256, j * 256 + 256)
         part = lax.dot_general(
             own_ref[:, :, cols].reshape(256, 256), g_own, CONTRACT0, preferred_element_type=F32
         ) + lax.dot_general(
             oth_ref[:, :, cols].reshape(256, 256), g_oth, CONTRACT0, preferred_element_type=F32
         )
-        for x in range(X):
-            o_ref[x, zl] = packed(part[x * 64 : x * 64 + 64]).astype(BF)
+        for i in range(4):
+            o_ref[j // 2, (j % 2) * 4 + i] = packed(part[i * 64 : i * 64 + 64]).astype(BF)
 
 
 def swap(x, axis):
@@ -372,6 +395,7 @@
     gain = norm_gain[None]
 
     by_zl = deal(call(direction_kernel, shape(ZL, 64, WIDE, dtype=BF), direction), "zl")
+    by_zl = by_zl.reshape(ZL * 64, WIDE)
     proj, toks = call(
         turn_kernel,
         (shape(ROWS, COLS, dtype=BF), shape(C, 256, COLS, dtype=BF)),
@@ -417,35 +441,41 @@
         part = call(sum_x_kernel, shape(ZL, PACK, 128, dtype=BF), deal(sent, "x"))
         return deal(part, "zl")
 
-    def token_sum(load, kernel, outs, *args):
-        part = call(sum_parts_kernel, shape(load.shape[1], 128), deal(load, ("c", "y")))
+    def token_sum(load, rows, kernel, outs, *args):
+        part = call(sum_parts_kernel, shape(rows, 128), deal(load, ("c", "y")))
         return call(kernel, outs, part, swap(part, "zh"), *args, own_tags)
 
-    rows_scratch = [pltpu.VMEM((ZL, X, 64, WIDE), BF), pltpu.SemaphoreType.DMA((X,))]
     h_loc, hdot0, load = call(
-        functools.partial(first_kernel, scratch=rows_scratch),
-        (shape(512, COLS), shape(512, COLS), shape(8, 136, 128)),
+        functools.partial(
+            first_kernel,
+            scratch=[
+                pltpu.VMEM((ROWS, COLS), BF),
+                pltpu.VMEM((X, ZL * 64, WIDE), BF),
+                pltpu.SemaphoreType.DMA((2 * X,)),
+            ],
+        ),
+        (shape(512, COLS), shape(512, COLS), shape(8, 208, 128, dtype=BF)),
         place,
+        proj,
         *u0,
         own,
         other,
-        proj,
         toks,
         gain,
         tag_proj,
         smem=1,
-        far=X,
-    )
-    total, mixed = token_sum(load, tokens0_kernel, (shape(136, 128), shape(8, 72, 128)))
+        far=X + 1,
+    )
+    total, mixed = token_sum(load, 136, tokens0_kernel, (shape(136, 128), shape(8, 80, 128, dtype=BF)))
     rows0, sent = call(
         sum_rows_kernel,
         (shape(64, COLS), shape(ZL, 64, WIDE, dtype=BF)),
         product(False, deal(mixed, ("c", "y")), h_loc, hdot0),
     )
-    full0 = spread(deal(sent, "zl").reshape(ZL * 64, WIDE), "x", X).reshape(X, ZL, 64, WIDE)
+    full0 = spread(deal(sent, "zl").reshape(ZL * 64, WIDE), "x", X).reshape(ROWS, WIDE)
     moved, load = call(
-        functools.partial(moved_kernel, scratch=rows_scratch[:1]),
-        (shape(512, COLS), shape(8, 72, 128)),
+        moved_kernel,
+        (shape(512, COLS), shape(8, 80, 128, dtype=BF)),
         place,
         full0,
         own,
@@ -455,7 +485,9 @@
         tag_proj,
         smem=1,
     )
-    mixed, inv = token_sum(load, tokens1_kernel, (shape(8, 72, 128), shape(8, 128)), total)
+    mixed, inv = token_sum(
+        load, 72, tokens1_kernel, (shape(8, 80, 128, dtype=BF), shape(8, 128)), total
+    )
     arrived = product(True, deal(mixed, ("c", "y")), h_loc, hdot0, moved, inv)
     return call(last_kernel, shape(64, COLS), arrived, rows0, direction, inv)
 

time: 281 us -> 272 us (0.968)
  blocking collectives: 171 us -> 164 us
    all_to_all x10, blocking collectives: 171 us -> 164 us  [deal(): return lax.all_to_all(x, axis, 0, 0, tiled=True)]
    unnamed x27 -> x25, local copies, waits for them, and re-layouts: 6.01 us -> 4.76 us
where the time goes in v8:
time: 272 us; the launch traced here: 271 us
  blocking collectives  164 us (60%)
  starting transfers between devices  55.2 us (20%)
  waiting for transfers between devices  27.2 us (10%)
  Pallas kernels  18.7 us (7%)
  local copies, waits for them, and re-layouts  5.19 us (2%)
    all_to_all x10, blocking collectives, deal(): return lax.all_to_all(x, axis, 0, 0, tiled=True)  164 us
    ppermute x4, starting transfers between devices, swap(): return lax.ppermute(x, axis, [(0, 1), (1, 0)])  26.4 us
    ppermute x4, waiting for transfers between devices, swap(): return lax.ppermute(x, axis, [(0, 1), (1, 0)])  19.5 us
    pallas_call x15, Pallas kernels, call(): pl.pallas_call(kernel, out_shape=out_shape, in_specs=specs, out_specs=[vm...  18.7 us
    all_to_all x2, starting transfers between devices, deal(): return lax.all_to_all(x, axis, 0, 0, tiled=True)  17.2 us
    ppermute x3, starting transfers between devices, local(): lax.ppermute(by_zl, 'x', [(i, (i + r) % X) for i in range(X)])  11.5 us
  transfers between devices with their start and end apart: 9, of which 7 were waited for; matrix products, arithmetic and copies ran while one was open for 1% of the time, Pallas kernels for 2%

profile of v8, /device:TPU:32, one launch (start us, length us, event | category | flops | bytes accessed | tf_op | source)
XLA Modules:
  0.0 271.4 jit_solution(7167794842661708577)
XLA Ops:
  0.0 0.9 copy-done.3
  0.9 0.9 shard_map.102
  1.8 12.6 %all-to-all-start.1 = ((bf16[8,64,256]{2,1,0:T(8,128)(2,1)}), bf16[8,64,256]{2,1,0:T(8,128)(2,1)S(1)}, u32[]{:S(2)}, u32[]{:S(2)}) async-start(bf16[8,64,256]{2,1,0:T(8,128)(2,1)} %shard_map.102), calls=%async_computation.1 | async-start | bytes 524288 | tf_op jit(solution)/shard_map/all_to_all | solution.py:379
  14.4 8.2 %collective-permute-start = (bf16[32,2048]{1,0:T(8,128)(2,1)}, bf16[32,2048]{1,0:T(8,128)(2,1)S(1)}, u32[]{:S(2)}, u32[]{:S(2)}) collective-permute-start(bf16[32,2048]{1,0:T(8,128)(2,1)} %bitcast.23), channel_id=1, source_target_pairs={{0,2},{2,0},{1,3},{3,1},{4,6},{6,4},{5,7},{7,5},{8,10},{10,8},{9,1... | collective-permute-start | bytes 393224 | tf_op jit(solution)/shard_map/ppermute | solution.py:375
  22.7 0.5 broadcast.3
  23.2 1.3 reduce.3
  24.4 0.1 reshape_squeeze.3
  24.5 0.1 reshape.13
  24.6 0.0 copy-done.2
  24.6 0.9 copy-done.5
  25.6 0.4 shard_map.100
  26.0 0.0 copy-start
  26.0 1.0 copy-done
  27.0 0.1 stack.23.place
  27.1 3.8 %collective-permute-done.oth_ref = bf16[32,2048]{1,0:T(8,128)(2,1)S(1)} collective-permute-done((bf16[32,2048]{1,0:T(8,128)(2,1)}, bf16[32,2048]{1,0:T(8,128)(2,1)S(1)}, u32[]{:S(2)}, u32[]{:S(2)}) %collective-permute-start) | collective-permute-done | bytes 131104 | tf_op jit(solution)/shard_map/ppermute | solution.py:375
  30.9 0.0 copy-done.6
  30.9 0.7 copy-done.8
  31.6 4.4 %shard_map.101 = bf16[4,2,32,2048]{3,2,1,0:T(8,128)(2,1)} custom-call(s32[5]{0:T(128)S(1)} %stack.23.place, s32[1,4]{1,0:T(1,128)S(1)} %copy-done.8, bf16[512,1024]{1,0:T(8,128)(2,1)} %bitcast.30, bf16[512,1024]{1,0:T(8,128)(2,1)} %bitcast.31, bf16[32,2048]{1,0:T(8,128)(2,1)S(1)} %bitcast.24, bf16[32,2048]{1,0:T(8,128)(2,1)S(1)} %collective-permute-done.oth_ref), custom_call_target="tpu_custom_call" | custom-call | tf_op jit(solution)/shard_map/pallas_call | solution.py:44
  36.0 3.4 %all-to-all-done.1 = bf16[8,64,256]{2,1,0:T(8,128)(2,1)S(1)} async-done(((bf16[8,64,256]{2,1,0:T(8,128)(2,1)}), bf16[8,64,256]{2,1,0:T(8,128)(2,1)S(1)}, u32[]{:S(2)}, u32[]{:S(2)}) %all-to-all-start.1) | async-done | bytes 262176 | tf_op jit(solution)/shard_map/all_to_all | solution.py:379
  39.4 4.6 %all-to-all-start = ((bf16[4,64,2048]{2,1,0:T(8,128)(2,1)}), bf16[4,64,2048]{2,1,0:T(8,128)(2,1)S(1)}, u32[]{:S(2)}, u32[]{:S(2)}) async-start(bf16[4,64,2048]{2,1,0:T(8,128)(2,1)} %bitcast.13), calls=%async_computation | async-start | bytes 2097152 | tf_op jit(solution)/shard_map/all_to_all | solution.py:379
  44.0 3.5 %collective-permute-start.1 = (bf16[512,256]{1,0:T(8,128)(2,1)S(1)}, bf16[512,256]{1,0:T(8,128)(2,1)S(1)}, u32[]{:S(2)}, u32[]{:S(2)}) collective-permute-start(bf16[512,256]{1,0:T(8,128)(2,1)S(1)} %bitcast.32), channel_id=1, source_target_pairs={{0,16},{16,32},{32,48},{48,0},{1,17},{17,33},{33,49},{49,1},{2,18}... | collective-permute-start | bytes 786440 | tf_op jit(solution)/shard_map/ppermute | solution.py:424
  47.5 4.6 %collective-permute-start.2 = (bf16[512,256]{1,0:T(8,128)(2,1)S(1)}, bf16[512,256]{1,0:T(8,128)(2,1)S(1)}, u32[]{:S(2)}, u32[]{:S(2)}) collective-permute-start(bf16[512,256]{1,0:T(8,128)(2,1)S(1)} %bitcast.33), channel_id=1, source_target_pairs={{0,32},{16,48},{32,0},{48,16},{1,33},{17,49},{33,1},{49,17},{2,34}... | collective-permute-start | bytes 786440 | tf_op jit(solution)/shard_map/ppermute | solution.py:424
  52.2 0.0 copy-done.9
  52.2 3.3 %collective-permute-start.3 = (bf16[512,256]{1,0:T(8,128)(2,1)S(1)}, bf16[512,256]{1,0:T(8,128)(2,1)}, u32[]{:S(2)}, u32[]{:S(2)}) collective-permute-start(bf16[512,256]{1,0:T(8,128)(2,1)S(1)} %bitcast.34), channel_id=1, source_target_pairs={{0,48},{16,0},{32,16},{48,32},{1,49},{17,1},{33,17},{49,33},{2,50}... | collective-permute-start | bytes 786440 | tf_op jit(solution)/shard_map/ppermute | solution.py:424
  55.5 0.0 all-to-all-done.own_ref.rest_0_.rest_2_
  55.5 0.0 collective-permute-done.1.u1
  55.5 0.0 copy-start.10
  55.5 1.8 collective-permute-done.2.u2
  57.4 0.0 copy-done.10
  57.4 0.7 copy-done.11
  58.1 2.5 collective-permute-done.3.u3
  60.5 1.9 collective-permute-start.4
  62.5 2.6 collective-permute-done.4.oth_ref.rest_1_.rest_3_
  65.1 0.0 copy-done.1
  65.1 0.0 copy-done.7
  65.1 4.4 %shard_map.103 = (f32[512,224]{1,0:T(8,128)S(1)}, f32[512,224]{1,0:T(8,128)S(1)}, bf16[8,208,128]{2,1,0:T(8,128)(2,1)S(1)}) custom-call(s32[5]{0:T(128)S(1)} %stack.23.place, bf16[2048,224]{1,0:T(8,128)(2,1)} %copy-done, bf16[512,256]{1,0:T(8,128)(2,1)} %bitcast.35, bf16[512,256]{1,0:T(8,128)(2,1)} %copy-done.10, bf16[512,256]{1,0:T(8,128)(2,1)} %copy-done.11, ...), custom_call_target="tpu_custom_call" | custom-call | tf_op jit(solution)/shard_map/pallas_call | solution.py:44
  69.5 13.3 %all_to_all.60.i_ref = bf16[8,208,128]{2,1,0:T(8,128)(2,1)S(1)} all-to-all(bf16[8,208,128]{2,1,0:T(8,128)(2,1)S(1)} %get-tuple-element.37), channel_id=1, replica_groups=mesh['zl'=8,'x'=4,'y'=4,'zh'=2,'c'=2] {'c','y'}, dimensions={0} | all-to-all | bytes 851968 | tf_op jit(solution)/shard_map/all_to_all | solution.py:379
  82.8 0.1 shard_map.104.mine_ref
  82.9 9.3 %collective-permute-start.5 = (f32[136,128]{1,0:T(8,128)S(1)}, f32[136,128]{1,0:T(8,128)S(1)}, u32[]{:S(2)}, u32[]{:S(2)}) collective-permute-start(f32[136,128]{1,0:T(8,128)S(1)} %shard_map.104.mine_ref), channel_id=1, source_target_pairs={{0,2},{2,0},{1,3},{3,1},{4,6},{6,4},{5,7},{7,5},{8,10},{10,8},{9,1... | collective-permute-start | bytes 208904 | tf_op jit(solution)/shard_map/ppermute | solution.py:375
  92.2 0.1 copy.12.tag_ref
  92.3 5.5 %collective-permute-done.5.their_ref = f32[136,128]{1,0:T(8,128)S(1)} collective-permute-done((f32[136,128]{1,0:T(8,128)S(1)}, f32[136,128]{1,0:T(8,128)S(1)}, u32[]{:S(2)}, u32[]{:S(2)}) %collective-permute-start.5) | collective-permute-done | bytes 69664 | tf_op jit(solution)/shard_map/ppermute | solution.py:375
  97.8 0.6 shard_map.105
  98.4 8.8 %all_to_all.61.m_ref = bf16[8,80,128]{2,1,0:T(8,128)(2,1)S(1)} all-to-all(bf16[8,80,128]{2,1,0:T(8,128)(2,1)S(1)} %get-tuple-element.39), channel_id=1, replica_groups=mesh['zl'=8,'x'=4,'y'=4,'zh'=2,'c'=2] {'c','y'}, dimensions={0} | all-to-all | bytes 327680 | tf_op jit(solution)/shard_map/all_to_all | solution.py:379
  107.1 1.9 shard_map.106
  109.0 17.7 %all_to_all.62.i_ref = bf16[4,8,112,128]{3,2,1,0:T(8,128)(2,1)S(1)} all-to-all(bf16[4,8,112,128]{3,2,1,0:T(8,128)(2,1)S(1)} %shard_map.106), channel_id=1, replica_groups=mesh['zl'=8,'x'=4,'y'=4,'zh'=2,'c'=2] {'x'}, dimensions={0} | all-to-all | bytes 1835008 | tf_op jit(solution)/shard_map/all_to_all | solution.py:379
  126.7 0.1 shard_map.107
  126.9 32.1 %all_to_all.63.i_ref = bf16[8,112,128]{2,1,0:T(8,128)(2,1)S(1)} all-to-all(bf16[8,112,128]{2,1,0:T(8,128)(2,1)S(1)} %shard_map.107), channel_id=1, replica_groups=mesh['zl'=8,'x'=4,'y'=4,'zh'=2,'c'=2] {'zl'}, dimensions={0} | all-to-all | bytes 458752 | tf_op jit(solution)/shard_map/all_to_all | solution.py:379
  159.0 0.2 shard_map.108
  159.2 20.5 %all_to_all.64 = bf16[8,64,256]{2,1,0:T(8,128)(2,1)S(1)} all-to-all(bf16[8,64,256]{2,1,0:T(8,128)(2,1)S(1)} %get-tuple-element.42), channel_id=1, replica_groups=mesh['zl'=8,'x'=4,'y'=4,'zh'=2,'c'=2] {'zl'}, dimensions={0} | all-to-all | bytes 524288 | tf_op jit(solution)/shard_map/all_to_all | solution.py:379
  179.8 0.1 broadcast_in_dim.12
  179.8 13.3 %all_to_all.65 = bf16[4,512,256]{2,1,0:T(8,128)(2,1)S(1)} all-to-all(bf16[4,512,256]{2,1,0:T(8,128)(2,1)S(1)} %broadcast_in_dim.12), channel_id=1, replica_groups=mesh['zl'=8,'x'=4,'y'=4,'zh'=2,'c'=2] {'x'}, dimensions={0} | all-to-all | bytes 2097152 | tf_op jit(solution)/shard_map/all_to_all | solution.py:379
  193.1 2.3 shard_map.109
  195.4 8.3 %all_to_all.66.i_ref = bf16[8,80,128]{2,1,0:T(8,128)(2,1)S(1)} all-to-all(bf16[8,80,128]{2,1,0:T(8,128)(2,1)S(1)} %get-tuple-element.43), channel_id=1, replica_groups=mesh['zl'=8,'x'=4,'y'=4,'zh'=2,'c'=2] {'c','y'}, dimensions={0} | all-to-all | bytes 327680 | tf_op jit(solution)/shard_map/all_to_all | solution.py:379
  203.7 7.0 %collective-permute-start.6 = (f32[72,128]{1,0:T(8,128)S(1)}, f32[72,128]{1,0:T(8,128)S(1)}, u32[]{:S(2)}, u32[]{:S(2)}) collective-permute-start(f32[72,128]{1,0:T(8,128)S(1)} %shard_map.110.mine_ref), channel_id=1, source_target_pairs={{0,2},{2,0},{1,3},{3,1},{4,6},{6,4},{5,7},{7,5},{8,10},{10,8},{9,1... | collective-permute-start | bytes 110600 | tf_op jit(solution)/shard_map/ppermute | solution.py:375
  210.8 7.5 %collective-permute-done.6.their_ref = f32[72,128]{1,0:T(8,128)S(1)} collective-permute-done((f32[72,128]{1,0:T(8,128)S(1)}, f32[72,128]{1,0:T(8,128)S(1)}, u32[]{:S(2)}, u32[]{:S(2)}) %collective-permute-start.6) | collective-permute-done | bytes 36896 | tf_op jit(solution)/shard_map/ppermute | solution.py:375
  218.3 0.6 shard_map.111
  218.9 9.4 %all_to_all.67.m_ref = bf16[8,80,128]{2,1,0:T(8,128)(2,1)S(1)} all-to-all(bf16[8,80,128]{2,1,0:T(8,128)(2,1)S(1)} %get-tuple-element.45), channel_id=1, replica_groups=mesh['zl'=8,'x'=4,'y'=4,'zh'=2,'c'=2] {'c','y'}, dimensions={0} | all-to-all | bytes 327680 | tf_op jit(solution)/shard_map/all_to_all | solution.py:379
  228.3 1.9 shard_map.112
  230.2 16.7 %all_to_all.68.i_ref = bf16[4,8,112,128]{3,2,1,0:T(8,128)(2,1)S(1)} all-to-all(bf16[4,8,112,128]{3,2,1,0:T(8,128)(2,1)S(1)} %shard_map.112), channel_id=1, replica_groups=mesh['zl'=8,'x'=4,'y'=4,'zh'=2,'c'=2] {'x'}, dimensions={0} | all-to-all | bytes 1835008 | tf_op jit(solution)/shard_map/all_to_all | solution.py:379
  246.9 0.1 shard_map.113
  247.0 0.0 copy-start.4
  247.1 23.7 %all_to_all.69.i_ref = bf16[8,112,128]{2,1,0:T(8,128)(2,1)S(1)} all-to-all(bf16[8,112,128]{2,1,0:T(8,128)(2,1)S(1)} %shard_map.113), channel_id=1, replica_groups=mesh['zl'=8,'x'=4,'y'=4,'zh'=2,'c'=2] {'zl'}, dimensions={0} | all-to-all | bytes 458752 | tf_op jit(solution)/shard_map/all_to_all | solution.py:379
  270.7 0.0 copy-done.4
  270.7 0.7 shard_map.114
  (12 shorter events, 0.1 us)
Async XLA Ops:
  0.0 24.6 %copy-start.2 = (bf16[2048,224]{0,1:T(8,128)(2,1)S(1)}, bf16[2048,224]{0,1:T(8,128)(2,1)}, u32[]{:S(2)}) copy-start(bf16[2048,224]{0,1:T(8,128)(2,1)} %param.14) | copy-start | bytes 2752516
  0.0 0.9 copy-start.3
  1.8 37.6 %all-to-all-start.1 = ((bf16[8,64,256]{2,1,0:T(8,128)(2,1)}), bf16[8,64,256]{2,1,0:T(8,128)(2,1)S(1)}, u32[]{:S(2)}, u32[]{:S(2)}) async-start(bf16[8,64,256]{2,1,0:T(8,128)(2,1)} %shard_map.102), calls=%async_computation.1 | async-start | bytes 524288 | tf_op jit(solution)/shard_map/all_to_all | solution.py:379
  14.4 16.5 %collective-permute-start = (bf16[32,2048]{1,0:T(8,128)(2,1)}, bf16[32,2048]{1,0:T(8,128)(2,1)S(1)}, u32[]{:S(2)}, u32[]{:S(2)}) collective-permute-start(bf16[32,2048]{1,0:T(8,128)(2,1)} %bitcast.23), channel_id=1, source_target_pairs={{0,2},{2,0},{1,3},{3,1},{4,6},{6,4},{5,7},{7,5},{8,10},{10,8},{9,1... | collective-permute-start | bytes 393224 | tf_op jit(solution)/shard_map/ppermute | solution.py:375
  24.6 0.9 copy-start.5
  25.6 5.4 %copy-start.6 = (bf16[1,32,2048]{2,1,0:T(8,128)(2,1)S(1)}, bf16[1,32,2048]{2,1,0:T(8,128)(2,1)}, u32[]{:S(2)}) copy-start(bf16[1,32,2048]{2,1,0:T(8,128)(2,1)} %param.10) | copy-start | bytes 393220
  26.0 1.0 copy-start
  30.9 0.7 copy-start.8
  39.4 12.8 %copy-start.9 = (bf16[8,64,256]{2,1,0:T(8,128)(2,1)}, bf16[8,64,256]{2,1,0:T(8,128)(2,1)S(1)}, u32[]{:S(2)}) copy-start(bf16[8,64,256]{2,1,0:T(8,128)(2,1)S(1)} %all-to-all-done.1) | copy-start | bytes 786436
  39.4 25.7 %copy-start.1 = (bf16[224,128]{1,0:T(8,128)(2,1)S(1)}, bf16[224,128]{1,0:T(8,128)(2,1)}, u32[]{:S(2)}) copy-start(bf16[224,128]{1,0:T(8,128)(2,1)} %rest_5_.1) | copy-start | bytes 172036
  39.4 16.1 %all-to-all-start = ((bf16[4,64,2048]{2,1,0:T(8,128)(2,1)}), bf16[4,64,2048]{2,1,0:T(8,128)(2,1)S(1)}, u32[]{:S(2)}, u32[]{:S(2)}) async-start(bf16[4,64,2048]{2,1,0:T(8,128)(2,1)} %bitcast.13), calls=%async_computation | async-start | bytes 2097152 | tf_op jit(solution)/shard_map/all_to_all | solution.py:379
  44.0 21.1 %copy-start.7 = (f32[224]{0:T(256)S(1)}, f32[224]{0:T(256)}, u32[]{:S(2)}) copy-start(f32[224]{0:T(256)} %param.15) | copy-start | bytes 2692
  44.0 11.5 %collective-permute-start.1 = (bf16[512,256]{1,0:T(8,128)(2,1)S(1)}, bf16[512,256]{1,0:T(8,128)(2,1)S(1)}, u32[]{:S(2)}, u32[]{:S(2)}) collective-permute-start(bf16[512,256]{1,0:T(8,128)(2,1)S(1)} %bitcast.32), channel_id=1, source_target_pairs={{0,16},{16,32},{32,48},{48,0},{1,17},{17,33},{33,49},{49,1},{2,18}... | collective-permute-start | bytes 786440 | tf_op jit(solution)/shard_map/ppermute | solution.py:424
  47.5 9.9 %collective-permute-start.2 = (bf16[512,256]{1,0:T(8,128)(2,1)S(1)}, bf16[512,256]{1,0:T(8,128)(2,1)S(1)}, u32[]{:S(2)}, u32[]{:S(2)}) collective-permute-start(bf16[512,256]{1,0:T(8,128)(2,1)S(1)} %bitcast.33), channel_id=1, source_target_pairs={{0,32},{16,48},{32,0},{48,16},{1,33},{17,49},{33,1},{49,17},{2,34}... | collective-permute-start | bytes 786440 | tf_op jit(solution)/shard_map/ppermute | solution.py:424
  52.2 8.4 %collective-permute-start.3 = (bf16[512,256]{1,0:T(8,128)(2,1)S(1)}, bf16[512,256]{1,0:T(8,128)(2,1)}, u32[]{:S(2)}, u32[]{:S(2)}) collective-permute-start(bf16[512,256]{1,0:T(8,128)(2,1)S(1)} %bitcast.34), channel_id=1, source_target_pairs={{0,48},{16,0},{32,16},{48,32},{1,49},{17,1},{33,17},{49,33},{2,50}... | collective-permute-start | bytes 786440 | tf_op jit(solution)/shard_map/ppermute | solution.py:424
  55.5 1.8 copy-start.10
  57.4 0.7 copy-start.11
  60.5 4.5 %collective-permute-start.4 = (bf16[4,64,2048]{2,1,0:T(8,128)(2,1)S(1)}, bf16[4,64,2048]{2,1,0:T(8,128)(2,1)S(1)}, u32[]{:S(2)}, u32[]{:S(2)}) collective-permute-start(bf16[4,64,2048]{2,1,0:T(8,128)(2,1)S(1)} %all-to-all-done.own_ref.rest_0_.rest_2_), channel_id=1, source_target_pairs={{0,1},{1,0},{2,3},{3,2},{4,5},{5,4},{6,7},{7,6},{8,9},{9,8},{10,11... | collective-permute-start | bytes 3145736 | tf_op jit(solution)/shard_map/ppermute | solution.py:375
  82.9 14.9 %collective-permute-start.5 = (f32[136,128]{1,0:T(8,128)S(1)}, f32[136,128]{1,0:T(8,128)S(1)}, u32[]{:S(2)}, u32[]{:S(2)}) collective-permute-start(f32[136,128]{1,0:T(8,128)S(1)} %shard_map.104.mine_ref), channel_id=1, source_target_pairs={{0,2},{2,0},{1,3},{3,1},{4,6},{6,4},{5,7},{7,5},{8,10},{10,8},{9,1... | collective-permute-start | bytes 208904 | tf_op jit(solution)/shard_map/ppermute | solution.py:375
  203.7 14.6 %collective-permute-start.6 = (f32[72,128]{1,0:T(8,128)S(1)}, f32[72,128]{1,0:T(8,128)S(1)}, u32[]{:S(2)}, u32[]{:S(2)}) collective-permute-start(f32[72,128]{1,0:T(8,128)S(1)} %shard_map.110.mine_ref), channel_id=1, source_target_pairs={{0,2},{2,0},{1,3},{3,1},{4,6},{6,4},{5,7},{7,5},{8,10},{10,8},{9,1... | collective-permute-start | bytes 110600 | tf_op jit(solution)/shard_map/ppermute | solution.py:375
  247.0 23.7 %copy-start.4 = (f32[64,224]{1,0:T(8,128)S(1)}, f32[64,224]{1,0:T(8,128)}, u32[]{:S(2)}) copy-start(f32[64,224]{1,0:T(8,128)} %d_ref.3) | copy-start | bytes 172036

commit v9 on v8

--- a/solution.py
+++ b/solution.py
@@ -18,6 +18,7 @@
 NORM_EPS = 1e-06
 MEAN_EPS = 1e-06
 ZL, X, Y, ZH, C = 8, 4, 4, 2, 2
+ZA, ZB = 2, 4
 ROWS = HQ * HD
 COLS = 224
 WIDE = 256
@@ -26,6 +27,7 @@
 PACK = 112
 BF = jnp.bfloat16
 F32 = jnp.float32
+ZAXES = ("za", "zb")
 CONTRACT0 = (((0,), (0,)), ((), ()))
 CONTRACT1 = (((1,), (1,)), ((), ()))
 
@@ -129,9 +131,14 @@
 
 
 def direction_kernel(d_ref, o_ref):
-    load = row_block(d_ref[...])
-    for i in range(ZL):
-        o_ref[i] = load
+    o_ref[...] = row_block(d_ref[...])
+
+
+def pair_kernel(place, mine_ref, their_ref, o_ref):
+    za = place[5]
+    for i in range(ZB):
+        o_ref[i, za] = mine_ref[...]
+        o_ref[i, 1 - za] = their_ref[...]
 
 
 def sum_x_kernel(i_ref, o_ref):
@@ -223,7 +230,10 @@
         span = pl.ds(r * 512, 512)
         copies.append(pltpu.make_async_copy(proj_far.at[span], proj_ref.at[span], sems.at[r]))
     for r, u in enumerate((u0, u1, u2, u3)):
-        copies.append(pltpu.make_async_copy(u, rows_ref.at[r], sems.at[X + r]))
+        for za in range(ZA):
+            copies.append(
+                pltpu.make_async_copy(u.at[:, za], rows_ref.at[r, za], sems.at[X + ZA * r + za])
+            )
     for copy in copies:
         copy.start()
     gain = gain_ref[...]
@@ -246,12 +256,14 @@
     hds = [jnp.zeros((256, WIDE), F32)] * 2
     norm = 0.0
     for r in range(X):
-        copies[X + r].wait()
+        copies[X + ZA * r].wait()
+        copies[X + ZA * r + 1].wait()
+        rows = rows_ref[r].reshape(512, WIDE)
         x = lax.rem(place[4] + X - r, X)
         span = pl.ds(pl.multiple_of(x * 512, 512), 512)
-        norm += square_of(rows_ref[r])
+        norm += square_of(rows)
         for i, (_, _, a_ref) in enumerate(halves):
-            hds[i] += dot(a_ref[:, :, span].reshape(256, 512), rows_ref[r])
+            hds[i] += dot(a_ref[:, :, span].reshape(256, 512), rows)
     for h, hd, (c, at, _) in zip(hs, hds, halves):
         hd = hd[:, :COLS]
         hd_ref[pl.ds(at, 256), :] = hd
@@ -389,22 +401,23 @@
     zhpos = lax.axis_index("zh")
     own_at = ((ypos * ZH + zhpos) * C + core) * 32
     oth_at = ((ypos * ZH + 1 - zhpos) * C + core) * 32
-    place = jnp.stack([core, own_at, oth_at, zhpos, lax.axis_index("x")]).astype(jnp.int32)
+    place = jnp.stack([core, own_at, oth_at, zhpos, lax.axis_index("x"), lax.axis_index("za")]).astype(jnp.int32)
     own_tags = tags[0].reshape(Y, ZH, C, 32).transpose(2, 0, 1, 3).reshape(C * Y, 64)[core * Y + ypos]
     own_tags = own_tags[:, None]
     gain = norm_gain[None]
 
-    by_zl = deal(call(direction_kernel, shape(ZL, 64, WIDE, dtype=BF), direction), "zl")
-    by_zl = by_zl.reshape(ZL * 64, WIDE)
+    row = call(direction_kernel, shape(64, WIDE, dtype=BF), direction)
     proj, toks = call(
         turn_kernel,
         (shape(ROWS, COLS, dtype=BF), shape(C, 256, COLS, dtype=BF)),
         out_proj.T,
         stream[0].T,
     )
-    theirs, proj, toks, own_tags = lax.optimization_barrier(
-        (swap(queries[0], "zh"), proj, toks, own_tags)
-    )
+    theirs, far, proj, toks, own_tags = lax.optimization_barrier(
+        (swap(queries[0], "zh"), swap(row, "za"), proj, toks, own_tags)
+    )
+    pairs = call(pair_kernel, shape(ZB, ZA, 64, WIDE, dtype=BF), place, row, far, smem=1)
+    by_zl = deal(pairs, "zb")
     pair = call(
         functools.partial(
             attend_kernel,
@@ -439,7 +452,7 @@
             smem=1,
         )
         part = call(sum_x_kernel, shape(ZL, PACK, 128, dtype=BF), deal(sent, "x"))
-        return deal(part, "zl")
+        return deal(part, ZAXES)
 
     def token_sum(load, rows, kernel, outs, *args):
         part = call(sum_parts_kernel, shape(rows, 128), deal(load, ("c", "y")))
@@ -450,8 +463,8 @@
             first_kernel,
             scratch=[
                 pltpu.VMEM((ROWS, COLS), BF),
-                pltpu.VMEM((X, ZL * 64, WIDE), BF),
-                pltpu.SemaphoreType.DMA((2 * X,)),
+                pltpu.VMEM((X, ZA, ZB, 64, WIDE), BF),
+                pltpu.SemaphoreType.DMA((3 * X,)),
             ],
         ),
         (shape(512, COLS), shape(512, COLS), shape(8, 208, 128, dtype=BF)),
@@ -472,7 +485,7 @@
         (shape(64, COLS), shape(ZL, 64, WIDE, dtype=BF)),
         product(False, deal(mixed, ("c", "y")), h_loc, hdot0),
     )
-    full0 = spread(deal(sent, "zl").reshape(ZL * 64, WIDE), "x", X).reshape(ROWS, WIDE)
+    full0 = spread(deal(sent, ZAXES).reshape(ZL * 64, WIDE), "x", X).reshape(ROWS, WIDE)
     moved, load = call(
         moved_kernel,
         (shape(512, COLS), shape(8, 80, 128, dtype=BF)),
@@ -493,8 +506,8 @@
 
 
 def solution(mesh):
-    fine = Mesh(mesh.devices.reshape(ZL, X, Y, ZH, C), ("zl", "x", "y", "zh", "c"))
-    dp, mp = ("zl", "x"), ("y", "zh", "c")
+    fine = Mesh(mesh.devices.reshape(ZA, ZB, X, Y, ZH, C), ("za", "zb", "x", "y", "zh", "c"))
+    dp, mp = ("za", "zb", "x"), ("y", "zh", "c")
     return jax.shard_map(
         local,
         mesh=fine,

time: 272 us -> 271 us (level)
  blocking collectives: 164 us -> 156 us
  waiting for transfers between devices: 27.2 us -> 33.3 us
    all_to_all x10, blocking collectives: 164 us -> 156 us  [deal(): return lax.all_to_all(x, axis, 0, 0, tiled=True)]
    all_to_all x2, starting transfers between devices: 17.2 us -> 10.2 us  [deal(): return lax.all_to_all(x, axis, 0, 0, tiled=True)]
    ppermute x4 -> x5, starting transfers between devices: 26.4 us -> 31.9 us  [swap(): return lax.ppermute(x, axis, [(0, 1), (1, 0)])]
    ppermute x4 -> x5, waiting for transfers between devices: 19.5 us -> 25 us  [swap(): return lax.ppermute(x, axis, [(0, 1), (1, 0)])]
    unnamed x25 -> x27, local copies, waits for them, and re-layouts: 4.76 us -> 6.02 us
    pallas_call x15 -> x16, Pallas kernels: 18.7 us -> 19.3 us  [call(): pl.pallas_call(kernel, out_shape=out_shape, in_specs=specs, out_specs=[vm...]
  transfers between devices with their start and end apart: 9 -> 10, of which waited for: 7 -> 8; matrix products, arithmetic and copies ran while one was open for 1% -> 1% of each run, Pallas kernels for 2% -> 2%
where the time goes in v9:
time: 271 us; the launch traced here: 269 us
  blocking collectives  156 us (58%)
  starting transfers between devices  53.6 us (20%)
  waiting for transfers between devices  33.3 us (12%)
  Pallas kernels  19.3 us (7%)
  local copies, waits for them, and re-layouts  6.45 us (2%)
    all_to_all x10, blocking collectives, deal(): return lax.all_to_all(x, axis, 0, 0, tiled=True)  156 us
    ppermute x5, starting transfers between devices, swap(): return lax.ppermute(x, axis, [(0, 1), (1, 0)])  31.9 us
    ppermute x5, waiting for transfers between devices, swap(): return lax.ppermute(x, axis, [(0, 1), (1, 0)])  25 us
    pallas_call x16, Pallas kernels, call(): pl.pallas_call(kernel, out_shape=out_shape, in_specs=specs, out_specs=[vm...  19.3 us
    ppermute x3, starting transfers between devices, local(): lax.ppermute(by_zl, 'x', [(i, (i + r) % X) for i in range(X)])  11.5 us
    all_to_all x2, starting transfers between devices, deal(): return lax.all_to_all(x, axis, 0, 0, tiled=True)  10.2 us
    unnamed x27, local copies, waits for them, and re-layouts  6.02 us
  transfers between devices with their start and end apart: 10, of which 8 were waited for; matrix products, arithmetic and copies ran while one was open for 1% of the time, Pallas kernels for 2%

profile of v9, /device:TPU:32, one launch (start us, length us, event | category | flops | bytes accessed | tf_op | source)
XLA Modules:
  0.0 269.5 jit_solution(18143664191567422207)
XLA Ops:
  0.0 14.8 %collective-permute-start = (bf16[32,2048]{1,0:T(8,128)(2,1)}, bf16[32,2048]{1,0:T(8,128)(2,1)S(1)}, u32[]{:S(2)}, u32[]{:S(2)}) collective-permute-start(bf16[32,2048]{1,0:T(8,128)(2,1)} %bitcast.23), channel_id=1, source_target_pairs={{0,2},{2,0},{1,3},{3,1},{4,6},{6,4},{5,7},{7,5},{8,10},{10,8},{9,1... | collective-permute-start | bytes 393224 | tf_op jit(solution)/shard_map/ppermute | solution.py:387
  14.8 0.0 copy-start.3
  14.8 0.8 copy-done.3
  15.7 0.2 shard_map.100.mine_ref
  15.8 4.3 %collective-permute-start.1 = (bf16[64,256]{1,0:T(8,128)(2,1)S(1)}, bf16[64,256]{1,0:T(8,128)(2,1)S(1)}, u32[]{:S(2)}, u32[]{:S(2)}) collective-permute-start(bf16[64,256]{1,0:T(8,128)(2,1)S(1)} %shard_map.100.mine_ref), channel_id=1, source_target_pairs={{0,256},{256,0},{1,257},{257,1},{2,258},{258,2},{3,259},{259,3},{4... | collective-permute-start | bytes 98312 | tf_op jit(solution)/shard_map/ppermute | solution.py:387
  20.1 0.0 copy-start.12
  20.1 0.6 broadcast.3
  20.7 0.1 copy-done.12
  20.8 0.7 reduce.3
  21.5 0.1 reshape_squeeze.3
  21.6 0.1 reshape.10
  21.7 1.2 copy-done.2
  22.9 0.9 copy-done.5
  23.8 0.4 shard_map.101
  24.2 1.0 copy-done
  25.3 0.1 stack.27.place
  25.3 3.9 %collective-permute-done.1.their_ref = bf16[64,256]{1,0:T(8,128)(2,1)S(1)} collective-permute-done((bf16[64,256]{1,0:T(8,128)(2,1)S(1)}, bf16[64,256]{1,0:T(8,128)(2,1)S(1)}, u32[]{:S(2)}, u32[]{:S(2)}) %collective-permute-start.1) | collective-permute-done | bytes 32800 | tf_op jit(solution)/shard_map/ppermute | solution.py:387
  29.2 0.0 collective-permute-done.oth_ref
  29.2 1.3 shard_map.103
  30.5 5.6 %all-to-all-start.1 = ((bf16[4,2,64,256]{3,2,1,0:T(8,128)(2,1)}), bf16[4,2,64,256]{3,2,1,0:T(8,128)(2,1)S(1)}, u32[]{:S(2)}, u32[]{:S(2)}) async-start(bf16[4,2,64,256]{3,2,1,0:T(8,128)(2,1)} %shard_map.103), calls=%async_computation.1 | async-start | bytes 524288 | tf_op jit(solution)/shard_map/all_to_all | solution.py:391
  36.0 0.0 copy-done.6
  36.0 0.7 copy-done.8
  36.7 4.4 %shard_map.102 = bf16[4,2,32,2048]{3,2,1,0:T(8,128)(2,1)} custom-call(s32[6]{0:T(128)S(1)} %stack.27.place, s32[1,4]{1,0:T(1,128)S(1)} %copy-done.8, bf16[512,1024]{1,0:T(8,128)(2,1)} %bitcast.30, bf16[512,1024]{1,0:T(8,128)(2,1)} %bitcast.31, bf16[32,2048]{1,0:T(8,128)(2,1)S(1)} %bitcast.24, bf16[32,2048]{1,0:T(8,128)(2,1)S(1)} %collective-permute-done.oth_ref), custom_call_target="tpu_custom_call" | custom-call | tf_op jit(solution)/shard_map/pallas_call | solution.py:46
  41.1 2.3 all-to-all-done.1.u0
  43.4 4.6 %all-to-all-start = ((bf16[4,64,2048]{2,1,0:T(8,128)(2,1)}), bf16[4,64,2048]{2,1,0:T(8,128)(2,1)S(1)}, u32[]{:S(2)}, u32[]{:S(2)}) async-start(bf16[4,64,2048]{2,1,0:T(8,128)(2,1)} %bitcast.14), calls=%async_computation | async-start | bytes 2097152 | tf_op jit(solution)/shard_map/all_to_all | solution.py:391
  48.0 3.5 %collective-permute-start.2 = (bf16[4,2,64,256]{3,2,1,0:T(8,128)(2,1)S(1)}, bf16[4,2,64,256]{3,2,1,0:T(8,128)(2,1)S(1)}, u32[]{:S(2)}, u32[]{:S(2)}) collective-permute-start(bf16[4,2,64,256]{3,2,1,0:T(8,128)(2,1)S(1)} %all-to-all-done.1.u0), channel_id=1, source_target_pairs={{0,16},{16,32},{32,48},{48,0},{1,17},{17,33},{33,49},{49,1},{2,18}... | collective-permute-start | bytes 786440 | tf_op jit(solution)/shard_map/ppermute | solution.py:437
  51.5 4.6 %collective-permute-start.3 = (bf16[4,2,64,256]{3,2,1,0:T(8,128)(2,1)S(1)}, bf16[4,2,64,256]{3,2,1,0:T(8,128)(2,1)S(1)}, u32[]{:S(2)}, u32[]{:S(2)}) collective-permute-start(bf16[4,2,64,256]{3,2,1,0:T(8,128)(2,1)S(1)} %all-to-all-done.1.u0), channel_id=1, source_target_pairs={{0,32},{16,48},{32,0},{48,16},{1,33},{17,49},{33,1},{49,17},{2,34}... | collective-permute-start | bytes 786440 | tf_op jit(solution)/shard_map/ppermute | solution.py:437
  56.2 3.3 %collective-permute-start.4 = (bf16[4,2,64,256]{3,2,1,0:T(8,128)(2,1)S(1)}, bf16[4,2,64,256]{3,2,1,0:T(8,128)(2,1)}, u32[]{:S(2)}, u32[]{:S(2)}) collective-permute-start(bf16[4,2,64,256]{3,2,1,0:T(8,128)(2,1)S(1)} %all-to-all-done.1.u0), channel_id=1, source_target_pairs={{0,48},{16,0},{32,16},{48,32},{1,49},{17,1},{33,17},{49,33},{2,50}... | collective-permute-start | bytes 786440 | tf_op jit(solution)/shard_map/ppermute | solution.py:437
  59.5 2.6 all-to-all-done.own_ref.rest_0_.rest_2_
  62.1 0.0 collective-permute-done.2.u1
  62.1 2.5 collective-permute-done.3.u2
  64.6 0.7 copy-done.11
  65.4 0.9 collective-permute-done.4.u3
  66.3 1.9 collective-permute-start.5
  68.2 2.6 collective-permute-done.5.oth_ref.rest_1_.rest_3_
  70.8 0.0 copy-done.1
  70.8 4.5 %shard_map.104 = (f32[512,224]{1,0:T(8,128)S(1)}, f32[512,224]{1,0:T(8,128)S(1)}, bf16[8,208,128]{2,1,0:T(8,128)(2,1)S(1)}) custom-call(s32[6]{0:T(128)S(1)} %stack.27.place, bf16[2048,224]{1,0:T(8,128)(2,1)} %copy-done, bf16[4,2,64,256]{3,2,1,0:T(8,128)(2,1)} %copy-done.9, bf16[4,2,64,256]{3,2,1,0:T(8,128)(2,1)} %copy-done.10, ...), custom_call_target="tpu_custom_call" | custom-call | tf_op jit(solution)/shard_map/pallas_call | solution.py:46
  75.3 13.1 %all_to_all.60.i_ref = bf16[8,208,128]{2,1,0:T(8,128)(2,1)S(1)} all-to-all(bf16[8,208,128]{2,1,0:T(8,128)(2,1)S(1)} %get-tuple-element.39), channel_id=1, replica_groups=mesh['za'=2,'zb'=4,'x'=4,'y'=4,'zh'=2,'c'=2] {'c','y'}, dimensions={0} | all-to-all | bytes 851968 | tf_op jit(solution)/shard_map/all_to_all | solution.py:391
  88.4 0.1 shard_map.105.mine_ref
  88.5 7.0 %collective-permute-start.6 = (f32[136,128]{1,0:T(8,128)S(1)}, f32[136,128]{1,0:T(8,128)S(1)}, u32[]{:S(2)}, u32[]{:S(2)}) collective-permute-start(f32[136,128]{1,0:T(8,128)S(1)} %shard_map.105.mine_ref), channel_id=1, source_target_pairs={{0,2},{2,0},{1,3},{3,1},{4,6},{6,4},{5,7},{7,5},{8,10},{10,8},{9,1... | collective-permute-start | bytes 208904 | tf_op jit(solution)/shard_map/ppermute | solution.py:387
  95.5 0.1 copy.12.tag_ref
  95.6 7.9 %collective-permute-done.6.their_ref = f32[136,128]{1,0:T(8,128)S(1)} collective-permute-done((f32[136,128]{1,0:T(8,128)S(1)}, f32[136,128]{1,0:T(8,128)S(1)}, u32[]{:S(2)}, u32[]{:S(2)}) %collective-permute-start.6) | collective-permute-done | bytes 69664 | tf_op jit(solution)/shard_map/ppermute | solution.py:387
  103.5 0.6 shard_map.106
  104.0 9.4 %all_to_all.61.m_ref = bf16[8,80,128]{2,1,0:T(8,128)(2,1)S(1)} all-to-all(bf16[8,80,128]{2,1,0:T(8,128)(2,1)S(1)} %get-tuple-element.41), channel_id=1, replica_groups=mesh['za'=2,'zb'=4,'x'=4,'y'=4,'zh'=2,'c'=2] {'c','y'}, dimensions={0} | all-to-all | bytes 327680 | tf_op jit(solution)/shard_map/all_to_all | solution.py:391
  113.4 1.9 shard_map.107
  115.3 18.0 %all_to_all.62.i_ref = bf16[4,8,112,128]{3,2,1,0:T(8,128)(2,1)S(1)} all-to-all(bf16[4,8,112,128]{3,2,1,0:T(8,128)(2,1)S(1)} %shard_map.107), channel_id=1, replica_groups=mesh['za'=2,'zb'=4,'x'=4,'y'=4,'zh'=2,'c'=2] {'x'}, dimensions={0} | all-to-all | bytes 1835008 | tf_op jit(solution)/shard_map/all_to_all | solution.py:391
  133.3 0.1 shard_map.108
  133.4 24.1 %all_to_all.63.i_ref = bf16[8,112,128]{2,1,0:T(8,128)(2,1)S(1)} all-to-all(bf16[8,112,128]{2,1,0:T(8,128)(2,1)S(1)} %shard_map.108), channel_id=1, replica_groups=mesh['za'=2,'zb'=4,'x'=4,'y'=4,'zh'=2,'c'=2] {'za','zb'}, dimensions={0} | all-to-all | bytes 458752 | tf_op jit(solution)/shard_map/all_to_all | solution.py:391
  157.5 0.2 shard_map.109
  157.8 20.5 %all_to_all.64 = bf16[8,64,256]{2,1,0:T(8,128)(2,1)S(1)} all-to-all(bf16[8,64,256]{2,1,0:T(8,128)(2,1)S(1)} %get-tuple-element.44), channel_id=1, replica_groups=mesh['za'=2,'zb'=4,'x'=4,'y'=4,'zh'=2,'c'=2] {'za','zb'}, dimensions={0} | all-to-all | bytes 524288 | tf_op jit(solution)/shard_map/all_to_all | solution.py:391
  178.3 0.1 broadcast_in_dim.12
  178.4 13.3 %all_to_all.65 = bf16[4,512,256]{2,1,0:T(8,128)(2,1)S(1)} all-to-all(bf16[4,512,256]{2,1,0:T(8,128)(2,1)S(1)} %broadcast_in_dim.12), channel_id=1, replica_groups=mesh['za'=2,'zb'=4,'x'=4,'y'=4,'zh'=2,'c'=2] {'x'}, dimensions={0} | all-to-all | bytes 2097152 | tf_op jit(solution)/shard_map/all_to_all | solution.py:391
  191.7 2.3 shard_map.110
  194.0 8.3 %all_to_all.66.i_ref = bf16[8,80,128]{2,1,0:T(8,128)(2,1)S(1)} all-to-all(bf16[8,80,128]{2,1,0:T(8,128)(2,1)S(1)} %get-tuple-element.45), channel_id=1, replica_groups=mesh['za'=2,'zb'=4,'x'=4,'y'=4,'zh'=2,'c'=2] {'c','y'}, dimensions={0} | all-to-all | bytes 327680 | tf_op jit(solution)/shard_map/all_to_all | solution.py:391
  202.3 3.9 %collective-permute-start.7 = (f32[72,128]{1,0:T(8,128)S(1)}, f32[72,128]{1,0:T(8,128)S(1)}, u32[]{:S(2)}, u32[]{:S(2)}) collective-permute-start(f32[72,128]{1,0:T(8,128)S(1)} %shard_map.111.mine_ref), channel_id=1, source_target_pairs={{0,2},{2,0},{1,3},{3,1},{4,6},{6,4},{5,7},{7,5},{8,10},{10,8},{9,1... | collective-permute-start | bytes 110600 | tf_op jit(solution)/shard_map/ppermute | solution.py:387
  206.2 10.7 %collective-permute-done.7.their_ref = f32[72,128]{1,0:T(8,128)S(1)} collective-permute-done((f32[72,128]{1,0:T(8,128)S(1)}, f32[72,128]{1,0:T(8,128)S(1)}, u32[]{:S(2)}, u32[]{:S(2)}) %collective-permute-start.7) | collective-permute-done | bytes 36896 | tf_op jit(solution)/shard_map/ppermute | solution.py:387
  216.9 0.6 shard_map.112
  217.5 8.9 %all_to_all.67.m_ref = bf16[8,80,128]{2,1,0:T(8,128)(2,1)S(1)} all-to-all(bf16[8,80,128]{2,1,0:T(8,128)(2,1)S(1)} %get-tuple-element.47), channel_id=1, replica_groups=mesh['za'=2,'zb'=4,'x'=4,'y'=4,'zh'=2,'c'=2] {'c','y'}, dimensions={0} | all-to-all | bytes 327680 | tf_op jit(solution)/shard_map/all_to_all | solution.py:391
  226.3 1.9 shard_map.113
  228.2 16.7 %all_to_all.68.i_ref = bf16[4,8,112,128]{3,2,1,0:T(8,128)(2,1)S(1)} all-to-all(bf16[4,8,112,128]{3,2,1,0:T(8,128)(2,1)S(1)} %shard_map.113), channel_id=1, replica_groups=mesh['za'=2,'zb'=4,'x'=4,'y'=4,'zh'=2,'c'=2] {'x'}, dimensions={0} | all-to-all | bytes 1835008 | tf_op jit(solution)/shard_map/all_to_all | solution.py:391
  244.9 0.1 shard_map.114
  245.1 0.0 copy-start.4
  245.1 23.7 %all_to_all.69.i_ref = bf16[8,112,128]{2,1,0:T(8,128)(2,1)S(1)} all-to-all(bf16[8,112,128]{2,1,0:T(8,128)(2,1)S(1)} %shard_map.114), channel_id=1, replica_groups=mesh['za'=2,'zb'=4,'x'=4,'y'=4,'zh'=2,'c'=2] {'za','zb'}, dimensions={0} | all-to-all | bytes 458752 | tf_op jit(solution)/shard_map/all_to_all | solution.py:391
  268.8 0.7 shard_map.115
  (17 shorter events, 0.1 us)
Async XLA Ops:
  0.0 29.2 %collective-permute-start = (bf16[32,2048]{1,0:T(8,128)(2,1)}, bf16[32,2048]{1,0:T(8,128)(2,1)S(1)}, u32[]{:S(2)}, u32[]{:S(2)}) collective-permute-start(bf16[32,2048]{1,0:T(8,128)(2,1)} %bitcast.23), channel_id=1, source_target_pairs={{0,2},{2,0},{1,3},{3,1},{4,6},{6,4},{5,7},{7,5},{8,10},{10,8},{9,1... | collective-permute-start | bytes 393224 | tf_op jit(solution)/shard_map/ppermute | solution.py:387
  14.8 0.8 copy-start.3
  15.8 13.4 %collective-permute-start.1 = (bf16[64,256]{1,0:T(8,128)(2,1)S(1)}, bf16[64,256]{1,0:T(8,128)(2,1)S(1)}, u32[]{:S(2)}, u32[]{:S(2)}) collective-permute-start(bf16[64,256]{1,0:T(8,128)(2,1)S(1)} %shard_map.100.mine_ref), channel_id=1, source_target_pairs={{0,256},{256,0},{1,257},{257,1},{2,258},{258,2},{3,259},{259,3},{4... | collective-permute-start | bytes 98312 | tf_op jit(solution)/shard_map/ppermute | solution.py:387
  20.1 0.7 copy-start.12
  21.7 1.2 copy-start.2
  22.9 0.9 copy-start.5
  24.2 1.0 copy-start
  30.5 5.6 %copy-start.6 = (bf16[1,32,2048]{2,1,0:T(8,128)(2,1)S(1)}, bf16[1,32,2048]{2,1,0:T(8,128)(2,1)}, u32[]{:S(2)}) copy-start(bf16[1,32,2048]{2,1,0:T(8,128)(2,1)} %param.10) | copy-start | bytes 393220
  30.5 12.9 %all-to-all-start.1 = ((bf16[4,2,64,256]{3,2,1,0:T(8,128)(2,1)}), bf16[4,2,64,256]{3,2,1,0:T(8,128)(2,1)S(1)}, u32[]{:S(2)}, u32[]{:S(2)}) async-start(bf16[4,2,64,256]{3,2,1,0:T(8,128)(2,1)} %shard_map.103), calls=%async_computation.1 | async-start | bytes 524288 | tf_op jit(solution)/shard_map/all_to_all | solution.py:391
  36.0 0.7 copy-start.8
  43.4 12.8 %copy-start.9 = (bf16[4,2,64,256]{3,2,1,0:T(8,128)(2,1)}, bf16[4,2,64,256]{3,2,1,0:T(8,128)(2,1)S(1)}, u32[]{:S(2)}) copy-start(bf16[4,2,64,256]{3,2,1,0:T(8,128)(2,1)S(1)} %all-to-all-done.1.u0) | copy-start | bytes 786436
  43.4 27.4 %copy-start.1 = (bf16[224,128]{1,0:T(8,128)(2,1)S(1)}, bf16[224,128]{1,0:T(8,128)(2,1)}, u32[]{:S(2)}) copy-start(bf16[224,128]{1,0:T(8,128)(2,1)} %rest_5_.1) | copy-start | bytes 172036
  43.4 18.7 %all-to-all-start = ((bf16[4,64,2048]{2,1,0:T(8,128)(2,1)}), bf16[4,64,2048]{2,1,0:T(8,128)(2,1)S(1)}, u32[]{:S(2)}, u32[]{:S(2)}) async-start(bf16[4,64,2048]{2,1,0:T(8,128)(2,1)} %bitcast.14), calls=%async_computation | async-start | bytes 2097152 | tf_op jit(solution)/shard_map/all_to_all | solution.py:391
  48.0 22.8 %copy-start.7 = (f32[224]{0:T(256)S(1)}, f32[224]{0:T(256)}, u32[]{:S(2)}) copy-start(f32[224]{0:T(256)} %param.15) | copy-start | bytes 2692
  48.0 14.1 %collective-permute-start.2 = (bf16[4,2,64,256]{3,2,1,0:T(8,128)(2,1)S(1)}, bf16[4,2,64,256]{3,2,1,0:T(8,128)(2,1)S(1)}, u32[]{:S(2)}, u32[]{:S(2)}) collective-permute-start(bf16[4,2,64,256]{3,2,1,0:T(8,128)(2,1)S(1)} %all-to-all-done.1.u0), channel_id=1, source_target_pairs={{0,16},{16,32},{32,48},{48,0},{1,17},{17,33},{33,49},{49,1},{2,18}... | collective-permute-start | bytes 786440 | tf_op jit(solution)/shard_map/ppermute | solution.py:437
  51.5 13.1 %collective-permute-start.3 = (bf16[4,2,64,256]{3,2,1,0:T(8,128)(2,1)S(1)}, bf16[4,2,64,256]{3,2,1,0:T(8,128)(2,1)S(1)}, u32[]{:S(2)}, u32[]{:S(2)}) collective-permute-start(bf16[4,2,64,256]{3,2,1,0:T(8,128)(2,1)S(1)} %all-to-all-done.1.u0), channel_id=1, source_target_pairs={{0,32},{16,48},{32,0},{48,16},{1,33},{17,49},{33,1},{49,17},{2,34}... | collective-permute-start | bytes 786440 | tf_op jit(solution)/shard_map/ppermute | solution.py:437
  56.2 10.1 %collective-permute-start.4 = (bf16[4,2,64,256]{3,2,1,0:T(8,128)(2,1)S(1)}, bf16[4,2,64,256]{3,2,1,0:T(8,128)(2,1)}, u32[]{:S(2)}, u32[]{:S(2)}) collective-permute-start(bf16[4,2,64,256]{3,2,1,0:T(8,128)(2,1)S(1)} %all-to-all-done.1.u0), channel_id=1, source_target_pairs={{0,48},{16,0},{32,16},{48,32},{1,49},{17,1},{33,17},{49,33},{2,50}... | collective-permute-start | bytes 786440 | tf_op jit(solution)/shard_map/ppermute | solution.py:437
  62.1 2.5 copy-start.10
  64.6 0.7 copy-start.11
  66.3 4.5 %collective-permute-start.5 = (bf16[4,64,2048]{2,1,0:T(8,128)(2,1)S(1)}, bf16[4,64,2048]{2,1,0:T(8,128)(2,1)S(1)}, u32[]{:S(2)}, u32[]{:S(2)}) collective-permute-start(bf16[4,64,2048]{2,1,0:T(8,128)(2,1)S(1)} %all-to-all-done.own_ref.rest_0_.rest_2_), channel_id=1, source_target_pairs={{0,1},{1,0},{2,3},{3,2},{4,5},{5,4},{6,7},{7,6},{8,9},{9,8},{10,11... | collective-permute-start | bytes 3145736 | tf_op jit(solution)/shard_map/ppermute | solution.py:387
  88.5 15.0 %collective-permute-start.6 = (f32[136,128]{1,0:T(8,128)S(1)}, f32[136,128]{1,0:T(8,128)S(1)}, u32[]{:S(2)}, u32[]{:S(2)}) collective-permute-start(f32[136,128]{1,0:T(8,128)S(1)} %shard_map.105.mine_ref), channel_id=1, source_target_pairs={{0,2},{2,0},{1,3},{3,1},{4,6},{6,4},{5,7},{7,5},{8,10},{10,8},{9,1... | collective-permute-start | bytes 208904 | tf_op jit(solution)/shard_map/ppermute | solution.py:387
  202.3 14.6 %collective-permute-start.7 = (f32[72,128]{1,0:T(8,128)S(1)}, f32[72,128]{1,0:T(8,128)S(1)}, u32[]{:S(2)}, u32[]{:S(2)}) collective-permute-start(f32[72,128]{1,0:T(8,128)S(1)} %shard_map.111.mine_ref), channel_id=1, source_target_pairs={{0,2},{2,0},{1,3},{3,1},{4,6},{6,4},{5,7},{7,5},{8,10},{10,8},{9,1... | collective-permute-start | bytes 110600 | tf_op jit(solution)/shard_map/ppermute | solution.py:387
  245.1 23.7 %copy-start.4 = (f32[64,224]{1,0:T(8,128)S(1)}, f32[64,224]{1,0:T(8,128)}, u32[]{:S(2)}) copy-start(f32[64,224]{1,0:T(8,128)} %d_ref.3) | copy-start | bytes 172036

commit v10 on v9

--- a/solution.py
+++ b/solution.py
@@ -280,21 +280,27 @@
         at = pl.multiple_of(c * 256, 256)
         moved = dot(a_ref[...].reshape(256, ROWS), u_ref[...])[:, :COLS]
         mv_ref[pl.ds(at, 256), :] = moved
-        put_scores(load_ref, c * Y, 0, scores_of(moved, gain, tag_ref))
+        z = scores_of(moved, gain, tag_ref)
         sums = (jnp.sum(h_ref[pl.ds(at, 256), :] * moved, -1, keepdims=True),)
-        put_sums(load_ref, c * Y, 64, sums, norm)
-
-
-def sum_parts_kernel(i_ref, o_ref):
+        for zh in range(ZH):
+            put_scores(load_ref, (zh * C + c) * Y, 0, z)
+            put_sums(load_ref, (zh * C + c) * Y, 64, sums, norm)
+
+
+def sum_parts(i_ref):
     total = i_ref[0].astype(F32)
-    for i in range(1, 8):
+    for i in range(1, i_ref.shape[0]):
         total += i_ref[i].astype(F32)
     scores = total[: total.shape[0] - 16]
     if scores.shape[0] == 192:
         scores = jnp.concatenate([scores[0:64] + scores[64:128], scores[128:192]], 0)
     sums = total[total.shape[0] - 16 :]
     joined = [sums[2 * i : 2 * i + 1] + sums[2 * i + 1 : 2 * i + 2] for i in range(8)]
-    o_ref[...] = jnp.concatenate([scores, *joined], 0)
+    return jnp.concatenate([scores, *joined], 0)
+
+
+def sum_parts_kernel(i_ref, o_ref):
+    o_ref[...] = sum_parts(i_ref)
 
 
 def columns_of(rows):
@@ -335,8 +341,8 @@
     )
 
 
-def tokens1_kernel(mine_ref, their_ref, total_ref, tag_ref, o_ref, inv_ref):
-    moved = mine_ref[...] + their_ref[...]
+def tokens1_kernel(i_ref, total_ref, tag_ref, o_ref, inv_ref):
+    moved = sum_parts(i_ref)
     product_sq = moved[65:66, 0:1]
     norm_sq = total_ref[130:131, 0:1]
     sigma = 2.0 * jnp.sqrt((product_sq / COUNT + MEAN_EPS) / (norm_sq / COUNT + MEAN_EPS))
@@ -454,10 +460,6 @@
         part = call(sum_x_kernel, shape(ZL, PACK, 128, dtype=BF), deal(sent, "x"))
         return deal(part, ZAXES)
 
-    def token_sum(load, rows, kernel, outs, *args):
-        part = call(sum_parts_kernel, shape(rows, 128), deal(load, ("c", "y")))
-        return call(kernel, outs, part, swap(part, "zh"), *args, own_tags)
-
     h_loc, hdot0, load = call(
         functools.partial(
             first_kernel,
@@ -479,7 +481,14 @@
         smem=1,
         far=X + 1,
     )
-    total, mixed = token_sum(load, 136, tokens0_kernel, (shape(136, 128), shape(8, 80, 128, dtype=BF)))
+    part = call(sum_parts_kernel, shape(136, 128), deal(load, ("c", "y")))
+    total, mixed = call(
+        tokens0_kernel,
+        (shape(136, 128), shape(8, 80, 128, dtype=BF)),
+        part,
+        swap(part, "zh"),
+        own_tags,
+    )
     rows0, sent = call(
         sum_rows_kernel,
         (shape(64, COLS), shape(ZL, 64, WIDE, dtype=BF)),
@@ -488,7 +497,7 @@
     full0 = spread(deal(sent, ZAXES).reshape(ZL * 64, WIDE), "x", X).reshape(ROWS, WIDE)
     moved, load = call(
         moved_kernel,
-        (shape(512, COLS), shape(8, 80, 128, dtype=BF)),
+        (shape(512, COLS), shape(16, 80, 128, dtype=BF)),
         place,
         full0,
         own,
@@ -498,8 +507,12 @@
         tag_proj,
         smem=1,
     )
-    mixed, inv = token_sum(
-        load, 72, tokens1_kernel, (shape(8, 80, 128, dtype=BF), shape(8, 128)), total
+    mixed, inv = call(
+        tokens1_kernel,
+        (shape(8, 80, 128, dtype=BF), shape(8, 128)),
+        deal(load, ("zh", "c", "y")),
+        total,
+        own_tags,
     )
     arrived = product(True, deal(mixed, ("c", "y")), h_loc, hdot0, moved, inv)
     return call(last_kernel, shape(64, COLS), arrived, rows0, direction, inv)

time: 271 us -> 277 us (1.022)
  blocking collectives: 156 us -> 177 us
  waiting for transfers between devices: 33.3 us -> 22.6 us
  starting transfers between devices: 53.6 us -> 49.7 us
    all_to_all x10, blocking collectives: 156 us -> 177 us  [deal(): return lax.all_to_all(x, axis, 0, 0, tiled=True)]
    ppermute x5 -> x4, waiting for transfers between devices: 25 us -> 14.3 us  [swap(): return lax.ppermute(x, axis, [(0, 1), (1, 0)])]
    ppermute x5 -> x4, starting transfers between devices: 31.9 us -> 28 us  [swap(): return lax.ppermute(x, axis, [(0, 1), (1, 0)])]
    pallas_call x16 -> x15, Pallas kernels: 19.3 us -> 19.3 us  [call(): pl.pallas_call(kernel, out_shape=out_shape, in_specs=specs, out_specs=[vm...]
  transfers between devices with their start and end apart: 10 -> 9, of which waited for: 8 -> 7; matrix products, arithmetic and copies ran while one was open for 1% -> 1% of each run, Pallas kernels for 2% -> 2%
where the time goes in v10:
time: 277 us; the launch traced here: 276 us
  blocking collectives  177 us (64%)
  starting transfers between devices  49.7 us (18%)
  waiting for transfers between devices  22.6 us (8%)
  Pallas kernels  19.3 us (7%)
  local copies, waits for them, and re-layouts  6.44 us (2%)
    all_to_all x10, blocking collectives, deal(): return lax.all_to_all(x, axis, 0, 0, tiled=True)  177 us
    ppermute x4, starting transfers between devices, swap(): return lax.ppermute(x, axis, [(0, 1), (1, 0)])  28 us
    pallas_call x15, Pallas kernels, call(): pl.pallas_call(kernel, out_shape=out_shape, in_specs=specs, out_specs=[vm...  19.3 us
    ppermute x4, waiting for transfers between devices, swap(): return lax.ppermute(x, axis, [(0, 1), (1, 0)])  14.3 us
    ppermute x3, starting transfers between devices, local(): lax.ppermute(by_zl, 'x', [(i, (i + r) % X) for i in range(X)])  11.5 us
    all_to_all x2, starting transfers between devices, deal(): return lax.all_to_all(x, axis, 0, 0, tiled=True)  10.2 us
    unnamed x27, local copies, waits for them, and re-layouts  6.01 us
  transfers between devices with their start and end apart: 9, of which 7 were waited for; matrix products, arithmetic and copies ran while one was open for 1% of the time, Pallas kernels for 2%

profile of v10, /device:TPU:32, one launch (start us, length us, event | category | flops | bytes accessed | tf_op | source)
XLA Modules:
  0.0 275.7 jit_solution(2699067932913174568)
XLA Ops:
  0.0 14.8 %collective-permute-start = (bf16[32,2048]{1,0:T(8,128)(2,1)}, bf16[32,2048]{1,0:T(8,128)(2,1)S(1)}, u32[]{:S(2)}, u32[]{:S(2)}) collective-permute-start(bf16[32,2048]{1,0:T(8,128)(2,1)} %bitcast.23), channel_id=1, source_target_pairs={{0,2},{2,0},{1,3},{3,1},{4,6},{6,4},{5,7},{7,5},{8,10},{10,8},{9,1... | collective-permute-start | bytes 393224 | tf_op jit(solution)/shard_map/ppermute | solution.py:393
  14.8 0.0 copy-start.3
  14.8 0.8 copy-done.3
  15.7 0.2 shard_map.100.mine_ref
  15.8 4.3 %collective-permute-start.1 = (bf16[64,256]{1,0:T(8,128)(2,1)S(1)}, bf16[64,256]{1,0:T(8,128)(2,1)S(1)}, u32[]{:S(2)}, u32[]{:S(2)}) collective-permute-start(bf16[64,256]{1,0:T(8,128)(2,1)S(1)} %shard_map.100.mine_ref), channel_id=1, source_target_pairs={{0,256},{256,0},{1,257},{257,1},{2,258},{258,2},{3,259},{259,3},{4... | collective-permute-start | bytes 98312 | tf_op jit(solution)/shard_map/ppermute | solution.py:393
  20.1 0.0 copy-start.12
  20.1 0.6 broadcast.3
  20.7 0.1 copy-done.12
  20.8 0.7 reduce.3
  21.5 0.1 reshape_squeeze.3
  21.6 0.1 reshape.10
  21.7 1.2 copy-done.2
  22.9 0.9 copy-done.5
  23.8 0.4 shard_map.101
  24.2 0.0 copy-start
  24.2 1.0 copy-done
  25.2 0.1 stack.27.place
  25.3 3.9 %collective-permute-done.1.their_ref = bf16[64,256]{1,0:T(8,128)(2,1)S(1)} collective-permute-done((bf16[64,256]{1,0:T(8,128)(2,1)S(1)}, bf16[64,256]{1,0:T(8,128)(2,1)S(1)}, u32[]{:S(2)}, u32[]{:S(2)}) %collective-permute-start.1) | collective-permute-done | bytes 32800 | tf_op jit(solution)/shard_map/ppermute | solution.py:393
  29.2 0.0 collective-permute-done.oth_ref
  29.2 1.3 shard_map.103
  30.4 5.6 %all-to-all-start.1 = ((bf16[4,2,64,256]{3,2,1,0:T(8,128)(2,1)}), bf16[4,2,64,256]{3,2,1,0:T(8,128)(2,1)S(1)}, u32[]{:S(2)}, u32[]{:S(2)}) async-start(bf16[4,2,64,256]{3,2,1,0:T(8,128)(2,1)} %shard_map.103), calls=%async_computation.1 | async-start | bytes 524288 | tf_op jit(solution)/shard_map/all_to_all | solution.py:397
  36.0 0.0 copy-done.6
  36.0 0.7 copy-done.8
  36.7 4.4 %shard_map.102 = bf16[4,2,32,2048]{3,2,1,0:T(8,128)(2,1)} custom-call(s32[6]{0:T(128)S(1)} %stack.27.place, s32[1,4]{1,0:T(1,128)S(1)} %copy-done.8, bf16[512,1024]{1,0:T(8,128)(2,1)} %bitcast.30, bf16[512,1024]{1,0:T(8,128)(2,1)} %bitcast.31, bf16[32,2048]{1,0:T(8,128)(2,1)S(1)} %bitcast.24, bf16[32,2048]{1,0:T(8,128)(2,1)S(1)} %collective-permute-done.oth_ref), custom_call_target="tpu_custom_call" | custom-call | tf_op jit(solution)/shard_map/pallas_call | solution.py:46
  41.1 2.3 all-to-all-done.1.u0
  43.4 4.6 %all-to-all-start = ((bf16[4,64,2048]{2,1,0:T(8,128)(2,1)}), bf16[4,64,2048]{2,1,0:T(8,128)(2,1)S(1)}, u32[]{:S(2)}, u32[]{:S(2)}) async-start(bf16[4,64,2048]{2,1,0:T(8,128)(2,1)} %bitcast.14), calls=%async_computation | async-start | bytes 2097152 | tf_op jit(solution)/shard_map/all_to_all | solution.py:397
  48.0 3.5 %collective-permute-start.2 = (bf16[4,2,64,256]{3,2,1,0:T(8,128)(2,1)S(1)}, bf16[4,2,64,256]{3,2,1,0:T(8,128)(2,1)S(1)}, u32[]{:S(2)}, u32[]{:S(2)}) collective-permute-start(bf16[4,2,64,256]{3,2,1,0:T(8,128)(2,1)S(1)} %all-to-all-done.1.u0), channel_id=1, source_target_pairs={{0,16},{16,32},{32,48},{48,0},{1,17},{17,33},{33,49},{49,1},{2,18}... | collective-permute-start | bytes 786440 | tf_op jit(solution)/shard_map/ppermute | solution.py:443
  51.5 4.6 %collective-permute-start.3 = (bf16[4,2,64,256]{3,2,1,0:T(8,128)(2,1)S(1)}, bf16[4,2,64,256]{3,2,1,0:T(8,128)(2,1)S(1)}, u32[]{:S(2)}, u32[]{:S(2)}) collective-permute-start(bf16[4,2,64,256]{3,2,1,0:T(8,128)(2,1)S(1)} %all-to-all-done.1.u0), channel_id=1, source_target_pairs={{0,32},{16,48},{32,0},{48,16},{1,33},{17,49},{33,1},{49,17},{2,34}... | collective-permute-start | bytes 786440 | tf_op jit(solution)/shard_map/ppermute | solution.py:443
  56.2 0.0 copy-done.9
  56.2 3.3 %collective-permute-start.4 = (bf16[4,2,64,256]{3,2,1,0:T(8,128)(2,1)S(1)}, bf16[4,2,64,256]{3,2,1,0:T(8,128)(2,1)}, u32[]{:S(2)}, u32[]{:S(2)}) collective-permute-start(bf16[4,2,64,256]{3,2,1,0:T(8,128)(2,1)S(1)} %all-to-all-done.1.u0), channel_id=1, source_target_pairs={{0,48},{16,0},{32,16},{48,32},{1,49},{17,1},{33,17},{49,33},{2,50}... | collective-permute-start | bytes 786440 | tf_op jit(solution)/shard_map/ppermute | solution.py:443
  59.5 2.6 all-to-all-done.own_ref.rest_0_.rest_2_
  62.1 0.0 collective-permute-done.2.u1
  62.1 2.5 collective-permute-done.3.u2
  64.6 0.7 copy-done.11
  65.3 0.9 collective-permute-done.4.u3
  66.2 1.9 collective-permute-start.5
  68.2 2.6 collective-permute-done.5.oth_ref.rest_1_.rest_3_
  70.8 0.0 copy-done.1
  70.8 4.5 %shard_map.104 = (f32[512,224]{1,0:T(8,128)S(1)}, f32[512,224]{1,0:T(8,128)S(1)}, bf16[8,208,128]{2,1,0:T(8,128)(2,1)S(1)}) custom-call(s32[6]{0:T(128)S(1)} %stack.27.place, bf16[2048,224]{1,0:T(8,128)(2,1)} %copy-done, bf16[4,2,64,256]{3,2,1,0:T(8,128)(2,1)} %copy-done.9, bf16[4,2,64,256]{3,2,1,0:T(8,128)(2,1)} %copy-done.10, ...), custom_call_target="tpu_custom_call" | custom-call | tf_op jit(solution)/shard_map/pallas_call | solution.py:46
  75.3 13.1 %all_to_all.60.i_ref = bf16[8,208,128]{2,1,0:T(8,128)(2,1)S(1)} all-to-all(bf16[8,208,128]{2,1,0:T(8,128)(2,1)S(1)} %get-tuple-element.39), channel_id=1, replica_groups=mesh['za'=2,'zb'=4,'x'=4,'y'=4,'zh'=2,'c'=2] {'c','y'}, dimensions={0} | all-to-all | bytes 851968 | tf_op jit(solution)/shard_map/all_to_all | solution.py:397
  88.4 0.1 shard_map.105.mine_ref
  88.5 7.0 %collective-permute-start.6 = (f32[136,128]{1,0:T(8,128)S(1)}, f32[136,128]{1,0:T(8,128)S(1)}, u32[]{:S(2)}, u32[]{:S(2)}) collective-permute-start(f32[136,128]{1,0:T(8,128)S(1)} %shard_map.105.mine_ref), channel_id=1, source_target_pairs={{0,2},{2,0},{1,3},{3,1},{4,6},{6,4},{5,7},{7,5},{8,10},{10,8},{9,1... | collective-permute-start | bytes 208904 | tf_op jit(solution)/shard_map/ppermute | solution.py:393
  95.5 0.1 copy.12.tag_ref
  95.6 7.8 %collective-permute-done.6.their_ref = f32[136,128]{1,0:T(8,128)S(1)} collective-permute-done((f32[136,128]{1,0:T(8,128)S(1)}, f32[136,128]{1,0:T(8,128)S(1)}, u32[]{:S(2)}, u32[]{:S(2)}) %collective-permute-start.6) | collective-permute-done | bytes 69664 | tf_op jit(solution)/shard_map/ppermute | solution.py:393
  103.4 0.6 shard_map.106
  104.0 9.4 %all_to_all.61.m_ref = bf16[8,80,128]{2,1,0:T(8,128)(2,1)S(1)} all-to-all(bf16[8,80,128]{2,1,0:T(8,128)(2,1)S(1)} %get-tuple-element.41), channel_id=1, replica_groups=mesh['za'=2,'zb'=4,'x'=4,'y'=4,'zh'=2,'c'=2] {'c','y'}, dimensions={0} | all-to-all | bytes 327680 | tf_op jit(solution)/shard_map/all_to_all | solution.py:397
  113.4 1.9 shard_map.107
  115.3 18.0 %all_to_all.62.i_ref = bf16[4,8,112,128]{3,2,1,0:T(8,128)(2,1)S(1)} all-to-all(bf16[4,8,112,128]{3,2,1,0:T(8,128)(2,1)S(1)} %shard_map.107), channel_id=1, replica_groups=mesh['za'=2,'zb'=4,'x'=4,'y'=4,'zh'=2,'c'=2] {'x'}, dimensions={0} | all-to-all | bytes 1835008 | tf_op jit(solution)/shard_map/all_to_all | solution.py:397
  133.3 0.1 shard_map.108
  133.4 24.1 %all_to_all.63.i_ref = bf16[8,112,128]{2,1,0:T(8,128)(2,1)S(1)} all-to-all(bf16[8,112,128]{2,1,0:T(8,128)(2,1)S(1)} %shard_map.108), channel_id=1, replica_groups=mesh['za'=2,'zb'=4,'x'=4,'y'=4,'zh'=2,'c'=2] {'za','zb'}, dimensions={0} | all-to-all | bytes 458752 | tf_op jit(solution)/shard_map/all_to_all | solution.py:397
  157.5 0.2 shard_map.109
  157.8 20.5 %all_to_all.64 = bf16[8,64,256]{2,1,0:T(8,128)(2,1)S(1)} all-to-all(bf16[8,64,256]{2,1,0:T(8,128)(2,1)S(1)} %get-tuple-element.44), channel_id=1, replica_groups=mesh['za'=2,'zb'=4,'x'=4,'y'=4,'zh'=2,'c'=2] {'za','zb'}, dimensions={0} | all-to-all | bytes 524288 | tf_op jit(solution)/shard_map/all_to_all | solution.py:397
  178.3 0.1 broadcast_in_dim.12
  178.4 13.3 %all_to_all.65 = bf16[4,512,256]{2,1,0:T(8,128)(2,1)S(1)} all-to-all(bf16[4,512,256]{2,1,0:T(8,128)(2,1)S(1)} %broadcast_in_dim.12), channel_id=1, replica_groups=mesh['za'=2,'zb'=4,'x'=4,'y'=4,'zh'=2,'c'=2] {'x'}, dimensions={0} | all-to-all | bytes 2097152 | tf_op jit(solution)/shard_map/all_to_all | solution.py:397
  191.7 2.3 shard_map.110
  194.0 31.6 %all_to_all.66.i_ref = bf16[16,80,128]{2,1,0:T(8,128)(2,1)S(1)} all-to-all(bf16[16,80,128]{2,1,0:T(8,128)(2,1)S(1)} %get-tuple-element.45), channel_id=1, replica_groups=mesh['za'=2,'zb'=4,'x'=4,'y'=4,'zh'=2,'c'=2] {'zh','c','y'}, dimensions={0} | all-to-all | bytes 655360 | tf_op jit(solution)/shard_map/all_to_all | solution.py:397
  225.6 0.7 shard_map.111
  226.3 8.2 %all_to_all.67.m_ref = bf16[8,80,128]{2,1,0:T(8,128)(2,1)S(1)} all-to-all(bf16[8,80,128]{2,1,0:T(8,128)(2,1)S(1)} %get-tuple-element.47), channel_id=1, replica_groups=mesh['za'=2,'zb'=4,'x'=4,'y'=4,'zh'=2,'c'=2] {'c','y'}, dimensions={0} | all-to-all | bytes 327680 | tf_op jit(solution)/shard_map/all_to_all | solution.py:397
  234.5 1.9 shard_map.112
  236.4 16.7 %all_to_all.68.i_ref = bf16[4,8,112,128]{3,2,1,0:T(8,128)(2,1)S(1)} all-to-all(bf16[4,8,112,128]{3,2,1,0:T(8,128)(2,1)S(1)} %shard_map.112), channel_id=1, replica_groups=mesh['za'=2,'zb'=4,'x'=4,'y'=4,'zh'=2,'c'=2] {'x'}, dimensions={0} | all-to-all | bytes 1835008 | tf_op jit(solution)/shard_map/all_to_all | solution.py:397
  253.1 0.1 shard_map.113
  253.3 0.0 copy-start.4
  253.3 21.7 %all_to_all.69.i_ref = bf16[8,112,128]{2,1,0:T(8,128)(2,1)S(1)} all-to-all(bf16[8,112,128]{2,1,0:T(8,128)(2,1)S(1)} %shard_map.113), channel_id=1, replica_groups=mesh['za'=2,'zb'=4,'x'=4,'y'=4,'zh'=2,'c'=2] {'za','zb'}, dimensions={0} | all-to-all | bytes 458752 | tf_op jit(solution)/shard_map/all_to_all | solution.py:397
  275.0 0.7 shard_map.114
  (14 shorter events, 0.0 us)
Async XLA Ops:
  0.0 29.2 %collective-permute-start = (bf16[32,2048]{1,0:T(8,128)(2,1)}, bf16[32,2048]{1,0:T(8,128)(2,1)S(1)}, u32[]{:S(2)}, u32[]{:S(2)}) collective-permute-start(bf16[32,2048]{1,0:T(8,128)(2,1)} %bitcast.23), channel_id=1, source_target_pairs={{0,2},{2,0},{1,3},{3,1},{4,6},{6,4},{5,7},{7,5},{8,10},{10,8},{9,1... | collective-permute-start | bytes 393224 | tf_op jit(solution)/shard_map/ppermute | solution.py:393
  14.8 0.8 copy-start.3
  15.8 13.4 %collective-permute-start.1 = (bf16[64,256]{1,0:T(8,128)(2,1)S(1)}, bf16[64,256]{1,0:T(8,128)(2,1)S(1)}, u32[]{:S(2)}, u32[]{:S(2)}) collective-permute-start(bf16[64,256]{1,0:T(8,128)(2,1)S(1)} %shard_map.100.mine_ref), channel_id=1, source_target_pairs={{0,256},{256,0},{1,257},{257,1},{2,258},{258,2},{3,259},{259,3},{4... | collective-permute-start | bytes 98312 | tf_op jit(solution)/shard_map/ppermute | solution.py:393
  20.1 0.7 copy-start.12
  21.7 1.2 copy-start.2
  22.9 0.9 copy-start.5
  24.2 1.0 copy-start
  30.4 5.6 %copy-start.6 = (bf16[1,32,2048]{2,1,0:T(8,128)(2,1)S(1)}, bf16[1,32,2048]{2,1,0:T(8,128)(2,1)}, u32[]{:S(2)}) copy-start(bf16[1,32,2048]{2,1,0:T(8,128)(2,1)} %param.10) | copy-start | bytes 393220
  30.4 12.9 %all-to-all-start.1 = ((bf16[4,2,64,256]{3,2,1,0:T(8,128)(2,1)}), bf16[4,2,64,256]{3,2,1,0:T(8,128)(2,1)S(1)}, u32[]{:S(2)}, u32[]{:S(2)}) async-start(bf16[4,2,64,256]{3,2,1,0:T(8,128)(2,1)} %shard_map.103), calls=%async_computation.1 | async-start | bytes 524288 | tf_op jit(solution)/shard_map/all_to_all | solution.py:397
  36.0 0.7 copy-start.8
  43.4 12.8 %copy-start.9 = (bf16[4,2,64,256]{3,2,1,0:T(8,128)(2,1)}, bf16[4,2,64,256]{3,2,1,0:T(8,128)(2,1)S(1)}, u32[]{:S(2)}) copy-start(bf16[4,2,64,256]{3,2,1,0:T(8,128)(2,1)S(1)} %all-to-all-done.1.u0) | copy-start | bytes 786436
  43.4 27.4 %copy-start.1 = (bf16[224,128]{1,0:T(8,128)(2,1)S(1)}, bf16[224,128]{1,0:T(8,128)(2,1)}, u32[]{:S(2)}) copy-start(bf16[224,128]{1,0:T(8,128)(2,1)} %rest_5_.1) | copy-start | bytes 172036
  43.4 18.7 %all-to-all-start = ((bf16[4,64,2048]{2,1,0:T(8,128)(2,1)}), bf16[4,64,2048]{2,1,0:T(8,128)(2,1)S(1)}, u32[]{:S(2)}, u32[]{:S(2)}) async-start(bf16[4,64,2048]{2,1,0:T(8,128)(2,1)} %bitcast.14), calls=%async_computation | async-start | bytes 2097152 | tf_op jit(solution)/shard_map/all_to_all | solution.py:397
  48.0 22.8 %copy-start.7 = (f32[224]{0:T(256)S(1)}, f32[224]{0:T(256)}, u32[]{:S(2)}) copy-start(f32[224]{0:T(256)} %param.15) | copy-start | bytes 2692
  48.0 14.1 %collective-permute-start.2 = (bf16[4,2,64,256]{3,2,1,0:T(8,128)(2,1)S(1)}, bf16[4,2,64,256]{3,2,1,0:T(8,128)(2,1)S(1)}, u32[]{:S(2)}, u32[]{:S(2)}) collective-permute-start(bf16[4,2,64,256]{3,2,1,0:T(8,128)(2,1)S(1)} %all-to-all-done.1.u0), channel_id=1, source_target_pairs={{0,16},{16,32},{32,48},{48,0},{1,17},{17,33},{33,49},{49,1},{2,18}... | collective-permute-start | bytes 786440 | tf_op jit(solution)/shard_map/ppermute | solution.py:443
  51.5 13.1 %collective-permute-start.3 = (bf16[4,2,64,256]{3,2,1,0:T(8,128)(2,1)S(1)}, bf16[4,2,64,256]{3,2,1,0:T(8,128)(2,1)S(1)}, u32[]{:S(2)}, u32[]{:S(2)}) collective-permute-start(bf16[4,2,64,256]{3,2,1,0:T(8,128)(2,1)S(1)} %all-to-all-done.1.u0), channel_id=1, source_target_pairs={{0,32},{16,48},{32,0},{48,16},{1,33},{17,49},{33,1},{49,17},{2,34}... | collective-permute-start | bytes 786440 | tf_op jit(solution)/shard_map/ppermute | solution.py:443
  56.2 10.1 %collective-permute-start.4 = (bf16[4,2,64,256]{3,2,1,0:T(8,128)(2,1)S(1)}, bf16[4,2,64,256]{3,2,1,0:T(8,128)(2,1)}, u32[]{:S(2)}, u32[]{:S(2)}) collective-permute-start(bf16[4,2,64,256]{3,2,1,0:T(8,128)(2,1)S(1)} %all-to-all-done.1.u0), channel_id=1, source_target_pairs={{0,48},{16,0},{32,16},{48,32},{1,49},{17,1},{33,17},{49,33},{2,50}... | collective-permute-start | bytes 786440 | tf_op jit(solution)/shard_map/ppermute | solution.py:443
  62.1 2.5 copy-start.10
  64.6 0.7 copy-start.11
  66.2 4.5 %collective-permute-start.5 = (bf16[4,64,2048]{2,1,0:T(8,128)(2,1)S(1)}, bf16[4,64,2048]{2,1,0:T(8,128)(2,1)S(1)}, u32[]{:S(2)}, u32[]{:S(2)}) collective-permute-start(bf16[4,64,2048]{2,1,0:T(8,128)(2,1)S(1)} %all-to-all-done.own_ref.rest_0_.rest_2_), channel_id=1, source_target_pairs={{0,1},{1,0},{2,3},{3,2},{4,5},{5,4},{6,7},{7,6},{8,9},{9,8},{10,11... | collective-permute-start | bytes 3145736 | tf_op jit(solution)/shard_map/ppermute | solution.py:393
  88.5 15.0 %collective-permute-start.6 = (f32[136,128]{1,0:T(8,128)S(1)}, f32[136,128]{1,0:T(8,128)S(1)}, u32[]{:S(2)}, u32[]{:S(2)}) collective-permute-start(f32[136,128]{1,0:T(8,128)S(1)} %shard_map.105.mine_ref), channel_id=1, source_target_pairs={{0,2},{2,0},{1,3},{3,1},{4,6},{6,4},{5,7},{7,5},{8,10},{10,8},{9,1... | collective-permute-start | bytes 208904 | tf_op jit(solution)/shard_map/ppermute | solution.py:393
  253.3 21.7 %copy-start.4 = (f32[64,224]{1,0:T(8,128)S(1)}, f32[64,224]{1,0:T(8,128)}, u32[]{:S(2)}) copy-start(f32[64,224]{1,0:T(8,128)} %d_ref.3) | copy-start | bytes 172036

commit v11 on v9

--- a/solution.py
+++ b/solution.py
@@ -68,13 +68,9 @@
     return a, b, (rest - b.astype(F32)).astype(BF)
 
 
-def attend_kernel(place, starts, k_far, v_far, own_ref, oth_ref, o_ref, k_ref, v_ref, sems):
+def attend_kernel(place, starts, k_ref, v_ref, own_ref, oth_ref, o_ref):
     own_at, oth_at, zh = place[1], place[2], place[3]
     first = pl.multiple_of(jnp.maximum(jnp.minimum(own_at, oth_at) - WINDOW, 0), 32)
-    k_copy = pltpu.make_async_copy(k_far.at[pl.ds(first, SPAN)], k_ref, sems.at[0])
-    v_copy = pltpu.make_async_copy(v_far.at[pl.ds(first, SPAN)], v_ref, sems.at[1])
-    k_copy.start()
-    v_copy.start()
     row = lax.broadcasted_iota(jnp.int32, (128, 1), 0)
     within = jnp.where(row < 64, row, row - 64)
     q_pos = jnp.where(within < 32, within + own_at, within - 32 + oth_at)
@@ -85,17 +81,16 @@
         q_file += jnp.where(starts[0, f] <= q_pos, 1, 0)
         k_file += jnp.where(starts[0, f] <= k_pos, 1, 0)
     allowed = (q_file == k_file) & (k_pos <= q_pos) & (q_pos - k_pos < WINDOW)
-    k_copy.wait()
-    v_copy.wait()
+    keys = pl.ds(first, SPAN)
     for g in range(HK):
         heads = [slice((2 * g + r) * HD, (2 * g + r + 1) * HD) for r in range(2)]
         q = jnp.concatenate([ref[:, head] for head in heads for ref in (own_ref, oth_ref)], 0)
         cols = slice(g * HD, (g + 1) * HD)
-        scores = lax.dot_general(q, k_ref[:, cols], CONTRACT1, preferred_element_type=F32)
+        scores = lax.dot_general(q, k_ref[keys, cols], CONTRACT1, preferred_element_type=F32)
         scores = 50.0 * jnp.tanh(scores * (1.0 / 16.0) / 50.0)
         expo = jnp.where(allowed, jnp.exp(scores), 0.0)
         weights = (expo / jnp.sum(expo, -1, keepdims=True)).astype(BF)
-        out = dot(weights, v_ref[:, cols])
+        out = dot(weights, v_ref[keys, cols])
         for x in range(X):
             span = slice(x * 64, x * 64 + 64)
             both = jnp.concatenate([out[0:64, span], out[64:128, span]], 1).astype(BF)
@@ -419,10 +414,7 @@
     pairs = call(pair_kernel, shape(ZB, ZA, 64, WIDE, dtype=BF), place, row, far, smem=1)
     by_zl = deal(pairs, "zb")
     pair = call(
-        functools.partial(
-            attend_kernel,
-            scratch=[pltpu.VMEM((SPAN, HK * HD), BF)] * 2 + [pltpu.SemaphoreType.DMA((2,))],
-        ),
+        attend_kernel,
         shape(Y, ZH, 32, ROWS, dtype=BF),
         place,
         starts,
@@ -431,12 +423,11 @@
         queries[0],
         theirs,
         smem=2,
-        far=2,
     )
     u0 = [by_zl] + [
         lax.ppermute(by_zl, "x", [(i, (i + r) % X) for i in range(X)]) for r in range(1, X)
     ]
-    own, *u0 = lax.optimization_barrier((deal(pair.reshape(Y, 64, ROWS), "y"), *u0))
+    own, *u0[:3] = lax.optimization_barrier((deal(pair.reshape(Y, 64, ROWS), "y"), *u0[:3]))
     other = swap(own, "c")
 
     def product(second, *args):

time: 271 us -> 276 us (1.018)
  waiting for transfers between devices: 33.3 us -> 44.5 us
  starting transfers between devices: 53.6 us -> 50.7 us
    ppermute x3, waiting for transfers between devices: 3.39 us -> 11.1 us  [local(): lax.ppermute(by_zl, 'x', [(i, (i + r) % X) for i in range(X)])]
    all_to_all x2, waiting for transfers between devices: 4.9 us -> 10.2 us  [deal(): return lax.all_to_all(x, axis, 0, 0, tiled=True)]
    unnamed x27 -> x29, local copies, waits for them, and re-layouts: 6.02 us -> 5.33 us
  transfers between devices with their start and end apart: 10 -> 10, of which waited for: 8 -> 7; matrix products, arithmetic and copies ran while one was open for 1% -> 1% of each run, Pallas kernels for 2% -> 1%
where the time goes in v11:
time: 276 us; the launch traced here: 275 us
  blocking collectives  155 us (56%)
  starting transfers between devices  50.7 us (18%)
  waiting for transfers between devices  44.5 us (16%)
  Pallas kernels  17.9 us (6%)
  local copies, waits for them, and re-layouts  5.75 us (2%)
    all_to_all x10, blocking collectives, deal(): return lax.all_to_all(x, axis, 0, 0, tiled=True)  155 us
    ppermute x5, starting transfers between devices, swap(): return lax.ppermute(x, axis, [(0, 1), (1, 0)])  30.5 us
    ppermute x5, waiting for transfers between devices, swap(): return lax.ppermute(x, axis, [(0, 1), (1, 0)])  23.2 us
    pallas_call x16, Pallas kernels, call(): pl.pallas_call(kernel, out_shape=out_shape, in_specs=specs, out_specs=[vm...  17.9 us
    ppermute x3, waiting for transfers between devices, local(): lax.ppermute(by_zl, 'x', [(i, (i + r) % X) for i in range(X)])  11.1 us
    ppermute x3, starting transfers between devices, local(): lax.ppermute(by_zl, 'x', [(i, (i + r) % X) for i in range(X)])  10.2 us
    all_to_all x2, waiting for transfers between devices, deal(): return lax.all_to_all(x, axis, 0, 0, tiled=True)  10.2 us
    all_to_all x2, starting transfers between devices, deal(): return lax.all_to_all(x, axis, 0, 0, tiled=True)  10 us
  transfers between devices with their start and end apart: 10, of which 7 were waited for; matrix products, arithmetic and copies ran while one was open for 1% of the time, Pallas kernels for 1%

profile of v11, /device:TPU:32, one launch (start us, length us, event | category | flops | bytes accessed | tf_op | source)
XLA Modules:
  0.0 275.2 jit_solution(12757069945388197242)
XLA Ops:
  0.0 14.8 %collective-permute-start = (bf16[32,2048]{1,0:T(8,128)(2,1)}, bf16[32,2048]{1,0:T(8,128)(2,1)S(1)}, u32[]{:S(2)}, u32[]{:S(2)}) collective-permute-start(bf16[32,2048]{1,0:T(8,128)(2,1)} %bitcast.25), channel_id=1, source_target_pairs={{0,2},{2,0},{1,3},{3,1},{4,6},{6,4},{5,7},{7,5},{8,10},{10,8},{9,1... | collective-permute-start | bytes 393224 | tf_op jit(solution)/shard_map/ppermute | solution.py:382
  14.8 0.0 copy-start.5
  14.8 0.8 copy-done.5
  15.7 0.2 shard_map.100.mine_ref
  15.8 4.3 %collective-permute-start.1 = (bf16[64,256]{1,0:T(8,128)(2,1)S(1)}, bf16[64,256]{1,0:T(8,128)(2,1)S(1)}, u32[]{:S(2)}, u32[]{:S(2)}) collective-permute-start(bf16[64,256]{1,0:T(8,128)(2,1)S(1)} %shard_map.100.mine_ref), channel_id=1, source_target_pairs={{0,256},{256,0},{1,257},{257,1},{2,258},{258,2},{3,259},{259,3},{4... | collective-permute-start | bytes 98312 | tf_op jit(solution)/shard_map/ppermute | solution.py:382
  20.1 0.5 broadcast.3
  20.7 1.3 reduce.3
  22.0 0.1 reshape_squeeze.3
  22.1 0.1 reshape.10
  22.2 1.3 copy-done.4
  23.5 0.9 copy-done.7
  24.4 0.4 shard_map.101
  24.9 0.0 copy-start.2
  24.9 1.0 copy-done.2
  25.8 0.1 stack.27.place
  25.9 3.3 %collective-permute-done.1.their_ref = bf16[64,256]{1,0:T(8,128)(2,1)S(1)} collective-permute-done((bf16[64,256]{1,0:T(8,128)(2,1)S(1)}, bf16[64,256]{1,0:T(8,128)(2,1)S(1)}, u32[]{:S(2)}, u32[]{:S(2)}) %collective-permute-start.1) | collective-permute-done | bytes 32800 | tf_op jit(solution)/shard_map/ppermute | solution.py:382
  29.2 0.0 collective-permute-done.oth_ref
  29.2 1.3 shard_map.103
  30.4 5.4 %all-to-all-start.1 = ((bf16[4,2,64,256]{3,2,1,0:T(8,128)(2,1)}), bf16[4,2,64,256]{3,2,1,0:T(8,128)(2,1)S(1)}, u32[]{:S(2)}, u32[]{:S(2)}) async-start(bf16[4,2,64,256]{3,2,1,0:T(8,128)(2,1)} %shard_map.103), calls=%async_computation.1 | async-start | bytes 524288 | tf_op jit(solution)/shard_map/all_to_all | solution.py:386
  35.9 0.0 copy-done.8
  35.9 0.0 copy-done.10
  35.9 0.0 copy-done
  35.9 0.0 copy-done.1
  35.9 3.1 %shard_map.102 = bf16[4,2,32,2048]{3,2,1,0:T(8,128)(2,1)} custom-call(s32[6]{0:T(128)S(1)} %stack.27.place, s32[1,4]{1,0:T(1,128)S(1)} %copy-done.10, bf16[512,1024]{1,0:T(8,128)(2,1)S(1)} %bitcast.21, bf16[512,1024]{1,0:T(8,128)(2,1)S(1)} %bitcast.22, bf16[32,2048]{1,0:T(8,128)(2,1)S(1)} %bitcast.26, bf16[32,2048]{1,0:T(8,128)(2,1)S(1)} %collective-permute-done.oth_ref), custom_call_target="tpu_custom_call" | custom-call | tf_op jit(solution)/shard_map/pallas_call | solution.py:46
  39.0 4.3 %all-to-all-done.1.u0 = bf16[4,2,64,256]{3,2,1,0:T(8,128)(2,1)S(1)} async-done(((bf16[4,2,64,256]{3,2,1,0:T(8,128)(2,1)}), bf16[4,2,64,256]{3,2,1,0:T(8,128)(2,1)S(1)}, u32[]{:S(2)}, u32[]{:S(2)}) %all-to-all-start.1) | async-done | bytes 262176 | tf_op jit(solution)/shard_map/all_to_all | solution.py:386
  43.3 4.6 %all-to-all-start = ((bf16[4,64,2048]{2,1,0:T(8,128)(2,1)}), bf16[4,64,2048]{2,1,0:T(8,128)(2,1)S(1)}, u32[]{:S(2)}, u32[]{:S(2)}) async-start(bf16[4,64,2048]{2,1,0:T(8,128)(2,1)} %bitcast.14), calls=%async_computation | async-start | bytes 2097152 | tf_op jit(solution)/shard_map/all_to_all | solution.py:386
  47.9 3.5 %collective-permute-start.2 = (bf16[4,2,64,256]{3,2,1,0:T(8,128)(2,1)S(1)}, bf16[4,2,64,256]{3,2,1,0:T(8,128)(2,1)S(1)}, u32[]{:S(2)}, u32[]{:S(2)}) collective-permute-start(bf16[4,2,64,256]{3,2,1,0:T(8,128)(2,1)S(1)} %all-to-all-done.1.u0), channel_id=1, source_target_pairs={{0,16},{16,32},{32,48},{48,0},{1,17},{17,33},{33,49},{49,1},{2,18}... | collective-permute-start | bytes 786440 | tf_op jit(solution)/shard_map/ppermute | solution.py:428
  51.4 4.6 %collective-permute-start.3 = (bf16[4,2,64,256]{3,2,1,0:T(8,128)(2,1)S(1)}, bf16[4,2,64,256]{3,2,1,0:T(8,128)(2,1)}, u32[]{:S(2)}, u32[]{:S(2)}) collective-permute-start(bf16[4,2,64,256]{3,2,1,0:T(8,128)(2,1)S(1)} %all-to-all-done.1.u0), channel_id=1, source_target_pairs={{0,32},{16,48},{32,0},{48,16},{1,33},{17,49},{33,1},{49,17},{2,34}... | collective-permute-start | bytes 786440 | tf_op jit(solution)/shard_map/ppermute | solution.py:428
  56.0 6.0 %all-to-all-done.own_ref.rest_0_.rest_2_ = bf16[4,64,2048]{2,1,0:T(8,128)(2,1)S(1)} async-done(((bf16[4,64,2048]{2,1,0:T(8,128)(2,1)}), bf16[4,64,2048]{2,1,0:T(8,128)(2,1)S(1)}, u32[]{:S(2)}, u32[]{:S(2)}) %all-to-all-start) | async-done | bytes 1048608 | tf_op jit(solution)/shard_map/all_to_all | solution.py:386
  62.0 0.0 collective-permute-done.2.u1
  62.0 2.6 collective-permute-done.3.u2
  64.6 1.9 collective-permute-start.5
  66.5 2.1 collective-permute-start.4
  68.6 8.5 %collective-permute-done.4.u3 = bf16[4,2,64,256]{3,2,1,0:T(8,128)(2,1)S(1)} collective-permute-done((bf16[4,2,64,256]{3,2,1,0:T(8,128)(2,1)S(1)}, bf16[4,2,64,256]{3,2,1,0:T(8,128)(2,1)S(1)}, u32[]{:S(2)}, u32[]{:S(2)}) %collective-permute-start.4) | collective-permute-done | bytes 262176 | tf_op jit(solution)/shard_map/ppermute | solution.py:428
  77.1 0.0 collective-permute-done.5.oth_ref.rest_1_.rest_3_
  77.1 0.7 copy-done.13
  77.8 4.5 %shard_map.104 = (f32[512,224]{1,0:T(8,128)S(1)}, f32[512,224]{1,0:T(8,128)S(1)}, bf16[8,208,128]{2,1,0:T(8,128)(2,1)S(1)}) custom-call(s32[6]{0:T(128)S(1)} %stack.27.place, bf16[2048,224]{1,0:T(8,128)(2,1)} %copy-done.2, bf16[4,2,64,256]{3,2,1,0:T(8,128)(2,1)} %copy-done.11, bf16[4,2,64,256]{3,2,1,0:T(8,128)(2,1)} %copy-done.12, ...), custom_call_target="tpu_custom_call" | custom-call | tf_op jit(solution)/shard_map/pallas_call | solution.py:46
  82.3 13.0 %all_to_all.60.i_ref = bf16[8,208,128]{2,1,0:T(8,128)(2,1)S(1)} all-to-all(bf16[8,208,128]{2,1,0:T(8,128)(2,1)S(1)} %get-tuple-element.37), channel_id=1, replica_groups=mesh['za'=2,'zb'=4,'x'=4,'y'=4,'zh'=2,'c'=2] {'c','y'}, dimensions={0} | all-to-all | bytes 851968 | tf_op jit(solution)/shard_map/all_to_all | solution.py:386
  95.3 0.1 shard_map.105.mine_ref
  95.4 5.7 %collective-permute-start.6 = (f32[136,128]{1,0:T(8,128)S(1)}, f32[136,128]{1,0:T(8,128)S(1)}, u32[]{:S(2)}, u32[]{:S(2)}) collective-permute-start(f32[136,128]{1,0:T(8,128)S(1)} %shard_map.105.mine_ref), channel_id=1, source_target_pairs={{0,2},{2,0},{1,3},{3,1},{4,6},{6,4},{5,7},{7,5},{8,10},{10,8},{9,1... | collective-permute-start | bytes 208904 | tf_op jit(solution)/shard_map/ppermute | solution.py:382
  101.1 0.1 copy.12.tag_ref
  101.2 9.1 %collective-permute-done.6.their_ref = f32[136,128]{1,0:T(8,128)S(1)} collective-permute-done((f32[136,128]{1,0:T(8,128)S(1)}, f32[136,128]{1,0:T(8,128)S(1)}, u32[]{:S(2)}, u32[]{:S(2)}) %collective-permute-start.6) | collective-permute-done | bytes 69664 | tf_op jit(solution)/shard_map/ppermute | solution.py:382
  110.3 0.6 shard_map.106
  110.9 9.5 %all_to_all.61.m_ref = bf16[8,80,128]{2,1,0:T(8,128)(2,1)S(1)} all-to-all(bf16[8,80,128]{2,1,0:T(8,128)(2,1)S(1)} %get-tuple-element.39), channel_id=1, replica_groups=mesh['za'=2,'zb'=4,'x'=4,'y'=4,'zh'=2,'c'=2] {'c','y'}, dimensions={0} | all-to-all | bytes 327680 | tf_op jit(solution)/shard_map/all_to_all | solution.py:386
  120.3 1.9 shard_map.107
  122.2 16.7 %all_to_all.62.i_ref = bf16[4,8,112,128]{3,2,1,0:T(8,128)(2,1)S(1)} all-to-all(bf16[4,8,112,128]{3,2,1,0:T(8,128)(2,1)S(1)} %shard_map.107), channel_id=1, replica_groups=mesh['za'=2,'zb'=4,'x'=4,'y'=4,'zh'=2,'c'=2] {'x'}, dimensions={0} | all-to-all | bytes 1835008 | tf_op jit(solution)/shard_map/all_to_all | solution.py:386
  138.9 0.1 shard_map.108
  139.0 24.2 %all_to_all.63.i_ref = bf16[8,112,128]{2,1,0:T(8,128)(2,1)S(1)} all-to-all(bf16[8,112,128]{2,1,0:T(8,128)(2,1)S(1)} %shard_map.108), channel_id=1, replica_groups=mesh['za'=2,'zb'=4,'x'=4,'y'=4,'zh'=2,'c'=2] {'za','zb'}, dimensions={0} | all-to-all | bytes 458752 | tf_op jit(solution)/shard_map/all_to_all | solution.py:386
  163.2 0.2 shard_map.109
  163.5 20.5 %all_to_all.64 = bf16[8,64,256]{2,1,0:T(8,128)(2,1)S(1)} all-to-all(bf16[8,64,256]{2,1,0:T(8,128)(2,1)S(1)} %get-tuple-element.42), channel_id=1, replica_groups=mesh['za'=2,'zb'=4,'x'=4,'y'=4,'zh'=2,'c'=2] {'za','zb'}, dimensions={0} | all-to-all | bytes 524288 | tf_op jit(solution)/shard_map/all_to_all | solution.py:386
  184.0 0.1 broadcast_in_dim.12
  184.1 13.3 %all_to_all.65 = bf16[4,512,256]{2,1,0:T(8,128)(2,1)S(1)} all-to-all(bf16[4,512,256]{2,1,0:T(8,128)(2,1)S(1)} %broadcast_in_dim.12), channel_id=1, replica_groups=mesh['za'=2,'zb'=4,'x'=4,'y'=4,'zh'=2,'c'=2] {'x'}, dimensions={0} | all-to-all | bytes 2097152 | tf_op jit(solution)/shard_map/all_to_all | solution.py:386
  197.4 2.3 shard_map.110
  199.7 8.3 %all_to_all.66.i_ref = bf16[8,80,128]{2,1,0:T(8,128)(2,1)S(1)} all-to-all(bf16[8,80,128]{2,1,0:T(8,128)(2,1)S(1)} %get-tuple-element.43), channel_id=1, replica_groups=mesh['za'=2,'zb'=4,'x'=4,'y'=4,'zh'=2,'c'=2] {'c','y'}, dimensions={0} | all-to-all | bytes 327680 | tf_op jit(solution)/shard_map/all_to_all | solution.py:386
  208.0 3.7 %collective-permute-start.7 = (f32[72,128]{1,0:T(8,128)S(1)}, f32[72,128]{1,0:T(8,128)S(1)}, u32[]{:S(2)}, u32[]{:S(2)}) collective-permute-start(f32[72,128]{1,0:T(8,128)S(1)} %shard_map.111.mine_ref), channel_id=1, source_target_pairs={{0,2},{2,0},{1,3},{3,1},{4,6},{6,4},{5,7},{7,5},{8,10},{10,8},{9,1... | collective-permute-start | bytes 110600 | tf_op jit(solution)/shard_map/ppermute | solution.py:382
  211.7 10.8 %collective-permute-done.7.their_ref = f32[72,128]{1,0:T(8,128)S(1)} collective-permute-done((f32[72,128]{1,0:T(8,128)S(1)}, f32[72,128]{1,0:T(8,128)S(1)}, u32[]{:S(2)}, u32[]{:S(2)}) %collective-permute-start.7) | collective-permute-done | bytes 36896 | tf_op jit(solution)/shard_map/ppermute | solution.py:382
  222.6 0.6 shard_map.112
  223.2 9.3 %all_to_all.67.m_ref = bf16[8,80,128]{2,1,0:T(8,128)(2,1)S(1)} all-to-all(bf16[8,80,128]{2,1,0:T(8,128)(2,1)S(1)} %get-tuple-element.45), channel_id=1, replica_groups=mesh['za'=2,'zb'=4,'x'=4,'y'=4,'zh'=2,'c'=2] {'c','y'}, dimensions={0} | all-to-all | bytes 327680 | tf_op jit(solution)/shard_map/all_to_all | solution.py:386
  232.5 1.9 shard_map.113
  234.4 16.7 %all_to_all.68.i_ref = bf16[4,8,112,128]{3,2,1,0:T(8,128)(2,1)S(1)} all-to-all(bf16[4,8,112,128]{3,2,1,0:T(8,128)(2,1)S(1)} %shard_map.113), channel_id=1, replica_groups=mesh['za'=2,'zb'=4,'x'=4,'y'=4,'zh'=2,'c'=2] {'x'}, dimensions={0} | all-to-all | bytes 1835008 | tf_op jit(solution)/shard_map/all_to_all | solution.py:386
  251.1 0.1 shard_map.114
  251.2 0.0 copy-start.6
  251.2 23.2 %all_to_all.69.i_ref = bf16[8,112,128]{2,1,0:T(8,128)(2,1)S(1)} all-to-all(bf16[8,112,128]{2,1,0:T(8,128)(2,1)S(1)} %shard_map.114), channel_id=1, replica_groups=mesh['za'=2,'zb'=4,'x'=4,'y'=4,'zh'=2,'c'=2] {'za','zb'}, dimensions={0} | all-to-all | bytes 458752 | tf_op jit(solution)/shard_map/all_to_all | solution.py:386
  274.4 0.7 shard_map.115
  (19 shorter events, 0.1 us)
Async XLA Ops:
  0.0 29.2 %collective-permute-start = (bf16[32,2048]{1,0:T(8,128)(2,1)}, bf16[32,2048]{1,0:T(8,128)(2,1)S(1)}, u32[]{:S(2)}, u32[]{:S(2)}) collective-permute-start(bf16[32,2048]{1,0:T(8,128)(2,1)} %bitcast.25), channel_id=1, source_target_pairs={{0,2},{2,0},{1,3},{3,1},{4,6},{6,4},{5,7},{7,5},{8,10},{10,8},{9,1... | collective-permute-start | bytes 393224 | tf_op jit(solution)/shard_map/ppermute | solution.py:382
  14.8 0.8 copy-start.5
  15.7 20.2 %copy-start.8 = (bf16[1,32,2048]{2,1,0:T(8,128)(2,1)S(1)}, bf16[1,32,2048]{2,1,0:T(8,128)(2,1)}, u32[]{:S(2)}) copy-start(bf16[1,32,2048]{2,1,0:T(8,128)(2,1)} %param.10) | copy-start | bytes 393220
  15.8 13.4 %collective-permute-start.1 = (bf16[64,256]{1,0:T(8,128)(2,1)S(1)}, bf16[64,256]{1,0:T(8,128)(2,1)S(1)}, u32[]{:S(2)}, u32[]{:S(2)}) collective-permute-start(bf16[64,256]{1,0:T(8,128)(2,1)S(1)} %shard_map.100.mine_ref), channel_id=1, source_target_pairs={{0,256},{256,0},{1,257},{257,1},{2,258},{258,2},{3,259},{259,3},{4... | collective-permute-start | bytes 98312 | tf_op jit(solution)/shard_map/ppermute | solution.py:382
  22.0 13.9 %copy-start.10 = (s32[1,4]{1,0:T(1,128)S(1)}, s32[1,4]{1,0:T(1,128)}, u32[]{:S(2)}) copy-start(s32[1,4]{1,0:T(1,128)} %starts.1) | copy-start | bytes 52
  22.1 13.8 %copy-start = (bf16[1,512,1024]{2,1,0:T(8,128)(2,1)S(1)}, bf16[1,512,1024]{2,1,0:T(8,128)(2,1)}, u32[]{:S(2)}) copy-start(bf16[1,512,1024]{2,1,0:T(8,128)(2,1)} %param.11) | copy-start | bytes 3145732
  22.1 13.8 %copy-start.1 = (bf16[1,512,1024]{2,1,0:T(8,128)(2,1)S(1)}, bf16[1,512,1024]{2,1,0:T(8,128)(2,1)}, u32[]{:S(2)}) copy-start(bf16[1,512,1024]{2,1,0:T(8,128)(2,1)} %param.12) | copy-start | bytes 3145732
  22.2 1.3 copy-start.4
  23.5 0.9 copy-start.7
  24.9 1.0 copy-start.2
  30.4 12.8 %all-to-all-start.1 = ((bf16[4,2,64,256]{3,2,1,0:T(8,128)(2,1)}), bf16[4,2,64,256]{3,2,1,0:T(8,128)(2,1)S(1)}, u32[]{:S(2)}, u32[]{:S(2)}) async-start(bf16[4,2,64,256]{3,2,1,0:T(8,128)(2,1)} %shard_map.103), calls=%async_computation.1 | async-start | bytes 524288 | tf_op jit(solution)/shard_map/all_to_all | solution.py:386
  43.3 23.3 %copy-start.11 = (bf16[4,2,64,256]{3,2,1,0:T(8,128)(2,1)}, bf16[4,2,64,256]{3,2,1,0:T(8,128)(2,1)S(1)}, u32[]{:S(2)}) copy-start(bf16[4,2,64,256]{3,2,1,0:T(8,128)(2,1)S(1)} %all-to-all-done.1.u0) | copy-start | bytes 786436
  43.3 34.6 %copy-start.3 = (bf16[224,128]{1,0:T(8,128)(2,1)S(1)}, bf16[224,128]{1,0:T(8,128)(2,1)}, u32[]{:S(2)}) copy-start(bf16[224,128]{1,0:T(8,128)(2,1)} %rest_5_.1) | copy-start | bytes 172036
  43.3 18.7 %all-to-all-start = ((bf16[4,64,2048]{2,1,0:T(8,128)(2,1)}), bf16[4,64,2048]{2,1,0:T(8,128)(2,1)S(1)}, u32[]{:S(2)}, u32[]{:S(2)}) async-start(bf16[4,64,2048]{2,1,0:T(8,128)(2,1)} %bitcast.14), calls=%async_computation | async-start | bytes 2097152 | tf_op jit(solution)/shard_map/all_to_all | solution.py:386
  47.9 30.0 %copy-start.9 = (f32[224]{0:T(256)S(1)}, f32[224]{0:T(256)}, u32[]{:S(2)}) copy-start(f32[224]{0:T(256)} %param.15) | copy-start | bytes 2692
  47.9 14.1 %collective-permute-start.2 = (bf16[4,2,64,256]{3,2,1,0:T(8,128)(2,1)S(1)}, bf16[4,2,64,256]{3,2,1,0:T(8,128)(2,1)S(1)}, u32[]{:S(2)}, u32[]{:S(2)}) collective-permute-start(bf16[4,2,64,256]{3,2,1,0:T(8,128)(2,1)S(1)} %all-to-all-done.1.u0), channel_id=1, source_target_pairs={{0,16},{16,32},{32,48},{48,0},{1,17},{17,33},{33,49},{49,1},{2,18}... | collective-permute-start | bytes 786440 | tf_op jit(solution)/shard_map/ppermute | solution.py:428
  51.4 13.2 %collective-permute-start.3 = (bf16[4,2,64,256]{3,2,1,0:T(8,128)(2,1)S(1)}, bf16[4,2,64,256]{3,2,1,0:T(8,128)(2,1)}, u32[]{:S(2)}, u32[]{:S(2)}) collective-permute-start(bf16[4,2,64,256]{3,2,1,0:T(8,128)(2,1)S(1)} %all-to-all-done.1.u0), channel_id=1, source_target_pairs={{0,32},{16,48},{32,0},{48,16},{1,33},{17,49},{33,1},{49,17},{2,34}... | collective-permute-start | bytes 786440 | tf_op jit(solution)/shard_map/ppermute | solution.py:428
  62.0 15.1 %copy-start.12 = (bf16[4,2,64,256]{3,2,1,0:T(8,128)(2,1)}, bf16[4,2,64,256]{3,2,1,0:T(8,128)(2,1)S(1)}, u32[]{:S(2)}) copy-start(bf16[4,2,64,256]{3,2,1,0:T(8,128)(2,1)S(1)} %collective-permute-done.2.u1) | copy-start | bytes 786436
  64.6 12.5 %collective-permute-start.5 = (bf16[4,64,2048]{2,1,0:T(8,128)(2,1)S(1)}, bf16[4,64,2048]{2,1,0:T(8,128)(2,1)S(1)}, u32[]{:S(2)}, u32[]{:S(2)}) collective-permute-start(bf16[4,64,2048]{2,1,0:T(8,128)(2,1)S(1)} %all-to-all-done.own_ref.rest_0_.rest_2_), channel_id=1, source_target_pairs={{0,1},{1,0},{2,3},{3,2},{4,5},{5,4},{6,7},{7,6},{8,9},{9,8},{10,11... | collective-permute-start | bytes 3145736 | tf_op jit(solution)/shard_map/ppermute | solution.py:382
  66.5 10.6 %collective-permute-start.4 = (bf16[4,2,64,256]{3,2,1,0:T(8,128)(2,1)S(1)}, bf16[4,2,64,256]{3,2,1,0:T(8,128)(2,1)S(1)}, u32[]{:S(2)}, u32[]{:S(2)}) collective-permute-start(bf16[4,2,64,256]{3,2,1,0:T(8,128)(2,1)S(1)} %all-to-all-done.1.u0), channel_id=1, source_target_pairs={{0,48},{16,0},{32,16},{48,32},{1,49},{17,1},{33,17},{49,33},{2,50}... | collective-permute-start | bytes 786440 | tf_op jit(solution)/shard_map/ppermute | solution.py:428
  77.1 0.7 copy-start.13
  95.4 14.9 %collective-permute-start.6 = (f32[136,128]{1,0:T(8,128)S(1)}, f32[136,128]{1,0:T(8,128)S(1)}, u32[]{:S(2)}, u32[]{:S(2)}) collective-permute-start(f32[136,128]{1,0:T(8,128)S(1)} %shard_map.105.mine_ref), channel_id=1, source_target_pairs={{0,2},{2,0},{1,3},{3,1},{4,6},{6,4},{5,7},{7,5},{8,10},{10,8},{9,1... | collective-permute-start | bytes 208904 | tf_op jit(solution)/shard_map/ppermute | solution.py:382
  208.0 14.6 %collective-permute-start.7 = (f32[72,128]{1,0:T(8,128)S(1)}, f32[72,128]{1,0:T(8,128)S(1)}, u32[]{:S(2)}, u32[]{:S(2)}) collective-permute-start(f32[72,128]{1,0:T(8,128)S(1)} %shard_map.111.mine_ref), channel_id=1, source_target_pairs={{0,2},{2,0},{1,3},{3,1},{4,6},{6,4},{5,7},{7,5},{8,10},{10,8},{9,1... | collective-permute-start | bytes 110600 | tf_op jit(solution)/shard_map/ppermute | solution.py:382
  251.2 23.3 %copy-start.6 = (f32[64,224]{1,0:T(8,128)S(1)}, f32[64,224]{1,0:T(8,128)}, u32[]{:S(2)}) copy-start(f32[64,224]{1,0:T(8,128)} %d_ref.3) | copy-start | bytes 172036

commit v12 on v11

--- a/solution.py
+++ b/solution.py
@@ -134,6 +134,11 @@
     for i in range(ZB):
         o_ref[i, za] = mine_ref[...]
         o_ref[i, 1 - za] = their_ref[...]
+
+
+def repeat_kernel(i_ref, o_ref):
+    for i in range(X):
+        o_ref[i] = i_ref[...]
 
 
 def sum_x_kernel(i_ref, o_ref):
@@ -386,10 +391,6 @@
     return lax.all_to_all(x, axis, 0, 0, tiled=True)
 
 
-def spread(x, axis, n):
-    return deal(jnp.broadcast_to(x[None], (n,) + x.shape), axis)
-
-
 def local(queries, keys, values, stream, out_proj, norm_gain, tag_proj, direction, starts, tags):
     core = lax.axis_index("c")
     ypos = lax.axis_index("y")
@@ -427,7 +428,7 @@
     u0 = [by_zl] + [
         lax.ppermute(by_zl, "x", [(i, (i + r) % X) for i in range(X)]) for r in range(1, X)
     ]
-    own, *u0[:3] = lax.optimization_barrier((deal(pair.reshape(Y, 64, ROWS), "y"), *u0[:3]))
+    own, *u0 = lax.optimization_barrier((deal(pair.reshape(Y, 64, ROWS), "y"), *u0))
     other = swap(own, "c")
 
     def product(second, *args):
@@ -476,7 +477,8 @@
         (shape(64, COLS), shape(ZL, 64, WIDE, dtype=BF)),
         product(False, deal(mixed, ("c", "y")), h_loc, hdot0),
     )
-    full0 = spread(deal(sent, ZAXES).reshape(ZL * 64, WIDE), "x", X).reshape(ROWS, WIDE)
+    rows = deal(sent, ZAXES).reshape(ZL * 64, WIDE)
+    full0 = deal(call(repeat_kernel, shape(X, ZL * 64, WIDE, dtype=BF), rows), "x").reshape(ROWS, WIDE)
     moved, load = call(
         moved_kernel,
         (shape(512, COLS), shape(8, 80, 128, dtype=BF)),

time: 276 us -> 270 us (0.978)
  waiting for transfers between devices: 44.5 us -> 34.7 us
  starting transfers between devices: 50.7 us -> 53.5 us
    ppermute x3, waiting for transfers between devices: 11.1 us -> 3.41 us  [local(): lax.ppermute(by_zl, 'x', [(i, (i + r) % X) for i in range(X)])]
    all_to_all x2, waiting for transfers between devices: 10.2 us -> 6.87 us  [deal(): return lax.all_to_all(x, axis, 0, 0, tiled=True)]
    pallas_call x16 -> x17, Pallas kernels: 17.9 us -> 18 us  [call(): pl.pallas_call(kernel, out_shape=out_shape, in_specs=specs, out_specs=[vm...]
  transfers between devices with their start and end apart: 10 -> 10, of which waited for: 7 -> 8; matrix products, arithmetic and copies ran while one was open for 1% -> 1% of each run, Pallas kernels for 1% -> 1%
where the time goes in v12:
time: 270 us; the launch traced here: 269 us
  blocking collectives  156 us (58%)
  starting transfers between devices  53.5 us (20%)
  waiting for transfers between devices  34.7 us (13%)
  Pallas kernels  18 us (7%)
  local copies, waits for them, and re-layouts  5.69 us (2%)
    all_to_all x10, blocking collectives, deal(): return lax.all_to_all(x, axis, 0, 0, tiled=True)  156 us
    ppermute x5, starting transfers between devices, swap(): return lax.ppermute(x, axis, [(0, 1), (1, 0)])  31.9 us
    ppermute x5, waiting for transfers between devices, swap(): return lax.ppermute(x, axis, [(0, 1), (1, 0)])  24.4 us
    pallas_call x17, Pallas kernels, call(): pl.pallas_call(kernel, out_shape=out_shape, in_specs=specs, out_specs=[vm...  18 us
    ppermute x3, starting transfers between devices, local(): lax.ppermute(by_zl, 'x', [(i, (i + r) % X) for i in range(X)])  11.5 us
    all_to_all x2, starting transfers between devices, deal(): return lax.all_to_all(x, axis, 0, 0, tiled=True)  10 us
    all_to_all x2, waiting for transfers between devices, deal(): return lax.all_to_all(x, axis, 0, 0, tiled=True)  6.87 us
  transfers between devices with their start and end apart: 10, of which 8 were waited for; matrix products, arithmetic and copies ran while one was open for 1% of the time, Pallas kernels for 1%

profile of v12, /device:TPU:32, one launch (start us, length us, event | category | flops | bytes accessed | tf_op | source)
XLA Modules:
  0.0 268.9 jit_solution(5192675605890256720)
XLA Ops:
  0.0 14.8 %collective-permute-start = (bf16[32,2048]{1,0:T(8,128)(2,1)}, bf16[32,2048]{1,0:T(8,128)(2,1)S(1)}, u32[]{:S(2)}, u32[]{:S(2)}) collective-permute-start(bf16[32,2048]{1,0:T(8,128)(2,1)} %bitcast.26), channel_id=1, source_target_pairs={{0,2},{2,0},{1,3},{3,1},{4,6},{6,4},{5,7},{7,5},{8,10},{10,8},{9,1... | collective-permute-start | bytes 393224 | tf_op jit(solution)/shard_map/ppermute | solution.py:387
  14.8 0.0 copy-start.5
  14.8 0.8 copy-done.5
  15.7 0.2 shard_map.100.mine_ref
  15.8 4.3 %collective-permute-start.1 = (bf16[64,256]{1,0:T(8,128)(2,1)S(1)}, bf16[64,256]{1,0:T(8,128)(2,1)S(1)}, u32[]{:S(2)}, u32[]{:S(2)}) collective-permute-start(bf16[64,256]{1,0:T(8,128)(2,1)S(1)} %shard_map.100.mine_ref), channel_id=1, source_target_pairs={{0,256},{256,0},{1,257},{257,1},{2,258},{258,2},{3,259},{259,3},{4... | collective-permute-start | bytes 98312 | tf_op jit(solution)/shard_map/ppermute | solution.py:387
  20.1 0.5 broadcast.3
  20.7 1.3 reduce.3
  22.0 0.1 reshape_squeeze.3
  22.1 0.1 reshape.12
  22.2 1.3 copy-done.4
  23.5 0.9 copy-done.7
  24.4 0.4 shard_map.101
  24.9 0.0 copy-start.2
  24.9 1.0 copy-done.2
  25.8 0.1 stack.27.place
  25.9 3.3 %collective-permute-done.1.their_ref = bf16[64,256]{1,0:T(8,128)(2,1)S(1)} collective-permute-done((bf16[64,256]{1,0:T(8,128)(2,1)S(1)}, bf16[64,256]{1,0:T(8,128)(2,1)S(1)}, u32[]{:S(2)}, u32[]{:S(2)}) %collective-permute-start.1) | collective-permute-done | bytes 32800 | tf_op jit(solution)/shard_map/ppermute | solution.py:387
  29.2 0.0 collective-permute-done.oth_ref
  29.2 1.3 shard_map.103
  30.4 5.4 %all-to-all-start.1 = ((bf16[4,2,64,256]{3,2,1,0:T(8,128)(2,1)}), bf16[4,2,64,256]{3,2,1,0:T(8,128)(2,1)S(1)}, u32[]{:S(2)}, u32[]{:S(2)}) async-start(bf16[4,2,64,256]{3,2,1,0:T(8,128)(2,1)} %shard_map.103), calls=%async_computation.1 | async-start | bytes 524288 | tf_op jit(solution)/shard_map/all_to_all | solution.py:391
  35.9 0.0 copy-done.8
  35.9 0.0 copy-done.10
  35.9 3.1 %shard_map.102 = bf16[4,2,32,2048]{3,2,1,0:T(8,128)(2,1)} custom-call(s32[6]{0:T(128)S(1)} %stack.27.place, s32[1,4]{1,0:T(1,128)S(1)} %copy-done.10, bf16[512,1024]{1,0:T(8,128)(2,1)S(1)} %bitcast.22, bf16[512,1024]{1,0:T(8,128)(2,1)S(1)} %bitcast.23, bf16[32,2048]{1,0:T(8,128)(2,1)S(1)} %bitcast.27, bf16[32,2048]{1,0:T(8,128)(2,1)S(1)} %collective-permute-done.oth_ref), custom_call_target="tpu_custom_call" | custom-call | tf_op jit(solution)/shard_map/pallas_call | solution.py:46
  39.0 4.3 %all-to-all-done.1.u0 = bf16[4,2,64,256]{3,2,1,0:T(8,128)(2,1)S(1)} async-done(((bf16[4,2,64,256]{3,2,1,0:T(8,128)(2,1)}), bf16[4,2,64,256]{3,2,1,0:T(8,128)(2,1)S(1)}, u32[]{:S(2)}, u32[]{:S(2)}) %all-to-all-start.1) | async-done | bytes 262176 | tf_op jit(solution)/shard_map/all_to_all | solution.py:391
  43.3 4.6 %all-to-all-start = ((bf16[4,64,2048]{2,1,0:T(8,128)(2,1)}), bf16[4,64,2048]{2,1,0:T(8,128)(2,1)S(1)}, u32[]{:S(2)}, u32[]{:S(2)}) async-start(bf16[4,64,2048]{2,1,0:T(8,128)(2,1)} %bitcast.14), calls=%async_computation | async-start | bytes 2097152 | tf_op jit(solution)/shard_map/all_to_all | solution.py:391
  47.9 3.5 %collective-permute-start.2 = (bf16[4,2,64,256]{3,2,1,0:T(8,128)(2,1)S(1)}, bf16[4,2,64,256]{3,2,1,0:T(8,128)(2,1)S(1)}, u32[]{:S(2)}, u32[]{:S(2)}) collective-permute-start(bf16[4,2,64,256]{3,2,1,0:T(8,128)(2,1)S(1)} %all-to-all-done.1.u0), channel_id=1, source_target_pairs={{0,16},{16,32},{32,48},{48,0},{1,17},{17,33},{33,49},{49,1},{2,18}... | collective-permute-start | bytes 786440 | tf_op jit(solution)/shard_map/ppermute | solution.py:429
  51.4 4.6 %collective-permute-start.3 = (bf16[4,2,64,256]{3,2,1,0:T(8,128)(2,1)S(1)}, bf16[4,2,64,256]{3,2,1,0:T(8,128)(2,1)S(1)}, u32[]{:S(2)}, u32[]{:S(2)}) collective-permute-start(bf16[4,2,64,256]{3,2,1,0:T(8,128)(2,1)S(1)} %all-to-all-done.1.u0), channel_id=1, source_target_pairs={{0,32},{16,48},{32,0},{48,16},{1,33},{17,49},{33,1},{49,17},{2,34}... | collective-permute-start | bytes 786440 | tf_op jit(solution)/shard_map/ppermute | solution.py:429
  56.0 0.0 copy-done.11
  56.0 3.3 %collective-permute-start.4 = (bf16[4,2,64,256]{3,2,1,0:T(8,128)(2,1)S(1)}, bf16[4,2,64,256]{3,2,1,0:T(8,128)(2,1)}, u32[]{:S(2)}, u32[]{:S(2)}) collective-permute-start(bf16[4,2,64,256]{3,2,1,0:T(8,128)(2,1)S(1)} %all-to-all-done.1.u0), channel_id=1, source_target_pairs={{0,48},{16,0},{32,16},{48,32},{1,49},{17,1},{33,17},{49,33},{2,50}... | collective-permute-start | bytes 786440 | tf_op jit(solution)/shard_map/ppermute | solution.py:429
  59.4 2.6 all-to-all-done.own_ref.rest_0_.rest_2_
  62.0 0.0 collective-permute-done.2.u1
  62.0 2.5 collective-permute-done.3.u2
  64.5 0.7 copy-done.13
  65.2 0.9 collective-permute-done.4.u3
  66.1 1.9 collective-permute-start.5
  68.0 2.6 collective-permute-done.5.oth_ref.rest_1_.rest_3_
  70.7 0.0 copy-done.3
  70.7 4.5 %shard_map.104 = (f32[512,224]{1,0:T(8,128)S(1)}, f32[512,224]{1,0:T(8,128)S(1)}, bf16[8,208,128]{2,1,0:T(8,128)(2,1)S(1)}) custom-call(s32[6]{0:T(128)S(1)} %stack.27.place, bf16[2048,224]{1,0:T(8,128)(2,1)} %copy-done.2, bf16[4,2,64,256]{3,2,1,0:T(8,128)(2,1)} %copy-done.11, bf16[4,2,64,256]{3,2,1,0:T(8,128)(2,1)} %copy-done.12, ...), custom_call_target="tpu_custom_call" | custom-call | tf_op jit(solution)/shard_map/pallas_call | solution.py:46
  75.2 13.1 %all_to_all.60.i_ref = bf16[8,208,128]{2,1,0:T(8,128)(2,1)S(1)} all-to-all(bf16[8,208,128]{2,1,0:T(8,128)(2,1)S(1)} %get-tuple-element.39), channel_id=1, replica_groups=mesh['za'=2,'zb'=4,'x'=4,'y'=4,'zh'=2,'c'=2] {'c','y'}, dimensions={0} | all-to-all | bytes 851968 | tf_op jit(solution)/shard_map/all_to_all | solution.py:391
  88.3 0.1 shard_map.105.mine_ref
  88.3 6.8 %collective-permute-start.6 = (f32[136,128]{1,0:T(8,128)S(1)}, f32[136,128]{1,0:T(8,128)S(1)}, u32[]{:S(2)}, u32[]{:S(2)}) collective-permute-start(f32[136,128]{1,0:T(8,128)S(1)} %shard_map.105.mine_ref), channel_id=1, source_target_pairs={{0,2},{2,0},{1,3},{3,1},{4,6},{6,4},{5,7},{7,5},{8,10},{10,8},{9,1... | collective-permute-start | bytes 208904 | tf_op jit(solution)/shard_map/ppermute | solution.py:387
  95.2 0.1 copy.12.tag_ref
  95.3 8.0 %collective-permute-done.6.their_ref = f32[136,128]{1,0:T(8,128)S(1)} collective-permute-done((f32[136,128]{1,0:T(8,128)S(1)}, f32[136,128]{1,0:T(8,128)S(1)}, u32[]{:S(2)}, u32[]{:S(2)}) %collective-permute-start.6) | collective-permute-done | bytes 69664 | tf_op jit(solution)/shard_map/ppermute | solution.py:387
  103.3 0.6 shard_map.106
  103.9 9.4 %all_to_all.61.m_ref = bf16[8,80,128]{2,1,0:T(8,128)(2,1)S(1)} all-to-all(bf16[8,80,128]{2,1,0:T(8,128)(2,1)S(1)} %get-tuple-element.41), channel_id=1, replica_groups=mesh['za'=2,'zb'=4,'x'=4,'y'=4,'zh'=2,'c'=2] {'c','y'}, dimensions={0} | all-to-all | bytes 327680 | tf_op jit(solution)/shard_map/all_to_all | solution.py:391
  113.3 1.9 shard_map.107
  115.2 18.0 %all_to_all.62.i_ref = bf16[4,8,112,128]{3,2,1,0:T(8,128)(2,1)S(1)} all-to-all(bf16[4,8,112,128]{3,2,1,0:T(8,128)(2,1)S(1)} %shard_map.107), channel_id=1, replica_groups=mesh['za'=2,'zb'=4,'x'=4,'y'=4,'zh'=2,'c'=2] {'x'}, dimensions={0} | all-to-all | bytes 1835008 | tf_op jit(solution)/shard_map/all_to_all | solution.py:391
  133.2 0.1 shard_map.108
  133.3 23.7 %all_to_all.63.i_ref = bf16[8,112,128]{2,1,0:T(8,128)(2,1)S(1)} all-to-all(bf16[8,112,128]{2,1,0:T(8,128)(2,1)S(1)} %shard_map.108), channel_id=1, replica_groups=mesh['za'=2,'zb'=4,'x'=4,'y'=4,'zh'=2,'c'=2] {'za','zb'}, dimensions={0} | all-to-all | bytes 458752 | tf_op jit(solution)/shard_map/all_to_all | solution.py:391
  156.9 0.2 shard_map.109
  157.2 20.5 %all_to_all.64 = bf16[8,64,256]{2,1,0:T(8,128)(2,1)S(1)} all-to-all(bf16[8,64,256]{2,1,0:T(8,128)(2,1)S(1)} %get-tuple-element.44), channel_id=1, replica_groups=mesh['za'=2,'zb'=4,'x'=4,'y'=4,'zh'=2,'c'=2] {'za','zb'}, dimensions={0} | all-to-all | bytes 524288 | tf_op jit(solution)/shard_map/all_to_all | solution.py:391
  177.7 0.1 shard_map.110
  177.8 13.3 %all_to_all.65 = bf16[4,512,256]{2,1,0:T(8,128)(2,1)S(1)} all-to-all(bf16[4,512,256]{2,1,0:T(8,128)(2,1)S(1)} %shard_map.110), channel_id=1, replica_groups=mesh['za'=2,'zb'=4,'x'=4,'y'=4,'zh'=2,'c'=2] {'x'}, dimensions={0} | all-to-all | bytes 2097152 | tf_op jit(solution)/shard_map/all_to_all | solution.py:391
  191.1 2.3 shard_map.111
  193.4 8.3 %all_to_all.66.i_ref = bf16[8,80,128]{2,1,0:T(8,128)(2,1)S(1)} all-to-all(bf16[8,80,128]{2,1,0:T(8,128)(2,1)S(1)} %get-tuple-element.45), channel_id=1, replica_groups=mesh['za'=2,'zb'=4,'x'=4,'y'=4,'zh'=2,'c'=2] {'c','y'}, dimensions={0} | all-to-all | bytes 327680 | tf_op jit(solution)/shard_map/all_to_all | solution.py:391
  201.7 4.1 %collective-permute-start.7 = (f32[72,128]{1,0:T(8,128)S(1)}, f32[72,128]{1,0:T(8,128)S(1)}, u32[]{:S(2)}, u32[]{:S(2)}) collective-permute-start(f32[72,128]{1,0:T(8,128)S(1)} %shard_map.112.mine_ref), channel_id=1, source_target_pairs={{0,2},{2,0},{1,3},{3,1},{4,6},{6,4},{5,7},{7,5},{8,10},{10,8},{9,1... | collective-permute-start | bytes 110600 | tf_op jit(solution)/shard_map/ppermute | solution.py:387
  205.7 10.5 %collective-permute-done.7.their_ref = f32[72,128]{1,0:T(8,128)S(1)} collective-permute-done((f32[72,128]{1,0:T(8,128)S(1)}, f32[72,128]{1,0:T(8,128)S(1)}, u32[]{:S(2)}, u32[]{:S(2)}) %collective-permute-start.7) | collective-permute-done | bytes 36896 | tf_op jit(solution)/shard_map/ppermute | solution.py:387
  216.2 0.6 shard_map.113
  216.8 8.9 %all_to_all.67.m_ref = bf16[8,80,128]{2,1,0:T(8,128)(2,1)S(1)} all-to-all(bf16[8,80,128]{2,1,0:T(8,128)(2,1)S(1)} %get-tuple-element.47), channel_id=1, replica_groups=mesh['za'=2,'zb'=4,'x'=4,'y'=4,'zh'=2,'c'=2] {'c','y'}, dimensions={0} | all-to-all | bytes 327680 | tf_op jit(solution)/shard_map/all_to_all | solution.py:391
  225.8 1.9 shard_map.114
  227.7 16.7 %all_to_all.68.i_ref = bf16[4,8,112,128]{3,2,1,0:T(8,128)(2,1)S(1)} all-to-all(bf16[4,8,112,128]{3,2,1,0:T(8,128)(2,1)S(1)} %shard_map.114), channel_id=1, replica_groups=mesh['za'=2,'zb'=4,'x'=4,'y'=4,'zh'=2,'c'=2] {'x'}, dimensions={0} | all-to-all | bytes 1835008 | tf_op jit(solution)/shard_map/all_to_all | solution.py:391
  244.4 0.1 shard_map.115
  244.5 0.0 copy-start.6
  244.5 23.6 %all_to_all.69.i_ref = bf16[8,112,128]{2,1,0:T(8,128)(2,1)S(1)} all-to-all(bf16[8,112,128]{2,1,0:T(8,128)(2,1)S(1)} %shard_map.115), channel_id=1, replica_groups=mesh['za'=2,'zb'=4,'x'=4,'y'=4,'zh'=2,'c'=2] {'za','zb'}, dimensions={0} | all-to-all | bytes 458752 | tf_op jit(solution)/shard_map/all_to_all | solution.py:391
  268.1 0.7 shard_map.116
  (19 shorter events, 0.1 us)
Async XLA Ops:
  0.0 29.2 %collective-permute-start = (bf16[32,2048]{1,0:T(8,128)(2,1)}, bf16[32,2048]{1,0:T(8,128)(2,1)S(1)}, u32[]{:S(2)}, u32[]{:S(2)}) collective-permute-start(bf16[32,2048]{1,0:T(8,128)(2,1)} %bitcast.26), channel_id=1, source_target_pairs={{0,2},{2,0},{1,3},{3,1},{4,6},{6,4},{5,7},{7,5},{8,10},{10,8},{9,1... | collective-permute-start | bytes 393224 | tf_op jit(solution)/shard_map/ppermute | solution.py:387
  14.8 0.8 copy-start.5
  15.7 20.2 %copy-start.8 = (bf16[1,32,2048]{2,1,0:T(8,128)(2,1)S(1)}, bf16[1,32,2048]{2,1,0:T(8,128)(2,1)}, u32[]{:S(2)}) copy-start(bf16[1,32,2048]{2,1,0:T(8,128)(2,1)} %param.10) | copy-start | bytes 393220
  15.8 13.4 %collective-permute-start.1 = (bf16[64,256]{1,0:T(8,128)(2,1)S(1)}, bf16[64,256]{1,0:T(8,128)(2,1)S(1)}, u32[]{:S(2)}, u32[]{:S(2)}) collective-permute-start(bf16[64,256]{1,0:T(8,128)(2,1)S(1)} %shard_map.100.mine_ref), channel_id=1, source_target_pairs={{0,256},{256,0},{1,257},{257,1},{2,258},{258,2},{3,259},{259,3},{4... | collective-permute-start | bytes 98312 | tf_op jit(solution)/shard_map/ppermute | solution.py:387
  22.0 13.9 %copy-start.10 = (s32[1,4]{1,0:T(1,128)S(1)}, s32[1,4]{1,0:T(1,128)}, u32[]{:S(2)}) copy-start(s32[1,4]{1,0:T(1,128)} %starts.1) | copy-start | bytes 52
  22.1 13.8 %copy-start = (bf16[1,512,1024]{2,1,0:T(8,128)(2,1)S(1)}, bf16[1,512,1024]{2,1,0:T(8,128)(2,1)}, u32[]{:S(2)}) copy-start(bf16[1,512,1024]{2,1,0:T(8,128)(2,1)} %param.11) | copy-start | bytes 3145732
  22.1 13.8 %copy-start.1 = (bf16[1,512,1024]{2,1,0:T(8,128)(2,1)S(1)}, bf16[1,512,1024]{2,1,0:T(8,128)(2,1)}, u32[]{:S(2)}) copy-start(bf16[1,512,1024]{2,1,0:T(8,128)(2,1)} %param.12) | copy-start | bytes 3145732
  22.2 1.3 copy-start.4
  23.5 0.9 copy-start.7
  24.9 1.0 copy-start.2
  30.4 12.8 %all-to-all-start.1 = ((bf16[4,2,64,256]{3,2,1,0:T(8,128)(2,1)}), bf16[4,2,64,256]{3,2,1,0:T(8,128)(2,1)S(1)}, u32[]{:S(2)}, u32[]{:S(2)}) async-start(bf16[4,2,64,256]{3,2,1,0:T(8,128)(2,1)} %shard_map.103), calls=%async_computation.1 | async-start | bytes 524288 | tf_op jit(solution)/shard_map/all_to_all | solution.py:391
  43.3 12.8 %copy-start.11 = (bf16[4,2,64,256]{3,2,1,0:T(8,128)(2,1)}, bf16[4,2,64,256]{3,2,1,0:T(8,128)(2,1)S(1)}, u32[]{:S(2)}) copy-start(bf16[4,2,64,256]{3,2,1,0:T(8,128)(2,1)S(1)} %all-to-all-done.1.u0) | copy-start | bytes 786436
  43.3 27.4 %copy-start.3 = (bf16[224,128]{1,0:T(8,128)(2,1)S(1)}, bf16[224,128]{1,0:T(8,128)(2,1)}, u32[]{:S(2)}) copy-start(bf16[224,128]{1,0:T(8,128)(2,1)} %rest_5_.1) | copy-start | bytes 172036
  43.3 18.7 %all-to-all-start = ((bf16[4,64,2048]{2,1,0:T(8,128)(2,1)}), bf16[4,64,2048]{2,1,0:T(8,128)(2,1)S(1)}, u32[]{:S(2)}, u32[]{:S(2)}) async-start(bf16[4,64,2048]{2,1,0:T(8,128)(2,1)} %bitcast.14), calls=%async_computation | async-start | bytes 2097152 | tf_op jit(solution)/shard_map/all_to_all | solution.py:391
  47.9 22.8 %copy-start.9 = (f32[224]{0:T(256)S(1)}, f32[224]{0:T(256)}, u32[]{:S(2)}) copy-start(f32[224]{0:T(256)} %param.15) | copy-start | bytes 2692
  47.9 14.1 %collective-permute-start.2 = (bf16[4,2,64,256]{3,2,1,0:T(8,128)(2,1)S(1)}, bf16[4,2,64,256]{3,2,1,0:T(8,128)(2,1)S(1)}, u32[]{:S(2)}, u32[]{:S(2)}) collective-permute-start(bf16[4,2,64,256]{3,2,1,0:T(8,128)(2,1)S(1)} %all-to-all-done.1.u0), channel_id=1, source_target_pairs={{0,16},{16,32},{32,48},{48,0},{1,17},{17,33},{33,49},{49,1},{2,18}... | collective-permute-start | bytes 786440 | tf_op jit(solution)/shard_map/ppermute | solution.py:429
  51.4 13.1 %collective-permute-start.3 = (bf16[4,2,64,256]{3,2,1,0:T(8,128)(2,1)S(1)}, bf16[4,2,64,256]{3,2,1,0:T(8,128)(2,1)S(1)}, u32[]{:S(2)}, u32[]{:S(2)}) collective-permute-start(bf16[4,2,64,256]{3,2,1,0:T(8,128)(2,1)S(1)} %all-to-all-done.1.u0), channel_id=1, source_target_pairs={{0,32},{16,48},{32,0},{48,16},{1,33},{17,49},{33,1},{49,17},{2,34}... | collective-permute-start | bytes 786440 | tf_op jit(solution)/shard_map/ppermute | solution.py:429
  56.0 10.1 %collective-permute-start.4 = (bf16[4,2,64,256]{3,2,1,0:T(8,128)(2,1)S(1)}, bf16[4,2,64,256]{3,2,1,0:T(8,128)(2,1)}, u32[]{:S(2)}, u32[]{:S(2)}) collective-permute-start(bf16[4,2,64,256]{3,2,1,0:T(8,128)(2,1)S(1)} %all-to-all-done.1.u0), channel_id=1, source_target_pairs={{0,48},{16,0},{32,16},{48,32},{1,49},{17,1},{33,17},{49,33},{2,50}... | collective-permute-start | bytes 786440 | tf_op jit(solution)/shard_map/ppermute | solution.py:429
  62.0 8.7 %copy-start.12 = (bf16[4,2,64,256]{3,2,1,0:T(8,128)(2,1)}, bf16[4,2,64,256]{3,2,1,0:T(8,128)(2,1)S(1)}, u32[]{:S(2)}) copy-start(bf16[4,2,64,256]{3,2,1,0:T(8,128)(2,1)S(1)} %collective-permute-done.2.u1) | copy-start | bytes 786436
  64.5 0.7 copy-start.13
  66.1 4.5 %collective-permute-start.5 = (bf16[4,64,2048]{2,1,0:T(8,128)(2,1)S(1)}, bf16[4,64,2048]{2,1,0:T(8,128)(2,1)S(1)}, u32[]{:S(2)}, u32[]{:S(2)}) collective-permute-start(bf16[4,64,2048]{2,1,0:T(8,128)(2,1)S(1)} %all-to-all-done.own_ref.rest_0_.rest_2_), channel_id=1, source_target_pairs={{0,1},{1,0},{2,3},{3,2},{4,5},{5,4},{6,7},{7,6},{8,9},{9,8},{10,11... | collective-permute-start | bytes 3145736 | tf_op jit(solution)/shard_map/ppermute | solution.py:387
  88.3 15.0 %collective-permute-start.6 = (f32[136,128]{1,0:T(8,128)S(1)}, f32[136,128]{1,0:T(8,128)S(1)}, u32[]{:S(2)}, u32[]{:S(2)}) collective-permute-start(f32[136,128]{1,0:T(8,128)S(1)} %shard_map.105.mine_ref), channel_id=1, source_target_pairs={{0,2},{2,0},{1,3},{3,1},{4,6},{6,4},{5,7},{7,5},{8,10},{10,8},{9,1... | collective-permute-start | bytes 208904 | tf_op jit(solution)/shard_map/ppermute | solution.py:387
  201.7 14.6 %collective-permute-start.7 = (f32[72,128]{1,0:T(8,128)S(1)}, f32[72,128]{1,0:T(8,128)S(1)}, u32[]{:S(2)}, u32[]{:S(2)}) collective-permute-start(f32[72,128]{1,0:T(8,128)S(1)} %shard_map.112.mine_ref), channel_id=1, source_target_pairs={{0,2},{2,0},{1,3},{3,1},{4,6},{6,4},{5,7},{7,5},{8,10},{10,8},{9,1... | collective-permute-start | bytes 110600 | tf_op jit(solution)/shard_map/ppermute | solution.py:387
  244.5 23.6 %copy-start.6 = (f32[64,224]{1,0:T(8,128)S(1)}, f32[64,224]{1,0:T(8,128)}, u32[]{:S(2)}) copy-start(f32[64,224]{1,0:T(8,128)} %d_ref.3) | copy-start | bytes 172036

commit v13 on v12

--- a/solution.py
+++ b/solution.py
@@ -409,9 +409,8 @@
         out_proj.T,
         stream[0].T,
     )
-    theirs, far, proj, toks, own_tags = lax.optimization_barrier(
-        (swap(queries[0], "zh"), swap(row, "za"), proj, toks, own_tags)
-    )
+    theirs = swap(queries[0], "zh")
+    far, proj, toks, own_tags = lax.optimization_barrier((swap(row, "za"), proj, toks, own_tags))
     pairs = call(pair_kernel, shape(ZB, ZA, 64, WIDE, dtype=BF), place, row, far, smem=1)
     by_zl = deal(pairs, "zb")
     pair = call(

time: 270 us -> 273 us (1.011)
  starting transfers between devices: 53.5 us -> 60.9 us
  blocking collectives: 156 us -> 150 us
    ppermute x5, waiting for transfers between devices: 24.4 us -> 31.7 us  [swap(): return lax.ppermute(x, axis, [(0, 1), (1, 0)])]
    ppermute x5, starting transfers between devices: 31.9 us -> 38.8 us  [swap(): return lax.ppermute(x, axis, [(0, 1), (1, 0)])]
    all_to_all x2, waiting for transfers between devices: 6.87 us -> 0.01 us  [deal(): return lax.all_to_all(x, axis, 0, 0, tiled=True)]
    all_to_all x10, blocking collectives: 156 us -> 150 us  [deal(): return lax.all_to_all(x, axis, 0, 0, tiled=True)]
  transfers between devices with their start and end apart: 10 -> 10, of which waited for: 8 -> 6; matrix products, arithmetic and copies ran while one was open for 1% -> 1% of each run, Pallas kernels for 1% -> 1%
where the time goes in v13:
time: 273 us; the launch traced here: 272 us
  blocking collectives  150 us (55%)
  starting transfers between devices  60.9 us (22%)
  waiting for transfers between devices  36 us (13%)
  Pallas kernels  18 us (7%)
  local copies, waits for them, and re-layouts  5.7 us (2%)
    all_to_all x10, blocking collectives, deal(): return lax.all_to_all(x, axis, 0, 0, tiled=True)  150 us
    ppermute x5, starting transfers between devices, swap(): return lax.ppermute(x, axis, [(0, 1), (1, 0)])  38.8 us
    ppermute x5, waiting for transfers between devices, swap(): return lax.ppermute(x, axis, [(0, 1), (1, 0)])  31.7 us
    pallas_call x17, Pallas kernels, call(): pl.pallas_call(kernel, out_shape=out_shape, in_specs=specs, out_specs=[vm...  18 us
    ppermute x3, starting transfers between devices, local(): lax.ppermute(by_zl, 'x', [(i, (i + r) % X) for i in range(X)])  11.5 us
    all_to_all x2, starting transfers between devices, deal(): return lax.all_to_all(x, axis, 0, 0, tiled=True)  10.6 us
  transfers between devices with their start and end apart: 10, of which 6 were waited for; matrix products, arithmetic and copies ran while one was open for 1% of the time, Pallas kernels for 1%

profile of v13, /device:TPU:32, one launch (start us, length us, event | category | flops | bytes accessed | tf_op | source)
XLA Modules:
  0.0 272.1 jit_solution(4142162686249364512)
XLA Ops:
  0.0 0.8 copy-done.5
  0.8 0.2 shard_map.100.mine_ref
  1.0 9.1 %collective-permute-start = (bf16[64,256]{1,0:T(8,128)(2,1)S(1)}, bf16[64,256]{1,0:T(8,128)(2,1)S(1)}, u32[]{:S(2)}, u32[]{:S(2)}) collective-permute-start(bf16[64,256]{1,0:T(8,128)(2,1)S(1)} %shard_map.100.mine_ref), channel_id=1, source_target_pairs={{0,256},{256,0},{1,257},{257,1},{2,258},{258,2},{3,259},{259,3},{4... | collective-permute-start | bytes 98312 | tf_op jit(solution)/shard_map/ppermute | solution.py:387
  10.1 0.5 broadcast.3
  10.6 1.3 reduce.3
  12.0 0.1 reshape_squeeze.3
  12.1 0.1 reshape.12
  12.2 1.3 copy-done.4
  13.5 0.9 copy-done.7
  14.4 0.4 shard_map.101
  14.8 0.0 copy-start.2
  14.8 1.0 copy-done.2
  15.8 0.1 stack.27.place
  15.9 0.0 collective-permute-done.their_ref
  15.9 1.3 shard_map.103
  17.2 6.0 %all-to-all-start.1 = ((bf16[4,2,64,256]{3,2,1,0:T(8,128)(2,1)}), bf16[4,2,64,256]{3,2,1,0:T(8,128)(2,1)S(1)}, u32[]{:S(2)}, u32[]{:S(2)}) async-start(bf16[4,2,64,256]{3,2,1,0:T(8,128)(2,1)} %shard_map.103), calls=%async_computation.1 | async-start | bytes 524288 | tf_op jit(solution)/shard_map/all_to_all | solution.py:391
  23.2 0.0 copy-done.8
  23.2 9.5 %collective-permute-start.1 = (bf16[32,2048]{1,0:T(8,128)(2,1)S(1)}, bf16[32,2048]{1,0:T(8,128)(2,1)S(1)}, u32[]{:S(2)}, u32[]{:S(2)}) collective-permute-start(bf16[32,2048]{1,0:T(8,128)(2,1)S(1)} %bitcast.26), channel_id=1, source_target_pairs={{0,2},{2,0},{1,3},{3,1},{4,6},{6,4},{5,7},{7,5},{8,10},{10,8},{9,1... | collective-permute-start | bytes 393224 | tf_op jit(solution)/shard_map/ppermute | solution.py:387
  32.7 13.4 %collective-permute-done.1.oth_ref = bf16[32,2048]{1,0:T(8,128)(2,1)S(1)} collective-permute-done((bf16[32,2048]{1,0:T(8,128)(2,1)S(1)}, bf16[32,2048]{1,0:T(8,128)(2,1)S(1)}, u32[]{:S(2)}, u32[]{:S(2)}) %collective-permute-start.1) | collective-permute-done | bytes 131104 | tf_op jit(solution)/shard_map/ppermute | solution.py:387
  46.1 0.0 copy-done.10
  46.1 0.0 copy-done
  46.1 3.1 %shard_map.102 = bf16[4,2,32,2048]{3,2,1,0:T(8,128)(2,1)} custom-call(s32[6]{0:T(128)S(1)} %stack.27.place, s32[1,4]{1,0:T(1,128)S(1)} %copy-done.10, bf16[512,1024]{1,0:T(8,128)(2,1)S(1)} %bitcast.22, bf16[512,1024]{1,0:T(8,128)(2,1)S(1)} %bitcast.23, bf16[32,2048]{1,0:T(8,128)(2,1)S(1)} %bitcast.27, bf16[32,2048]{1,0:T(8,128)(2,1)S(1)} %collective-permute-done.1.oth_ref), custom_call_target="tpu_custom_call" | custom-call | tf_op jit(solution)/shard_map/pallas_call | solution.py:46
  49.2 0.0 all-to-all-done.1.u0
  49.2 4.6 %all-to-all-start = ((bf16[4,64,2048]{2,1,0:T(8,128)(2,1)}), bf16[4,64,2048]{2,1,0:T(8,128)(2,1)S(1)}, u32[]{:S(2)}, u32[]{:S(2)}) async-start(bf16[4,64,2048]{2,1,0:T(8,128)(2,1)} %bitcast.14), calls=%async_computation | async-start | bytes 2097152 | tf_op jit(solution)/shard_map/all_to_all | solution.py:391
  53.8 3.5 %collective-permute-start.2 = (bf16[4,2,64,256]{3,2,1,0:T(8,128)(2,1)S(1)}, bf16[4,2,64,256]{3,2,1,0:T(8,128)(2,1)S(1)}, u32[]{:S(2)}, u32[]{:S(2)}) collective-permute-start(bf16[4,2,64,256]{3,2,1,0:T(8,128)(2,1)S(1)} %all-to-all-done.1.u0), channel_id=1, source_target_pairs={{0,16},{16,32},{32,48},{48,0},{1,17},{17,33},{33,49},{49,1},{2,18}... | collective-permute-start | bytes 786440 | tf_op jit(solution)/shard_map/ppermute | solution.py:428
  57.4 4.6 %collective-permute-start.3 = (bf16[4,2,64,256]{3,2,1,0:T(8,128)(2,1)S(1)}, bf16[4,2,64,256]{3,2,1,0:T(8,128)(2,1)S(1)}, u32[]{:S(2)}, u32[]{:S(2)}) collective-permute-start(bf16[4,2,64,256]{3,2,1,0:T(8,128)(2,1)S(1)} %all-to-all-done.1.u0), channel_id=1, source_target_pairs={{0,32},{16,48},{32,0},{48,16},{1,33},{17,49},{33,1},{49,17},{2,34}... | collective-permute-start | bytes 786440 | tf_op jit(solution)/shard_map/ppermute | solution.py:428
  62.0 3.3 %collective-permute-start.4 = (bf16[4,2,64,256]{3,2,1,0:T(8,128)(2,1)S(1)}, bf16[4,2,64,256]{3,2,1,0:T(8,128)(2,1)}, u32[]{:S(2)}, u32[]{:S(2)}) collective-permute-start(bf16[4,2,64,256]{3,2,1,0:T(8,128)(2,1)S(1)} %all-to-all-done.1.u0), channel_id=1, source_target_pairs={{0,48},{16,0},{32,16},{48,32},{1,49},{17,1},{33,17},{49,33},{2,50}... | collective-permute-start | bytes 786440 | tf_op jit(solution)/shard_map/ppermute | solution.py:428
  65.4 0.0 all-to-all-done.own_ref.rest_0_.rest_2_
  65.4 0.0 collective-permute-done.2.u1
  65.4 2.4 collective-permute-done.3.u2
  67.8 0.7 copy-done.13
  68.5 1.9 collective-permute-done.4.u3
  70.4 1.9 collective-permute-start.5
  72.3 2.6 collective-permute-done.5.oth_ref.rest_1_.rest_3_
  74.9 0.0 copy-done.9
  74.9 4.5 %shard_map.104 = (f32[512,224]{1,0:T(8,128)S(1)}, f32[512,224]{1,0:T(8,128)S(1)}, bf16[8,208,128]{2,1,0:T(8,128)(2,1)S(1)}) custom-call(s32[6]{0:T(128)S(1)} %stack.27.place, bf16[2048,224]{1,0:T(8,128)(2,1)} %copy-done.2, bf16[4,2,64,256]{3,2,1,0:T(8,128)(2,1)} %copy-done.11, bf16[4,2,64,256]{3,2,1,0:T(8,128)(2,1)} %copy-done.12, ...), custom_call_target="tpu_custom_call" | custom-call | tf_op jit(solution)/shard_map/pallas_call | solution.py:46
  79.4 13.3 %all_to_all.60.i_ref = bf16[8,208,128]{2,1,0:T(8,128)(2,1)S(1)} all-to-all(bf16[8,208,128]{2,1,0:T(8,128)(2,1)S(1)} %get-tuple-element.37), channel_id=1, replica_groups=mesh['za'=2,'zb'=4,'x'=4,'y'=4,'zh'=2,'c'=2] {'c','y'}, dimensions={0} | all-to-all | bytes 851968 | tf_op jit(solution)/shard_map/all_to_all | solution.py:391
  92.7 0.1 shard_map.105.mine_ref
  92.8 8.2 %collective-permute-start.6 = (f32[136,128]{1,0:T(8,128)S(1)}, f32[136,128]{1,0:T(8,128)S(1)}, u32[]{:S(2)}, u32[]{:S(2)}) collective-permute-start(f32[136,128]{1,0:T(8,128)S(1)} %shard_map.105.mine_ref), channel_id=1, source_target_pairs={{0,2},{2,0},{1,3},{3,1},{4,6},{6,4},{5,7},{7,5},{8,10},{10,8},{9,1... | collective-permute-start | bytes 208904 | tf_op jit(solution)/shard_map/ppermute | solution.py:387
  101.0 0.1 copy.12.tag_ref
  101.1 11.1 %collective-permute-done.6.their_ref = f32[136,128]{1,0:T(8,128)S(1)} collective-permute-done((f32[136,128]{1,0:T(8,128)S(1)}, f32[136,128]{1,0:T(8,128)S(1)}, u32[]{:S(2)}, u32[]{:S(2)}) %collective-permute-start.6) | collective-permute-done | bytes 69664 | tf_op jit(solution)/shard_map/ppermute | solution.py:387
  112.2 0.6 shard_map.106
  112.8 8.2 %all_to_all.61.m_ref = bf16[8,80,128]{2,1,0:T(8,128)(2,1)S(1)} all-to-all(bf16[8,80,128]{2,1,0:T(8,128)(2,1)S(1)} %get-tuple-element.39), channel_id=1, replica_groups=mesh['za'=2,'zb'=4,'x'=4,'y'=4,'zh'=2,'c'=2] {'c','y'}, dimensions={0} | all-to-all | bytes 327680 | tf_op jit(solution)/shard_map/all_to_all | solution.py:391
  121.0 1.9 shard_map.107
  122.9 17.7 %all_to_all.62.i_ref = bf16[4,8,112,128]{3,2,1,0:T(8,128)(2,1)S(1)} all-to-all(bf16[4,8,112,128]{3,2,1,0:T(8,128)(2,1)S(1)} %shard_map.107), channel_id=1, replica_groups=mesh['za'=2,'zb'=4,'x'=4,'y'=4,'zh'=2,'c'=2] {'x'}, dimensions={0} | all-to-all | bytes 1835008 | tf_op jit(solution)/shard_map/all_to_all | solution.py:391
  140.6 0.1 shard_map.108
  140.7 19.0 %all_to_all.63.i_ref = bf16[8,112,128]{2,1,0:T(8,128)(2,1)S(1)} all-to-all(bf16[8,112,128]{2,1,0:T(8,128)(2,1)S(1)} %shard_map.108), channel_id=1, replica_groups=mesh['za'=2,'zb'=4,'x'=4,'y'=4,'zh'=2,'c'=2] {'za','zb'}, dimensions={0} | all-to-all | bytes 458752 | tf_op jit(solution)/shard_map/all_to_all | solution.py:391
  159.8 0.2 shard_map.109
  160.0 20.5 %all_to_all.64 = bf16[8,64,256]{2,1,0:T(8,128)(2,1)S(1)} all-to-all(bf16[8,64,256]{2,1,0:T(8,128)(2,1)S(1)} %get-tuple-element.42), channel_id=1, replica_groups=mesh['za'=2,'zb'=4,'x'=4,'y'=4,'zh'=2,'c'=2] {'za','zb'}, dimensions={0} | all-to-all | bytes 524288 | tf_op jit(solution)/shard_map/all_to_all | solution.py:391
  180.5 0.1 shard_map.110
  180.6 13.3 %all_to_all.65 = bf16[4,512,256]{2,1,0:T(8,128)(2,1)S(1)} all-to-all(bf16[4,512,256]{2,1,0:T(8,128)(2,1)S(1)} %shard_map.110), channel_id=1, replica_groups=mesh['za'=2,'zb'=4,'x'=4,'y'=4,'zh'=2,'c'=2] {'x'}, dimensions={0} | all-to-all | bytes 2097152 | tf_op jit(solution)/shard_map/all_to_all | solution.py:391
  193.9 2.3 shard_map.111
  196.2 8.3 %all_to_all.66.i_ref = bf16[8,80,128]{2,1,0:T(8,128)(2,1)S(1)} all-to-all(bf16[8,80,128]{2,1,0:T(8,128)(2,1)S(1)} %get-tuple-element.43), channel_id=1, replica_groups=mesh['za'=2,'zb'=4,'x'=4,'y'=4,'zh'=2,'c'=2] {'c','y'}, dimensions={0} | all-to-all | bytes 327680 | tf_op jit(solution)/shard_map/all_to_all | solution.py:391
  204.5 10.1 %collective-permute-start.7 = (f32[72,128]{1,0:T(8,128)S(1)}, f32[72,128]{1,0:T(8,128)S(1)}, u32[]{:S(2)}, u32[]{:S(2)}) collective-permute-start(f32[72,128]{1,0:T(8,128)S(1)} %shard_map.112.mine_ref), channel_id=1, source_target_pairs={{0,2},{2,0},{1,3},{3,1},{4,6},{6,4},{5,7},{7,5},{8,10},{10,8},{9,1... | collective-permute-start | bytes 110600 | tf_op jit(solution)/shard_map/ppermute | solution.py:387
  214.6 4.5 %collective-permute-done.7.their_ref = f32[72,128]{1,0:T(8,128)S(1)} collective-permute-done((f32[72,128]{1,0:T(8,128)S(1)}, f32[72,128]{1,0:T(8,128)S(1)}, u32[]{:S(2)}, u32[]{:S(2)}) %collective-permute-start.7) | collective-permute-done | bytes 36896 | tf_op jit(solution)/shard_map/ppermute | solution.py:387
  219.1 0.6 shard_map.113
  219.7 9.2 %all_to_all.67.m_ref = bf16[8,80,128]{2,1,0:T(8,128)(2,1)S(1)} all-to-all(bf16[8,80,128]{2,1,0:T(8,128)(2,1)S(1)} %get-tuple-element.45), channel_id=1, replica_groups=mesh['za'=2,'zb'=4,'x'=4,'y'=4,'zh'=2,'c'=2] {'c','y'}, dimensions={0} | all-to-all | bytes 327680 | tf_op jit(solution)/shard_map/all_to_all | solution.py:391
  229.0 1.9 shard_map.114
  230.9 16.7 %all_to_all.68.i_ref = bf16[4,8,112,128]{3,2,1,0:T(8,128)(2,1)S(1)} all-to-all(bf16[4,8,112,128]{3,2,1,0:T(8,128)(2,1)S(1)} %shard_map.114), channel_id=1, replica_groups=mesh['za'=2,'zb'=4,'x'=4,'y'=4,'zh'=2,'c'=2] {'x'}, dimensions={0} | all-to-all | bytes 1835008 | tf_op jit(solution)/shard_map/all_to_all | solution.py:391
  247.6 0.1 shard_map.115
  247.7 0.0 copy-start.6
  247.7 23.7 %all_to_all.69.i_ref = bf16[8,112,128]{2,1,0:T(8,128)(2,1)S(1)} all-to-all(bf16[8,112,128]{2,1,0:T(8,128)(2,1)S(1)} %shard_map.115), channel_id=1, replica_groups=mesh['za'=2,'zb'=4,'x'=4,'y'=4,'zh'=2,'c'=2] {'za','zb'}, dimensions={0} | all-to-all | bytes 458752 | tf_op jit(solution)/shard_map/all_to_all | solution.py:391
  271.4 0.0 copy-done.6
  271.4 0.7 shard_map.116
  (19 shorter events, 0.1 us)
Async XLA Ops:
  0.0 0.8 copy-start.5
  0.8 22.3 %copy-start.8 = (bf16[1,32,2048]{2,1,0:T(8,128)(2,1)S(1)}, bf16[1,32,2048]{2,1,0:T(8,128)(2,1)}, u32[]{:S(2)}) copy-start(bf16[1,32,2048]{2,1,0:T(8,128)(2,1)} %param.10) | copy-start | bytes 393220
  1.0 14.9 %collective-permute-start = (bf16[64,256]{1,0:T(8,128)(2,1)S(1)}, bf16[64,256]{1,0:T(8,128)(2,1)S(1)}, u32[]{:S(2)}, u32[]{:S(2)}) collective-permute-start(bf16[64,256]{1,0:T(8,128)(2,1)S(1)} %shard_map.100.mine_ref), channel_id=1, source_target_pairs={{0,256},{256,0},{1,257},{257,1},{2,258},{258,2},{3,259},{259,3},{4... | collective-permute-start | bytes 98312 | tf_op jit(solution)/shard_map/ppermute | solution.py:387
  12.0 34.1 %copy-start.10 = (s32[1,4]{1,0:T(1,128)S(1)}, s32[1,4]{1,0:T(1,128)}, u32[]{:S(2)}) copy-start(s32[1,4]{1,0:T(1,128)} %starts.1) | copy-start | bytes 52
  12.1 34.1 %copy-start = (bf16[1,512,1024]{2,1,0:T(8,128)(2,1)S(1)}, bf16[1,512,1024]{2,1,0:T(8,128)(2,1)}, u32[]{:S(2)}) copy-start(bf16[1,512,1024]{2,1,0:T(8,128)(2,1)} %param.11) | copy-start | bytes 3145732
  12.1 34.1 %copy-start.1 = (bf16[1,512,1024]{2,1,0:T(8,128)(2,1)S(1)}, bf16[1,512,1024]{2,1,0:T(8,128)(2,1)}, u32[]{:S(2)}) copy-start(bf16[1,512,1024]{2,1,0:T(8,128)(2,1)} %param.12) | copy-start | bytes 3145732
  12.2 1.3 copy-start.4
  13.5 0.9 copy-start.7
  14.8 1.0 copy-start.2
  17.2 32.0 %all-to-all-start.1 = ((bf16[4,2,64,256]{3,2,1,0:T(8,128)(2,1)}), bf16[4,2,64,256]{3,2,1,0:T(8,128)(2,1)S(1)}, u32[]{:S(2)}, u32[]{:S(2)}) async-start(bf16[4,2,64,256]{3,2,1,0:T(8,128)(2,1)} %shard_map.103), calls=%async_computation.1 | async-start | bytes 524288 | tf_op jit(solution)/shard_map/all_to_all | solution.py:391
  23.2 22.9 %collective-permute-start.1 = (bf16[32,2048]{1,0:T(8,128)(2,1)S(1)}, bf16[32,2048]{1,0:T(8,128)(2,1)S(1)}, u32[]{:S(2)}, u32[]{:S(2)}) collective-permute-start(bf16[32,2048]{1,0:T(8,128)(2,1)S(1)} %bitcast.26), channel_id=1, source_target_pairs={{0,2},{2,0},{1,3},{3,1},{4,6},{6,4},{5,7},{7,5},{8,10},{10,8},{9,1... | collective-permute-start | bytes 393224 | tf_op jit(solution)/shard_map/ppermute | solution.py:387
  49.2 12.8 %copy-start.11 = (bf16[4,2,64,256]{3,2,1,0:T(8,128)(2,1)}, bf16[4,2,64,256]{3,2,1,0:T(8,128)(2,1)S(1)}, u32[]{:S(2)}) copy-start(bf16[4,2,64,256]{3,2,1,0:T(8,128)(2,1)S(1)} %all-to-all-done.1.u0) | copy-start | bytes 786436
  49.2 25.7 %copy-start.3 = (bf16[224,128]{1,0:T(8,128)(2,1)S(1)}, bf16[224,128]{1,0:T(8,128)(2,1)}, u32[]{:S(2)}) copy-start(bf16[224,128]{1,0:T(8,128)(2,1)} %rest_5_.1) | copy-start | bytes 172036
  49.2 16.1 %all-to-all-start = ((bf16[4,64,2048]{2,1,0:T(8,128)(2,1)}), bf16[4,64,2048]{2,1,0:T(8,128)(2,1)S(1)}, u32[]{:S(2)}, u32[]{:S(2)}) async-start(bf16[4,64,2048]{2,1,0:T(8,128)(2,1)} %bitcast.14), calls=%async_computation | async-start | bytes 2097152 | tf_op jit(solution)/shard_map/all_to_all | solution.py:391
  53.8 21.1 %copy-start.9 = (f32[224]{0:T(256)S(1)}, f32[224]{0:T(256)}, u32[]{:S(2)}) copy-start(f32[224]{0:T(256)} %param.15) | copy-start | bytes 2692
  53.8 11.5 %collective-permute-start.2 = (bf16[4,2,64,256]{3,2,1,0:T(8,128)(2,1)S(1)}, bf16[4,2,64,256]{3,2,1,0:T(8,128)(2,1)S(1)}, u32[]{:S(2)}, u32[]{:S(2)}) collective-permute-start(bf16[4,2,64,256]{3,2,1,0:T(8,128)(2,1)S(1)} %all-to-all-done.1.u0), channel_id=1, source_target_pairs={{0,16},{16,32},{32,48},{48,0},{1,17},{17,33},{33,49},{49,1},{2,18}... | collective-permute-start | bytes 786440 | tf_op jit(solution)/shard_map/ppermute | solution.py:428
  57.4 10.4 %collective-permute-start.3 = (bf16[4,2,64,256]{3,2,1,0:T(8,128)(2,1)S(1)}, bf16[4,2,64,256]{3,2,1,0:T(8,128)(2,1)S(1)}, u32[]{:S(2)}, u32[]{:S(2)}) collective-permute-start(bf16[4,2,64,256]{3,2,1,0:T(8,128)(2,1)S(1)} %all-to-all-done.1.u0), channel_id=1, source_target_pairs={{0,32},{16,48},{32,0},{48,16},{1,33},{17,49},{33,1},{49,17},{2,34}... | collective-permute-start | bytes 786440 | tf_op jit(solution)/shard_map/ppermute | solution.py:428
  62.0 8.4 %collective-permute-start.4 = (bf16[4,2,64,256]{3,2,1,0:T(8,128)(2,1)S(1)}, bf16[4,2,64,256]{3,2,1,0:T(8,128)(2,1)}, u32[]{:S(2)}, u32[]{:S(2)}) collective-permute-start(bf16[4,2,64,256]{3,2,1,0:T(8,128)(2,1)S(1)} %all-to-all-done.1.u0), channel_id=1, source_target_pairs={{0,48},{16,0},{32,16},{48,32},{1,49},{17,1},{33,17},{49,33},{2,50}... | collective-permute-start | bytes 786440 | tf_op jit(solution)/shard_map/ppermute | solution.py:428
  65.4 9.5 %copy-start.12 = (bf16[4,2,64,256]{3,2,1,0:T(8,128)(2,1)}, bf16[4,2,64,256]{3,2,1,0:T(8,128)(2,1)S(1)}, u32[]{:S(2)}) copy-start(bf16[4,2,64,256]{3,2,1,0:T(8,128)(2,1)S(1)} %collective-permute-done.2.u1) | copy-start | bytes 786436
  67.8 0.7 copy-start.13
  70.4 4.5 %collective-permute-start.5 = (bf16[4,64,2048]{2,1,0:T(8,128)(2,1)S(1)}, bf16[4,64,2048]{2,1,0:T(8,128)(2,1)S(1)}, u32[]{:S(2)}, u32[]{:S(2)}) collective-permute-start(bf16[4,64,2048]{2,1,0:T(8,128)(2,1)S(1)} %all-to-all-done.own_ref.rest_0_.rest_2_), channel_id=1, source_target_pairs={{0,1},{1,0},{2,3},{3,2},{4,5},{5,4},{6,7},{7,6},{8,9},{9,8},{10,11... | collective-permute-start | bytes 3145736 | tf_op jit(solution)/shard_map/ppermute | solution.py:387
  92.8 19.4 %collective-permute-start.6 = (f32[136,128]{1,0:T(8,128)S(1)}, f32[136,128]{1,0:T(8,128)S(1)}, u32[]{:S(2)}, u32[]{:S(2)}) collective-permute-start(f32[136,128]{1,0:T(8,128)S(1)} %shard_map.105.mine_ref), channel_id=1, source_target_pairs={{0,2},{2,0},{1,3},{3,1},{4,6},{6,4},{5,7},{7,5},{8,10},{10,8},{9,1... | collective-permute-start | bytes 208904 | tf_op jit(solution)/shard_map/ppermute | solution.py:387
  204.5 14.6 %collective-permute-start.7 = (f32[72,128]{1,0:T(8,128)S(1)}, f32[72,128]{1,0:T(8,128)S(1)}, u32[]{:S(2)}, u32[]{:S(2)}) collective-permute-start(f32[72,128]{1,0:T(8,128)S(1)} %shard_map.112.mine_ref), channel_id=1, source_target_pairs={{0,2},{2,0},{1,3},{3,1},{4,6},{6,4},{5,7},{7,5},{8,10},{10,8},{9,1... | collective-permute-start | bytes 110600 | tf_op jit(solution)/shard_map/ppermute | solution.py:387
  247.7 23.7 %copy-start.6 = (f32[64,224]{1,0:T(8,128)S(1)}, f32[64,224]{1,0:T(8,128)}, u32[]{:S(2)}) copy-start(f32[64,224]{1,0:T(8,128)} %d_ref.3) | copy-start | bytes 172036
